TPU v7x, 32 devices: a whole 2x2x4 slice. The times are simulated.
32 devices in a mesh: depth: 4 (over x, core), sx: 4 (over z), sy: 2 (over y).
Axes of the slice: x: 2, y: 2, z: 4, core: 2. Of those that a mesh axis runs over, the one named last changes fastest.
Arguments:
- density: float32 [128, 64, 1024], P('sx', 'sy', 'depth'), may hold values from -6 to 6
- kernel_taps: bfloat16 [2, 33], replicated, may hold values from 0.099609375 to 0.3984375
- tf_centre: float32 [8, 4], replicated, may hold values from -2 to 2
- tf_width: float32 [8, 4], replicated, may hold values from 0.4 to 1.5
- tf_color: float32 [8, 4, 3], replicated, may hold values from 0.05 to 1
- tf_opacity: float32 [8, 4], replicated, may hold values from 0.0005 to 0.004
- brick_tf: int32 [8, 4, 8], P('sx', 'sy', 'depth'), may hold values from 0 to 7
- view_order: int32 [8, 4], P('sx', 'sy'), may hold values from 0 to 1
Outputs:
- picture: float32 [4, 4, 4, 8, 64], P(None, 'sx', 'depth', None, 'sy')
Inputs may be any that keep to these rules, and one draw needn't show every extreme that they name: `view_order`: 0: the viewer of that column of bricks faces z = 0; 1: it faces z = 1023.
All inputs are finite; a program needn't handle non-finite values.
Results may differ from a plain program's by a relative error of at most 0.0003.
Values may be sent and summed in bfloat16 or wider, within the bound.
No kernel may reach another device: no remote copies, remote signals or barrier semaphores. Data moves between devices by JAX's collectives and lax.ppermute only.
A program may use at most 64 MiB of HBM per device.

v0:
```python
import functools
import math
import jax
import jax.numpy as jnp
from jax import lax
from jax.experimental import pallas as pl
from jax.experimental.pallas import tpu as pltpu
from jax.sharding import PartitionSpec as P

LOG2E = math.log2(math.e)
VMEM = pl.BlockSpec(memory_space=pltpu.VMEM)
HBM = pl.BlockSpec(memory_space=pltpu.HBM)
MIB = 1024 * 1024
F32, BF16 = jnp.float32, jnp.bfloat16


def iota(shape, dim):
    return lax.broadcasted_iota(jnp.int32, shape, dim)


def line_swaps(count, shift):
    pairs = [(i, i + 1) for i in range(shift, count - 1, 2)]
    return pairs + [(b, a) for a, b in pairs]


class Place:
    def __init__(self):
        self.depth = lax.axis_index("depth")
        x_parity = lax.rem(lax.axis_index("sx") + self.depth, 2)
        y_parity = lax.rem(lax.axis_index("sy"), 2)
        self.half = (1 - x_parity, x_parity)
        self.group = (1 - y_parity, y_parity)


def group_rows(place, rim, g):
    return pl.ds(pl.multiple_of(place.group[g] * rim, rim), rim)


def half_rows(place, rim, h):
    return pl.ds(place.half[h] * rim, rim)


def first_kernel(rim, density, coarse, held, sems):
    place = Place()
    pieces = 4
    size = rim // pieces
    copies = []
    for i in range(pieces):
        copy = pltpu.make_async_copy(
            density.at[pl.ds(place.half[0] * rim + i * size, size)],
            held.at[i * size:(i + 1) * size],
            sems.at[i],
        )
        copy.start()
        copies.append(copy)
    for i, copy in enumerate(copies):
        copy.wait()
        rows = slice(i * size, (i + 1) * size)
        for g in range(2):
            coarse[g, rows] = held[rows, group_rows(place, rim, g), :].astype(BF16)


def toeplitz(taps, rim):
    return pltpu.roll(jnp.broadcast_to(taps, (rim, 128)), 0, 1, stride=1, stride_axis=0)


def blur_matrices(rim, place, taps):
    size = rim * rim
    wide = 3 * size
    shift = rim.bit_length() - 1
    pick = lambda mask: jnp.where(mask, 1.0, 0.0).astype(BF16)
    row_hi = pick(iota((size, rim), 0) >> shift == iota((size, rim), 1))
    row_lo = pick(iota((size, rim), 0) & (rim - 1) == iota((size, rim), 1))
    col = iota((128, wide), 1)
    src = iota((128, wide), 0)
    k, j, b = col >> 2 * shift, col >> shift & (rim - 1), col & (rim - 1)
    k_x = jnp.where(place.half[0] == 1, k, 2 - k)
    k_y = jnp.where(place.group[0] == 1, k, 2 - k)
    tx = toeplitz(taps[0:1], rim).astype(BF16)
    ty = toeplitz(taps[1:2] * 0.5, rim).astype(BF16)
    dot = functools.partial(jnp.dot, preferred_element_type=F32)
    full_x = dot(row_hi, dot(tx, pick(k_x * rim + j == src)).astype(BF16))
    full_y = dot(row_lo, dot(ty, pick(k_y * rim + b == src)).astype(BF16))
    r, c = iota((size, wide), 0), iota((size, wide), 1)
    mx = jnp.where(r & (rim - 1) == c & (rim - 1), full_x, 0.0)
    my = jnp.where(r >> shift == c >> shift & (rim - 1), full_y, 0.0)
    return mx.astype(BF16), my.astype(BF16)


def matrices_kernel(rim, taps, mx, my, padded):
    padded[...] = jnp.zeros(padded.shape, F32)
    padded[0:2, 0:taps.shape[1]] = taps[...].astype(F32)
    mx[...], my[...] = blur_matrices(rim, Place(), padded[...])


def cells_kernel(rim, bumps, h, *refs):
    tables, (density, *refs) = refs[:6], refs[6:]
    coarse = None
    if h == 1:
        coarse, *refs = refs
    shaded, total, order_map, optical_s, emitted_s, *refs = refs
    held, (*locals_, sems) = refs[0] if h == 1 else density, refs[h:]
    place = Place()
    copies = [
        pltpu.make_async_copy(src, dst, sems.at[i])
        for i, (src, dst) in enumerate(zip(tables, locals_))
    ]
    parts = []
    if h == 1:
        for g in range(2):
            at = group_rows(place, rim, g)
            parts.append(
                pltpu.make_async_copy(
                    density.at[half_rows(place, rim, h), at, :], held.at[:, at, :], sems.at[6 + g]
                )
            )
    for copy in copies + parts:
        copy.start()
    for copy in copies:
        copy.wait()
    centre, width, colour, opacity, brick_tf, view_order = locals_
    bricks = brick_tf.shape[2]
    rows_z = held.shape[2]
    depth = rows_z // bricks
    lane = iota((rim, 128), 1)
    for g in range(2):
        bx, by = place.half[h], place.group[g]
        cells = held.at[:, group_rows(place, rim, g), :]
        if h == 1:
            parts[g].wait()
            coarse[g] = cells[...].astype(BF16)
        for bz in range(bricks):
            zs = slice(bz * depth, (bz + 1) * depth)
            k = brick_tf[bx, by, bz]
            cen, neg, opa, col = [], [], [], []
            for j in range(bumps):
                cen.append(centre[j, k])
                wide = jnp.full((8, depth), width[j, k], F32)
                neg.append((-LOG2E / (wide * wide))[None])
                opa.append(opacity[j, k] * (-LOG2E))
                col.append([colour[c, j, k] * 0.5 for c in range(3)])
            for x in range(rim):
                d = cells[x, :, zs].reshape(rim // 8, 8, depth)
                opt, em = None, [None] * 3
                for j in range(bumps):
                    w = d - cen[j]
                    b = jnp.exp2((w * w) * neg[j])
                    opt = opa[j] * b if opt is None else opt + opa[j] * b
                    for c in range(3):
                        em[c] = col[j][c] * b if em[c] is None else em[c] + col[j][c] * b
                rows = slice(x * rim, (x + 1) * rim)
                optical_s[g, rows, zs] = opt.reshape(rim, depth)
                for c in range(3):
                    emitted_s[c, g, rows, zs] = em[c].reshape(rim, depth)
        order = view_order[bx, by]
        behind = iota((rows_z, rows_z), 1) - iota((rows_z, rows_z), 0)
        tri = jnp.where(behind * (1 - 2 * order) > 0, 1.0, 0.0).astype(BF16)
        opt = optical_s[g]
        hi = opt.astype(BF16)
        lo = (opt - hi.astype(F32)).astype(BF16)
        ahead = jnp.dot(hi, tri, preferred_element_type=F32)
        ahead = ahead + jnp.dot(lo, tri, preferred_element_type=F32)
        weight = jnp.exp2(ahead) * (1.0 - jnp.exp2(opt))
        for c in range(3):
            shaded[c, g] = (weight * emitted_s[c, g]).reshape(rim, rim, rows_z)
        total[g] = rays(opt.reshape(rim, rim, rows_z), bx * rim, lane)
    shape = order_map.shape
    block = shape[0]
    order = jnp.zeros(shape, jnp.int32)
    for y in range(2):
        order = jnp.where(
            iota(shape, 1) // rim == y, view_order[place.depth * block // rim, y], order
        )
    order_map[...] = order


def rays(cells, first_lane, lane):
    folded = cells[:, :, :128]
    for z in range(128, cells.shape[2], 128):
        folded = folded + cells[:, :, z:z + 128]
    summed = jnp.sum(folded, axis=2, keepdims=True)
    acc = jnp.zeros(lane.shape, F32)
    for x in range(cells.shape[0]):
        acc = jnp.where(lane == first_lane + x, summed[x], acc)
    return acc


def across_kernel(rim, mx, first, second, third, *outs):
    rows_z = first.shape[3]
    flat = (rim * rim, rows_z)
    for g, out in enumerate(outs):
        cells = jnp.concatenate([r[g].reshape(flat) for r in (first, second, third)], axis=0)
        blurred = jnp.dot(mx[...], cells, preferred_element_type=F32)
        out[...] = blurred.astype(BF16).reshape(out.shape)


def lit(rim, my_blocks, pieces, shaded, g, first_lane, lane):
    rows_z = pieces[0].shape[2]
    cells = jnp.concatenate([p.reshape(rim * rim, rows_z) for p in pieces], axis=0)
    occlusion = jnp.dot(my_blocks, cells, preferred_element_type=F32)
    shade = (1.0 - jnp.tanh(occlusion)).reshape(rim, rim, rows_z)
    return [rays(shade * shaded[c, g], first_lane, lane) for c in range(3)]


def early_kernel(rim, my, s0, e0, s1, e1, shaded0, shaded1, out):
    place = Place()
    size = rim * rim
    lane = iota((rim, 128), 1)
    acc = None
    for h, (s, e, shaded) in enumerate(((s0, e0, shaded0), (s1, e1, shaded1))):
        part = lit(rim, my[:, size:], (e[...], s[...]), shaded, 1, place.half[h] * rim, lane)
        acc = part if acc is None else [a + b for a, b in zip(acc, part)]
    for c in range(3):
        out[c] = acc[c]


def late_kernel(rim, h, reverse, my, s, e, halo, shaded, before, out):
    place = Place()
    lane = iota((rim, 128), 1)
    pieces = (halo[...], e[...], s[...]) if reverse else (e[...], s[...], halo[...])
    part = lit(rim, my[...], pieces, shaded, int(reverse), place.half[h] * rim, lane)
    for c in range(3):
        out[c] = part[c] if before is None else part[c] + before[c]


def blocks_kernel(rim, depth_count, late_s, late_e, total0, total1, *refs):
    outs, (img,) = refs[:depth_count], refs[depth_count:]
    place = Place()
    rows = 2 * rim
    for g, colours in enumerate((late_s, late_e)):
        at = group_rows(place, rim, g)
        for c in range(3):
            img[c, at, :] = colours[c]
        img[3, at, :] = jnp.exp2(total0[g] + total1[g])
    for c in range(4):
        img[4 + c, :, 0:rows] = img[c].T[:rows, :]
    block = rows // depth_count
    for k in range(depth_count):
        at = pl.multiple_of((place.depth ^ k) * block, block)
        outs[k][...] = img[4:8, pl.ds(at, block), 0:rows]


def picture_kernel(depth_count, order_map, *refs):
    parts = [ref[...] for ref in refs[:depth_count]]
    out = refs[depth_count]
    me = lax.axis_index("depth")
    bit = 0
    while len(parts) > 1:
        mine = (me >> bit & 1) == order_map[...]
        merged = []
        for a, b in zip(parts[::2], parts[1::2]):
            front = jnp.where(mine[None], a, b)
            back = jnp.where(mine[None], b, a)
            merged.append(
                jnp.concatenate([front[:3] + front[3:] * back[:3], front[3:] * back[3:]])
            )
        parts = merged
        bit += 1
    final = jnp.concatenate([parts[0][:3], 1.0 - parts[0][3:]])
    out[...] = final.reshape(out.shape)


def call(kernel, name, ins, outs, scratch=(), limit=16 * MIB, **more):
    return pl.pallas_call(
        kernel,
        out_shape=outs,
        in_specs=ins,
        out_specs=jax.tree.map(lambda _: VMEM, outs),
        scratch_shapes=list(scratch),
        compiler_params=pltpu.CompilerParams(vmem_limit_bytes=limit),
        name=name,
        **more,
    )


def per_device(
    density, kernel_taps, tf_centre, tf_width, tf_color, tf_opacity, brick_tf, view_order
):
    rows_x, rows_y, rows_z = density.shape
    rim = (kernel_taps.shape[1] - 1) // 2
    bumps = tf_centre.shape[1]
    size = rim * rim
    depth_count = lax.axis_size("depth")
    count_x, count_y = lax.axis_size("sx"), lax.axis_size("sy")
    struct = jax.ShapeDtypeStruct
    block = rows_x // depth_count

    def swap_x(piece, first):
        pairs = []
        for d in range(depth_count):
            pairs += [
                (d * count_x + a, d * count_x + b) for a, b in line_swaps(count_x, (first + d) % 2)
            ]
        return lax.ppermute(piece, ("depth", "sx"), pairs)

    def swap_y(piece, shift):
        pairs = line_swaps(count_y, shift)
        return lax.ppermute(piece, "sy", pairs) if pairs else None

    coarse = [None, None]
    coarse[0], held = call(
        functools.partial(first_kernel, rim),
        "first",
        [HBM],
        [struct((2, rim, rim, rows_z), BF16), struct((rim, rows_y, rows_z), F32)],
        [pltpu.SemaphoreType.DMA((4,))],
    )(density)
    halo_x = [swap_x(coarse[0], 0), None]
    shaded, total, order_map = [None, None], [None, None], None
    tables = (tf_centre.T, tf_width.T, tf_color.T, tf_opacity.T, brick_tf, view_order)
    for h in (1, 0):
        outs = [struct((2, rim, rim, rows_z), BF16)] if h == 1 else []
        outs += [struct((3, 2, rim, rim, rows_z), F32), struct((2, rim, 128), F32)]
        outs += [struct((block, rows_y), jnp.int32)]
        results = call(
            functools.partial(cells_kernel, rim, bumps, h),
            f"cells{h}",
            [HBM] * 6 + [HBM if h == 1 else VMEM],
            outs,
            [pltpu.VMEM((2, size, rows_z), F32), pltpu.VMEM((3, 2, size, rows_z), F32)]
            + ([pltpu.VMEM((rim, rows_y, rows_z), F32)] if h == 1 else [])
            + [pltpu.SMEM(t.shape, t.dtype) for t in tables]
            + [pltpu.SemaphoreType.DMA((8,))],
            cost_estimate=pl.CostEstimate(
                flops=density.size * 30, bytes_accessed=density.size * 10, transcendentals=density.size * 3
            ),
        )(*tables, density if h == 1 else held)
        if h == 1:
            coarse[1] = results[0]
            halo_x[1] = swap_x(coarse[1], 1)
        shaded[h], total[h], order_map = results[-3:]
    mx, my = call(
        functools.partial(matrices_kernel, rim),
        "matrices",
        [VMEM],
        [struct((size, 3 * size), BF16)] * 2,
        [pltpu.VMEM((8, 128), F32)],
    )(kernel_taps)

    strips, halo_y = [None, None], [None, None]
    for h in range(2):
        first, second, third = (
            (coarse[1], coarse[0], halo_x[0]) if h == 0 else (halo_x[1], coarse[1], coarse[0])
        )
        strips[h] = call(
            functools.partial(across_kernel, rim),
            f"across{h}",
            [VMEM] * 4,
            [struct((rim, rim, rows_z), BF16)] * 2,
        )(mx, first, second, third)
        halo_y[h] = [swap_y(strips[h][g], g) for g in range(2)]

    def late(h, g, before):
        halo = halo_y[h][g]
        if halo is None:
            halo = jnp.zeros_like(strips[h][g])
        args = [my, *strips[h], halo, shaded[h]] + ([] if before is None else [before])
        kernel = functools.partial(late_kernel, rim, h, g == 1)
        if before is None:
            kernel = lambda *refs: late_kernel(rim, h, g == 1, *refs[:5], None, *refs[5:])
        return call(
            kernel, f"late{h}{g}", [VMEM] * len(args), struct((3, rim, 128), F32)
        )(*args)

    if halo_y[0][1] is None:
        group1 = call(
            functools.partial(early_kernel, rim), "early", [VMEM] * 7, struct((3, rim, 128), F32)
        )(my, *strips[0], *strips[1], *shaded)
    else:
        group1 = late(1, 1, late(0, 1, None))
    group0 = late(1, 0, late(0, 0, None))

    parts = call(
        functools.partial(blocks_kernel, rim, depth_count),
        "blocks",
        [VMEM] * 4,
        [struct((4, block, rows_y), F32)] * depth_count,
        [pltpu.VMEM((8, rows_y, 128), F32)],
    )(group0, group1, *total)
    pieces = [parts[0]] + [
        lax.ppermute(parts[k], "depth", [(i, i ^ k) for i in range(depth_count)])
        for k in range(1, depth_count)
    ]
    return call(
        functools.partial(picture_kernel, depth_count),
        "picture",
        [VMEM] * (1 + depth_count),
        struct((4, 1, 1, block, rows_y), F32),
        limit=2 * MIB,
    )(order_map, *pieces)


def solution(mesh):
    return jax.shard_map(
        per_device,
        mesh=mesh,
        in_specs=(
            P("sx", "sy", "depth"),
            P(),
            P(),
            P(),
            P(),
            P(),
            P("sx", "sy", "depth"),
            P("sx", "sy"),
        ),
        out_specs=P(None, "sx", "depth", None, "sy"),
        check_vma=False,
    )
```

profile of v0, /device:TPU:17, one launch (start us, length us, event | category | flops | bytes accessed | tf_op | source)
XLA Modules:
  0.0 32.2 jit_solution(13324246287829451637)
XLA Ops:
  0.0 1.2 %copy-done = f32[32,32,256]{2,1,0:T(8,128)S(1)} copy-done((f32[32,32,256]{2,1,0:T(8,128)S(1)}, f32[32,32,256]{2,1,0:T(8,128)}, u32[]{:S(2)}) %copy-start) | copy-done | bytes 1048600
  1.2 0.7 %first.1 = (bf16[2,16,16,256]{3,2,1,0:T(8,128)(2,1)S(1)}, f32[16,32,256]{2,1,0:T(8,128)S(1)}) custom-call(f32[32,32,256]{2,1,0:T(8,128)S(1)} %copy-done), custom_call_target="tpu_custom_call" | custom-call | tf_op jit(solution)/shard_map/first/pallas_call | solution.py:301
  2.0 2.1 %collective-permute-start.2 = (bf16[2,16,16,256]{3,2,1,0:T(8,128)(2,1)S(1)}, bf16[2,16,16,256]{3,2,1,0:T(8,128)(2,1)S(1)}, u32[]{:S(2)}, u32[]{:S(2)}) collective-permute-start(bf16[2,16,16,256]{3,2,1,0:T(8,128)(2,1)S(1)} %get-tuple-element.28.third.second), channel_id=1, source_target_pairs={{0,2},{4,6},{2,0},{6,4},{10,12},{12,10},{16,18},{20,22},{18,16},{2... | collective-permute-start | bytes 786440 | tf_op jit(solution)/shard_map/ppermute | solution.py:294
  4.1 0.7 %copy-done.1 = f32[8,4,3]{0,1,2:T(4,128)S(1)} copy-done((f32[8,4,3]{0,1,2:T(4,128)S(1)}, f32[8,4,3]{0,1,2:T(4,128)}, u32[]{:S(2)}) %copy-start.1) | copy-done | bytes 408
  4.7 0.7 %copy-done.3 = f32[8,4]{0,1:T(4,128)S(1)} copy-done((f32[8,4]{0,1:T(4,128)S(1)}, f32[8,4]{0,1:T(4,128)}, u32[]{:S(2)}) %copy-start.3) | copy-done | bytes 152
  5.4 0.7 %copy-done.5 = f32[8,4]{0,1:T(4,128)S(1)} copy-done((f32[8,4]{0,1:T(4,128)S(1)}, f32[8,4]{0,1:T(4,128)}, u32[]{:S(2)}) %copy-start.5) | copy-done | bytes 152
  6.1 0.7 %copy-done.7 = f32[8,4]{0,1:T(4,128)S(1)} copy-done((f32[8,4]{0,1:T(4,128)S(1)}, f32[8,4]{0,1:T(4,128)}, u32[]{:S(2)}) %copy-start.7) | copy-done | bytes 152
  6.8 0.7 %copy-done.9 = s32[2,2,2]{2,1,0:T(2,128)S(1)} copy-done((s32[2,2,2]{2,1,0:T(2,128)S(1)}, s32[2,2,2]{2,1,0:T(2,128)}, u32[]{:S(2)}) %copy-start.9) | copy-done | bytes 56
  7.5 0.7 %copy-done.11 = s32[2,2]{1,0:T(2,128)S(1)} copy-done((s32[2,2]{1,0:T(2,128)S(1)}, s32[2,2]{1,0:T(2,128)}, u32[]{:S(2)}) %copy-start.11) | copy-done | bytes 40
  8.2 2.7 %cells1.1 = (bf16[2,16,16,256]{3,2,1,0:T(8,128)(2,1)S(1)}, f32[3,2,16,16,256]{4,3,2,1,0:T(8,128)S(1)}, f32[2,16,128]{2,1,0:T(8,128)S(1)}, s32[8,32]{1,0:T(8,128)}) custom-call(f32[4,8]{1,0:T(4,128)S(1)} %bitcast.6, f32[4,8]{1,0:T(4,128)S(1)} %bitcast.8, f32[3,4,8]{2,1,0:T(4,128)S(1)} %bitcast.4, f32[4,8]{1,0:T(4,128)S(1)} %bitcast.10, ...), custom_call_target="tpu_custom_call" | custom-call | flops 7864320 | bytes 2621440 | tf_op jit(solution)/shard_map/cells1/pallas_call | solution.py:315
  10.9 1.9 %collective-permute-start = (bf16[2,16,16,256]{3,2,1,0:T(8,128)(2,1)S(1)}, bf16[2,16,16,256]{3,2,1,0:T(8,128)(2,1)S(1)}, u32[]{:S(2)}, u32[]{:S(2)}) collective-permute-start(bf16[2,16,16,256]{3,2,1,0:T(8,128)(2,1)S(1)} %get-tuple-element.27.second.first), channel_id=1, source_target_pairs={{2,4},{4,2},{8,10},{12,14},{10,8},{14,12},{18,20},{20,18},{24,26},... | collective-permute-start | bytes 786440 | tf_op jit(solution)/shard_map/ppermute | solution.py:294
  12.8 0.6 %matrices.1 = (bf16[256,768]{1,0:T(8,128)(2,1)S(1)}, bf16[256,768]{1,0:T(8,128)(2,1)S(1)}) custom-call(bf16[2,33]{1,0:T(2,128)(2,1)S(1)} %copy-done.13), custom_call_target="tpu_custom_call" | custom-call | tf_op jit(solution)/shard_map/matrices/pallas_call | solution.py:332
  13.8 1.3 %collective-permute-start.3 = (bf16[16,16,256]{2,1,0:T(8,128)(2,1)S(1)}, bf16[16,16,256]{2,1,0:T(8,128)(2,1)S(1)}, u32[]{:S(2)}, u32[]{:S(2)}) collective-permute-start(bf16[16,16,256]{2,1,0:T(8,128)(2,1)S(1)} %get-tuple-element.32.refs_1_.s0), channel_id=1, source_target_pairs={{0,1},{1,0},{2,3},{3,2},{4,5},{5,4},{6,7},{7,6},{8,9},{9,8},{10,11... | collective-permute-start | bytes 393224 | tf_op jit(solution)/shard_map/ppermute | solution.py:298
  15.1 3.2 %collective-permute-done.first = bf16[2,16,16,256]{3,2,1,0:T(8,128)(2,1)S(1)} collective-permute-done((bf16[2,16,16,256]{3,2,1,0:T(8,128)(2,1)S(1)}, bf16[2,16,16,256]{3,2,1,0:T(8,128)(2,1)S(1)}, u32[]{:S(2)}, u32[]{:S(2)}) %collective-permute-start) | collective-permute-done | bytes 262176 | tf_op jit(solution)/shard_map/ppermute | solution.py:294
  18.7 1.3 %collective-permute-start.1 = (bf16[16,16,256]{2,1,0:T(8,128)(2,1)S(1)}, bf16[16,16,256]{2,1,0:T(8,128)(2,1)S(1)}, u32[]{:S(2)}, u32[]{:S(2)}) collective-permute-start(bf16[16,16,256]{2,1,0:T(8,128)(2,1)S(1)} %get-tuple-element.29.s.s1), channel_id=1, source_target_pairs={{0,1},{1,0},{2,3},{3,2},{4,5},{5,4},{6,7},{7,6},{8,9},{9,8},{10,11... | collective-permute-start | bytes 393224 | tf_op jit(solution)/shard_map/ppermute | solution.py:298
  20.0 2.0 %cells0.1 = (f32[3,2,16,16,256]{4,3,2,1,0:T(8,128)S(1)}, f32[2,16,128]{2,1,0:T(8,128)S(1)}, s32[8,32]{1,0:T(8,128)S(1)}) custom-call(f32[4,8]{1,0:T(4,128)S(1)} %bitcast.7, f32[4,8]{1,0:T(4,128)S(1)} %bitcast.9, f32[3,4,8]{2,1,0:T(4,128)S(1)} %bitcast.5, f32[4,8]{1,0:T(4,128)S(1)} %bitcast.11, s32[2,2,2]{2,1,0:T(2,128)S(1)} %copy-done.10, ...), custom_call_target="tpu_custom_call" | custom-call | flops 7864320 | bytes 2621440 | tf_op jit(solution)/shard_map/cells0/pallas_call | solution.py:315
  22.0 0.6 %early.1.late_e = f32[3,16,128]{2,1,0:T(8,128)S(1)} custom-call(bf16[256,768]{1,0:T(8,128)(2,1)S(1)} %get-tuple-element.25.refs_0_.my, bf16[16,16,256]{2,1,0:T(8,128)(2,1)S(1)} %get-tuple-element.32.refs_1_.s0, bf16[16,16,256]{2,1,0:T(8,128)(2,1)S(1)} %get-tuple-element.33.refs_2_.e0, bf16[16,16,256]{2,1,0:T(8,128)(2,1)S(1)} %get-tuple-element.29.s.s1, ...), custom_call_target="tpu_custom_call" | custom-call | tf_op jit(solution)/shard_map/early/pallas_call | solution.py:366
  22.6 0.4 %late00.1.before = f32[3,16,128]{2,1,0:T(8,128)S(1)} custom-call(bf16[256,768]{1,0:T(8,128)(2,1)S(1)} %get-tuple-element.25.refs_0_.my, bf16[16,16,256]{2,1,0:T(8,128)(2,1)S(1)} %get-tuple-element.32.refs_1_.s0, bf16[16,16,256]{2,1,0:T(8,128)(2,1)S(1)} %get-tuple-element.33.refs_2_.e0, bf16[16,16,256]{2,1,0:T(8,128)(2,1)S(1)} %collective-permute-done.3.refs_3_, ...), custom_call_target="tpu_custom_call" | custom-call | tf_op jit(solution)/shard_map/late00/pallas_call | solution.py:361
  23.5 3.7 %collective-permute-start.4 = (f32[4,8,32]{2,1,0:T(8,128)S(1)}, f32[4,8,32]{2,1,0:T(8,128)S(1)}, u32[]{:S(2)}, u32[]{:S(2)}) collective-permute-start(f32[4,8,32]{2,1,0:T(8,128)S(1)} %get-tuple-element.38), channel_id=1, source_target_pairs={{0,8},{8,0},{16,24},{24,16},{1,9},{9,1},{17,25},{25,17},{2,10},{10... | collective-permute-start | bytes 12296 | tf_op jit(solution)/shard_map/ppermute | solution.py:381
  27.2 1.2 %collective-permute-start.5 = (f32[4,8,32]{2,1,0:T(8,128)S(1)}, f32[4,8,32]{2,1,0:T(8,128)S(1)}, u32[]{:S(2)}, u32[]{:S(2)}) collective-permute-start(f32[4,8,32]{2,1,0:T(8,128)S(1)} %get-tuple-element.39), channel_id=1, source_target_pairs={{0,16},{8,24},{16,0},{24,8},{1,17},{9,25},{17,1},{25,9},{2,18},{10... | collective-permute-start | bytes 12296 | tf_op jit(solution)/shard_map/ppermute | solution.py:381
  28.4 0.5 %collective-permute-start.6 = (f32[4,8,32]{2,1,0:T(8,128)S(1)}, f32[4,8,32]{2,1,0:T(8,128)S(1)}, u32[]{:S(2)}, u32[]{:S(2)}) collective-permute-start(f32[4,8,32]{2,1,0:T(8,128)S(1)} %get-tuple-element.40), channel_id=1, source_target_pairs={{0,24},{8,16},{16,8},{24,0},{1,25},{9,17},{17,9},{25,1},{2,26},{10... | collective-permute-start | bytes 12296 | tf_op jit(solution)/shard_map/ppermute | solution.py:381
  28.9 0.9 %collective-permute-done.5.refs_2_ = f32[4,8,32]{2,1,0:T(8,128)S(1)} collective-permute-done((f32[4,8,32]{2,1,0:T(8,128)S(1)}, f32[4,8,32]{2,1,0:T(8,128)S(1)}, u32[]{:S(2)}, u32[]{:S(2)}) %collective-permute-start.5) | collective-permute-done | bytes 4128 | tf_op jit(solution)/shard_map/ppermute | solution.py:381
  29.8 1.8 %collective-permute-done.6.refs_3_ = f32[4,8,32]{2,1,0:T(8,128)S(1)} collective-permute-done((f32[4,8,32]{2,1,0:T(8,128)S(1)}, f32[4,8,32]{2,1,0:T(8,128)S(1)}, u32[]{:S(2)}, u32[]{:S(2)}) %collective-permute-start.6) | collective-permute-done | bytes 4128 | tf_op jit(solution)/shard_map/ppermute | solution.py:381
  31.6 0.6 %picture.1 = f32[4,1,1,8,32]{4,3,2,1,0:T(8,128)} custom-call(s32[8,32]{1,0:T(8,128)S(1)} %get-tuple-element.24.order_map, f32[4,8,32]{2,1,0:T(8,128)S(1)} %get-tuple-element.37.refs_0_, f32[4,8,32]{2,1,0:T(8,128)S(1)} %collective-permute-done.4.refs_1_, f32[4,8,32]{2,1,0:T(8,128)S(1)} %collective-permute-done.5.refs_2_, ...), custom_call_target="tpu_custom_call" | custom-call | tf_op jit(solution)/shard_map/picture/pallas_call | solution.py:384
  (29 shorter events, 1.3 us)
Async XLA Ops:
  0.0 1.2 %copy-start = (f32[32,32,256]{2,1,0:T(8,128)S(1)}, f32[32,32,256]{2,1,0:T(8,128)}, u32[]{:S(2)}) copy-start(f32[32,32,256]{2,1,0:T(8,128)} %refs_6_.1) | copy-start | bytes 3145732
  1.2 11.6 %copy-start.13 = (bf16[2,33]{1,0:T(2,128)(2,1)S(1)}, bf16[2,33]{1,0:T(2,128)(2,1)}, u32[]{:S(2)}) copy-start(bf16[2,33]{1,0:T(2,128)(2,1)} %taps.1) | copy-start | bytes 400
  2.0 11.5 %collective-permute-start.2 = (bf16[2,16,16,256]{3,2,1,0:T(8,128)(2,1)S(1)}, bf16[2,16,16,256]{3,2,1,0:T(8,128)(2,1)S(1)}, u32[]{:S(2)}, u32[]{:S(2)}) collective-permute-start(bf16[2,16,16,256]{3,2,1,0:T(8,128)(2,1)S(1)} %get-tuple-element.28.third.second), channel_id=1, source_target_pairs={{0,2},{4,6},{2,0},{6,4},{10,12},{12,10},{16,18},{20,22},{18,16},{2... | collective-permute-start | bytes 786440 | tf_op jit(solution)/shard_map/ppermute | solution.py:294
  4.0 0.7 %copy-start.1 = (f32[8,4,3]{0,1,2:T(4,128)S(1)}, f32[8,4,3]{0,1,2:T(4,128)}, u32[]{:S(2)}) copy-start(f32[8,4,3]{0,1,2:T(4,128)} %param.12) | copy-start | bytes 1156
  4.7 0.7 %copy-start.3 = (f32[8,4]{0,1:T(4,128)S(1)}, f32[8,4]{0,1:T(4,128)}, u32[]{:S(2)}) copy-start(f32[8,4]{0,1:T(4,128)} %param.10) | copy-start | bytes 388
  5.4 0.7 %copy-start.5 = (f32[8,4]{0,1:T(4,128)S(1)}, f32[8,4]{0,1:T(4,128)}, u32[]{:S(2)}) copy-start(f32[8,4]{0,1:T(4,128)} %param.11) | copy-start | bytes 388
  6.1 0.7 %copy-start.7 = (f32[8,4]{0,1:T(4,128)S(1)}, f32[8,4]{0,1:T(4,128)}, u32[]{:S(2)}) copy-start(f32[8,4]{0,1:T(4,128)} %param.13) | copy-start | bytes 388
  6.8 0.7 %copy-start.9 = (s32[2,2,2]{2,1,0:T(2,128)S(1)}, s32[2,2,2]{2,1,0:T(2,128)}, u32[]{:S(2)}) copy-start(s32[2,2,2]{2,1,0:T(2,128)} %refs_4_.3) | copy-start | bytes 100
  7.5 0.7 %copy-start.11 = (s32[2,2]{1,0:T(2,128)S(1)}, s32[2,2]{1,0:T(2,128)}, u32[]{:S(2)}) copy-start(s32[2,2]{1,0:T(2,128)} %refs_5_.3) | copy-start | bytes 52
  8.1 11.8 %copy-start.2 = (f32[8,4,3]{0,1,2:T(4,128)S(1)}, f32[8,4,3]{0,1,2:T(4,128)}, u32[]{:S(2)}) copy-start(f32[8,4,3]{0,1,2:T(4,128)} %param.12) | copy-start | bytes 1156
  8.1 11.8 %copy-start.4 = (f32[8,4]{0,1:T(4,128)S(1)}, f32[8,4]{0,1:T(4,128)}, u32[]{:S(2)}) copy-start(f32[8,4]{0,1:T(4,128)} %param.10) | copy-start | bytes 388
  8.2 11.8 %copy-start.6 = (f32[8,4]{0,1:T(4,128)S(1)}, f32[8,4]{0,1:T(4,128)}, u32[]{:S(2)}) copy-start(f32[8,4]{0,1:T(4,128)} %param.11) | copy-start | bytes 388
  8.2 11.8 %copy-start.8 = (f32[8,4]{0,1:T(4,128)S(1)}, f32[8,4]{0,1:T(4,128)}, u32[]{:S(2)}) copy-start(f32[8,4]{0,1:T(4,128)} %param.13) | copy-start | bytes 388
  8.2 11.8 %copy-start.10 = (s32[2,2,2]{2,1,0:T(2,128)S(1)}, s32[2,2,2]{2,1,0:T(2,128)}, u32[]{:S(2)}) copy-start(s32[2,2,2]{2,1,0:T(2,128)} %refs_4_.3) | copy-start | bytes 100
  8.2 11.8 %copy-start.12 = (s32[2,2]{1,0:T(2,128)S(1)}, s32[2,2]{1,0:T(2,128)}, u32[]{:S(2)}) copy-start(s32[2,2]{1,0:T(2,128)} %refs_5_.3) | copy-start | bytes 52
  10.9 7.4 %collective-permute-start = (bf16[2,16,16,256]{3,2,1,0:T(8,128)(2,1)S(1)}, bf16[2,16,16,256]{3,2,1,0:T(8,128)(2,1)S(1)}, u32[]{:S(2)}, u32[]{:S(2)}) collective-permute-start(bf16[2,16,16,256]{3,2,1,0:T(8,128)(2,1)S(1)} %get-tuple-element.27.second.first), channel_id=1, source_target_pairs={{2,4},{4,2},{8,10},{12,14},{10,8},{14,12},{18,20},{20,18},{24,26},... | collective-permute-start | bytes 786440 | tf_op jit(solution)/shard_map/ppermute | solution.py:294
  13.8 8.8 %collective-permute-start.3 = (bf16[16,16,256]{2,1,0:T(8,128)(2,1)S(1)}, bf16[16,16,256]{2,1,0:T(8,128)(2,1)S(1)}, u32[]{:S(2)}, u32[]{:S(2)}) collective-permute-start(bf16[16,16,256]{2,1,0:T(8,128)(2,1)S(1)} %get-tuple-element.32.refs_1_.s0), channel_id=1, source_target_pairs={{0,1},{1,0},{2,3},{3,2},{4,5},{5,4},{6,7},{7,6},{8,9},{9,8},{10,11... | collective-permute-start | bytes 393224 | tf_op jit(solution)/shard_map/ppermute | solution.py:298
  18.7 4.4 %collective-permute-start.1 = (bf16[16,16,256]{2,1,0:T(8,128)(2,1)S(1)}, bf16[16,16,256]{2,1,0:T(8,128)(2,1)S(1)}, u32[]{:S(2)}, u32[]{:S(2)}) collective-permute-start(bf16[16,16,256]{2,1,0:T(8,128)(2,1)S(1)} %get-tuple-element.29.s.s1), channel_id=1, source_target_pairs={{0,1},{1,0},{2,3},{3,2},{4,5},{5,4},{6,7},{7,6},{8,9},{9,8},{10,11... | collective-permute-start | bytes 393224 | tf_op jit(solution)/shard_map/ppermute | solution.py:298
  23.5 5.4 %collective-permute-start.4 = (f32[4,8,32]{2,1,0:T(8,128)S(1)}, f32[4,8,32]{2,1,0:T(8,128)S(1)}, u32[]{:S(2)}, u32[]{:S(2)}) collective-permute-start(f32[4,8,32]{2,1,0:T(8,128)S(1)} %get-tuple-element.38), channel_id=1, source_target_pairs={{0,8},{8,0},{16,24},{24,16},{1,9},{9,1},{17,25},{25,17},{2,10},{10... | collective-permute-start | bytes 12296 | tf_op jit(solution)/shard_map/ppermute | solution.py:381
  27.2 2.6 %collective-permute-start.5 = (f32[4,8,32]{2,1,0:T(8,128)S(1)}, f32[4,8,32]{2,1,0:T(8,128)S(1)}, u32[]{:S(2)}, u32[]{:S(2)}) collective-permute-start(f32[4,8,32]{2,1,0:T(8,128)S(1)} %get-tuple-element.39), channel_id=1, source_target_pairs={{0,16},{8,24},{16,0},{24,8},{1,17},{9,25},{17,1},{25,9},{2,18},{10... | collective-permute-start | bytes 12296 | tf_op jit(solution)/shard_map/ppermute | solution.py:381
  28.4 3.2 %collective-permute-start.6 = (f32[4,8,32]{2,1,0:T(8,128)S(1)}, f32[4,8,32]{2,1,0:T(8,128)S(1)}, u32[]{:S(2)}, u32[]{:S(2)}) collective-permute-start(f32[4,8,32]{2,1,0:T(8,128)S(1)} %get-tuple-element.40), channel_id=1, source_target_pairs={{0,24},{8,16},{16,8},{24,0},{1,25},{9,17},{17,9},{25,1},{2,26},{10... | collective-permute-start | bytes 12296 | tf_op jit(solution)/shard_map/ppermute | solution.py:381
where the time goes:
time: 32.5 us; the launch traced here: 32.2 us
  starting transfers between devices  12 us (37%)
  Pallas kernels  8.86 us (27%)
  waiting for transfers between devices  5.84 us (18%)
  local copies, waits for them, and re-layouts  5.34 us (16%)
    ppermute x3, starting transfers between devices, per_device(): lax.ppermute(parts[k], 'depth', [(i, i ^ k) for i in range(depth_count)])  5.38 us
    unnamed x28, local copies, waits for them, and re-layouts  5.34 us
    pallas_call x2, Pallas kernels, per_device(): call(functools.partial(cells_kernel, rim, bumps, h), f'cells{h}', [HBM] *...  4.73 us
    ppermute x2, starting transfers between devices, swap_x(): return lax.ppermute(piece, ('depth', 'sx'), pairs)  4 us
    ppermute x2, waiting for transfers between devices, swap_x(): return lax.ppermute(piece, ('depth', 'sx'), pairs)  3.15 us
    ppermute x3, waiting for transfers between devices, per_device(): lax.ppermute(parts[k], 'depth', [(i, i ^ k) for i in range(depth_count)])  2.68 us
    ppermute x2, starting transfers between devices, swap_y(): return lax.ppermute(piece, 'sy', pairs) if pairs else None  2.61 us
    pallas_call x2, Pallas kernels, late(): call(kernel, f'late{h}{g}', [VMEM] * len(args), struct((3, rim, 128), F32))  0.77 us
  transfers between devices with their start and end apart: 7, of which 3 were waited for; matrix products, arithmetic and copies ran while one was open for 0% of the time, Pallas kernels for 22%

commit v1 on v0

--- a/solution.py
+++ b/solution.py
@@ -18,9 +18,27 @@
     return lax.broadcasted_iota(jnp.int32, shape, dim)
 
 
-def line_swaps(count, shift):
-    pairs = [(i, i + 1) for i in range(shift, count - 1, 2)]
+def both_ways(pairs):
     return pairs + [(b, a) for a, b in pairs]
+
+
+def line_pairs(count, shift):
+    return [(i, i + 1) for i in range(shift, count - 1, 2)]
+
+
+def plane_swaps(depth_count, count, first):
+    pairs, left = [], {}
+    for d in range(depth_count):
+        used = set()
+        for a, b in line_pairs(count, (first + d) % 2):
+            pairs.append((d * count + a, d * count + b))
+            used |= {a, b}
+        for a in range(count):
+            if a not in used:
+                left.setdefault(a, []).append(d * count + a)
+    for over in left.values():
+        pairs += list(zip(over[::2], over[1::2]))
+    return both_ways(pairs)
 
 
 class Place:
@@ -29,6 +47,11 @@
         x_parity = lax.rem(lax.axis_index("sx") + self.depth, 2)
         y_parity = lax.rem(lax.axis_index("sy"), 2)
         self.half = (1 - x_parity, x_parity)
+        at, last = lax.axis_index("sx"), lax.axis_size("sx") - 1
+        self.has_halo = [
+            jnp.logical_or(jnp.logical_and(h == 1, at < last), jnp.logical_and(h == 0, at > 0))
+            for h in self.half
+        ]
         self.group = (1 - y_parity, y_parity)
 
 
@@ -164,14 +187,14 @@
         for c in range(3):
             shaded[c, g] = (weight * emitted_s[c, g]).reshape(rim, rim, rows_z)
         total[g] = rays(opt.reshape(rim, rim, rows_z), bx * rim, lane)
-    shape = order_map.shape
-    block = shape[0]
-    order = jnp.zeros(shape, jnp.int32)
-    for y in range(2):
-        order = jnp.where(
-            iota(shape, 1) // rim == y, view_order[place.depth * block // rim, y], order
-        )
-    order_map[...] = order
+    for n in range(order_map.shape[0]):
+        shape = order_map.shape[1:]
+        order = jnp.zeros(shape, jnp.int32)
+        for y in range(2):
+            order = jnp.where(
+                iota(shape, 1) // rim == y, view_order[n * shape[0] // rim, y], order
+            )
+        order_map[n] = order
 
 
 def rays(cells, first_lane, lane):
@@ -185,11 +208,15 @@
     return acc
 
 
-def across_kernel(rim, mx, first, second, third, *outs):
+def across_kernel(rim, h, mx, first, second, third, *outs):
+    place = Place()
     rows_z = first.shape[3]
     flat = (rim * rim, rows_z)
     for g, out in enumerate(outs):
-        cells = jnp.concatenate([r[g].reshape(flat) for r in (first, second, third)], axis=0)
+        blocks = [r[g].reshape(flat) for r in (first, second, third)]
+        halo = 0 if h == 1 else 2
+        blocks[halo] = jnp.where(place.has_halo[h], blocks[halo], jnp.zeros_like(blocks[halo]))
+        cells = jnp.concatenate(blocks, axis=0)
         blurred = jnp.dot(mx[...], cells, preferred_element_type=F32)
         out[...] = blurred.astype(BF16).reshape(out.shape)
 
@@ -224,7 +251,7 @@
 
 
 def blocks_kernel(rim, depth_count, late_s, late_e, total0, total1, *refs):
-    outs, (img,) = refs[:depth_count], refs[depth_count:]
+    outs, (img,) = refs[:2], refs[2:]
     place = Place()
     rows = 2 * rim
     for g, colours in enumerate((late_s, late_e)):
@@ -235,29 +262,31 @@
     for c in range(4):
         img[4 + c, :, 0:rows] = img[c].T[:rows, :]
     block = rows // depth_count
-    for k in range(depth_count):
-        at = pl.multiple_of((place.depth ^ k) * block, block)
-        outs[k][...] = img[4:8, pl.ds(at, block), 0:rows]
-
-
-def picture_kernel(depth_count, order_map, *refs):
-    parts = [ref[...] for ref in refs[:depth_count]]
-    out = refs[depth_count]
+    bit = place.depth & 1
+    for n in range(depth_count // 2):
+        for out, b in ((outs[0], bit), (outs[1], 1 - bit)):
+            out[n] = img[4:8, pl.ds(pl.multiple_of((2 * n + b) * block, block), block), 0:rows]
+
+
+def merge_kernel(level, order_map, kept, theirs, *outs):
     me = lax.axis_index("depth")
-    bit = 0
-    while len(parts) > 1:
-        mine = (me >> bit & 1) == order_map[...]
-        merged = []
-        for a, b in zip(parts[::2], parts[1::2]):
-            front = jnp.where(mine[None], a, b)
-            back = jnp.where(mine[None], b, a)
-            merged.append(
-                jnp.concatenate([front[:3] + front[3:] * back[:3], front[3:] * back[3:]])
-            )
-        parts = merged
-        bit += 1
-    final = jnp.concatenate([parts[0][:3], 1.0 - parts[0][3:]])
-    out[...] = final.reshape(out.shape)
+    bit = me >> level & 1
+    low = me & (2 << level) - 1
+    merged = []
+    for n in range(kept.shape[0]):
+        mine = (bit == order_map[(n << level + 1) + low])[None]
+        front = jnp.where(mine, kept[n], theirs[n])
+        back = jnp.where(mine, theirs[n], kept[n])
+        merged.append((front[:3] + front[3:] * back[:3], front[3:] * back[3:]))
+    if len(merged) == 1:
+        colour, through = merged[0]
+        outs[0][...] = jnp.concatenate([colour, 1.0 - through]).reshape(outs[0].shape)
+        return
+    up = me >> level + 1 & 1
+    for n in range(len(merged) // 2):
+        even, odd = (jnp.concatenate(merged[2 * n + i]) for i in range(2))
+        outs[0][n] = jnp.where(up == 1, odd, even)
+        outs[1][n] = jnp.where(up == 1, even, odd)
 
 
 def call(kernel, name, ins, outs, scratch=(), limit=16 * MIB, **more):
@@ -286,17 +315,14 @@
     block = rows_x // depth_count
 
     def swap_x(piece, first):
-        pairs = []
-        for d in range(depth_count):
-            pairs += [
-                (d * count_x + a, d * count_x + b) for a, b in line_swaps(count_x, (first + d) % 2)
-            ]
-        return lax.ppermute(piece, ("depth", "sx"), pairs)
+        return lax.ppermute(piece, ("depth", "sx"), plane_swaps(depth_count, count_x, first))
 
     def swap_y(piece, shift):
-        pairs = line_swaps(count_y, shift)
+        pairs = both_ways(line_pairs(count_y, shift))
         return lax.ppermute(piece, "sy", pairs) if pairs else None
 
+    in_hbm = lambda array: pltpu.with_memory_space_constraint(array, pltpu.HBM)
+    density = in_hbm(density)
     coarse = [None, None]
     coarse[0], held = call(
         functools.partial(first_kernel, rim),
@@ -308,10 +334,11 @@
     halo_x = [swap_x(coarse[0], 0), None]
     shaded, total, order_map = [None, None], [None, None], None
     tables = (tf_centre.T, tf_width.T, tf_color.T, tf_opacity.T, brick_tf, view_order)
+    tables = [in_hbm(table) for table in tables]
     for h in (1, 0):
         outs = [struct((2, rim, rim, rows_z), BF16)] if h == 1 else []
         outs += [struct((3, 2, rim, rim, rows_z), F32), struct((2, rim, 128), F32)]
-        outs += [struct((block, rows_y), jnp.int32)]
+        outs += [struct((depth_count, block, rows_y), jnp.int32)]
         results = call(
             functools.partial(cells_kernel, rim, bumps, h),
             f"cells{h}",
@@ -343,7 +370,7 @@
             (coarse[1], coarse[0], halo_x[0]) if h == 0 else (halo_x[1], coarse[1], coarse[0])
         )
         strips[h] = call(
-            functools.partial(across_kernel, rim),
+            functools.partial(across_kernel, rim, h),
             f"across{h}",
             [VMEM] * 4,
             [struct((rim, rim, rows_z), BF16)] * 2,
@@ -370,24 +397,29 @@
         group1 = late(1, 1, late(0, 1, None))
     group0 = late(1, 0, late(0, 0, None))
 
-    parts = call(
+    kept, given = call(
         functools.partial(blocks_kernel, rim, depth_count),
         "blocks",
         [VMEM] * 4,
-        [struct((4, block, rows_y), F32)] * depth_count,
+        [struct((depth_count // 2, 4, block, rows_y), F32)] * 2,
         [pltpu.VMEM((8, rows_y, 128), F32)],
     )(group0, group1, *total)
-    pieces = [parts[0]] + [
-        lax.ppermute(parts[k], "depth", [(i, i ^ k) for i in range(depth_count)])
-        for k in range(1, depth_count)
-    ]
-    return call(
-        functools.partial(picture_kernel, depth_count),
-        "picture",
-        [VMEM] * (1 + depth_count),
-        struct((4, 1, 1, block, rows_y), F32),
-        limit=2 * MIB,
-    )(order_map, *pieces)
+    level = 0
+    while True:
+        theirs = lax.ppermute(given, "depth", [(i, i ^ 1 << level) for i in range(depth_count)])
+        left = kept.shape[0] // 2
+        outs = [struct((left, 4, block, rows_y), F32)] * 2
+        merged = call(
+            functools.partial(merge_kernel, level),
+            f"merge{level}",
+            [VMEM] * 3,
+            outs if left else struct((4, 1, 1, block, rows_y), F32),
+            limit=2 * MIB,
+        )(order_map, kept, theirs)
+        if not left:
+            return merged
+        kept, given = merged
+        level += 1
 
 
 def solution(mesh):

time: 32.5 us -> 25.4 us (0.78)
  the two profiles are of different devices: /device:TPU:17 before, /device:TPU:0 now
where the time goes in v1:
time: 25.4 us; the launch traced here: 25.2 us
  Pallas kernels  9.61 us (38%)
  starting transfers between devices  9.44 us (37%)
  waiting for transfers between devices  6.02 us (24%)
    pallas_call x2, Pallas kernels, per_device(): call(functools.partial(cells_kernel, rim, bumps, h), f'cells{h}', [HBM] *...  5.05 us
    ppermute x2, starting transfers between devices, swap_x(): lax.ppermute(piece, ('depth', 'sx'), plane_swaps(depth_count, count_x, fi...  4.65 us
    ppermute x2, waiting for transfers between devices, per_device(): lax.ppermute(given, 'depth', [(i, i ^ 1 << level) for i in range(depth_co...  3.45 us
    ppermute x2, starting transfers between devices, swap_y(): return lax.ppermute(piece, 'sy', pairs) if pairs else None  3.17 us
    ppermute x2, waiting for transfers between devices, swap_x(): lax.ppermute(piece, ('depth', 'sx'), plane_swaps(depth_count, count_x, fi...  2.28 us
    ppermute x2, starting transfers between devices, per_device(): lax.ppermute(given, 'depth', [(i, i ^ 1 << level) for i in range(depth_co...  1.62 us
    pallas_call x1, Pallas kernels, per_device(): call(functools.partial(first_kernel, rim), 'first', [HBM], [struct((2, ri...  1.15 us
    pallas_call x2, Pallas kernels, late(): call(kernel, f'late{h}{g}', [VMEM] * len(args), struct((3, rim, 128), F32))  0.77 us
  transfers between devices with their start and end apart: 6, of which 4 were waited for; matrix products, arithmetic and copies ran while one was open for 0% of the time, Pallas kernels for 29%

profile of v1, /device:TPU:0, one launch (start us, length us, event | category | flops | bytes accessed | tf_op | source)
XLA Modules:
  0.0 25.2 jit_solution(2457321067002762372)
XLA Ops:
  0.0 1.1 %first.1 = (bf16[2,16,16,256]{3,2,1,0:T(8,128)(2,1)S(1)}, f32[16,32,256]{2,1,0:T(8,128)S(1)}) custom-call(f32[32,32,256]{2,1,0:T(8,128)} %refs_6_.1), custom_call_target="tpu_custom_call" | custom-call | tf_op jit(solution)/shard_map/first/pallas_call | solution.py:327
  1.2 3.1 %collective-permute-start.2 = (bf16[2,16,16,256]{3,2,1,0:T(8,128)(2,1)S(1)}, bf16[2,16,16,256]{3,2,1,0:T(8,128)(2,1)S(1)}, u32[]{:S(2)}, u32[]{:S(2)}) collective-permute-start(bf16[2,16,16,256]{3,2,1,0:T(8,128)(2,1)S(1)} %get-tuple-element.28.third.second), channel_id=1, source_target_pairs={{0,2},{4,6},{10,12},{16,18},{20,22},{26,28},{8,24},{14,30},{2,0},{... | collective-permute-start | bytes 786440 | tf_op jit(solution)/shard_map/ppermute | solution.py:318
  4.2 2.9 %cells1.1 = (bf16[2,16,16,256]{3,2,1,0:T(8,128)(2,1)S(1)}, f32[3,2,16,16,256]{4,3,2,1,0:T(8,128)S(1)}, f32[2,16,128]{2,1,0:T(8,128)S(1)}, s32[4,8,32]{2,1,0:T(8,128)}) custom-call(f32[4,8]{1,0:T(4,128)} %bitcast.6, f32[4,8]{1,0:T(4,128)} %bitcast.8, f32[3,4,8]{2,1,0:T(4,128)} %bitcast.4, f32[4,8]{1,0:T(4,128)} %bitcast.10, s32[2,2,2]{2,1,0:T(2,128)} %refs_4_.3, ...), custom_call_target="tpu_custom_call" | custom-call | flops 7864320 | bytes 2621440 | tf_op jit(solution)/shard_map/cells1/pallas_call | solution.py:342
  7.1 1.6 %collective-permute-start = (bf16[2,16,16,256]{3,2,1,0:T(8,128)(2,1)S(1)}, bf16[2,16,16,256]{3,2,1,0:T(8,128)(2,1)S(1)}, u32[]{:S(2)}, u32[]{:S(2)}) collective-permute-start(bf16[2,16,16,256]{3,2,1,0:T(8,128)(2,1)S(1)} %get-tuple-element.27.second.first), channel_id=1, source_target_pairs={{2,4},{8,10},{12,14},{18,20},{24,26},{28,30},{0,16},{6,22},{4,2},{... | collective-permute-start | bytes 786440 | tf_op jit(solution)/shard_map/ppermute | solution.py:318
  8.7 0.0 copy-done
  8.7 0.6 %matrices.1 = (bf16[256,768]{1,0:T(8,128)(2,1)S(1)}, bf16[256,768]{1,0:T(8,128)(2,1)S(1)}) custom-call(bf16[2,33]{1,0:T(2,128)(2,1)S(1)} %copy-done), custom_call_target="tpu_custom_call" | custom-call | tf_op jit(solution)/shard_map/matrices/pallas_call | solution.py:359
  9.3 0.0 collective-permute-done.2.third
  9.3 0.4 %across0.1 = (bf16[16,16,256]{2,1,0:T(8,128)(2,1)S(1)}, bf16[16,16,256]{2,1,0:T(8,128)(2,1)S(1)}) custom-call(bf16[256,768]{1,0:T(8,128)(2,1)S(1)} %get-tuple-element.26.mx, bf16[2,16,16,256]{3,2,1,0:T(8,128)(2,1)S(1)} %get-tuple-element.27.second.first, bf16[2,16,16,256]{3,2,1,0:T(8,128)(2,1)S(1)} %get-tuple-element.28.third.second, ...), custom_call_target="tpu_custom_call" | custom-call | tf_op jit(solution)/shard_map/across0/pallas_call | solution.py:372
  9.7 1.6 %collective-permute-start.3 = (bf16[16,16,256]{2,1,0:T(8,128)(2,1)S(1)}, bf16[16,16,256]{2,1,0:T(8,128)(2,1)S(1)}, u32[]{:S(2)}, u32[]{:S(2)}) collective-permute-start(bf16[16,16,256]{2,1,0:T(8,128)(2,1)S(1)} %get-tuple-element.32.refs_1_.s0), channel_id=1, source_target_pairs={{0,1},{1,0},{2,3},{3,2},{4,5},{5,4},{6,7},{7,6},{8,9},{9,8},{10,11... | collective-permute-start | bytes 393224 | tf_op jit(solution)/shard_map/ppermute | solution.py:322
  11.3 2.3 %collective-permute-done.first = bf16[2,16,16,256]{3,2,1,0:T(8,128)(2,1)S(1)} collective-permute-done((bf16[2,16,16,256]{3,2,1,0:T(8,128)(2,1)S(1)}, bf16[2,16,16,256]{3,2,1,0:T(8,128)(2,1)S(1)}, u32[]{:S(2)}, u32[]{:S(2)}) %collective-permute-start) | collective-permute-done | bytes 262176 | tf_op jit(solution)/shard_map/ppermute | solution.py:318
  13.6 0.4 %across1.1 = (bf16[16,16,256]{2,1,0:T(8,128)(2,1)S(1)}, bf16[16,16,256]{2,1,0:T(8,128)(2,1)S(1)}) custom-call(bf16[256,768]{1,0:T(8,128)(2,1)S(1)} %get-tuple-element.26.mx, bf16[2,16,16,256]{3,2,1,0:T(8,128)(2,1)S(1)} %collective-permute-done.first, bf16[2,16,16,256]{3,2,1,0:T(8,128)(2,1)S(1)} %get-tuple-element.27.second.first, ...), custom_call_target="tpu_custom_call" | custom-call | tf_op jit(solution)/shard_map/across1/pallas_call | solution.py:372
  13.9 1.6 %collective-permute-start.1 = (bf16[16,16,256]{2,1,0:T(8,128)(2,1)S(1)}, bf16[16,16,256]{2,1,0:T(8,128)(2,1)S(1)}, u32[]{:S(2)}, u32[]{:S(2)}) collective-permute-start(bf16[16,16,256]{2,1,0:T(8,128)(2,1)S(1)} %get-tuple-element.29.s.s1), channel_id=1, source_target_pairs={{0,1},{1,0},{2,3},{3,2},{4,5},{5,4},{6,7},{7,6},{8,9},{9,8},{10,11... | collective-permute-start | bytes 393224 | tf_op jit(solution)/shard_map/ppermute | solution.py:322
  15.5 2.2 %cells0.1 = (f32[3,2,16,16,256]{4,3,2,1,0:T(8,128)S(1)}, f32[2,16,128]{2,1,0:T(8,128)S(1)}, s32[4,8,32]{2,1,0:T(8,128)S(1)}) custom-call(f32[4,8]{1,0:T(4,128)} %bitcast.7, f32[4,8]{1,0:T(4,128)} %bitcast.9, f32[3,4,8]{2,1,0:T(4,128)} %bitcast.5, f32[4,8]{1,0:T(4,128)} %bitcast.11, s32[2,2,2]{2,1,0:T(2,128)} %refs_4_.3, s32[2,2]{1,0:T(2,128)} %refs_5_.3, ...), custom_call_target="tpu_custom_call" | custom-call | flops 7864320 | bytes 2621440 | tf_op jit(solution)/shard_map/cells0/pallas_call | solution.py:342
  17.7 0.5 %early.1.late_e = f32[3,16,128]{2,1,0:T(8,128)S(1)} custom-call(bf16[256,768]{1,0:T(8,128)(2,1)S(1)} %get-tuple-element.25.refs_0_.my, bf16[16,16,256]{2,1,0:T(8,128)(2,1)S(1)} %get-tuple-element.32.refs_1_.s0, bf16[16,16,256]{2,1,0:T(8,128)(2,1)S(1)} %get-tuple-element.33.refs_2_.e0, bf16[16,16,256]{2,1,0:T(8,128)(2,1)S(1)} %get-tuple-element.29.s.s1, ...), custom_call_target="tpu_custom_call" | custom-call | tf_op jit(solution)/shard_map/early/pallas_call | solution.py:393
  18.3 0.0 collective-permute-done.3.refs_3_
  18.3 0.4 %late00.1.before = f32[3,16,128]{2,1,0:T(8,128)S(1)} custom-call(bf16[256,768]{1,0:T(8,128)(2,1)S(1)} %get-tuple-element.25.refs_0_.my, bf16[16,16,256]{2,1,0:T(8,128)(2,1)S(1)} %get-tuple-element.32.refs_1_.s0, bf16[16,16,256]{2,1,0:T(8,128)(2,1)S(1)} %get-tuple-element.33.refs_2_.e0, bf16[16,16,256]{2,1,0:T(8,128)(2,1)S(1)} %collective-permute-done.3.refs_3_, ...), custom_call_target="tpu_custom_call" | custom-call | tf_op jit(solution)/shard_map/late00/pallas_call | solution.py:388
  18.7 0.3 %collective-permute-done.1.halo = bf16[16,16,256]{2,1,0:T(8,128)(2,1)S(1)} collective-permute-done((bf16[16,16,256]{2,1,0:T(8,128)(2,1)S(1)}, bf16[16,16,256]{2,1,0:T(8,128)(2,1)S(1)}, u32[]{:S(2)}, u32[]{:S(2)}) %collective-permute-start.1) | collective-permute-done | bytes 131104 | tf_op jit(solution)/shard_map/ppermute | solution.py:322
  19.0 0.4 %late10.1.late_s = f32[3,16,128]{2,1,0:T(8,128)S(1)} custom-call(bf16[256,768]{1,0:T(8,128)(2,1)S(1)} %get-tuple-element.25.refs_0_.my, bf16[16,16,256]{2,1,0:T(8,128)(2,1)S(1)} %get-tuple-element.29.s.s1, bf16[16,16,256]{2,1,0:T(8,128)(2,1)S(1)} %get-tuple-element.30.e.e1, bf16[16,16,256]{2,1,0:T(8,128)(2,1)S(1)} %collective-permute-done.1.halo, ...), custom_call_target="tpu_custom_call" | custom-call | tf_op jit(solution)/shard_map/late10/pallas_call | solution.py:388
  19.4 0.1 blocks.1
  19.5 0.1 collective-permute-start.4
  19.6 1.2 %collective-permute-done.4.theirs = f32[2,4,8,32]{3,2,1,0:T(8,128)S(1)} collective-permute-done((f32[2,4,8,32]{3,2,1,0:T(8,128)S(1)}, f32[2,4,8,32]{3,2,1,0:T(8,128)S(1)}, u32[]{:S(2)}, u32[]{:S(2)}) %collective-permute-start.4) | collective-permute-done | bytes 8224 | tf_op jit(solution)/shard_map/ppermute | solution.py:409
  20.8 1.6 %collective-permute-start.5 = (f32[1,4,8,32]{3,2,1,0:T(8,128)S(1)}, f32[1,4,8,32]{3,2,1,0:T(8,128)S(1)}, u32[]{:S(2)}, u32[]{:S(2)}) collective-permute-start(f32[1,4,8,32]{3,2,1,0:T(8,128)S(1)} %get-tuple-element.40), channel_id=1, source_target_pairs={{0,16},{8,24},{16,0},{24,8},{1,17},{9,25},{17,1},{25,9},{2,18},{10... | collective-permute-start | bytes 12296 | tf_op jit(solution)/shard_map/ppermute | solution.py:409
  22.3 2.3 %collective-permute-done.5.theirs = f32[1,4,8,32]{3,2,1,0:T(8,128)S(1)} collective-permute-done((f32[1,4,8,32]{3,2,1,0:T(8,128)S(1)}, f32[1,4,8,32]{3,2,1,0:T(8,128)S(1)}, u32[]{:S(2)}, u32[]{:S(2)}) %collective-permute-start.5) | collective-permute-done | bytes 4128 | tf_op jit(solution)/shard_map/ppermute | solution.py:409
  24.6 0.6 %merge1.1 = f32[4,1,1,8,32]{4,3,2,1,0:T(8,128)} custom-call(s32[4,8,32]{2,1,0:T(8,128)S(1)} %get-tuple-element.24.order_map, f32[1,4,8,32]{3,2,1,0:T(8,128)S(1)} %get-tuple-element.39.kept, f32[1,4,8,32]{3,2,1,0:T(8,128)S(1)} %collective-permute-done.5.theirs), custom_call_target="tpu_custom_call" | custom-call | tf_op jit(solution)/shard_map/merge1/pallas_call | solution.py:412
  (2 shorter events, 0.0 us)
Async XLA Ops:
  0.0 8.7 %copy-start = (bf16[2,33]{1,0:T(2,128)(2,1)S(1)}, bf16[2,33]{1,0:T(2,128)(2,1)}, u32[]{:S(2)}) copy-start(bf16[2,33]{1,0:T(2,128)(2,1)} %taps.1) | copy-start | bytes 400
  1.2 8.2 %collective-permute-start.2 = (bf16[2,16,16,256]{3,2,1,0:T(8,128)(2,1)S(1)}, bf16[2,16,16,256]{3,2,1,0:T(8,128)(2,1)S(1)}, u32[]{:S(2)}, u32[]{:S(2)}) collective-permute-start(bf16[2,16,16,256]{3,2,1,0:T(8,128)(2,1)S(1)} %get-tuple-element.28.third.second), channel_id=1, source_target_pairs={{0,2},{4,6},{10,12},{16,18},{20,22},{26,28},{8,24},{14,30},{2,0},{... | collective-permute-start | bytes 786440 | tf_op jit(solution)/shard_map/ppermute | solution.py:318
  7.1 6.4 %collective-permute-start = (bf16[2,16,16,256]{3,2,1,0:T(8,128)(2,1)S(1)}, bf16[2,16,16,256]{3,2,1,0:T(8,128)(2,1)S(1)}, u32[]{:S(2)}, u32[]{:S(2)}) collective-permute-start(bf16[2,16,16,256]{3,2,1,0:T(8,128)(2,1)S(1)} %get-tuple-element.27.second.first), channel_id=1, source_target_pairs={{2,4},{8,10},{12,14},{18,20},{24,26},{28,30},{0,16},{6,22},{4,2},{... | collective-permute-start | bytes 786440 | tf_op jit(solution)/shard_map/ppermute | solution.py:318
  9.7 8.6 %collective-permute-start.3 = (bf16[16,16,256]{2,1,0:T(8,128)(2,1)S(1)}, bf16[16,16,256]{2,1,0:T(8,128)(2,1)S(1)}, u32[]{:S(2)}, u32[]{:S(2)}) collective-permute-start(bf16[16,16,256]{2,1,0:T(8,128)(2,1)S(1)} %get-tuple-element.32.refs_1_.s0), channel_id=1, source_target_pairs={{0,1},{1,0},{2,3},{3,2},{4,5},{5,4},{6,7},{7,6},{8,9},{9,8},{10,11... | collective-permute-start | bytes 393224 | tf_op jit(solution)/shard_map/ppermute | solution.py:322
  13.9 5.0 %collective-permute-start.1 = (bf16[16,16,256]{2,1,0:T(8,128)(2,1)S(1)}, bf16[16,16,256]{2,1,0:T(8,128)(2,1)S(1)}, u32[]{:S(2)}, u32[]{:S(2)}) collective-permute-start(bf16[16,16,256]{2,1,0:T(8,128)(2,1)S(1)} %get-tuple-element.29.s.s1), channel_id=1, source_target_pairs={{0,1},{1,0},{2,3},{3,2},{4,5},{5,4},{6,7},{7,6},{8,9},{9,8},{10,11... | collective-permute-start | bytes 393224 | tf_op jit(solution)/shard_map/ppermute | solution.py:322
  19.5 1.3 %collective-permute-start.4 = (f32[2,4,8,32]{3,2,1,0:T(8,128)S(1)}, f32[2,4,8,32]{3,2,1,0:T(8,128)S(1)}, u32[]{:S(2)}, u32[]{:S(2)}) collective-permute-start(f32[2,4,8,32]{3,2,1,0:T(8,128)S(1)} %get-tuple-element.38), channel_id=1, source_target_pairs={{0,8},{8,0},{16,24},{24,16},{1,9},{9,1},{17,25},{25,17},{2,10},{10... | collective-permute-start | bytes 24584 | tf_op jit(solution)/shard_map/ppermute | solution.py:409
  20.8 3.8 %collective-permute-start.5 = (f32[1,4,8,32]{3,2,1,0:T(8,128)S(1)}, f32[1,4,8,32]{3,2,1,0:T(8,128)S(1)}, u32[]{:S(2)}, u32[]{:S(2)}) collective-permute-start(f32[1,4,8,32]{3,2,1,0:T(8,128)S(1)} %get-tuple-element.40), channel_id=1, source_target_pairs={{0,16},{8,24},{16,0},{24,8},{1,17},{9,25},{17,1},{25,9},{2,18},{10... | collective-permute-start | bytes 12296 | tf_op jit(solution)/shard_map/ppermute | solution.py:409

commit v2 on v1

--- a/solution.py
+++ b/solution.py
@@ -63,24 +63,19 @@
     return pl.ds(place.half[h] * rim, rim)
 
 
-def first_kernel(rim, density, coarse, held, sems):
-    place = Place()
-    pieces = 4
-    size = rim // pieces
-    copies = []
-    for i in range(pieces):
-        copy = pltpu.make_async_copy(
-            density.at[pl.ds(place.half[0] * rim + i * size, size)],
-            held.at[i * size:(i + 1) * size],
-            sems.at[i],
+def first_kernel(rim, density, held, coarse0, coarse1, sems):
+    place = Place()
+    copies = [
+        pltpu.make_async_copy(
+            density.at[half_rows(place, rim, h), group_rows(place, rim, 0), :], held.at[h], sems.at[h]
         )
+        for h in range(2)
+    ]
+    for copy in copies:
         copy.start()
-        copies.append(copy)
-    for i, copy in enumerate(copies):
-        copy.wait()
-        rows = slice(i * size, (i + 1) * size)
-        for g in range(2):
-            coarse[g, rows] = held[rows, group_rows(place, rim, g), :].astype(BF16)
+    for h, coarse in enumerate((coarse0, coarse1)):
+        copies[h].wait()
+        coarse[...] = held[h].astype(BF16)
 
 
 def toeplitz(taps, rim):
@@ -116,42 +111,41 @@
     mx[...], my[...] = blur_matrices(rim, Place(), padded[...])
 
 
-def cells_kernel(rim, bumps, h, *refs):
+def cells_kernel(rim, bumps, g, *refs):
     tables, (density, *refs) = refs[:6], refs[6:]
-    coarse = None
-    if h == 1:
-        coarse, *refs = refs
+    coarse, held = None, density
+    if g == 1:
+        *coarse, = refs[:2]
+        refs = refs[2:]
     shaded, total, order_map, optical_s, emitted_s, *refs = refs
-    held, (*locals_, sems) = refs[0] if h == 1 else density, refs[h:]
+    if g == 1:
+        held, *refs = refs
+    *locals_, sems = refs
     place = Place()
     copies = [
         pltpu.make_async_copy(src, dst, sems.at[i])
         for i, (src, dst) in enumerate(zip(tables, locals_))
     ]
     parts = []
-    if h == 1:
-        for g in range(2):
-            at = group_rows(place, rim, g)
-            parts.append(
-                pltpu.make_async_copy(
-                    density.at[half_rows(place, rim, h), at, :], held.at[:, at, :], sems.at[6 + g]
-                )
-            )
-    for copy in copies + parts:
+    if g == 1:
+        for h in range(2):
+            rows = density.at[half_rows(place, rim, h), group_rows(place, rim, g), :]
+            parts.append(pltpu.make_async_copy(rows, held.at[h], sems.at[6 + h]))
+    for copy in parts + copies:
         copy.start()
     for copy in copies:
         copy.wait()
     centre, width, colour, opacity, brick_tf, view_order = locals_
     bricks = brick_tf.shape[2]
-    rows_z = held.shape[2]
+    rows_z = held.shape[3]
     depth = rows_z // bricks
     lane = iota((rim, 128), 1)
-    for g in range(2):
+    for h in range(2):
         bx, by = place.half[h], place.group[g]
-        cells = held.at[:, group_rows(place, rim, g), :]
-        if h == 1:
-            parts[g].wait()
-            coarse[g] = cells[...].astype(BF16)
+        cells = held.at[h]
+        if g == 1:
+            parts[h].wait()
+            coarse[h][...] = cells[...].astype(BF16)
         for bz in range(bricks):
             zs = slice(bz * depth, (bz + 1) * depth)
             k = brick_tf[bx, by, bz]
@@ -172,21 +166,22 @@
                     for c in range(3):
                         em[c] = col[j][c] * b if em[c] is None else em[c] + col[j][c] * b
                 rows = slice(x * rim, (x + 1) * rim)
-                optical_s[g, rows, zs] = opt.reshape(rim, depth)
+                optical_s[h, rows, zs] = opt.reshape(rim, depth)
                 for c in range(3):
-                    emitted_s[c, g, rows, zs] = em[c].reshape(rim, depth)
+                    emitted_s[c, h, rows, zs] = em[c].reshape(rim, depth)
         order = view_order[bx, by]
         behind = iota((rows_z, rows_z), 1) - iota((rows_z, rows_z), 0)
         tri = jnp.where(behind * (1 - 2 * order) > 0, 1.0, 0.0).astype(BF16)
-        opt = optical_s[g]
+        opt = optical_s[h]
         hi = opt.astype(BF16)
         lo = (opt - hi.astype(F32)).astype(BF16)
         ahead = jnp.dot(hi, tri, preferred_element_type=F32)
         ahead = ahead + jnp.dot(lo, tri, preferred_element_type=F32)
         weight = jnp.exp2(ahead) * (1.0 - jnp.exp2(opt))
         for c in range(3):
-            shaded[c, g] = (weight * emitted_s[c, g]).reshape(rim, rim, rows_z)
-        total[g] = rays(opt.reshape(rim, rim, rows_z), bx * rim, lane)
+            shaded[c, h] = (weight * emitted_s[c, h]).reshape(rim, rim, rows_z)
+        part = rays(opt.reshape(rim, rim, rows_z), bx * rim, lane)
+        total[...] = part if h == 0 else total[...] + part
     for n in range(order_map.shape[0]):
         shape = order_map.shape[1:]
         order = jnp.zeros(shape, jnp.int32)
@@ -208,34 +203,36 @@
     return acc
 
 
-def across_kernel(rim, h, mx, first, second, third, *outs):
-    place = Place()
-    rows_z = first.shape[3]
-    flat = (rim * rim, rows_z)
-    for g, out in enumerate(outs):
-        blocks = [r[g].reshape(flat) for r in (first, second, third)]
-        halo = 0 if h == 1 else 2
-        blocks[halo] = jnp.where(place.has_halo[h], blocks[halo], jnp.zeros_like(blocks[halo]))
-        cells = jnp.concatenate(blocks, axis=0)
+def across_kernel(rim, mx, coarse0, coarse1, halo0, halo1, *outs):
+    place = Place()
+    rows_z = coarse0.shape[2]
+    flat = lambda r: r[...].reshape(rim * rim, rows_z)
+    halos = []
+    for h, halo in enumerate((halo0, halo1)):
+        cells = flat(halo)
+        halos.append(jnp.where(place.has_halo[h], cells, jnp.zeros_like(cells)))
+    blocks = [halos[1], flat(coarse1), flat(coarse0), halos[0]]
+    for h, out in enumerate(outs):
+        cells = jnp.concatenate(blocks[1 - h:4 - h], axis=0)
         blurred = jnp.dot(mx[...], cells, preferred_element_type=F32)
         out[...] = blurred.astype(BF16).reshape(out.shape)
 
 
-def lit(rim, my_blocks, pieces, shaded, g, first_lane, lane):
+def lit(rim, my_blocks, pieces, shaded, h, first_lane, lane):
     rows_z = pieces[0].shape[2]
     cells = jnp.concatenate([p.reshape(rim * rim, rows_z) for p in pieces], axis=0)
     occlusion = jnp.dot(my_blocks, cells, preferred_element_type=F32)
     shade = (1.0 - jnp.tanh(occlusion)).reshape(rim, rim, rows_z)
-    return [rays(shade * shaded[c, g], first_lane, lane) for c in range(3)]
-
-
-def early_kernel(rim, my, s0, e0, s1, e1, shaded0, shaded1, out):
-    place = Place()
-    size = rim * rim
+    return [rays(shade * shaded[c, h], first_lane, lane) for c in range(3)]
+
+
+def early_kernel(rim, my, s0, s1, e0, e1, shaded, out):
+    place = Place()
     lane = iota((rim, 128), 1)
     acc = None
-    for h, (s, e, shaded) in enumerate(((s0, e0, shaded0), (s1, e1, shaded1))):
-        part = lit(rim, my[:, size:], (e[...], s[...]), shaded, 1, place.half[h] * rim, lane)
+    for h, (s, e) in enumerate(((s0, e0), (s1, e1))):
+        pieces = (e[...], s[...])
+        part = lit(rim, my[:, rim * rim:], pieces, shaded, h, place.half[h] * rim, lane)
         acc = part if acc is None else [a + b for a, b in zip(acc, part)]
     for c in range(3):
         out[c] = acc[c]
@@ -245,7 +242,7 @@
     place = Place()
     lane = iota((rim, 128), 1)
     pieces = (halo[...], e[...], s[...]) if reverse else (e[...], s[...], halo[...])
-    part = lit(rim, my[...], pieces, shaded, int(reverse), place.half[h] * rim, lane)
+    part = lit(rim, my[...], pieces, shaded, h, place.half[h] * rim, lane)
     for c in range(3):
         out[c] = part[c] if before is None else part[c] + before[c]
 
@@ -258,7 +255,7 @@
         at = group_rows(place, rim, g)
         for c in range(3):
             img[c, at, :] = colours[c]
-        img[3, at, :] = jnp.exp2(total0[g] + total1[g])
+        img[3, at, :] = jnp.exp2((total0, total1)[g][...])
     for c in range(4):
         img[4 + c, :, 0:rows] = img[c].T[:rows, :]
     block = rows // depth_count
@@ -323,39 +320,40 @@
 
     in_hbm = lambda array: pltpu.with_memory_space_constraint(array, pltpu.HBM)
     density = in_hbm(density)
-    coarse = [None, None]
-    coarse[0], held = call(
+    piece = struct((rim, rim, rows_z), BF16)
+    coarse, halo_x = [None, None], [None, None]
+    held, *coarse[0] = call(
         functools.partial(first_kernel, rim),
         "first",
         [HBM],
-        [struct((2, rim, rim, rows_z), BF16), struct((rim, rows_y, rows_z), F32)],
-        [pltpu.SemaphoreType.DMA((4,))],
+        [struct((2, rim, rim, rows_z), F32), piece, piece],
+        [pltpu.SemaphoreType.DMA((2,))],
     )(density)
-    halo_x = [swap_x(coarse[0], 0), None]
+    halo_x[0] = [swap_x(coarse[0][h], h) for h in range(2)]
     shaded, total, order_map = [None, None], [None, None], None
     tables = (tf_centre.T, tf_width.T, tf_color.T, tf_opacity.T, brick_tf, view_order)
     tables = [in_hbm(table) for table in tables]
-    for h in (1, 0):
-        outs = [struct((2, rim, rim, rows_z), BF16)] if h == 1 else []
-        outs += [struct((3, 2, rim, rim, rows_z), F32), struct((2, rim, 128), F32)]
+    for g in (1, 0):
+        outs = [piece, piece] if g == 1 else []
+        outs += [struct((3, 2, rim, rim, rows_z), F32), struct((rim, 128), F32)]
         outs += [struct((depth_count, block, rows_y), jnp.int32)]
         results = call(
-            functools.partial(cells_kernel, rim, bumps, h),
-            f"cells{h}",
-            [HBM] * 6 + [HBM if h == 1 else VMEM],
+            functools.partial(cells_kernel, rim, bumps, g),
+            f"cells{g}",
+            [HBM] * 6 + [HBM if g == 1 else VMEM],
             outs,
             [pltpu.VMEM((2, size, rows_z), F32), pltpu.VMEM((3, 2, size, rows_z), F32)]
-            + ([pltpu.VMEM((rim, rows_y, rows_z), F32)] if h == 1 else [])
+            + ([pltpu.VMEM((2, rim, rim, rows_z), F32)] if g == 1 else [])
             + [pltpu.SMEM(t.shape, t.dtype) for t in tables]
             + [pltpu.SemaphoreType.DMA((8,))],
             cost_estimate=pl.CostEstimate(
                 flops=density.size * 30, bytes_accessed=density.size * 10, transcendentals=density.size * 3
             ),
-        )(*tables, density if h == 1 else held)
-        if h == 1:
-            coarse[1] = results[0]
-            halo_x[1] = swap_x(coarse[1], 1)
-        shaded[h], total[h], order_map = results[-3:]
+        )(*tables, density if g == 1 else held)
+        if g == 1:
+            coarse[1] = results[:2]
+            halo_x[1] = [swap_x(coarse[1][h], h) for h in range(2)]
+        shaded[g], total[g], order_map = results[-3:]
     mx, my = call(
         functools.partial(matrices_kernel, rim),
         "matrices",
@@ -365,23 +363,16 @@
     )(kernel_taps)
 
     strips, halo_y = [None, None], [None, None]
-    for h in range(2):
-        first, second, third = (
-            (coarse[1], coarse[0], halo_x[0]) if h == 0 else (halo_x[1], coarse[1], coarse[0])
-        )
-        strips[h] = call(
-            functools.partial(across_kernel, rim, h),
-            f"across{h}",
-            [VMEM] * 4,
-            [struct((rim, rim, rows_z), BF16)] * 2,
-        )(mx, first, second, third)
-        halo_y[h] = [swap_y(strips[h][g], g) for g in range(2)]
+    for g in range(2):
+        strips[g] = call(
+            functools.partial(across_kernel, rim), f"across{g}", [VMEM] * 5, [piece, piece]
+        )(mx, *coarse[g], *halo_x[g])
+        halo_y[g] = [swap_y(strips[g][h], g) for h in range(2)]
 
     def late(h, g, before):
-        halo = halo_y[h][g]
-        if halo is None:
-            halo = jnp.zeros_like(strips[h][g])
-        args = [my, *strips[h], halo, shaded[h]] + ([] if before is None else [before])
+        halo = halo_y[g][h]
+        args = [my, strips[0][h], strips[1][h], halo, shaded[g]]
+        args += [] if before is None else [before]
         kernel = functools.partial(late_kernel, rim, h, g == 1)
         if before is None:
             kernel = lambda *refs: late_kernel(rim, h, g == 1, *refs[:5], None, *refs[5:])
@@ -389,10 +380,10 @@
             kernel, f"late{h}{g}", [VMEM] * len(args), struct((3, rim, 128), F32)
         )(*args)
 
-    if halo_y[0][1] is None:
+    if halo_y[1][0] is None:
         group1 = call(
-            functools.partial(early_kernel, rim), "early", [VMEM] * 7, struct((3, rim, 128), F32)
-        )(my, *strips[0], *strips[1], *shaded)
+            functools.partial(early_kernel, rim), "early", [VMEM] * 6, struct((3, rim, 128), F32)
+        )(my, *strips[0], *strips[1], shaded[1])
     else:
         group1 = late(1, 1, late(0, 1, None))
     group0 = late(1, 0, late(0, 0, None))

time: 25.4 us -> 26.3 us (1.035)
  starting transfers between devices: 9.44 us -> 10.6 us
    ppermute x2 -> x4, starting transfers between devices: 4.65 us -> 7.8 us  [swap_x(): lax.ppermute(piece, ('depth', 'sx'), plane_swaps(depth_count, count_x, fi...]
    ppermute x2 -> x4, waiting for transfers between devices: 2.28 us -> 0.01 us  [swap_x(): lax.ppermute(piece, ('depth', 'sx'), plane_swaps(depth_count, count_x, fi...]
    ppermute x2, starting transfers between devices: 3.17 us -> 2.09 us  [swap_y(): return lax.ppermute(piece, 'sy', pairs) if pairs else None]
    ppermute x2, waiting for transfers between devices: 0.3 us -> 1.35 us  [swap_y(): return lax.ppermute(piece, 'sy', pairs) if pairs else None]
    ppermute x2, starting transfers between devices: 1.62 us -> 0.67 us  [per_device(): lax.ppermute(given, 'depth', [(i, i ^ 1 << level) for i in range(depth_co...]
    ppermute x2, waiting for transfers between devices: 3.45 us -> 4.4 us  [per_device(): lax.ppermute(given, 'depth', [(i, i ^ 1 << level) for i in range(depth_co...]
  transfers between devices with their start and end apart: 6 -> 8, of which waited for: 4 -> 4; matrix products, arithmetic and copies ran while one was open for 0% -> 0% of each run, Pallas kernels for 29% -> 29%
where the time goes in v2:
time: 26.3 us; the launch traced here: 26.1 us
  starting transfers between devices  10.6 us (40%)
  Pallas kernels  9.66 us (37%)
  waiting for transfers between devices  5.77 us (22%)
    ppermute x4, starting transfers between devices, swap_x(): lax.ppermute(piece, ('depth', 'sx'), plane_swaps(depth_count, count_x, fi...  7.8 us
    pallas_call x2, Pallas kernels, per_device(): call(functools.partial(cells_kernel, rim, bumps, g), f'cells{g}', [HBM] *...  5.16 us
    ppermute x2, waiting for transfers between devices, per_device(): lax.ppermute(given, 'depth', [(i, i ^ 1 << level) for i in range(depth_co...  4.4 us
    ppermute x2, starting transfers between devices, swap_y(): return lax.ppermute(piece, 'sy', pairs) if pairs else None  2.09 us
    ppermute x2, waiting for transfers between devices, swap_y(): return lax.ppermute(piece, 'sy', pairs) if pairs else None  1.35 us
    pallas_call x1, Pallas kernels, per_device(): call(functools.partial(first_kernel, rim), 'first', [HBM], [struct((2, ri...  1.07 us
    pallas_call x2, Pallas kernels, late(): call(kernel, f'late{h}{g}', [VMEM] * len(args), struct((3, rim, 128), F32))  0.77 us
    pallas_call x2, Pallas kernels, per_device(): call(functools.partial(across_kernel, rim), f'across{g}', [VMEM] * 5, [pi...  0.75 us
  transfers between devices with their start and end apart: 8, of which 4 were waited for; matrix products, arithmetic and copies ran while one was open for 0% of the time, Pallas kernels for 29%

profile of v2, /device:TPU:0, one launch (start us, length us, event | category | flops | bytes accessed | tf_op | source)
XLA Modules:
  0.0 26.1 jit_solution(16420906725304411839)
XLA Ops:
  0.0 1.1 %first.1 = (f32[2,16,16,256]{3,2,1,0:T(8,128)S(1)}, bf16[16,16,256]{2,1,0:T(8,128)(2,1)S(1)}, bf16[16,16,256]{2,1,0:T(8,128)(2,1)S(1)}) custom-call(f32[32,32,256]{2,1,0:T(8,128)} %refs_6_.1), custom_call_target="tpu_custom_call" | custom-call | tf_op jit(solution)/shard_map/first/pallas_call | solution.py:325
  1.1 3.1 %collective-permute-start = (bf16[16,16,256]{2,1,0:T(8,128)(2,1)S(1)}, bf16[16,16,256]{2,1,0:T(8,128)(2,1)S(1)}, u32[]{:S(2)}, u32[]{:S(2)}) collective-permute-start(bf16[16,16,256]{2,1,0:T(8,128)(2,1)S(1)} %get-tuple-element.29.coarse0), channel_id=1, source_target_pairs={{0,2},{4,6},{10,12},{16,18},{20,22},{26,28},{8,24},{14,30},{2,0},{... | collective-permute-start | bytes 393224 | tf_op jit(solution)/shard_map/ppermute | solution.py:315
  4.2 1.5 %collective-permute-start.1 = (bf16[16,16,256]{2,1,0:T(8,128)(2,1)S(1)}, bf16[16,16,256]{2,1,0:T(8,128)(2,1)S(1)}, u32[]{:S(2)}, u32[]{:S(2)}) collective-permute-start(bf16[16,16,256]{2,1,0:T(8,128)(2,1)S(1)} %get-tuple-element.30.coarse1), channel_id=1, source_target_pairs={{2,4},{8,10},{12,14},{18,20},{24,26},{28,30},{0,16},{6,22},{4,2},{... | collective-permute-start | bytes 393224 | tf_op jit(solution)/shard_map/ppermute | solution.py:315
  5.7 3.0 %cells1.1 = (bf16[16,16,256]{2,1,0:T(8,128)(2,1)S(1)}, bf16[16,16,256]{2,1,0:T(8,128)(2,1)S(1)}, f32[3,2,16,16,256]{4,3,2,1,0:T(8,128)S(1)}, f32[16,128]{1,0:T(8,128)S(1)}, s32[4,8,32]{2,1,0:T(8,128)}) custom-call(f32[4,8]{1,0:T(4,128)} %bitcast.6, f32[4,8]{1,0:T(4,128)} %bitcast.8, f32[3,4,8]{2,1,0:T(4,128)} %bitcast.4, f32[4,8]{1,0:T(4,128)} %bitcast.10, ...), custom_call_target="tpu_custom_call" | custom-call | flops 7864320 | bytes 2621440 | tf_op jit(solution)/shard_map/cells1/pallas_call | solution.py:340
  8.6 1.7 %collective-permute-start.2 = (bf16[16,16,256]{2,1,0:T(8,128)(2,1)S(1)}, bf16[16,16,256]{2,1,0:T(8,128)(2,1)S(1)}, u32[]{:S(2)}, u32[]{:S(2)}) collective-permute-start(bf16[16,16,256]{2,1,0:T(8,128)(2,1)S(1)} %get-tuple-element.32.coarse0), channel_id=1, source_target_pairs={{0,2},{4,6},{10,12},{16,18},{20,22},{26,28},{8,24},{14,30},{2,0},{... | collective-permute-start | bytes 393224 | tf_op jit(solution)/shard_map/ppermute | solution.py:315
  10.4 1.5 %collective-permute-start.3 = (bf16[16,16,256]{2,1,0:T(8,128)(2,1)S(1)}, bf16[16,16,256]{2,1,0:T(8,128)(2,1)S(1)}, u32[]{:S(2)}, u32[]{:S(2)}) collective-permute-start(bf16[16,16,256]{2,1,0:T(8,128)(2,1)S(1)} %get-tuple-element.33.coarse1), channel_id=1, source_target_pairs={{2,4},{8,10},{12,14},{18,20},{24,26},{28,30},{0,16},{6,22},{4,2},{... | collective-permute-start | bytes 393224 | tf_op jit(solution)/shard_map/ppermute | solution.py:315
  11.9 0.6 %matrices.1 = (bf16[256,768]{1,0:T(8,128)(2,1)S(1)}, bf16[256,768]{1,0:T(8,128)(2,1)S(1)}) custom-call(bf16[2,33]{1,0:T(2,128)(2,1)S(1)} %copy-done), custom_call_target="tpu_custom_call" | custom-call | tf_op jit(solution)/shard_map/matrices/pallas_call | solution.py:357
  12.5 0.0 collective-permute-done.halo0
  12.5 0.4 %across0.1 = (bf16[16,16,256]{2,1,0:T(8,128)(2,1)S(1)}, bf16[16,16,256]{2,1,0:T(8,128)(2,1)S(1)}) custom-call(bf16[256,768]{1,0:T(8,128)(2,1)S(1)} %get-tuple-element.28.mx, bf16[16,16,256]{2,1,0:T(8,128)(2,1)S(1)} %get-tuple-element.29.coarse0, bf16[16,16,256]{2,1,0:T(8,128)(2,1)S(1)} %get-tuple-element.30.coarse1, ...), custom_call_target="tpu_custom_call" | custom-call | tf_op jit(solution)/shard_map/across0/pallas_call | solution.py:367
  12.9 1.6 %collective-permute-start.5 = (bf16[16,16,256]{2,1,0:T(8,128)(2,1)S(1)}, bf16[16,16,256]{2,1,0:T(8,128)(2,1)S(1)}, u32[]{:S(2)}, u32[]{:S(2)}) collective-permute-start(bf16[16,16,256]{2,1,0:T(8,128)(2,1)S(1)} %get-tuple-element.36.refs_1_.s0), channel_id=1, source_target_pairs={{0,1},{1,0},{2,3},{3,2},{4,5},{5,4},{6,7},{7,6},{8,9},{9,8},{10,11... | collective-permute-start | bytes 393224 | tf_op jit(solution)/shard_map/ppermute | solution.py:319
  14.5 0.5 %collective-permute-start.4 = (bf16[16,16,256]{2,1,0:T(8,128)(2,1)S(1)}, bf16[16,16,256]{2,1,0:T(8,128)(2,1)S(1)}, u32[]{:S(2)}, u32[]{:S(2)}) collective-permute-start(bf16[16,16,256]{2,1,0:T(8,128)(2,1)S(1)} %get-tuple-element.31.s.s1), channel_id=1, source_target_pairs={{0,1},{1,0},{2,3},{3,2},{4,5},{5,4},{6,7},{7,6},{8,9},{9,8},{10,11... | collective-permute-start | bytes 393224 | tf_op jit(solution)/shard_map/ppermute | solution.py:319
  15.0 2.2 %cells0.1 = (f32[3,2,16,16,256]{4,3,2,1,0:T(8,128)S(1)}, f32[16,128]{1,0:T(8,128)S(1)}, s32[4,8,32]{2,1,0:T(8,128)S(1)}) custom-call(f32[4,8]{1,0:T(4,128)} %bitcast.7, f32[4,8]{1,0:T(4,128)} %bitcast.9, f32[3,4,8]{2,1,0:T(4,128)} %bitcast.5, f32[4,8]{1,0:T(4,128)} %bitcast.11, s32[2,2,2]{2,1,0:T(2,128)} %refs_4_.3, s32[2,2]{1,0:T(2,128)} %refs_5_.3, ...), custom_call_target="tpu_custom_call" | custom-call | flops 7864320 | bytes 2621440 | tf_op jit(solution)/shard_map/cells0/pallas_call | solution.py:340
  17.2 0.4 %across1.1 = (bf16[16,16,256]{2,1,0:T(8,128)(2,1)S(1)}, bf16[16,16,256]{2,1,0:T(8,128)(2,1)S(1)}) custom-call(bf16[256,768]{1,0:T(8,128)(2,1)S(1)} %get-tuple-element.28.mx, bf16[16,16,256]{2,1,0:T(8,128)(2,1)S(1)} %get-tuple-element.32.coarse0, bf16[16,16,256]{2,1,0:T(8,128)(2,1)S(1)} %get-tuple-element.33.coarse1, ...), custom_call_target="tpu_custom_call" | custom-call | tf_op jit(solution)/shard_map/across1/pallas_call | solution.py:367
  17.6 0.5 %early.1.late_e = f32[3,16,128]{2,1,0:T(8,128)S(1)} custom-call(bf16[256,768]{1,0:T(8,128)(2,1)S(1)} %get-tuple-element.27.refs_0_.my, bf16[16,16,256]{2,1,0:T(8,128)(2,1)S(1)} %get-tuple-element.36.refs_1_.s0, bf16[16,16,256]{2,1,0:T(8,128)(2,1)S(1)} %get-tuple-element.31.s.s1, bf16[16,16,256]{2,1,0:T(8,128)(2,1)S(1)} %get-tuple-element.37.refs_2_.e0, ...), custom_call_target="tpu_custom_call" | custom-call | tf_op jit(solution)/shard_map/early/pallas_call | solution.py:384
  18.1 0.3 %collective-permute-done.5.refs_3_ = bf16[16,16,256]{2,1,0:T(8,128)(2,1)S(1)} collective-permute-done((bf16[16,16,256]{2,1,0:T(8,128)(2,1)S(1)}, bf16[16,16,256]{2,1,0:T(8,128)(2,1)S(1)}, u32[]{:S(2)}, u32[]{:S(2)}) %collective-permute-start.5) | collective-permute-done | bytes 131104 | tf_op jit(solution)/shard_map/ppermute | solution.py:319
  18.5 0.4 %late00.1.before = f32[3,16,128]{2,1,0:T(8,128)S(1)} custom-call(bf16[256,768]{1,0:T(8,128)(2,1)S(1)} %get-tuple-element.27.refs_0_.my, bf16[16,16,256]{2,1,0:T(8,128)(2,1)S(1)} %get-tuple-element.36.refs_1_.s0, bf16[16,16,256]{2,1,0:T(8,128)(2,1)S(1)} %get-tuple-element.37.refs_2_.e0, bf16[16,16,256]{2,1,0:T(8,128)(2,1)S(1)} %collective-permute-done.5.refs_3_, ...), custom_call_target="tpu_custom_call" | custom-call | tf_op jit(solution)/shard_map/late00/pallas_call | solution.py:379
  18.9 1.0 %collective-permute-done.4.halo = bf16[16,16,256]{2,1,0:T(8,128)(2,1)S(1)} collective-permute-done((bf16[16,16,256]{2,1,0:T(8,128)(2,1)S(1)}, bf16[16,16,256]{2,1,0:T(8,128)(2,1)S(1)}, u32[]{:S(2)}, u32[]{:S(2)}) %collective-permute-start.4) | collective-permute-done | bytes 131104 | tf_op jit(solution)/shard_map/ppermute | solution.py:319
  19.9 0.4 %late10.1.late_s = f32[3,16,128]{2,1,0:T(8,128)S(1)} custom-call(bf16[256,768]{1,0:T(8,128)(2,1)S(1)} %get-tuple-element.27.refs_0_.my, bf16[16,16,256]{2,1,0:T(8,128)(2,1)S(1)} %get-tuple-element.31.s.s1, bf16[16,16,256]{2,1,0:T(8,128)(2,1)S(1)} %get-tuple-element.34.e.e1, bf16[16,16,256]{2,1,0:T(8,128)(2,1)S(1)} %collective-permute-done.4.halo, ...), custom_call_target="tpu_custom_call" | custom-call | tf_op jit(solution)/shard_map/late10/pallas_call | solution.py:379
  20.3 0.1 blocks.1
  20.4 0.1 collective-permute-start.6
  20.5 1.2 %collective-permute-done.6.theirs = f32[2,4,8,32]{3,2,1,0:T(8,128)S(1)} collective-permute-done((f32[2,4,8,32]{3,2,1,0:T(8,128)S(1)}, f32[2,4,8,32]{3,2,1,0:T(8,128)S(1)}, u32[]{:S(2)}, u32[]{:S(2)}) %collective-permute-start.6) | collective-permute-done | bytes 8224 | tf_op jit(solution)/shard_map/ppermute | solution.py:400
  21.7 0.6 %collective-permute-start.7 = (f32[1,4,8,32]{3,2,1,0:T(8,128)S(1)}, f32[1,4,8,32]{3,2,1,0:T(8,128)S(1)}, u32[]{:S(2)}, u32[]{:S(2)}) collective-permute-start(f32[1,4,8,32]{3,2,1,0:T(8,128)S(1)} %get-tuple-element.44), channel_id=1, source_target_pairs={{0,16},{8,24},{16,0},{24,8},{1,17},{9,25},{17,1},{25,9},{2,18},{10... | collective-permute-start | bytes 12296 | tf_op jit(solution)/shard_map/ppermute | solution.py:400
  22.3 3.2 %collective-permute-done.7.theirs = f32[1,4,8,32]{3,2,1,0:T(8,128)S(1)} collective-permute-done((f32[1,4,8,32]{3,2,1,0:T(8,128)S(1)}, f32[1,4,8,32]{3,2,1,0:T(8,128)S(1)}, u32[]{:S(2)}, u32[]{:S(2)}) %collective-permute-start.7) | collective-permute-done | bytes 4128 | tf_op jit(solution)/shard_map/ppermute | solution.py:400
  25.5 0.6 %merge1.1 = f32[4,1,1,8,32]{4,3,2,1,0:T(8,128)} custom-call(s32[4,8,32]{2,1,0:T(8,128)S(1)} %get-tuple-element.26.order_map, f32[1,4,8,32]{3,2,1,0:T(8,128)S(1)} %get-tuple-element.43.kept, f32[1,4,8,32]{3,2,1,0:T(8,128)S(1)} %collective-permute-done.7.theirs), custom_call_target="tpu_custom_call" | custom-call | tf_op jit(solution)/shard_map/merge1/pallas_call | solution.py:403
  (6 shorter events, 0.0 us)
Async XLA Ops:
  0.0 11.9 %copy-start = (bf16[2,33]{1,0:T(2,128)(2,1)S(1)}, bf16[2,33]{1,0:T(2,128)(2,1)}, u32[]{:S(2)}) copy-start(bf16[2,33]{1,0:T(2,128)(2,1)} %taps.1) | copy-start | bytes 400
  1.1 11.4 %collective-permute-start = (bf16[16,16,256]{2,1,0:T(8,128)(2,1)S(1)}, bf16[16,16,256]{2,1,0:T(8,128)(2,1)S(1)}, u32[]{:S(2)}, u32[]{:S(2)}) collective-permute-start(bf16[16,16,256]{2,1,0:T(8,128)(2,1)S(1)} %get-tuple-element.29.coarse0), channel_id=1, source_target_pairs={{0,2},{4,6},{10,12},{16,18},{20,22},{26,28},{8,24},{14,30},{2,0},{... | collective-permute-start | bytes 393224 | tf_op jit(solution)/shard_map/ppermute | solution.py:315
  4.2 8.3 %collective-permute-start.1 = (bf16[16,16,256]{2,1,0:T(8,128)(2,1)S(1)}, bf16[16,16,256]{2,1,0:T(8,128)(2,1)S(1)}, u32[]{:S(2)}, u32[]{:S(2)}) collective-permute-start(bf16[16,16,256]{2,1,0:T(8,128)(2,1)S(1)} %get-tuple-element.30.coarse1), channel_id=1, source_target_pairs={{2,4},{8,10},{12,14},{18,20},{24,26},{28,30},{0,16},{6,22},{4,2},{... | collective-permute-start | bytes 393224 | tf_op jit(solution)/shard_map/ppermute | solution.py:315
  8.6 8.5 %collective-permute-start.2 = (bf16[16,16,256]{2,1,0:T(8,128)(2,1)S(1)}, bf16[16,16,256]{2,1,0:T(8,128)(2,1)S(1)}, u32[]{:S(2)}, u32[]{:S(2)}) collective-permute-start(bf16[16,16,256]{2,1,0:T(8,128)(2,1)S(1)} %get-tuple-element.32.coarse0), channel_id=1, source_target_pairs={{0,2},{4,6},{10,12},{16,18},{20,22},{26,28},{8,24},{14,30},{2,0},{... | collective-permute-start | bytes 393224 | tf_op jit(solution)/shard_map/ppermute | solution.py:315
  10.4 6.8 %collective-permute-start.3 = (bf16[16,16,256]{2,1,0:T(8,128)(2,1)S(1)}, bf16[16,16,256]{2,1,0:T(8,128)(2,1)S(1)}, u32[]{:S(2)}, u32[]{:S(2)}) collective-permute-start(bf16[16,16,256]{2,1,0:T(8,128)(2,1)S(1)} %get-tuple-element.33.coarse1), channel_id=1, source_target_pairs={{2,4},{8,10},{12,14},{18,20},{24,26},{28,30},{0,16},{6,22},{4,2},{... | collective-permute-start | bytes 393224 | tf_op jit(solution)/shard_map/ppermute | solution.py:315
  12.9 5.6 %collective-permute-start.5 = (bf16[16,16,256]{2,1,0:T(8,128)(2,1)S(1)}, bf16[16,16,256]{2,1,0:T(8,128)(2,1)S(1)}, u32[]{:S(2)}, u32[]{:S(2)}) collective-permute-start(bf16[16,16,256]{2,1,0:T(8,128)(2,1)S(1)} %get-tuple-element.36.refs_1_.s0), channel_id=1, source_target_pairs={{0,1},{1,0},{2,3},{3,2},{4,5},{5,4},{6,7},{7,6},{8,9},{9,8},{10,11... | collective-permute-start | bytes 393224 | tf_op jit(solution)/shard_map/ppermute | solution.py:319
  14.5 5.4 %collective-permute-start.4 = (bf16[16,16,256]{2,1,0:T(8,128)(2,1)S(1)}, bf16[16,16,256]{2,1,0:T(8,128)(2,1)S(1)}, u32[]{:S(2)}, u32[]{:S(2)}) collective-permute-start(bf16[16,16,256]{2,1,0:T(8,128)(2,1)S(1)} %get-tuple-element.31.s.s1), channel_id=1, source_target_pairs={{0,1},{1,0},{2,3},{3,2},{4,5},{5,4},{6,7},{7,6},{8,9},{9,8},{10,11... | collective-permute-start | bytes 393224 | tf_op jit(solution)/shard_map/ppermute | solution.py:319
  20.4 1.3 %collective-permute-start.6 = (f32[2,4,8,32]{3,2,1,0:T(8,128)S(1)}, f32[2,4,8,32]{3,2,1,0:T(8,128)S(1)}, u32[]{:S(2)}, u32[]{:S(2)}) collective-permute-start(f32[2,4,8,32]{3,2,1,0:T(8,128)S(1)} %get-tuple-element.42), channel_id=1, source_target_pairs={{0,8},{8,0},{16,24},{24,16},{1,9},{9,1},{17,25},{25,17},{2,10},{10... | collective-permute-start | bytes 24584 | tf_op jit(solution)/shard_map/ppermute | solution.py:400
  21.7 3.8 %collective-permute-start.7 = (f32[1,4,8,32]{3,2,1,0:T(8,128)S(1)}, f32[1,4,8,32]{3,2,1,0:T(8,128)S(1)}, u32[]{:S(2)}, u32[]{:S(2)}) collective-permute-start(f32[1,4,8,32]{3,2,1,0:T(8,128)S(1)} %get-tuple-element.44), channel_id=1, source_target_pairs={{0,16},{8,24},{16,0},{24,8},{1,17},{9,25},{17,1},{25,9},{2,18},{10... | collective-permute-start | bytes 12296 | tf_op jit(solution)/shard_map/ppermute | solution.py:400

commit v3 on v2

v3 whole, which is shorter than its diff:
```python
import functools
import math
import jax
import jax.numpy as jnp
from jax import lax
from jax.experimental import pallas as pl
from jax.experimental.pallas import tpu as pltpu
from jax.sharding import PartitionSpec as P

LOG2E = math.log2(math.e)
VMEM = pl.BlockSpec(memory_space=pltpu.VMEM)
HBM = pl.BlockSpec(memory_space=pltpu.HBM)
MIB = 1024 * 1024
F32, BF16 = jnp.float32, jnp.bfloat16
dot = functools.partial(jnp.dot, preferred_element_type=F32)


def iota(shape, dim):
    return lax.broadcasted_iota(jnp.int32, shape, dim)


def line_pairs(count, shift):
    return [(i, i + 1) for i in range(shift, count - 1, 2)]


def swaps(counts, x_round, y_round):
    depth_count, count_x, count_y = counts
    index = lambda d, x, y: (d * count_x + x) * count_y + y
    stay = lambda count: [(i, i) for i in range(count)]
    pairs_x = stay(count_x) if x_round is None else line_pairs(count_x, x_round)
    pairs_y = stay(count_y) if y_round is None else line_pairs(count_y, y_round)
    ends = {((a, c), (b, e)) for a, b in pairs_x for c, e in pairs_y}
    if x_round is not None and y_round is not None:
        ends |= {((a, e), (b, c)) for a, b in pairs_x for c, e in pairs_y}
    used = {end for pair in ends for end in pair}
    pairs = []
    for d in range(depth_count):
        pairs += [(index(d, *a), index(d, *b)) for a, b in sorted(ends)]
    for x in range(count_x):
        for y in range(count_y):
            if (x, y) not in used:
                pairs += [
                    (index(d, x, y), index(d + 1, x, y)) for d in range(0, depth_count - 1, 2)
                ]
    return pairs + [(b, a) for a, b in pairs]


class Place:
    def __init__(self):
        self.depth = lax.axis_index("depth")
        self.half, self.has_x = self.sides("sx")
        self.group, self.has_y = self.sides("sy")

    def sides(self, axis):
        at, last = lax.axis_index(axis), lax.axis_size(axis) - 1
        parity = lax.rem(at, 2)
        upper, lower = at < last, at > 0
        order = (1 - parity, parity)
        either = lambda side: jnp.where(side == 1, upper.astype(jnp.int32), lower.astype(jnp.int32))
        return order, [either(side) == 1 for side in order]


def group_rows(place, rim, g):
    return pl.ds(pl.multiple_of(place.group[g] * rim, rim), rim)


def half_rows(place, rim, h):
    return pl.ds(place.half[h] * rim, rim)


def first_kernel(rim, rounds, density, *refs):
    place = Place()
    n_tables = (len(refs) - 4 - 2 * rounds) // 2
    tables, refs = refs[:n_tables], refs[n_tables:]
    held, xs, refs = refs[0], refs[1:3], refs[3:]
    strips, refs = refs[:2 * rounds], refs[2 * rounds:]
    tables_out, sems = refs[:n_tables], refs[n_tables]
    copies = []
    for g in range(2):
        for h in range(2):
            rows = density.at[half_rows(place, rim, h), group_rows(place, rim, g), :]
            copies.append(pltpu.make_async_copy(rows, held.at[g, h], sems.at[2 * g + h]))
    for i, (src, dst) in enumerate(zip(tables, tables_out)):
        copies.append(pltpu.make_async_copy(src, dst, sems.at[4 + i]))
    for copy in copies:
        copy.start()
    for g in range(2):
        for h in range(2):
            copies[2 * g + h].wait()
            coarse = held[g, h].astype(BF16)
            xs[h][g] = coarse
            if g < rounds:
                strips[2 * g + h][...] = coarse
    for copy in copies[4:]:
        copy.wait()


def toeplitz(taps, rim):
    return pltpu.roll(jnp.broadcast_to(taps, (rim, 128)), 0, 1, stride=1, stride_axis=0)


def blur_matrices(rim, place, taps):
    size = rim * rim
    wide = 3 * size
    shift = rim.bit_length() - 1
    pick = lambda mask: jnp.where(mask, 1.0, 0.0).astype(BF16)
    row_hi = pick(iota((size, rim), 0) >> shift == iota((size, rim), 1))
    row_lo = pick(iota((size, rim), 0) & (rim - 1) == iota((size, rim), 1))
    col = iota((128, wide), 1)
    src = iota((128, wide), 0)
    k, j, b = col >> 2 * shift, col >> shift & (rim - 1), col & (rim - 1)
    k_x = jnp.where(place.half[0] == 1, k, 2 - k)
    k_y = jnp.where(place.group[0] == 1, k, 2 - k)
    tx = toeplitz(taps[0:1], rim).astype(BF16)
    ty = toeplitz(taps[1:2] * 0.5, rim).astype(BF16)
    full_x = dot(row_hi, dot(tx, pick(k_x * rim + j == src)).astype(BF16))
    full_y = dot(row_lo, dot(ty, pick(k_y * rim + b == src)).astype(BF16))
    r, c = iota((size, size), 0), iota((size, size), 1)
    same_x = r & (rim - 1) == c & (rim - 1)
    same_y = r >> shift == c >> shift
    parts = []
    for full, same in ((full_x, same_x), (full_y, same_y)):
        blocks = [
            jnp.where(same, full[:, n * size:(n + 1) * size], 0.0).astype(BF16) for n in range(3)
        ]
        parts.append(jnp.concatenate(blocks, axis=1))
    return parts


def prepare_kernel(
    rim, taps, centre, width, colour, opacity, brick_tf, view_order,
    mx, my, table, signs, order_map, padded
):
    place = Place()
    padded[...] = jnp.zeros(padded.shape, F32)
    padded[0:2, 0:taps.shape[1]] = taps[...].astype(F32)
    mx[...], my[...] = blur_matrices(rim, place, padded[...])
    wide = width[...]
    rows = [centre[...], (-LOG2E) / (wide * wide), opacity[...] * (-LOG2E)]
    rows += [colour[c] * 0.5 for c in range(3)]
    rows = jnp.concatenate(rows, axis=0)
    which = iota(rows.shape, 1)
    n = 0
    for g in range(2):
        for h in range(2):
            bricks = brick_tf[place.half[h]]
            bricks = jnp.where(place.group[g] == 0, bricks[0:1], bricks[1:2])
            for bz in range(bricks.shape[1]):
                mine = jnp.where(which == bricks[:, bz:bz + 1], rows, 0.0)
                mine = jnp.sum(mine, axis=1, keepdims=True)
                table[n] = jnp.broadcast_to(mine, table.shape[1:])
                n += 1
            orders = view_order[...]
            orders = jnp.where(place.half[h] == 0, orders[0:1], orders[1:2])
            order = jnp.where(place.group[g] == 0, orders[:, 0:1], orders[:, 1:2])
            signs[g, h] = jnp.broadcast_to(1 - 2 * order, signs.shape[2:])
    block, shape = order_map.shape[1], order_map.shape[1:]
    for n in range(order_map.shape[0]):
        brick = n * block // rim
        orders = view_order[brick:brick + 1]
        order_map[n] = jnp.where(
            iota(shape, 1) < rim,
            jnp.broadcast_to(orders[:, 0:1], shape),
            jnp.broadcast_to(orders[:, 1:2], shape),
        )


def cells_kernel(rim, bumps, g, held, table, signs, shaded, total, optical_s, emitted_s):
    place = Place()
    rows_z = held.shape[4]
    depth = 128
    bricks = rows_z // depth
    lane = iota((rim, 128), 1)
    for h in range(2):
        cells = held.at[g, h]
        for bz in range(bricks):
            zs = slice(bz * depth, (bz + 1) * depth)
            at = (2 * g + h) * bricks + bz
            row = lambda i: jnp.broadcast_to(table[at, i:i + 1, :], (8, depth))[None]
            cen = [row(j) for j in range(bumps)]
            neg = [row(bumps + j) for j in range(bumps)]
            opa = [row(2 * bumps + j) for j in range(bumps)]
            col = [[row((3 + c) * bumps + j) for c in range(3)] for j in range(bumps)]
            for x in range(rim):
                d = cells[x, :, zs].reshape(rim // 8, 8, depth)
                opt, em = None, [None] * 3
                for j in range(bumps):
                    w = d - cen[j]
                    b = jnp.exp2((w * w) * neg[j])
                    opt = opa[j] * b if opt is None else opt + opa[j] * b
                    for c in range(3):
                        em[c] = col[j][c] * b if em[c] is None else em[c] + col[j][c] * b
                rows = slice(x * rim, (x + 1) * rim)
                optical_s[h, rows, zs] = opt.reshape(rim, depth)
                for c in range(3):
                    emitted_s[c, h, rows, zs] = em[c].reshape(rim, depth)
        behind = iota((rows_z, rows_z), 1) - iota((rows_z, rows_z), 0)
        sign = jnp.broadcast_to(signs[g, h][0:1, 0:1], (rows_z, rows_z))
        tri = jnp.where(behind * sign > 0, 1.0, 0.0).astype(BF16)
        opt = optical_s[h]
        hi = opt.astype(BF16)
        lo = (opt - hi.astype(F32)).astype(BF16)
        ahead = dot(hi, tri) + dot(lo, tri)
        weight = jnp.exp2(ahead) * (1.0 - jnp.exp2(opt))
        for c in range(3):
            shaded[c, h] = (weight * emitted_s[c, h]).reshape(rim, rim, rows_z)
        part = rays(opt.reshape(rim, rim, rows_z), place.half[h] * rim, lane)
        total[...] = part if h == 0 else total[...] + part


def rays(cells, first_lane, lane):
    folded = cells[:, :, :128]
    for z in range(128, cells.shape[2], 128):
        folded = folded + cells[:, :, z:z + 128]
    summed = jnp.sum(folded, axis=2, keepdims=True)
    acc = jnp.zeros(lane.shape, F32)
    for x in range(cells.shape[0]):
        acc = jnp.where(lane == first_lane + x, summed[x], acc)
    return acc


def blur_x(place, rim, mx, near, halos):
    flat = lambda cells: cells.reshape(rim * rim, cells.shape[-1])
    edges = []
    for h, halo in enumerate(halos):
        cells = flat(halo)
        edges.append(jnp.where(place.has_x[h], cells, jnp.zeros_like(cells)))
    blocks = [edges[1], flat(near[1]), flat(near[0]), edges[0]]
    return [
        dot(mx[...], jnp.concatenate(blocks[1 - h:4 - h], axis=0)).astype(BF16) for h in range(2)
    ]


def lit(place, rim, occlusion, shaded, h):
    rows_z = occlusion.shape[1]
    lane = iota((rim, 128), 1)
    shade = (1.0 - jnp.tanh(occlusion)).reshape(rim, rim, rows_z)
    return [rays(shade * shaded[c, h], place.half[h] * rim, lane) for c in range(3)]


def own_kernel(rim, early, mx, my, xs0, xs1, halo0, halo1, *refs):
    place = Place()
    size = rim * rim
    across = [
        blur_x(place, rim, mx, [xs0[g], xs1[g]], [halo0[g], halo1[g]]) for g in range(2)
    ]
    if early:
        shaded, out, partial = refs
    else:
        partial, = refs
    for h in range(2):
        s, e = across[0][h], across[1][h]
        partial[0, h] = dot(my[:, :2 * size], jnp.concatenate([e, s], axis=0))
        other = dot(my[:, size:], jnp.concatenate([e, s], axis=0))
        if not early:
            partial[1, h] = other
            continue
        part = lit(place, rim, other, shaded, h)
        for c in range(3):
            out[c] = part[c] if h == 0 else out[c] + part[c]


def late_kernel(rim, g, mx, my, near0, near1, halo0, halo1, partial, shaded, out):
    place = Place()
    size = rim * rim
    across = blur_x(place, rim, mx, [near0[...], near1[...]], [halo0[...], halo1[...]])
    block = my[:, 2 * size:] if g == 0 else my[:, :size]
    for h in range(2):
        cells = jnp.where(place.has_y[g], across[h], jnp.zeros_like(across[h]))
        part = lit(place, rim, partial[g, h] + dot(block, cells), shaded, h)
        for c in range(3):
            out[c] = part[c] if h == 0 else out[c] + part[c]


def blocks_kernel(rim, depth_count, late_s, late_e, total0, total1, *refs):
    outs, (img,) = refs[:2], refs[2:]
    place = Place()
    rows = 2 * rim
    for g, (colours, total) in enumerate(((late_s, total0), (late_e, total1))):
        at = group_rows(place, rim, g)
        for c in range(3):
            img[c, at, :] = colours[c]
        img[3, at, :] = jnp.exp2(total[...])
    for c in range(4):
        img[4 + c, :, 0:rows] = img[c].T[:rows, :]
    block = rows // depth_count
    bit = place.depth & 1
    for n in range(depth_count // 2):
        for out, b in ((outs[0], bit), (outs[1], 1 - bit)):
            out[n] = img[4:8, pl.ds(pl.multiple_of((2 * n + b) * block, block), block), 0:rows]


def merge_kernel(level, order_map, kept, theirs, *outs):
    me = lax.axis_index("depth")
    bit = me >> level & 1
    low = me & (2 << level) - 1
    merged = []
    for n in range(kept.shape[0]):
        mine = (bit == order_map[(n << level + 1) + low])[None]
        front = jnp.where(mine, kept[n], theirs[n])
        back = jnp.where(mine, theirs[n], kept[n])
        merged.append((front[:3] + front[3:] * back[:3], front[3:] * back[3:]))
    if len(merged) == 1:
        colour, through = merged[0]
        outs[0][...] = jnp.concatenate([colour, 1.0 - through]).reshape(outs[0].shape)
        return
    up = me >> level + 1 & 1
    for n in range(len(merged) // 2):
        even, odd = (jnp.concatenate(merged[2 * n + i]) for i in range(2))
        outs[0][n] = jnp.where(up == 1, odd, even)
        outs[1][n] = jnp.where(up == 1, even, odd)


def call(kernel, name, ins, outs, scratch=(), limit=16 * MIB, **more):
    return pl.pallas_call(
        kernel,
        out_shape=outs,
        in_specs=ins,
        out_specs=jax.tree.map(lambda _: VMEM, outs),
        scratch_shapes=list(scratch),
        compiler_params=pltpu.CompilerParams(vmem_limit_bytes=limit),
        name=name,
        **more,
    )


def per_device(
    density, kernel_taps, tf_centre, tf_width, tf_color, tf_opacity, brick_tf, view_order
):
    rows_x, rows_y, rows_z = density.shape
    rim = (kernel_taps.shape[1] - 1) // 2
    bumps = tf_centre.shape[1]
    size = rim * rim
    axes = ("depth", "sx", "sy")
    counts = tuple(lax.axis_size(axis) for axis in axes)
    depth_count, count_y = counts[0], counts[2]
    struct = jax.ShapeDtypeStruct
    block = rows_x // depth_count
    rounds = sum(1 for shift in range(2) if line_pairs(count_y, shift))

    def swap(piece, x_round, y_round):
        return lax.ppermute(piece, axes, swaps(counts, x_round, y_round))

    in_hbm = lambda array: pltpu.with_memory_space_constraint(array, pltpu.HBM)
    tables = (
        kernel_taps, tf_centre.T, tf_width.T, tf_color.T, tf_opacity.T, brick_tf, view_order
    )
    piece = struct((rim, rim, rows_z), BF16)
    both = struct((2, rim, rim, rows_z), BF16)
    held, xs0, xs1, *refs = call(
        functools.partial(first_kernel, rim, rounds),
        "first",
        [HBM] * (1 + len(tables)),
        [struct((2, 2, rim, rim, rows_z), F32), both, both]
        + [piece] * (2 * rounds)
        + [struct(t.shape, t.dtype) for t in tables],
        [pltpu.SemaphoreType.DMA((4 + len(tables),))],
    )(in_hbm(density), *[in_hbm(t) for t in tables])
    strips, tables = refs[:2 * rounds], refs[2 * rounds:]
    near, corner = [], []
    for r in range(rounds):
        near.append([swap(strips[2 * r + h], None, r) for h in range(2)])
    halo_x = [swap(cells, h, None) for h, cells in enumerate((xs0, xs1))]
    bricks = rows_z // 128
    mx, my, table, signs, order_map = call(
        functools.partial(prepare_kernel, rim),
        "prepare",
        [VMEM] * len(tables),
        [struct((size, 3 * size), BF16)] * 2
        + [struct((4 * bricks, 6 * bumps, 128), F32), struct((2, 2, 8, 128), jnp.int32)]
        + [struct((depth_count, block, rows_y), jnp.int32)],
        [pltpu.VMEM((8, 128), F32)],
    )(*tables)
    shaded, total = [None, None], [None, None]
    for g in (1, 0):
        shaded[g], total[g] = call(
            functools.partial(cells_kernel, rim, bumps, g),
            f"cells{g}",
            [VMEM] * 3,
            [struct((3, 2, rim, rim, rows_z), F32), struct((rim, 128), F32)],
            [pltpu.VMEM((2, size, rows_z), F32), pltpu.VMEM((3, 2, size, rows_z), F32)],
            cost_estimate=pl.CostEstimate(
                flops=density.size * 30, bytes_accessed=density.size * 10, transcendentals=density.size * 3
            ),
        )(held, table, signs)

    for r in range(rounds):
        first, total[1] = lax.optimization_barrier((near[r][0], total[1]))
        corner.append([swap(first, 0, None), swap(strips[2 * r + 1], 1, r)])

    early = rounds < 2
    colours = struct((3, rim, 128), F32)
    partial = struct((2, 2, size, rows_z), F32)
    own = call(
        functools.partial(own_kernel, rim, early),
        "own",
        [VMEM] * (7 if early else 6),
        [colours, partial] if early else [partial],
    )(mx, my, xs0, xs1, *halo_x, *([shaded[1]] if early else []))
    partial = own[-1]
    lights = [None, own[0]]
    for r in range(rounds):
        lights[r] = call(
            functools.partial(late_kernel, rim, r), f"late{r}", [VMEM] * 8, colours
        )(mx, my, *near[r], *corner[r], partial, shaded[r])

    kept, given = call(
        functools.partial(blocks_kernel, rim, depth_count),
        "blocks",
        [VMEM] * 4,
        [struct((depth_count // 2, 4, block, rows_y), F32)] * 2,
        [pltpu.VMEM((8, rows_y, 128), F32)],
    )(*lights, *total)
    level = 0
    while True:
        theirs = lax.ppermute(given, "depth", [(i, i ^ 1 << level) for i in range(depth_count)])
        left = kept.shape[0] // 2
        outs = [struct((left, 4, block, rows_y), F32)] * 2
        merged = call(
            functools.partial(merge_kernel, level),
            f"merge{level}",
            [VMEM] * 3,
            outs if left else struct((4, 1, 1, block, rows_y), F32),
            limit=2 * MIB,
        )(order_map, kept, theirs)
        if not left:
            return merged
        kept, given = merged
        level += 1


def solution(mesh):
    return jax.shard_map(
        per_device,
        mesh=mesh,
        in_specs=(
            P("sx", "sy", "depth"),
            P(),
            P(),
            P(),
            P(),
            P(),
            P("sx", "sy", "depth"),
            P("sx", "sy"),
        ),
        out_specs=P(None, "sx", "depth", None, "sy"),
        check_vma=False,
    )
```

time: 26.3 us -> 25.2 us (0.958)
  the two profiles are of different devices: /device:TPU:0 before, /device:TPU:12 now
where the time goes in v3:
time: 25.2 us; the launch traced here: 25 us
  waiting for transfers between devices  11.2 us (44%)
  starting transfers between devices  6.88 us (27%)
  Pallas kernels  6.84 us (27%)
    ppermute x6, waiting for transfers between devices, swap(): return lax.ppermute(piece, axes, swaps(counts, x_round, y_round))  7.77 us
    ppermute x6, starting transfers between devices, swap(): return lax.ppermute(piece, axes, swaps(counts, x_round, y_round))  5.25 us
    ppermute x2, waiting for transfers between devices, per_device(): lax.ppermute(given, 'depth', [(i, i ^ 1 << level) for i in range(depth_co...  3.44 us
    pallas_call x2, Pallas kernels, per_device(): call(functools.partial(cells_kernel, rim, bumps, g), f'cells{g}', [VMEM]...  2.25 us
    ppermute x2, starting transfers between devices, per_device(): lax.ppermute(given, 'depth', [(i, i ^ 1 << level) for i in range(depth_co...  1.63 us
    pallas_call x1, Pallas kernels, per_device(): call(functools.partial(first_kernel, rim, rounds), 'first', [HBM] * (1 +...  1.31 us
    pallas_call x1, Pallas kernels, per_device(): call(functools.partial(own_kernel, rim, early), 'own', [VMEM] * (7 if ear...  1.1 us
    pallas_call x1, Pallas kernels, per_device(): call(functools.partial(late_kernel, rim, r), f'late{r}', [VMEM] * 8, colo...  0.79 us
  transfers between devices with their start and end apart: 8, of which 4 were waited for; matrix products, arithmetic and copies ran while one was open for 0% of the time, Pallas kernels for 16%

profile of v3, /device:TPU:12, one launch (start us, length us, event | category | flops | bytes accessed | tf_op | source)
XLA Modules:
  0.0 25.0 jit_solution(7135318517559800510)
XLA Ops:
  0.0 1.3 %first.1 = (f32[2,2,16,16,256]{4,3,2,1,0:T(8,128)S(1)}, bf16[2,16,16,256]{3,2,1,0:T(8,128)(2,1)S(1)}, bf16[2,16,16,256]{3,2,1,0:T(8,128)(2,1)S(1)}, bf16[16,16,2...) custom-call(f32[32,32,256]{2,1,0:T(8,128)} %density.1, ...), custom_call_target="tpu_custom_call" | custom-call | tf_op jit(solution)/shard_map/first/pallas_call | solution.py:350
  1.3 0.5 %collective-permute-start.4 = (bf16[2,16,16,256]{3,2,1,0:T(8,128)(2,1)S(1)}, bf16[2,16,16,256]{3,2,1,0:T(8,128)(2,1)S(1)}, u32[]{:S(2)}, u32[]{:S(2)}) collective-permute-start(bf16[2,16,16,256]{3,2,1,0:T(8,128)(2,1)S(1)} %get-tuple-element.51.xs0), channel_id=1, source_target_pairs={{0,2},{1,3},{4,6},{5,7},{8,10},{9,11},{12,14},{13,15},{16,18},{17,... | collective-permute-start | bytes 786440 | tf_op jit(solution)/shard_map/ppermute | solution.py:342
  1.8 2.7 %collective-permute-start.5 = (bf16[2,16,16,256]{3,2,1,0:T(8,128)(2,1)S(1)}, bf16[2,16,16,256]{3,2,1,0:T(8,128)(2,1)S(1)}, u32[]{:S(2)}, u32[]{:S(2)}) collective-permute-start(bf16[2,16,16,256]{3,2,1,0:T(8,128)(2,1)S(1)} %get-tuple-element.52.xs1), channel_id=1, source_target_pairs={{2,4},{3,5},{10,12},{11,13},{18,20},{19,21},{26,28},{27,29},{0,8},... | collective-permute-start | bytes 786440 | tf_op jit(solution)/shard_map/ppermute | solution.py:342
  4.5 0.5 %collective-permute-start = (bf16[16,16,256]{2,1,0:T(8,128)(2,1)S(1)}, bf16[16,16,256]{2,1,0:T(8,128)(2,1)S(1)}, u32[]{:S(2)}, u32[]{:S(2)}) collective-permute-start(bf16[16,16,256]{2,1,0:T(8,128)(2,1)S(1)} %get-tuple-element.44), channel_id=1, source_target_pairs={{0,1},{2,3},{4,5},{6,7},{8,9},{10,11},{12,13},{14,15},{16,17},{18,... | collective-permute-start | bytes 393224 | tf_op jit(solution)/shard_map/ppermute | solution.py:342
  5.0 1.5 %collective-permute-start.1 = (bf16[16,16,256]{2,1,0:T(8,128)(2,1)S(1)}, bf16[16,16,256]{2,1,0:T(8,128)(2,1)S(1)}, u32[]{:S(2)}, u32[]{:S(2)}) collective-permute-start(bf16[16,16,256]{2,1,0:T(8,128)(2,1)S(1)} %get-tuple-element.45), channel_id=1, source_target_pairs={{0,1},{2,3},{4,5},{6,7},{8,9},{10,11},{12,13},{14,15},{16,17},{18,... | collective-permute-start | bytes 393224 | tf_op jit(solution)/shard_map/ppermute | solution.py:342
  6.6 0.0 collective-permute-start.3
  6.6 0.6 %prepare.1 = (bf16[256,768]{1,0:T(8,128)(2,1)S(1)}, bf16[256,768]{1,0:T(8,128)(2,1)S(1)}, f32[8,24,128]{2,1,0:T(8,128)S(1)}, s32[2,2,8,128]{3,2,1,0:T(8,128)S(1)}, s32[4,8,32]{2,1,0:T(8,128)S(1)}) custom-call(bf16[2,33]{1,0:T(2,128)(2,1)S(1)} %get-tuple-element.34.taps, f32[4,8]{1,0:T(4,128)S(1)} %get-tuple-element.35.centre, ...), custom_call_target="tpu_custom_call" | custom-call | tf_op jit(solution)/shard_map/prepare/pallas_call | solution.py:365
  7.2 1.1 %cells1.1 = (f32[3,2,16,16,256]{4,3,2,1,0:T(8,128)S(1)}, f32[16,128]{1,0:T(8,128)S(1)}) custom-call(f32[2,2,16,16,256]{4,3,2,1,0:T(8,128)S(1)} %get-tuple-element.46.held, f32[8,24,128]{2,1,0:T(8,128)S(1)} %get-tuple-element.47.table, s32[2,2,8,128]{3,2,1,0:T(8,128)S(1)} %get-tuple-element.48.signs), custom_call_target="tpu_custom_call" | custom-call | flops 7864320 | bytes 2621440 | tf_op jit(solution)/shard_map/cells1/pallas_call | solution.py:376
  8.3 5.1 %collective-permute-done.near0 = bf16[16,16,256]{2,1,0:T(8,128)(2,1)S(1)} collective-permute-done((bf16[16,16,256]{2,1,0:T(8,128)(2,1)S(1)}, bf16[16,16,256]{2,1,0:T(8,128)(2,1)S(1)}, u32[]{:S(2)}, u32[]{:S(2)}) %collective-permute-start) | collective-permute-done | bytes 131104 | tf_op jit(solution)/shard_map/ppermute | solution.py:342
  13.4 0.0 collective-permute-start.2
  13.4 1.1 %cells0.1 = (f32[3,2,16,16,256]{4,3,2,1,0:T(8,128)S(1)}, f32[16,128]{1,0:T(8,128)S(1)}) custom-call(f32[2,2,16,16,256]{4,3,2,1,0:T(8,128)S(1)} %get-tuple-element.46.held, f32[8,24,128]{2,1,0:T(8,128)S(1)} %get-tuple-element.47.table, s32[2,2,8,128]{3,2,1,0:T(8,128)S(1)} %get-tuple-element.48.signs), custom_call_target="tpu_custom_call" | custom-call | flops 7864320 | bytes 2621440 | tf_op jit(solution)/shard_map/cells0/pallas_call | solution.py:376
  14.6 0.0 collective-permute-done.4.halo0
  14.6 0.0 collective-permute-done.5.halo1
  14.6 1.1 %own.1 = (f32[3,16,128]{2,1,0:T(8,128)S(1)}, f32[2,2,256,256]{3,2,1,0:T(8,128)S(1)}) custom-call(bf16[256,768]{1,0:T(8,128)(2,1)S(1)} %get-tuple-element.42.mx, bf16[256,768]{1,0:T(8,128)(2,1)S(1)} %get-tuple-element.43.my, bf16[2,16,16,256]{3,2,1,0:T(8,128)(2,1)S(1)} %get-tuple-element.51.xs0, bf16[2,16,16,256]{3,2,1,0:T(8,128)(2,1)S(1)} %get-tuple-element.52.xs1, ...), custom_call_target="tpu_custom_call" | custom-call | tf_op jit(solution)/shard_map/own/pallas_call | solution.py:394
  15.7 0.0 collective-permute-done.1.near1
  15.7 0.0 collective-permute-done.3.halo1
  15.7 2.7 %collective-permute-done.2.halo0 = bf16[16,16,256]{2,1,0:T(8,128)(2,1)S(1)} collective-permute-done((bf16[16,16,256]{2,1,0:T(8,128)(2,1)S(1)}, bf16[16,16,256]{2,1,0:T(8,128)(2,1)S(1)}, u32[]{:S(2)}, u32[]{:S(2)}) %collective-permute-start.2) | collective-permute-done | bytes 131104 | tf_op jit(solution)/shard_map/ppermute | solution.py:342
  18.4 0.8 %late0.1.late_s = f32[3,16,128]{2,1,0:T(8,128)S(1)} custom-call(bf16[256,768]{1,0:T(8,128)(2,1)S(1)} %get-tuple-element.42.mx, bf16[256,768]{1,0:T(8,128)(2,1)S(1)} %get-tuple-element.43.my, bf16[16,16,256]{2,1,0:T(8,128)(2,1)S(1)} %collective-permute-done.near0, bf16[16,16,256]{2,1,0:T(8,128)(2,1)S(1)} %collective-permute-done.1.near1, ...), custom_call_target="tpu_custom_call" | custom-call | tf_op jit(solution)/shard_map/late0/pallas_call | solution.py:403
  19.2 0.1 blocks.1
  19.3 0.1 collective-permute-start.6
  19.4 1.2 %collective-permute-done.6.theirs = f32[2,4,8,32]{3,2,1,0:T(8,128)S(1)} collective-permute-done((f32[2,4,8,32]{3,2,1,0:T(8,128)S(1)}, f32[2,4,8,32]{3,2,1,0:T(8,128)S(1)}, u32[]{:S(2)}, u32[]{:S(2)}) %collective-permute-start.6) | collective-permute-done | bytes 8224 | tf_op jit(solution)/shard_map/ppermute | solution.py:416
  20.6 1.6 %collective-permute-start.7 = (f32[1,4,8,32]{3,2,1,0:T(8,128)S(1)}, f32[1,4,8,32]{3,2,1,0:T(8,128)S(1)}, u32[]{:S(2)}, u32[]{:S(2)}) collective-permute-start(f32[1,4,8,32]{3,2,1,0:T(8,128)S(1)} %get-tuple-element.62), channel_id=1, source_target_pairs={{0,16},{8,24},{16,0},{24,8},{1,17},{9,25},{17,1},{25,9},{2,18},{10... | collective-permute-start | bytes 12296 | tf_op jit(solution)/shard_map/ppermute | solution.py:416
  22.2 2.2 %collective-permute-done.7.theirs = f32[1,4,8,32]{3,2,1,0:T(8,128)S(1)} collective-permute-done((f32[1,4,8,32]{3,2,1,0:T(8,128)S(1)}, f32[1,4,8,32]{3,2,1,0:T(8,128)S(1)}, u32[]{:S(2)}, u32[]{:S(2)}) %collective-permute-start.7) | collective-permute-done | bytes 4128 | tf_op jit(solution)/shard_map/ppermute | solution.py:416
  24.4 0.6 %merge1.1 = f32[4,1,1,8,32]{4,3,2,1,0:T(8,128)} custom-call(s32[4,8,32]{2,1,0:T(8,128)S(1)} %get-tuple-element.41.order_map, f32[1,4,8,32]{3,2,1,0:T(8,128)S(1)} %get-tuple-element.61.kept, f32[1,4,8,32]{3,2,1,0:T(8,128)S(1)} %collective-permute-done.7.theirs), custom_call_target="tpu_custom_call" | custom-call | tf_op jit(solution)/shard_map/merge1/pallas_call | solution.py:419
  (1 shorter events, 0.0 us)
Async XLA Ops:
  1.3 13.2 %collective-permute-start.4 = (bf16[2,16,16,256]{3,2,1,0:T(8,128)(2,1)S(1)}, bf16[2,16,16,256]{3,2,1,0:T(8,128)(2,1)S(1)}, u32[]{:S(2)}, u32[]{:S(2)}) collective-permute-start(bf16[2,16,16,256]{3,2,1,0:T(8,128)(2,1)S(1)} %get-tuple-element.51.xs0), channel_id=1, source_target_pairs={{0,2},{1,3},{4,6},{5,7},{8,10},{9,11},{12,14},{13,15},{16,18},{17,... | collective-permute-start | bytes 786440 | tf_op jit(solution)/shard_map/ppermute | solution.py:342
  1.8 12.7 %collective-permute-start.5 = (bf16[2,16,16,256]{3,2,1,0:T(8,128)(2,1)S(1)}, bf16[2,16,16,256]{3,2,1,0:T(8,128)(2,1)S(1)}, u32[]{:S(2)}, u32[]{:S(2)}) collective-permute-start(bf16[2,16,16,256]{3,2,1,0:T(8,128)(2,1)S(1)} %get-tuple-element.52.xs1), channel_id=1, source_target_pairs={{2,4},{3,5},{10,12},{11,13},{18,20},{19,21},{26,28},{27,29},{0,8},... | collective-permute-start | bytes 786440 | tf_op jit(solution)/shard_map/ppermute | solution.py:342
  4.5 8.9 %collective-permute-start = (bf16[16,16,256]{2,1,0:T(8,128)(2,1)S(1)}, bf16[16,16,256]{2,1,0:T(8,128)(2,1)S(1)}, u32[]{:S(2)}, u32[]{:S(2)}) collective-permute-start(bf16[16,16,256]{2,1,0:T(8,128)(2,1)S(1)} %get-tuple-element.44), channel_id=1, source_target_pairs={{0,1},{2,3},{4,5},{6,7},{8,9},{10,11},{12,13},{14,15},{16,17},{18,... | collective-permute-start | bytes 393224 | tf_op jit(solution)/shard_map/ppermute | solution.py:342
  5.0 10.7 %collective-permute-start.1 = (bf16[16,16,256]{2,1,0:T(8,128)(2,1)S(1)}, bf16[16,16,256]{2,1,0:T(8,128)(2,1)S(1)}, u32[]{:S(2)}, u32[]{:S(2)}) collective-permute-start(bf16[16,16,256]{2,1,0:T(8,128)(2,1)S(1)} %get-tuple-element.45), channel_id=1, source_target_pairs={{0,1},{2,3},{4,5},{6,7},{8,9},{10,11},{12,13},{14,15},{16,17},{18,... | collective-permute-start | bytes 393224 | tf_op jit(solution)/shard_map/ppermute | solution.py:342
  6.6 9.1 %collective-permute-start.3 = (bf16[16,16,256]{2,1,0:T(8,128)(2,1)S(1)}, bf16[16,16,256]{2,1,0:T(8,128)(2,1)S(1)}, u32[]{:S(2)}, u32[]{:S(2)}) collective-permute-start(bf16[16,16,256]{2,1,0:T(8,128)(2,1)S(1)} %get-tuple-element.45), channel_id=1, source_target_pairs={{2,5},{3,4},{10,13},{11,12},{18,21},{19,20},{26,29},{27,28},{0,8},... | collective-permute-start | bytes 393224 | tf_op jit(solution)/shard_map/ppermute | solution.py:342
  13.4 5.0 %collective-permute-start.2 = (bf16[16,16,256]{2,1,0:T(8,128)(2,1)S(1)}, bf16[16,16,256]{2,1,0:T(8,128)(2,1)S(1)}, u32[]{:S(2)}, u32[]{:S(2)}) collective-permute-start(bf16[16,16,256]{2,1,0:T(8,128)(2,1)S(1)} %collective-permute-done.near0), channel_id=1, source_target_pairs={{0,2},{1,3},{4,6},{5,7},{8,10},{9,11},{12,14},{13,15},{16,18},{17,... | collective-permute-start | bytes 393224 | tf_op jit(solution)/shard_map/ppermute | solution.py:342
  19.3 1.3 %collective-permute-start.6 = (f32[2,4,8,32]{3,2,1,0:T(8,128)S(1)}, f32[2,4,8,32]{3,2,1,0:T(8,128)S(1)}, u32[]{:S(2)}, u32[]{:S(2)}) collective-permute-start(f32[2,4,8,32]{3,2,1,0:T(8,128)S(1)} %get-tuple-element.60), channel_id=1, source_target_pairs={{0,8},{8,0},{16,24},{24,16},{1,9},{9,1},{17,25},{25,17},{2,10},{10... | collective-permute-start | bytes 24584 | tf_op jit(solution)/shard_map/ppermute | solution.py:416
  20.6 3.8 %collective-permute-start.7 = (f32[1,4,8,32]{3,2,1,0:T(8,128)S(1)}, f32[1,4,8,32]{3,2,1,0:T(8,128)S(1)}, u32[]{:S(2)}, u32[]{:S(2)}) collective-permute-start(f32[1,4,8,32]{3,2,1,0:T(8,128)S(1)} %get-tuple-element.62), channel_id=1, source_target_pairs={{0,16},{8,24},{16,0},{24,8},{1,17},{9,25},{17,1},{25,9},{2,18},{10... | collective-permute-start | bytes 12296 | tf_op jit(solution)/shard_map/ppermute | solution.py:416

commit v4 on v3

--- a/solution.py
+++ b/solution.py
@@ -357,10 +357,9 @@
         [pltpu.SemaphoreType.DMA((4 + len(tables),))],
     )(in_hbm(density), *[in_hbm(t) for t in tables])
     strips, tables = refs[:2 * rounds], refs[2 * rounds:]
-    near, corner = [], []
-    for r in range(rounds):
-        near.append([swap(strips[2 * r + h], None, r) for h in range(2)])
+    near = [[swap(strips[2 * r], None, r), None] for r in range(rounds)]
     halo_x = [swap(cells, h, None) for h, cells in enumerate((xs0, xs1))]
+
     bricks = rows_z // 128
     mx, my, table, signs, order_map = call(
         functools.partial(prepare_kernel, rim),
@@ -371,6 +370,11 @@
         + [struct((depth_count, block, rows_y), jnp.int32)],
         [pltpu.VMEM((8, 128), F32)],
     )(*tables)
+    corner = [[None, None] for r in range(rounds)]
+    for r in range(rounds):
+        strip, table = lax.optimization_barrier((strips[2 * r + 1], table))
+        corner[r][1] = swap(strip, 1, r)
+        near[r][1] = swap(strip, None, r)
     shaded, total = [None, None], [None, None]
     for g in (1, 0):
         shaded[g], total[g] = call(
@@ -385,8 +389,8 @@
         )(held, table, signs)
 
     for r in range(rounds):
-        first, total[1] = lax.optimization_barrier((near[r][0], total[1]))
-        corner.append([swap(first, 0, None), swap(strips[2 * r + 1], 1, r)])
+        strip, total[1] = lax.optimization_barrier((near[r][0], total[1]))
+        corner[r][0] = swap(strip, 0, None)
 
     early = rounds < 2
     colours = struct((3, rim, 128), F32)

time: 25.2 us -> 25.2 us (level)
  no operation moved by 1% of the time
where the time goes in v4:
time: 25.2 us; the launch traced here: 25 us
  waiting for transfers between devices  11.1 us (44%)
  starting transfers between devices  6.94 us (28%)
  Pallas kernels  6.84 us (27%)
    ppermute x6, waiting for transfers between devices, swap(): return lax.ppermute(piece, axes, swaps(counts, x_round, y_round))  7.71 us
    ppermute x6, starting transfers between devices, swap(): return lax.ppermute(piece, axes, swaps(counts, x_round, y_round))  5.32 us
    ppermute x2, waiting for transfers between devices, per_device(): lax.ppermute(given, 'depth', [(i, i ^ 1 << level) for i in range(depth_co...  3.44 us
    pallas_call x2, Pallas kernels, per_device(): call(functools.partial(cells_kernel, rim, bumps, g), f'cells{g}', [VMEM]...  2.25 us
    ppermute x2, starting transfers between devices, per_device(): lax.ppermute(given, 'depth', [(i, i ^ 1 << level) for i in range(depth_co...  1.63 us
    pallas_call x1, Pallas kernels, per_device(): call(functools.partial(first_kernel, rim, rounds), 'first', [HBM] * (1 +...  1.31 us
    pallas_call x1, Pallas kernels, per_device(): call(functools.partial(own_kernel, rim, early), 'own', [VMEM] * (7 if ear...  1.1 us
    pallas_call x1, Pallas kernels, per_device(): call(functools.partial(late_kernel, rim, r), f'late{r}', [VMEM] * 8, colo...  0.79 us
  transfers between devices with their start and end apart: 8, of which 4 were waited for; matrix products, arithmetic and copies ran while one was open for 0% of the time, Pallas kernels for 16%

profile of v4, /device:TPU:12, one launch (start us, length us, event | category | flops | bytes accessed | tf_op | source)
XLA Modules:
  0.0 25.0 jit_solution(16153492919519164788)
XLA Ops:
  0.0 1.3 %first.1 = (f32[2,2,16,16,256]{4,3,2,1,0:T(8,128)S(1)}, bf16[2,16,16,256]{3,2,1,0:T(8,128)(2,1)S(1)}, bf16[2,16,16,256]{3,2,1,0:T(8,128)(2,1)S(1)}, bf16[16,16,2...) custom-call(f32[32,32,256]{2,1,0:T(8,128)} %density.1, ...), custom_call_target="tpu_custom_call" | custom-call | tf_op jit(solution)/shard_map/first/pallas_call | solution.py:350
  1.3 0.5 %collective-permute-start.4 = (bf16[2,16,16,256]{3,2,1,0:T(8,128)(2,1)S(1)}, bf16[2,16,16,256]{3,2,1,0:T(8,128)(2,1)S(1)}, u32[]{:S(2)}, u32[]{:S(2)}) collective-permute-start(bf16[2,16,16,256]{3,2,1,0:T(8,128)(2,1)S(1)} %get-tuple-element.55.xs0), channel_id=1, source_target_pairs={{0,2},{1,3},{4,6},{5,7},{8,10},{9,11},{12,14},{13,15},{16,18},{17,... | collective-permute-start | bytes 786440 | tf_op jit(solution)/shard_map/ppermute | solution.py:342
  1.8 2.7 %collective-permute-start.5 = (bf16[2,16,16,256]{3,2,1,0:T(8,128)(2,1)S(1)}, bf16[2,16,16,256]{3,2,1,0:T(8,128)(2,1)S(1)}, u32[]{:S(2)}, u32[]{:S(2)}) collective-permute-start(bf16[2,16,16,256]{3,2,1,0:T(8,128)(2,1)S(1)} %get-tuple-element.56.xs1), channel_id=1, source_target_pairs={{2,4},{3,5},{10,12},{11,13},{18,20},{19,21},{26,28},{27,29},{0,8},... | collective-permute-start | bytes 786440 | tf_op jit(solution)/shard_map/ppermute | solution.py:342
  4.5 0.5 %collective-permute-start = (bf16[16,16,256]{2,1,0:T(8,128)(2,1)S(1)}, bf16[16,16,256]{2,1,0:T(8,128)(2,1)S(1)}, u32[]{:S(2)}, u32[]{:S(2)}) collective-permute-start(bf16[16,16,256]{2,1,0:T(8,128)(2,1)S(1)} %get-tuple-element.46), channel_id=1, source_target_pairs={{0,1},{2,3},{4,5},{6,7},{8,9},{10,11},{12,13},{14,15},{16,17},{18,... | collective-permute-start | bytes 393224 | tf_op jit(solution)/shard_map/ppermute | solution.py:342
  5.0 0.6 %prepare.1 = (bf16[256,768]{1,0:T(8,128)(2,1)S(1)}, bf16[256,768]{1,0:T(8,128)(2,1)S(1)}, f32[8,24,128]{2,1,0:T(8,128)S(1)}, s32[2,2,8,128]{3,2,1,0:T(8,128)S(1)}, s32[4,8,32]{2,1,0:T(8,128)S(1)}) custom-call(bf16[2,33]{1,0:T(2,128)(2,1)S(1)} %get-tuple-element.36.taps, f32[4,8]{1,0:T(4,128)S(1)} %get-tuple-element.37.centre, ...), custom_call_target="tpu_custom_call" | custom-call | tf_op jit(solution)/shard_map/prepare/pallas_call | solution.py:364
  5.7 1.6 %collective-permute-start.1 = (bf16[16,16,256]{2,1,0:T(8,128)(2,1)S(1)}, bf16[16,16,256]{2,1,0:T(8,128)(2,1)S(1)}, u32[]{:S(2)}, u32[]{:S(2)}) collective-permute-start(bf16[16,16,256]{2,1,0:T(8,128)(2,1)S(1)} %get-tuple-element.49), channel_id=1, source_target_pairs={{0,1},{2,3},{4,5},{6,7},{8,9},{10,11},{12,13},{14,15},{16,17},{18,... | collective-permute-start | bytes 393224 | tf_op jit(solution)/shard_map/ppermute | solution.py:342
  7.3 0.0 collective-permute-start.3
  7.3 1.1 %cells1.1 = (f32[3,2,16,16,256]{4,3,2,1,0:T(8,128)S(1)}, f32[16,128]{1,0:T(8,128)S(1)}) custom-call(f32[2,2,16,16,256]{4,3,2,1,0:T(8,128)S(1)} %get-tuple-element.50.held, f32[8,24,128]{2,1,0:T(8,128)S(1)} %get-tuple-element.51.table, s32[2,2,8,128]{3,2,1,0:T(8,128)S(1)} %get-tuple-element.52.signs), custom_call_target="tpu_custom_call" | custom-call | flops 7864320 | bytes 2621440 | tf_op jit(solution)/shard_map/cells1/pallas_call | solution.py:380
  8.4 5.0 %collective-permute-done.near0 = bf16[16,16,256]{2,1,0:T(8,128)(2,1)S(1)} collective-permute-done((bf16[16,16,256]{2,1,0:T(8,128)(2,1)S(1)}, bf16[16,16,256]{2,1,0:T(8,128)(2,1)S(1)}, u32[]{:S(2)}, u32[]{:S(2)}) %collective-permute-start) | collective-permute-done | bytes 131104 | tf_op jit(solution)/shard_map/ppermute | solution.py:342
  13.4 0.0 collective-permute-start.2
  13.4 1.1 %cells0.1 = (f32[3,2,16,16,256]{4,3,2,1,0:T(8,128)S(1)}, f32[16,128]{1,0:T(8,128)S(1)}) custom-call(f32[2,2,16,16,256]{4,3,2,1,0:T(8,128)S(1)} %get-tuple-element.50.held, f32[8,24,128]{2,1,0:T(8,128)S(1)} %get-tuple-element.51.table, s32[2,2,8,128]{3,2,1,0:T(8,128)S(1)} %get-tuple-element.52.signs), custom_call_target="tpu_custom_call" | custom-call | flops 7864320 | bytes 2621440 | tf_op jit(solution)/shard_map/cells0/pallas_call | solution.py:380
  14.6 0.0 collective-permute-done.4.halo0
  14.6 0.0 collective-permute-done.5.halo1
  14.6 1.1 %own.1 = (f32[3,16,128]{2,1,0:T(8,128)S(1)}, f32[2,2,256,256]{3,2,1,0:T(8,128)S(1)}) custom-call(bf16[256,768]{1,0:T(8,128)(2,1)S(1)} %get-tuple-element.44.mx, bf16[256,768]{1,0:T(8,128)(2,1)S(1)} %get-tuple-element.45.my, bf16[2,16,16,256]{3,2,1,0:T(8,128)(2,1)S(1)} %get-tuple-element.55.xs0, bf16[2,16,16,256]{3,2,1,0:T(8,128)(2,1)S(1)} %get-tuple-element.56.xs1, ...), custom_call_target="tpu_custom_call" | custom-call | tf_op jit(solution)/shard_map/own/pallas_call | solution.py:398
  15.7 0.0 collective-permute-done.1.near1
  15.7 0.0 collective-permute-done.3.halo1
  15.7 2.7 %collective-permute-done.2.halo0 = bf16[16,16,256]{2,1,0:T(8,128)(2,1)S(1)} collective-permute-done((bf16[16,16,256]{2,1,0:T(8,128)(2,1)S(1)}, bf16[16,16,256]{2,1,0:T(8,128)(2,1)S(1)}, u32[]{:S(2)}, u32[]{:S(2)}) %collective-permute-start.2) | collective-permute-done | bytes 131104 | tf_op jit(solution)/shard_map/ppermute | solution.py:342
  18.4 0.8 %late0.1.late_s = f32[3,16,128]{2,1,0:T(8,128)S(1)} custom-call(bf16[256,768]{1,0:T(8,128)(2,1)S(1)} %get-tuple-element.44.mx, bf16[256,768]{1,0:T(8,128)(2,1)S(1)} %get-tuple-element.45.my, bf16[16,16,256]{2,1,0:T(8,128)(2,1)S(1)} %collective-permute-done.near0, bf16[16,16,256]{2,1,0:T(8,128)(2,1)S(1)} %collective-permute-done.1.near1, ...), custom_call_target="tpu_custom_call" | custom-call | tf_op jit(solution)/shard_map/late0/pallas_call | solution.py:407
  19.2 0.1 blocks.1
  19.3 0.1 collective-permute-start.6
  19.4 1.2 %collective-permute-done.6.theirs = f32[2,4,8,32]{3,2,1,0:T(8,128)S(1)} collective-permute-done((f32[2,4,8,32]{3,2,1,0:T(8,128)S(1)}, f32[2,4,8,32]{3,2,1,0:T(8,128)S(1)}, u32[]{:S(2)}, u32[]{:S(2)}) %collective-permute-start.6) | collective-permute-done | bytes 8224 | tf_op jit(solution)/shard_map/ppermute | solution.py:420
  20.6 1.6 %collective-permute-start.7 = (f32[1,4,8,32]{3,2,1,0:T(8,128)S(1)}, f32[1,4,8,32]{3,2,1,0:T(8,128)S(1)}, u32[]{:S(2)}, u32[]{:S(2)}) collective-permute-start(f32[1,4,8,32]{3,2,1,0:T(8,128)S(1)} %get-tuple-element.66), channel_id=1, source_target_pairs={{0,16},{8,24},{16,0},{24,8},{1,17},{9,25},{17,1},{25,9},{2,18},{10... | collective-permute-start | bytes 12296 | tf_op jit(solution)/shard_map/ppermute | solution.py:420
  22.2 2.2 %collective-permute-done.7.theirs = f32[1,4,8,32]{3,2,1,0:T(8,128)S(1)} collective-permute-done((f32[1,4,8,32]{3,2,1,0:T(8,128)S(1)}, f32[1,4,8,32]{3,2,1,0:T(8,128)S(1)}, u32[]{:S(2)}, u32[]{:S(2)}) %collective-permute-start.7) | collective-permute-done | bytes 4128 | tf_op jit(solution)/shard_map/ppermute | solution.py:420
  24.4 0.6 %merge1.1 = f32[4,1,1,8,32]{4,3,2,1,0:T(8,128)} custom-call(s32[4,8,32]{2,1,0:T(8,128)S(1)} %get-tuple-element.43.order_map, f32[1,4,8,32]{3,2,1,0:T(8,128)S(1)} %get-tuple-element.65.kept, f32[1,4,8,32]{3,2,1,0:T(8,128)S(1)} %collective-permute-done.7.theirs), custom_call_target="tpu_custom_call" | custom-call | tf_op jit(solution)/shard_map/merge1/pallas_call | solution.py:423
  (1 shorter events, 0.0 us)
Async XLA Ops:
  1.3 13.2 %collective-permute-start.4 = (bf16[2,16,16,256]{3,2,1,0:T(8,128)(2,1)S(1)}, bf16[2,16,16,256]{3,2,1,0:T(8,128)(2,1)S(1)}, u32[]{:S(2)}, u32[]{:S(2)}) collective-permute-start(bf16[2,16,16,256]{3,2,1,0:T(8,128)(2,1)S(1)} %get-tuple-element.55.xs0), channel_id=1, source_target_pairs={{0,2},{1,3},{4,6},{5,7},{8,10},{9,11},{12,14},{13,15},{16,18},{17,... | collective-permute-start | bytes 786440 | tf_op jit(solution)/shard_map/ppermute | solution.py:342
  1.8 12.7 %collective-permute-start.5 = (bf16[2,16,16,256]{3,2,1,0:T(8,128)(2,1)S(1)}, bf16[2,16,16,256]{3,2,1,0:T(8,128)(2,1)S(1)}, u32[]{:S(2)}, u32[]{:S(2)}) collective-permute-start(bf16[2,16,16,256]{3,2,1,0:T(8,128)(2,1)S(1)} %get-tuple-element.56.xs1), channel_id=1, source_target_pairs={{2,4},{3,5},{10,12},{11,13},{18,20},{19,21},{26,28},{27,29},{0,8},... | collective-permute-start | bytes 786440 | tf_op jit(solution)/shard_map/ppermute | solution.py:342
  4.5 8.9 %collective-permute-start = (bf16[16,16,256]{2,1,0:T(8,128)(2,1)S(1)}, bf16[16,16,256]{2,1,0:T(8,128)(2,1)S(1)}, u32[]{:S(2)}, u32[]{:S(2)}) collective-permute-start(bf16[16,16,256]{2,1,0:T(8,128)(2,1)S(1)} %get-tuple-element.46), channel_id=1, source_target_pairs={{0,1},{2,3},{4,5},{6,7},{8,9},{10,11},{12,13},{14,15},{16,17},{18,... | collective-permute-start | bytes 393224 | tf_op jit(solution)/shard_map/ppermute | solution.py:342
  5.7 10.0 %collective-permute-start.1 = (bf16[16,16,256]{2,1,0:T(8,128)(2,1)S(1)}, bf16[16,16,256]{2,1,0:T(8,128)(2,1)S(1)}, u32[]{:S(2)}, u32[]{:S(2)}) collective-permute-start(bf16[16,16,256]{2,1,0:T(8,128)(2,1)S(1)} %get-tuple-element.49), channel_id=1, source_target_pairs={{0,1},{2,3},{4,5},{6,7},{8,9},{10,11},{12,13},{14,15},{16,17},{18,... | collective-permute-start | bytes 393224 | tf_op jit(solution)/shard_map/ppermute | solution.py:342
  7.3 8.4 %collective-permute-start.3 = (bf16[16,16,256]{2,1,0:T(8,128)(2,1)S(1)}, bf16[16,16,256]{2,1,0:T(8,128)(2,1)S(1)}, u32[]{:S(2)}, u32[]{:S(2)}) collective-permute-start(bf16[16,16,256]{2,1,0:T(8,128)(2,1)S(1)} %get-tuple-element.49), channel_id=1, source_target_pairs={{2,5},{3,4},{10,13},{11,12},{18,21},{19,20},{26,29},{27,28},{0,8},... | collective-permute-start | bytes 393224 | tf_op jit(solution)/shard_map/ppermute | solution.py:342
  13.4 5.0 %collective-permute-start.2 = (bf16[16,16,256]{2,1,0:T(8,128)(2,1)S(1)}, bf16[16,16,256]{2,1,0:T(8,128)(2,1)S(1)}, u32[]{:S(2)}, u32[]{:S(2)}) collective-permute-start(bf16[16,16,256]{2,1,0:T(8,128)(2,1)S(1)} %collective-permute-done.near0), channel_id=1, source_target_pairs={{0,2},{1,3},{4,6},{5,7},{8,10},{9,11},{12,14},{13,15},{16,18},{17,... | collective-permute-start | bytes 393224 | tf_op jit(solution)/shard_map/ppermute | solution.py:342
  19.3 1.3 %collective-permute-start.6 = (f32[2,4,8,32]{3,2,1,0:T(8,128)S(1)}, f32[2,4,8,32]{3,2,1,0:T(8,128)S(1)}, u32[]{:S(2)}, u32[]{:S(2)}) collective-permute-start(f32[2,4,8,32]{3,2,1,0:T(8,128)S(1)} %get-tuple-element.64), channel_id=1, source_target_pairs={{0,8},{8,0},{16,24},{24,16},{1,9},{9,1},{17,25},{25,17},{2,10},{10... | collective-permute-start | bytes 24584 | tf_op jit(solution)/shard_map/ppermute | solution.py:420
  20.6 3.8 %collective-permute-start.7 = (f32[1,4,8,32]{3,2,1,0:T(8,128)S(1)}, f32[1,4,8,32]{3,2,1,0:T(8,128)S(1)}, u32[]{:S(2)}, u32[]{:S(2)}) collective-permute-start(f32[1,4,8,32]{3,2,1,0:T(8,128)S(1)} %get-tuple-element.66), channel_id=1, source_target_pairs={{0,16},{8,24},{16,0},{24,8},{1,17},{9,25},{17,1},{25,9},{2,18},{10... | collective-permute-start | bytes 12296 | tf_op jit(solution)/shard_map/ppermute | solution.py:420

commit v5 on v3

--- a/solution.py
+++ b/solution.py
@@ -357,10 +357,9 @@
         [pltpu.SemaphoreType.DMA((4 + len(tables),))],
     )(in_hbm(density), *[in_hbm(t) for t in tables])
     strips, tables = refs[:2 * rounds], refs[2 * rounds:]
-    near, corner = [], []
-    for r in range(rounds):
-        near.append([swap(strips[2 * r + h], None, r) for h in range(2)])
-    halo_x = [swap(cells, h, None) for h, cells in enumerate((xs0, xs1))]
+    near = [[swap(strips[2 * r], None, r), None] for r in range(rounds)]
+    halo_x = [swap(xs0, 0, None), None]
+
     bricks = rows_z // 128
     mx, my, table, signs, order_map = call(
         functools.partial(prepare_kernel, rim),
@@ -371,6 +370,8 @@
         + [struct((depth_count, block, rows_y), jnp.int32)],
         [pltpu.VMEM((8, 128), F32)],
     )(*tables)
+    cells, table = lax.optimization_barrier((xs1, table))
+    halo_x[1] = swap(cells, 1, None)
     shaded, total = [None, None], [None, None]
     for g in (1, 0):
         shaded[g], total[g] = call(
@@ -384,9 +385,12 @@
             ),
         )(held, table, signs)
 
+    corner = [[None, None] for r in range(rounds)]
     for r in range(rounds):
-        first, total[1] = lax.optimization_barrier((near[r][0], total[1]))
-        corner.append([swap(first, 0, None), swap(strips[2 * r + 1], 1, r)])
+        strip, total[1] = lax.optimization_barrier((strips[2 * r + 1], total[1]))
+        arrived, total[1] = lax.optimization_barrier((near[r][0], total[1]))
+        corner[r] = [swap(arrived, 0, None), swap(strip, 1, r)]
+        near[r][1] = swap(strip, None, r)
 
     early = rounds < 2
     colours = struct((3, rim, 128), F32)

time: 25.2 us -> 24.5 us (0.972)
  the two profiles are of different devices: /device:TPU:12 before, /device:TPU:14 now
where the time goes in v5:
time: 24.5 us; the launch traced here: 24.3 us
  waiting for transfers between devices  11.4 us (47%)
  Pallas kernels  6.84 us (28%)
  starting transfers between devices  6.07 us (25%)
    ppermute x6, waiting for transfers between devices, swap(): return lax.ppermute(piece, axes, swaps(counts, x_round, y_round))  6.97 us
    ppermute x6, starting transfers between devices, swap(): return lax.ppermute(piece, axes, swaps(counts, x_round, y_round))  5.4 us
    ppermute x2, waiting for transfers between devices, per_device(): lax.ppermute(given, 'depth', [(i, i ^ 1 << level) for i in range(depth_co...  4.4 us
    pallas_call x2, Pallas kernels, per_device(): call(functools.partial(cells_kernel, rim, bumps, g), f'cells{g}', [VMEM]...  2.25 us
    pallas_call x1, Pallas kernels, per_device(): call(functools.partial(first_kernel, rim, rounds), 'first', [HBM] * (1 +...  1.31 us
    pallas_call x1, Pallas kernels, per_device(): call(functools.partial(own_kernel, rim, early), 'own', [VMEM] * (7 if ear...  1.1 us
    pallas_call x1, Pallas kernels, per_device(): call(functools.partial(late_kernel, rim, r), f'late{r}', [VMEM] * 8, colo...  0.79 us
    ppermute x2, starting transfers between devices, per_device(): lax.ppermute(given, 'depth', [(i, i ^ 1 << level) for i in range(depth_co...  0.67 us
  transfers between devices with their start and end apart: 8, of which 5 were waited for; matrix products, arithmetic and copies ran while one was open for 0% of the time, Pallas kernels for 16%

profile of v5, /device:TPU:14, one launch (start us, length us, event | category | flops | bytes accessed | tf_op | source)
XLA Modules:
  0.0 24.3 jit_solution(14733466561931265126)
XLA Ops:
  0.0 1.3 %first.1 = (f32[2,2,16,16,256]{4,3,2,1,0:T(8,128)S(1)}, bf16[2,16,16,256]{3,2,1,0:T(8,128)(2,1)S(1)}, bf16[2,16,16,256]{3,2,1,0:T(8,128)(2,1)S(1)}, bf16[16,16,2...) custom-call(f32[32,32,256]{2,1,0:T(8,128)} %density.1, ...), custom_call_target="tpu_custom_call" | custom-call | tf_op jit(solution)/shard_map/first/pallas_call | solution.py:350
  1.3 0.5 %collective-permute-start.4 = (bf16[2,16,16,256]{3,2,1,0:T(8,128)(2,1)S(1)}, bf16[2,16,16,256]{3,2,1,0:T(8,128)(2,1)S(1)}, u32[]{:S(2)}, u32[]{:S(2)}) collective-permute-start(bf16[2,16,16,256]{3,2,1,0:T(8,128)(2,1)S(1)} %get-tuple-element.59.xs0), channel_id=1, source_target_pairs={{0,2},{1,3},{4,6},{5,7},{8,10},{9,11},{12,14},{13,15},{16,18},{17,... | collective-permute-start | bytes 786440 | tf_op jit(solution)/shard_map/ppermute | solution.py:342
  1.8 0.6 %prepare.1 = (bf16[256,768]{1,0:T(8,128)(2,1)S(1)}, bf16[256,768]{1,0:T(8,128)(2,1)S(1)}, f32[8,24,128]{2,1,0:T(8,128)S(1)}, s32[2,2,8,128]{3,2,1,0:T(8,128)S(1)}, s32[4,8,32]{2,1,0:T(8,128)S(1)}) custom-call(bf16[2,33]{1,0:T(2,128)(2,1)S(1)} %get-tuple-element.38.taps, f32[4,8]{1,0:T(4,128)S(1)} %get-tuple-element.39.centre, ...), custom_call_target="tpu_custom_call" | custom-call | tf_op jit(solution)/shard_map/prepare/pallas_call | solution.py:364
  2.5 2.8 %collective-permute-start.5 = (bf16[2,16,16,256]{3,2,1,0:T(8,128)(2,1)S(1)}, bf16[2,16,16,256]{3,2,1,0:T(8,128)(2,1)S(1)}, u32[]{:S(2)}, u32[]{:S(2)}) collective-permute-start(bf16[2,16,16,256]{3,2,1,0:T(8,128)(2,1)S(1)} %get-tuple-element.60.xs1), channel_id=1, source_target_pairs={{2,4},{3,5},{10,12},{11,13},{18,20},{19,21},{26,28},{27,29},{0,8},... | collective-permute-start | bytes 786440 | tf_op jit(solution)/shard_map/ppermute | solution.py:342
  5.2 0.5 %collective-permute-start = (bf16[16,16,256]{2,1,0:T(8,128)(2,1)S(1)}, bf16[16,16,256]{2,1,0:T(8,128)(2,1)S(1)}, u32[]{:S(2)}, u32[]{:S(2)}) collective-permute-start(bf16[16,16,256]{2,1,0:T(8,128)(2,1)S(1)} %get-tuple-element.48), channel_id=1, source_target_pairs={{0,1},{2,3},{4,5},{6,7},{8,9},{10,11},{12,13},{14,15},{16,17},{18,... | collective-permute-start | bytes 393224 | tf_op jit(solution)/shard_map/ppermute | solution.py:342
  5.8 1.1 %cells1.1 = (f32[3,2,16,16,256]{4,3,2,1,0:T(8,128)S(1)}, f32[16,128]{1,0:T(8,128)S(1)}) custom-call(f32[2,2,16,16,256]{4,3,2,1,0:T(8,128)S(1)} %get-tuple-element.50.held, f32[8,24,128]{2,1,0:T(8,128)S(1)} %get-tuple-element.53.table, s32[2,2,8,128]{3,2,1,0:T(8,128)S(1)} %get-tuple-element.54.signs), custom_call_target="tpu_custom_call" | custom-call | flops 7864320 | bytes 2621440 | tf_op jit(solution)/shard_map/cells1/pallas_call | solution.py:377
  6.9 1.6 %collective-permute-start.1 = (bf16[16,16,256]{2,1,0:T(8,128)(2,1)S(1)}, bf16[16,16,256]{2,1,0:T(8,128)(2,1)S(1)}, u32[]{:S(2)}, u32[]{:S(2)}) collective-permute-start(bf16[16,16,256]{2,1,0:T(8,128)(2,1)S(1)} %get-tuple-element.56), channel_id=1, source_target_pairs={{0,1},{2,3},{4,5},{6,7},{8,9},{10,11},{12,13},{14,15},{16,17},{18,... | collective-permute-start | bytes 393224 | tf_op jit(solution)/shard_map/ppermute | solution.py:342
  8.5 0.0 collective-permute-start.3
  8.5 4.3 %collective-permute-done.near0 = bf16[16,16,256]{2,1,0:T(8,128)(2,1)S(1)} collective-permute-done((bf16[16,16,256]{2,1,0:T(8,128)(2,1)S(1)}, bf16[16,16,256]{2,1,0:T(8,128)(2,1)S(1)}, u32[]{:S(2)}, u32[]{:S(2)}) %collective-permute-start) | collective-permute-done | bytes 131104 | tf_op jit(solution)/shard_map/ppermute | solution.py:342
  12.8 0.0 collective-permute-start.2
  12.8 1.1 %cells0.1 = (f32[3,2,16,16,256]{4,3,2,1,0:T(8,128)S(1)}, f32[16,128]{1,0:T(8,128)S(1)}) custom-call(f32[2,2,16,16,256]{4,3,2,1,0:T(8,128)S(1)} %get-tuple-element.50.held, f32[8,24,128]{2,1,0:T(8,128)S(1)} %get-tuple-element.53.table, s32[2,2,8,128]{3,2,1,0:T(8,128)S(1)} %get-tuple-element.54.signs), custom_call_target="tpu_custom_call" | custom-call | flops 7864320 | bytes 2621440 | tf_op jit(solution)/shard_map/cells0/pallas_call | solution.py:377
  13.9 0.0 collective-permute-done.4.halo0
  13.9 0.0 collective-permute-done.5.halo1
  13.9 1.1 %own.1 = (f32[3,16,128]{2,1,0:T(8,128)S(1)}, f32[2,2,256,256]{3,2,1,0:T(8,128)S(1)}) custom-call(bf16[256,768]{1,0:T(8,128)(2,1)S(1)} %get-tuple-element.46.mx, bf16[256,768]{1,0:T(8,128)(2,1)S(1)} %get-tuple-element.47.my, bf16[2,16,16,256]{3,2,1,0:T(8,128)(2,1)S(1)} %get-tuple-element.59.xs0, bf16[2,16,16,256]{3,2,1,0:T(8,128)(2,1)S(1)} %get-tuple-element.60.xs1, ...), custom_call_target="tpu_custom_call" | custom-call | tf_op jit(solution)/shard_map/own/pallas_call | solution.py:398
  15.0 0.5 %collective-permute-done.1.near1 = bf16[16,16,256]{2,1,0:T(8,128)(2,1)S(1)} collective-permute-done((bf16[16,16,256]{2,1,0:T(8,128)(2,1)S(1)}, bf16[16,16,256]{2,1,0:T(8,128)(2,1)S(1)}, u32[]{:S(2)}, u32[]{:S(2)}) %collective-permute-start.1) | collective-permute-done | bytes 131104 | tf_op jit(solution)/shard_map/ppermute | solution.py:342
  15.6 0.0 collective-permute-done.3.halo1
  15.6 2.2 %collective-permute-done.2.halo0 = bf16[16,16,256]{2,1,0:T(8,128)(2,1)S(1)} collective-permute-done((bf16[16,16,256]{2,1,0:T(8,128)(2,1)S(1)}, bf16[16,16,256]{2,1,0:T(8,128)(2,1)S(1)}, u32[]{:S(2)}, u32[]{:S(2)}) %collective-permute-start.2) | collective-permute-done | bytes 131104 | tf_op jit(solution)/shard_map/ppermute | solution.py:342
  17.7 0.8 %late0.1.late_s = f32[3,16,128]{2,1,0:T(8,128)S(1)} custom-call(bf16[256,768]{1,0:T(8,128)(2,1)S(1)} %get-tuple-element.46.mx, bf16[256,768]{1,0:T(8,128)(2,1)S(1)} %get-tuple-element.47.my, bf16[16,16,256]{2,1,0:T(8,128)(2,1)S(1)} %collective-permute-done.near0, bf16[16,16,256]{2,1,0:T(8,128)(2,1)S(1)} %collective-permute-done.1.near1, ...), custom_call_target="tpu_custom_call" | custom-call | tf_op jit(solution)/shard_map/late0/pallas_call | solution.py:407
  18.5 0.1 blocks.1
  18.6 0.1 collective-permute-start.6
  18.7 1.2 %collective-permute-done.6.theirs = f32[2,4,8,32]{3,2,1,0:T(8,128)S(1)} collective-permute-done((f32[2,4,8,32]{3,2,1,0:T(8,128)S(1)}, f32[2,4,8,32]{3,2,1,0:T(8,128)S(1)}, u32[]{:S(2)}, u32[]{:S(2)}) %collective-permute-start.6) | collective-permute-done | bytes 8224 | tf_op jit(solution)/shard_map/ppermute | solution.py:420
  19.9 0.6 %collective-permute-start.7 = (f32[1,4,8,32]{3,2,1,0:T(8,128)S(1)}, f32[1,4,8,32]{3,2,1,0:T(8,128)S(1)}, u32[]{:S(2)}, u32[]{:S(2)}) collective-permute-start(f32[1,4,8,32]{3,2,1,0:T(8,128)S(1)} %get-tuple-element.70), channel_id=1, source_target_pairs={{0,16},{8,24},{16,0},{24,8},{1,17},{9,25},{17,1},{25,9},{2,18},{10... | collective-permute-start | bytes 12296 | tf_op jit(solution)/shard_map/ppermute | solution.py:420
  20.5 3.2 %collective-permute-done.7.theirs = f32[1,4,8,32]{3,2,1,0:T(8,128)S(1)} collective-permute-done((f32[1,4,8,32]{3,2,1,0:T(8,128)S(1)}, f32[1,4,8,32]{3,2,1,0:T(8,128)S(1)}, u32[]{:S(2)}, u32[]{:S(2)}) %collective-permute-start.7) | collective-permute-done | bytes 4128 | tf_op jit(solution)/shard_map/ppermute | solution.py:420
  23.7 0.6 %merge1.1 = f32[4,1,1,8,32]{4,3,2,1,0:T(8,128)} custom-call(s32[4,8,32]{2,1,0:T(8,128)S(1)} %get-tuple-element.45.order_map, f32[1,4,8,32]{3,2,1,0:T(8,128)S(1)} %get-tuple-element.69.kept, f32[1,4,8,32]{3,2,1,0:T(8,128)S(1)} %collective-permute-done.7.theirs), custom_call_target="tpu_custom_call" | custom-call | tf_op jit(solution)/shard_map/merge1/pallas_call | solution.py:423
  (1 shorter events, 0.0 us)
Async XLA Ops:
  1.3 12.6 %collective-permute-start.4 = (bf16[2,16,16,256]{3,2,1,0:T(8,128)(2,1)S(1)}, bf16[2,16,16,256]{3,2,1,0:T(8,128)(2,1)S(1)}, u32[]{:S(2)}, u32[]{:S(2)}) collective-permute-start(bf16[2,16,16,256]{3,2,1,0:T(8,128)(2,1)S(1)} %get-tuple-element.59.xs0), channel_id=1, source_target_pairs={{0,2},{1,3},{4,6},{5,7},{8,10},{9,11},{12,14},{13,15},{16,18},{17,... | collective-permute-start | bytes 786440 | tf_op jit(solution)/shard_map/ppermute | solution.py:342
  2.5 11.4 %collective-permute-start.5 = (bf16[2,16,16,256]{3,2,1,0:T(8,128)(2,1)S(1)}, bf16[2,16,16,256]{3,2,1,0:T(8,128)(2,1)S(1)}, u32[]{:S(2)}, u32[]{:S(2)}) collective-permute-start(bf16[2,16,16,256]{3,2,1,0:T(8,128)(2,1)S(1)} %get-tuple-element.60.xs1), channel_id=1, source_target_pairs={{2,4},{3,5},{10,12},{11,13},{18,20},{19,21},{26,28},{27,29},{0,8},... | collective-permute-start | bytes 786440 | tf_op jit(solution)/shard_map/ppermute | solution.py:342
  5.2 7.5 %collective-permute-start = (bf16[16,16,256]{2,1,0:T(8,128)(2,1)S(1)}, bf16[16,16,256]{2,1,0:T(8,128)(2,1)S(1)}, u32[]{:S(2)}, u32[]{:S(2)}) collective-permute-start(bf16[16,16,256]{2,1,0:T(8,128)(2,1)S(1)} %get-tuple-element.48), channel_id=1, source_target_pairs={{0,1},{2,3},{4,5},{6,7},{8,9},{10,11},{12,13},{14,15},{16,17},{18,... | collective-permute-start | bytes 393224 | tf_op jit(solution)/shard_map/ppermute | solution.py:342
  6.9 8.7 %collective-permute-start.1 = (bf16[16,16,256]{2,1,0:T(8,128)(2,1)S(1)}, bf16[16,16,256]{2,1,0:T(8,128)(2,1)S(1)}, u32[]{:S(2)}, u32[]{:S(2)}) collective-permute-start(bf16[16,16,256]{2,1,0:T(8,128)(2,1)S(1)} %get-tuple-element.56), channel_id=1, source_target_pairs={{0,1},{2,3},{4,5},{6,7},{8,9},{10,11},{12,13},{14,15},{16,17},{18,... | collective-permute-start | bytes 393224 | tf_op jit(solution)/shard_map/ppermute | solution.py:342
  8.5 7.1 %collective-permute-start.3 = (bf16[16,16,256]{2,1,0:T(8,128)(2,1)S(1)}, bf16[16,16,256]{2,1,0:T(8,128)(2,1)S(1)}, u32[]{:S(2)}, u32[]{:S(2)}) collective-permute-start(bf16[16,16,256]{2,1,0:T(8,128)(2,1)S(1)} %get-tuple-element.56), channel_id=1, source_target_pairs={{2,5},{3,4},{10,13},{11,12},{18,21},{19,20},{26,29},{27,28},{0,8},... | collective-permute-start | bytes 393224 | tf_op jit(solution)/shard_map/ppermute | solution.py:342
  12.8 5.0 %collective-permute-start.2 = (bf16[16,16,256]{2,1,0:T(8,128)(2,1)S(1)}, bf16[16,16,256]{2,1,0:T(8,128)(2,1)S(1)}, u32[]{:S(2)}, u32[]{:S(2)}) collective-permute-start(bf16[16,16,256]{2,1,0:T(8,128)(2,1)S(1)} %collective-permute-done.near0), channel_id=1, source_target_pairs={{0,2},{1,3},{4,6},{5,7},{8,10},{9,11},{12,14},{13,15},{16,18},{17,... | collective-permute-start | bytes 393224 | tf_op jit(solution)/shard_map/ppermute | solution.py:342
  18.6 1.3 %collective-permute-start.6 = (f32[2,4,8,32]{3,2,1,0:T(8,128)S(1)}, f32[2,4,8,32]{3,2,1,0:T(8,128)S(1)}, u32[]{:S(2)}, u32[]{:S(2)}) collective-permute-start(f32[2,4,8,32]{3,2,1,0:T(8,128)S(1)} %get-tuple-element.68), channel_id=1, source_target_pairs={{0,8},{8,0},{16,24},{24,16},{1,9},{9,1},{17,25},{25,17},{2,10},{10... | collective-permute-start | bytes 24584 | tf_op jit(solution)/shard_map/ppermute | solution.py:420
  19.9 3.8 %collective-permute-start.7 = (f32[1,4,8,32]{3,2,1,0:T(8,128)S(1)}, f32[1,4,8,32]{3,2,1,0:T(8,128)S(1)}, u32[]{:S(2)}, u32[]{:S(2)}) collective-permute-start(f32[1,4,8,32]{3,2,1,0:T(8,128)S(1)} %get-tuple-element.70), channel_id=1, source_target_pairs={{0,16},{8,24},{16,0},{24,8},{1,17},{9,25},{17,1},{25,9},{2,18},{10... | collective-permute-start | bytes 12296 | tf_op jit(solution)/shard_map/ppermute | solution.py:420

commit v6 on v5

--- a/solution.py
+++ b/solution.py
@@ -387,8 +387,9 @@
 
     corner = [[None, None] for r in range(rounds)]
     for r in range(rounds):
-        strip, total[1] = lax.optimization_barrier((strips[2 * r + 1], total[1]))
-        arrived, total[1] = lax.optimization_barrier((near[r][0], total[1]))
+        strip, arrived, total[1] = lax.optimization_barrier(
+            (strips[2 * r + 1], near[r][0], total[1])
+        )
         corner[r] = [swap(arrived, 0, None), swap(strip, 1, r)]
         near[r][1] = swap(strip, None, r)
 

time: 24.5 us -> 22.3 us (0.910)
  the two profiles are of different devices: /device:TPU:14 before, /device:TPU:18 now
where the time goes in v6:
time: 22.3 us; the launch traced here: 22.2 us
  waiting for transfers between devices  8.11 us (36%)
  starting transfers between devices  7.18 us (32%)
  Pallas kernels  6.84 us (31%)
    ppermute x6, starting transfers between devices, swap(): return lax.ppermute(piece, axes, swaps(counts, x_round, y_round))  6.51 us
    ppermute x2, waiting for transfers between devices, per_device(): lax.ppermute(given, 'depth', [(i, i ^ 1 << level) for i in range(depth_co...  4.4 us
    ppermute x6, waiting for transfers between devices, swap(): return lax.ppermute(piece, axes, swaps(counts, x_round, y_round))  3.71 us
    pallas_call x2, Pallas kernels, per_device(): call(functools.partial(cells_kernel, rim, bumps, g), f'cells{g}', [VMEM]...  2.25 us
    pallas_call x1, Pallas kernels, per_device(): call(functools.partial(first_kernel, rim, rounds), 'first', [HBM] * (1 +...  1.31 us
    pallas_call x1, Pallas kernels, per_device(): call(functools.partial(own_kernel, rim, early), 'own', [VMEM] * (7 if ear...  1.1 us
    pallas_call x1, Pallas kernels, per_device(): call(functools.partial(late_kernel, rim, r), f'late{r}', [VMEM] * 8, colo...  0.79 us
    ppermute x2, starting transfers between devices, per_device(): lax.ppermute(given, 'depth', [(i, i ^ 1 << level) for i in range(depth_co...  0.67 us
  transfers between devices with their start and end apart: 8, of which 6 were waited for; matrix products, arithmetic and copies ran while one was open for 0% of the time, Pallas kernels for 18%

profile of v6, /device:TPU:18, one launch (start us, length us, event | category | flops | bytes accessed | tf_op | source)
XLA Modules:
  0.0 22.2 jit_solution(14842190063758216543)
XLA Ops:
  0.0 1.3 %first.1 = (f32[2,2,16,16,256]{4,3,2,1,0:T(8,128)S(1)}, bf16[2,16,16,256]{3,2,1,0:T(8,128)(2,1)S(1)}, bf16[2,16,16,256]{3,2,1,0:T(8,128)(2,1)S(1)}, bf16[16,16,2...) custom-call(f32[32,32,256]{2,1,0:T(8,128)} %density.1, ...), custom_call_target="tpu_custom_call" | custom-call | tf_op jit(solution)/shard_map/first/pallas_call | solution.py:350
  1.3 1.6 %collective-permute-start = (bf16[16,16,256]{2,1,0:T(8,128)(2,1)S(1)}, bf16[16,16,256]{2,1,0:T(8,128)(2,1)S(1)}, u32[]{:S(2)}, u32[]{:S(2)}) collective-permute-start(bf16[16,16,256]{2,1,0:T(8,128)(2,1)S(1)} %get-tuple-element.47), channel_id=1, source_target_pairs={{0,1},{2,3},{4,5},{6,7},{8,9},{10,11},{12,13},{14,15},{16,17},{18,... | collective-permute-start | bytes 393224 | tf_op jit(solution)/shard_map/ppermute | solution.py:342
  2.9 1.6 %collective-permute-start.4 = (bf16[2,16,16,256]{3,2,1,0:T(8,128)(2,1)S(1)}, bf16[2,16,16,256]{3,2,1,0:T(8,128)(2,1)S(1)}, u32[]{:S(2)}, u32[]{:S(2)}) collective-permute-start(bf16[2,16,16,256]{3,2,1,0:T(8,128)(2,1)S(1)} %get-tuple-element.57.xs0), channel_id=1, source_target_pairs={{0,2},{1,3},{4,6},{5,7},{8,10},{9,11},{12,14},{13,15},{16,18},{17,... | collective-permute-start | bytes 786440 | tf_op jit(solution)/shard_map/ppermute | solution.py:342
  4.5 0.6 %prepare.1 = (bf16[256,768]{1,0:T(8,128)(2,1)S(1)}, bf16[256,768]{1,0:T(8,128)(2,1)S(1)}, f32[8,24,128]{2,1,0:T(8,128)S(1)}, s32[2,2,8,128]{3,2,1,0:T(8,128)S(1)}, s32[4,8,32]{2,1,0:T(8,128)S(1)}) custom-call(bf16[2,33]{1,0:T(2,128)(2,1)S(1)} %get-tuple-element.37.taps, f32[4,8]{1,0:T(4,128)S(1)} %get-tuple-element.38.centre, ...), custom_call_target="tpu_custom_call" | custom-call | tf_op jit(solution)/shard_map/prepare/pallas_call | solution.py:364
  5.1 0.1 collective-permute-start.5
  5.2 1.1 %cells1.1 = (f32[3,2,16,16,256]{4,3,2,1,0:T(8,128)S(1)}, f32[16,128]{1,0:T(8,128)S(1)}) custom-call(f32[2,2,16,16,256]{4,3,2,1,0:T(8,128)S(1)} %get-tuple-element.49.held, f32[8,24,128]{2,1,0:T(8,128)S(1)} %get-tuple-element.52.table, s32[2,2,8,128]{3,2,1,0:T(8,128)S(1)} %get-tuple-element.53.signs), custom_call_target="tpu_custom_call" | custom-call | flops 7864320 | bytes 2621440 | tf_op jit(solution)/shard_map/cells1/pallas_call | solution.py:377
  6.3 0.3 %collective-permute-done.near0 = bf16[16,16,256]{2,1,0:T(8,128)(2,1)S(1)} collective-permute-done((bf16[16,16,256]{2,1,0:T(8,128)(2,1)S(1)}, bf16[16,16,256]{2,1,0:T(8,128)(2,1)S(1)}, u32[]{:S(2)}, u32[]{:S(2)}) %collective-permute-start) | collective-permute-done | bytes 131104 | tf_op jit(solution)/shard_map/ppermute | solution.py:342
  6.6 1.5 %collective-permute-start.1 = (bf16[16,16,256]{2,1,0:T(8,128)(2,1)S(1)}, bf16[16,16,256]{2,1,0:T(8,128)(2,1)S(1)}, u32[]{:S(2)}, u32[]{:S(2)}) collective-permute-start(bf16[16,16,256]{2,1,0:T(8,128)(2,1)S(1)} %get-tuple-element.55), channel_id=1, source_target_pairs={{0,1},{2,3},{4,5},{6,7},{8,9},{10,11},{12,13},{14,15},{16,17},{18,... | collective-permute-start | bytes 393224 | tf_op jit(solution)/shard_map/ppermute | solution.py:342
  8.1 1.6 %collective-permute-start.2 = (bf16[16,16,256]{2,1,0:T(8,128)(2,1)S(1)}, bf16[16,16,256]{2,1,0:T(8,128)(2,1)S(1)}, u32[]{:S(2)}, u32[]{:S(2)}) collective-permute-start(bf16[16,16,256]{2,1,0:T(8,128)(2,1)S(1)} %collective-permute-done.near0), channel_id=1, source_target_pairs={{0,2},{1,3},{4,6},{5,7},{8,10},{9,11},{12,14},{13,15},{16,18},{17,... | collective-permute-start | bytes 393224 | tf_op jit(solution)/shard_map/ppermute | solution.py:342
  9.7 0.2 collective-permute-start.3
  9.9 1.1 %cells0.1 = (f32[3,2,16,16,256]{4,3,2,1,0:T(8,128)S(1)}, f32[16,128]{1,0:T(8,128)S(1)}) custom-call(f32[2,2,16,16,256]{4,3,2,1,0:T(8,128)S(1)} %get-tuple-element.49.held, f32[8,24,128]{2,1,0:T(8,128)S(1)} %get-tuple-element.52.table, s32[2,2,8,128]{3,2,1,0:T(8,128)S(1)} %get-tuple-element.53.signs), custom_call_target="tpu_custom_call" | custom-call | flops 7864320 | bytes 2621440 | tf_op jit(solution)/shard_map/cells0/pallas_call | solution.py:377
  11.0 0.8 %collective-permute-done.4.halo0 = bf16[2,16,16,256]{3,2,1,0:T(8,128)(2,1)S(1)} collective-permute-done((bf16[2,16,16,256]{3,2,1,0:T(8,128)(2,1)S(1)}, bf16[2,16,16,256]{3,2,1,0:T(8,128)(2,1)S(1)}, u32[]{:S(2)}, u32[]{:S(2)}) %collective-permute-start.4) | collective-permute-done | bytes 262176 | tf_op jit(solution)/shard_map/ppermute | solution.py:342
  11.9 2.2 %collective-permute-done.5.halo1 = bf16[2,16,16,256]{3,2,1,0:T(8,128)(2,1)S(1)} collective-permute-done((bf16[2,16,16,256]{3,2,1,0:T(8,128)(2,1)S(1)}, bf16[2,16,16,256]{3,2,1,0:T(8,128)(2,1)S(1)}, u32[]{:S(2)}, u32[]{:S(2)}) %collective-permute-start.5) | collective-permute-done | bytes 262176 | tf_op jit(solution)/shard_map/ppermute | solution.py:342
  14.1 1.1 %own.1 = (f32[3,16,128]{2,1,0:T(8,128)S(1)}, f32[2,2,256,256]{3,2,1,0:T(8,128)S(1)}) custom-call(bf16[256,768]{1,0:T(8,128)(2,1)S(1)} %get-tuple-element.45.mx, bf16[256,768]{1,0:T(8,128)(2,1)S(1)} %get-tuple-element.46.my, bf16[2,16,16,256]{3,2,1,0:T(8,128)(2,1)S(1)} %get-tuple-element.57.xs0, bf16[2,16,16,256]{3,2,1,0:T(8,128)(2,1)S(1)} %get-tuple-element.58.xs1, ...), custom_call_target="tpu_custom_call" | custom-call | tf_op jit(solution)/shard_map/own/pallas_call | solution.py:399
  15.2 0.0 collective-permute-done.1.near1
  15.2 0.0 collective-permute-done.2.halo0
  15.2 0.4 %collective-permute-done.3.halo1 = bf16[16,16,256]{2,1,0:T(8,128)(2,1)S(1)} collective-permute-done((bf16[16,16,256]{2,1,0:T(8,128)(2,1)S(1)}, bf16[16,16,256]{2,1,0:T(8,128)(2,1)S(1)}, u32[]{:S(2)}, u32[]{:S(2)}) %collective-permute-start.3) | collective-permute-done | bytes 131104 | tf_op jit(solution)/shard_map/ppermute | solution.py:342
  15.6 0.8 %late0.1.late_s = f32[3,16,128]{2,1,0:T(8,128)S(1)} custom-call(bf16[256,768]{1,0:T(8,128)(2,1)S(1)} %get-tuple-element.45.mx, bf16[256,768]{1,0:T(8,128)(2,1)S(1)} %get-tuple-element.46.my, bf16[16,16,256]{2,1,0:T(8,128)(2,1)S(1)} %collective-permute-done.near0, bf16[16,16,256]{2,1,0:T(8,128)(2,1)S(1)} %collective-permute-done.1.near1, ...), custom_call_target="tpu_custom_call" | custom-call | tf_op jit(solution)/shard_map/late0/pallas_call | solution.py:408
  16.4 0.1 blocks.1
  16.5 0.1 collective-permute-start.6
  16.6 1.2 %collective-permute-done.6.theirs = f32[2,4,8,32]{3,2,1,0:T(8,128)S(1)} collective-permute-done((f32[2,4,8,32]{3,2,1,0:T(8,128)S(1)}, f32[2,4,8,32]{3,2,1,0:T(8,128)S(1)}, u32[]{:S(2)}, u32[]{:S(2)}) %collective-permute-start.6) | collective-permute-done | bytes 8224 | tf_op jit(solution)/shard_map/ppermute | solution.py:421
  17.8 0.6 %collective-permute-start.7 = (f32[1,4,8,32]{3,2,1,0:T(8,128)S(1)}, f32[1,4,8,32]{3,2,1,0:T(8,128)S(1)}, u32[]{:S(2)}, u32[]{:S(2)}) collective-permute-start(f32[1,4,8,32]{3,2,1,0:T(8,128)S(1)} %get-tuple-element.68), channel_id=1, source_target_pairs={{0,16},{8,24},{16,0},{24,8},{1,17},{9,25},{17,1},{25,9},{2,18},{10... | collective-permute-start | bytes 12296 | tf_op jit(solution)/shard_map/ppermute | solution.py:421
  18.4 3.2 %collective-permute-done.7.theirs = f32[1,4,8,32]{3,2,1,0:T(8,128)S(1)} collective-permute-done((f32[1,4,8,32]{3,2,1,0:T(8,128)S(1)}, f32[1,4,8,32]{3,2,1,0:T(8,128)S(1)}, u32[]{:S(2)}, u32[]{:S(2)}) %collective-permute-start.7) | collective-permute-done | bytes 4128 | tf_op jit(solution)/shard_map/ppermute | solution.py:421
  21.6 0.6 %merge1.1 = f32[4,1,1,8,32]{4,3,2,1,0:T(8,128)} custom-call(s32[4,8,32]{2,1,0:T(8,128)S(1)} %get-tuple-element.44.order_map, f32[1,4,8,32]{3,2,1,0:T(8,128)S(1)} %get-tuple-element.67.kept, f32[1,4,8,32]{3,2,1,0:T(8,128)S(1)} %collective-permute-done.7.theirs), custom_call_target="tpu_custom_call" | custom-call | tf_op jit(solution)/shard_map/merge1/pallas_call | solution.py:424
  (1 shorter events, 0.0 us)
Async XLA Ops:
  1.3 5.3 %collective-permute-start = (bf16[16,16,256]{2,1,0:T(8,128)(2,1)S(1)}, bf16[16,16,256]{2,1,0:T(8,128)(2,1)S(1)}, u32[]{:S(2)}, u32[]{:S(2)}) collective-permute-start(bf16[16,16,256]{2,1,0:T(8,128)(2,1)S(1)} %get-tuple-element.47), channel_id=1, source_target_pairs={{0,1},{2,3},{4,5},{6,7},{8,9},{10,11},{12,13},{14,15},{16,17},{18,... | collective-permute-start | bytes 393224 | tf_op jit(solution)/shard_map/ppermute | solution.py:342
  2.9 9.0 %collective-permute-start.4 = (bf16[2,16,16,256]{3,2,1,0:T(8,128)(2,1)S(1)}, bf16[2,16,16,256]{3,2,1,0:T(8,128)(2,1)S(1)}, u32[]{:S(2)}, u32[]{:S(2)}) collective-permute-start(bf16[2,16,16,256]{3,2,1,0:T(8,128)(2,1)S(1)} %get-tuple-element.57.xs0), channel_id=1, source_target_pairs={{0,2},{1,3},{4,6},{5,7},{8,10},{9,11},{12,14},{13,15},{16,18},{17,... | collective-permute-start | bytes 786440 | tf_op jit(solution)/shard_map/ppermute | solution.py:342
  5.1 9.0 %collective-permute-start.5 = (bf16[2,16,16,256]{3,2,1,0:T(8,128)(2,1)S(1)}, bf16[2,16,16,256]{3,2,1,0:T(8,128)(2,1)S(1)}, u32[]{:S(2)}, u32[]{:S(2)}) collective-permute-start(bf16[2,16,16,256]{3,2,1,0:T(8,128)(2,1)S(1)} %get-tuple-element.58.xs1), channel_id=1, source_target_pairs={{2,4},{3,5},{10,12},{11,13},{18,20},{19,21},{26,28},{27,29},{0,8},... | collective-permute-start | bytes 786440 | tf_op jit(solution)/shard_map/ppermute | solution.py:342
  6.6 8.6 %collective-permute-start.1 = (bf16[16,16,256]{2,1,0:T(8,128)(2,1)S(1)}, bf16[16,16,256]{2,1,0:T(8,128)(2,1)S(1)}, u32[]{:S(2)}, u32[]{:S(2)}) collective-permute-start(bf16[16,16,256]{2,1,0:T(8,128)(2,1)S(1)} %get-tuple-element.55), channel_id=1, source_target_pairs={{0,1},{2,3},{4,5},{6,7},{8,9},{10,11},{12,13},{14,15},{16,17},{18,... | collective-permute-start | bytes 393224 | tf_op jit(solution)/shard_map/ppermute | solution.py:342
  8.1 7.1 %collective-permute-start.2 = (bf16[16,16,256]{2,1,0:T(8,128)(2,1)S(1)}, bf16[16,16,256]{2,1,0:T(8,128)(2,1)S(1)}, u32[]{:S(2)}, u32[]{:S(2)}) collective-permute-start(bf16[16,16,256]{2,1,0:T(8,128)(2,1)S(1)} %collective-permute-done.near0), channel_id=1, source_target_pairs={{0,2},{1,3},{4,6},{5,7},{8,10},{9,11},{12,14},{13,15},{16,18},{17,... | collective-permute-start | bytes 393224 | tf_op jit(solution)/shard_map/ppermute | solution.py:342
  9.7 5.9 %collective-permute-start.3 = (bf16[16,16,256]{2,1,0:T(8,128)(2,1)S(1)}, bf16[16,16,256]{2,1,0:T(8,128)(2,1)S(1)}, u32[]{:S(2)}, u32[]{:S(2)}) collective-permute-start(bf16[16,16,256]{2,1,0:T(8,128)(2,1)S(1)} %get-tuple-element.55), channel_id=1, source_target_pairs={{2,5},{3,4},{10,13},{11,12},{18,21},{19,20},{26,29},{27,28},{0,8},... | collective-permute-start | bytes 393224 | tf_op jit(solution)/shard_map/ppermute | solution.py:342
  16.5 1.3 %collective-permute-start.6 = (f32[2,4,8,32]{3,2,1,0:T(8,128)S(1)}, f32[2,4,8,32]{3,2,1,0:T(8,128)S(1)}, u32[]{:S(2)}, u32[]{:S(2)}) collective-permute-start(f32[2,4,8,32]{3,2,1,0:T(8,128)S(1)} %get-tuple-element.66), channel_id=1, source_target_pairs={{0,8},{8,0},{16,24},{24,16},{1,9},{9,1},{17,25},{25,17},{2,10},{10... | collective-permute-start | bytes 24584 | tf_op jit(solution)/shard_map/ppermute | solution.py:421
  17.8 3.8 %collective-permute-start.7 = (f32[1,4,8,32]{3,2,1,0:T(8,128)S(1)}, f32[1,4,8,32]{3,2,1,0:T(8,128)S(1)}, u32[]{:S(2)}, u32[]{:S(2)}) collective-permute-start(f32[1,4,8,32]{3,2,1,0:T(8,128)S(1)} %get-tuple-element.68), channel_id=1, source_target_pairs={{0,16},{8,24},{16,0},{24,8},{1,17},{9,25},{17,1},{25,9},{2,18},{10... | collective-permute-start | bytes 12296 | tf_op jit(solution)/shard_map/ppermute | solution.py:421

commit v7 on v6

--- a/solution.py
+++ b/solution.py
@@ -127,14 +127,16 @@
     return parts
 
 
-def prepare_kernel(
-    rim, taps, centre, width, colour, opacity, brick_tf, view_order,
-    mx, my, table, signs, order_map, padded
-):
-    place = Place()
+def matrices_kernel(rim, taps, mx, my, padded):
     padded[...] = jnp.zeros(padded.shape, F32)
     padded[0:2, 0:taps.shape[1]] = taps[...].astype(F32)
-    mx[...], my[...] = blur_matrices(rim, place, padded[...])
+    mx[...], my[...] = blur_matrices(rim, Place(), padded[...])
+
+
+def prepare_kernel(
+    rim, centre, width, colour, opacity, brick_tf, view_order, table, signs, order_map
+):
+    place = Place()
     wide = width[...]
     rows = [centre[...], (-LOG2E) / (wide * wide), opacity[...] * (-LOG2E)]
     rows += [colour[c] * 0.5 for c in range(3)]
@@ -219,16 +221,13 @@
     return acc
 
 
-def blur_x(place, rim, mx, near, halos):
+def blur_x(place, rim, mx, h, near, halo):
     flat = lambda cells: cells.reshape(rim * rim, cells.shape[-1])
-    edges = []
-    for h, halo in enumerate(halos):
-        cells = flat(halo)
-        edges.append(jnp.where(place.has_x[h], cells, jnp.zeros_like(cells)))
-    blocks = [edges[1], flat(near[1]), flat(near[0]), edges[0]]
-    return [
-        dot(mx[...], jnp.concatenate(blocks[1 - h:4 - h], axis=0)).astype(BF16) for h in range(2)
-    ]
+    edge = flat(halo)
+    edge = jnp.where(place.has_x[h], edge, jnp.zeros_like(edge))
+    own = [flat(near[1]), flat(near[0])]
+    blocks = own + [edge] if h == 0 else [edge] + own
+    return dot(mx[...], jnp.concatenate(blocks, axis=0)).astype(BF16)
 
 
 def lit(place, rim, occlusion, shaded, h):
@@ -238,55 +237,54 @@
     return [rays(shade * shaded[c, h], place.half[h] * rim, lane) for c in range(3)]
 
 
-def own_kernel(rim, early, mx, my, xs0, xs1, halo0, halo1, *refs):
+def own_kernel(rim, h, early, mx, my, xs0, xs1, halo, *refs):
     place = Place()
     size = rim * rim
-    across = [
-        blur_x(place, rim, mx, [xs0[g], xs1[g]], [halo0[g], halo1[g]]) for g in range(2)
-    ]
-    if early:
-        shaded, out, partial = refs
-    else:
-        partial, = refs
-    for h in range(2):
-        s, e = across[0][h], across[1][h]
-        partial[0, h] = dot(my[:, :2 * size], jnp.concatenate([e, s], axis=0))
-        other = dot(my[:, size:], jnp.concatenate([e, s], axis=0))
-        if not early:
-            partial[1, h] = other
-            continue
-        part = lit(place, rim, other, shaded, h)
-        for c in range(3):
-            out[c] = part[c] if h == 0 else out[c] + part[c]
-
-
-def late_kernel(rim, g, mx, my, near0, near1, halo0, halo1, partial, shaded, out):
+    s, e = (blur_x(place, rim, mx, h, [xs0[g], xs1[g]], halo[g]) for g in range(2))
+    cells = jnp.concatenate([e, s], axis=0)
+    partial = refs[-1]
+    partial[0] = dot(my[:, :2 * size], cells)
+    other = dot(my[:, size:], cells)
+    if not early:
+        partial[1] = other
+        return
+    shaded, out, partial = refs
+    for c, part in enumerate(lit(place, rim, other, shaded, h)):
+        out[c] = part
+
+
+def late(rim, g, h, mx, my, near0, near1, halo, partial, shaded):
     place = Place()
     size = rim * rim
-    across = blur_x(place, rim, mx, [near0[...], near1[...]], [halo0[...], halo1[...]])
+    across = blur_x(place, rim, mx, h, [near0[...], near1[...]], halo[...])
+    across = jnp.where(place.has_y[g], across, jnp.zeros_like(across))
     block = my[:, 2 * size:] if g == 0 else my[:, :size]
-    for h in range(2):
-        cells = jnp.where(place.has_y[g], across[h], jnp.zeros_like(across[h]))
-        part = lit(place, rim, partial[g, h] + dot(block, cells), shaded, h)
-        for c in range(3):
-            out[c] = part[c] if h == 0 else out[c] + part[c]
-
-
-def blocks_kernel(rim, depth_count, late_s, late_e, total0, total1, *refs):
-    outs, (img,) = refs[:2], refs[2:]
+    return lit(place, rim, partial[g] + dot(block, across), shaded, h)
+
+
+def late_kernel(rim, g, h, *refs):
+    *refs, out = refs
+    for c, part in enumerate(late(rim, g, h, *refs)):
+        out[c] = part
+
+
+def last_kernel(rim, depth_count, *refs):
+    (light_s, light_e0, light_e1, total0, total1), refs = refs[:5], refs[5:]
+    refs, (kept, given, img) = refs[:7], refs[7:]
     place = Place()
     rows = 2 * rim
-    for g, (colours, total) in enumerate(((late_s, total0), (late_e, total1))):
-        at = group_rows(place, rim, g)
-        for c in range(3):
-            img[c, at, :] = colours[c]
-        img[3, at, :] = jnp.exp2(total[...])
+    at_s, at_e = group_rows(place, rim, 0), group_rows(place, rim, 1)
+    for c, part in enumerate(late(rim, 0, 1, *refs)):
+        img[c, at_s, :] = light_s[c] + part
+        img[c, at_e, :] = light_e0[c] + light_e1[c]
+    img[3, at_s, :] = jnp.exp2(total0[...])
+    img[3, at_e, :] = jnp.exp2(total1[...])
     for c in range(4):
         img[4 + c, :, 0:rows] = img[c].T[:rows, :]
     block = rows // depth_count
     bit = place.depth & 1
     for n in range(depth_count // 2):
-        for out, b in ((outs[0], bit), (outs[1], 1 - bit)):
+        for out, b in ((kept, bit), (given, 1 - bit)):
             out[n] = img[4:8, pl.ds(pl.multiple_of((2 * n + b) * block, block), block), 0:rows]
 
 
@@ -358,20 +356,23 @@
     )(in_hbm(density), *[in_hbm(t) for t in tables])
     strips, tables = refs[:2 * rounds], refs[2 * rounds:]
     near = [[swap(strips[2 * r], None, r), None] for r in range(rounds)]
-    halo_x = [swap(xs0, 0, None), None]
 
     bricks = rows_z // 128
-    mx, my, table, signs, order_map = call(
+    table, signs, order_map = call(
         functools.partial(prepare_kernel, rim),
         "prepare",
-        [VMEM] * len(tables),
-        [struct((size, 3 * size), BF16)] * 2
-        + [struct((4 * bricks, 6 * bumps, 128), F32), struct((2, 2, 8, 128), jnp.int32)]
+        [VMEM] * (len(tables) - 1),
+        [struct((4 * bricks, 6 * bumps, 128), F32), struct((2, 2, 8, 128), jnp.int32)]
         + [struct((depth_count, block, rows_y), jnp.int32)],
+    )(*tables[1:])
+    halo_x = [swap(cells, h, None) for h, cells in enumerate((xs0, xs1))]
+    mx, my = call(
+        functools.partial(matrices_kernel, rim),
+        "matrices",
+        [VMEM],
+        [struct((size, 3 * size), BF16)] * 2,
         [pltpu.VMEM((8, 128), F32)],
-    )(*tables)
-    cells, table = lax.optimization_barrier((xs1, table))
-    halo_x[1] = swap(cells, 1, None)
+    )(tables[0])
     shaded, total = [None, None], [None, None]
     for g in (1, 0):
         shaded[g], total[g] = call(
@@ -381,7 +382,9 @@
             [struct((3, 2, rim, rim, rows_z), F32), struct((rim, 128), F32)],
             [pltpu.VMEM((2, size, rows_z), F32), pltpu.VMEM((3, 2, size, rows_z), F32)],
             cost_estimate=pl.CostEstimate(
-                flops=density.size * 30, bytes_accessed=density.size * 10, transcendentals=density.size * 3
+                flops=density.size * (100000 if g == 0 else 1),
+                bytes_accessed=density.size * (10000 if g == 0 else 1),
+                transcendentals=density.size * 3,
             ),
         )(held, table, signs)
 
@@ -395,27 +398,30 @@
 
     early = rounds < 2
     colours = struct((3, rim, 128), F32)
-    partial = struct((2, 2, size, rows_z), F32)
-    own = call(
-        functools.partial(own_kernel, rim, early),
-        "own",
-        [VMEM] * (7 if early else 6),
-        [colours, partial] if early else [partial],
-    )(mx, my, xs0, xs1, *halo_x, *([shaded[1]] if early else []))
-    partial = own[-1]
-    lights = [None, own[0]]
-    for r in range(rounds):
-        lights[r] = call(
-            functools.partial(late_kernel, rim, r), f"late{r}", [VMEM] * 8, colours
-        )(mx, my, *near[r], *corner[r], partial, shaded[r])
-
+    partial, lights = [None, None], [[None, None], [None, None]]
+    for h in range(2):
+        unlit = struct((2 - early, size, rows_z), F32)
+        results = call(
+            functools.partial(own_kernel, rim, h, early),
+            f"own{h}",
+            [VMEM] * (6 if early else 5),
+            [colours, unlit] if early else [unlit],
+        )(mx, my, xs0, xs1, halo_x[h], *([shaded[1]] if early else []))
+        partial[h] = results[-1]
+        if early:
+            lights[1][h] = results[0]
+    for g in range(rounds):
+        for h in range(2 if g == 1 else 1):
+            lights[g][h] = call(
+                functools.partial(late_kernel, rim, g, h), f"late{g}{h}", [VMEM] * 7, colours
+            )(mx, my, *near[g], corner[g][h], partial[h], shaded[g])
     kept, given = call(
-        functools.partial(blocks_kernel, rim, depth_count),
-        "blocks",
-        [VMEM] * 4,
+        functools.partial(last_kernel, rim, depth_count),
+        "last",
+        [VMEM] * 12,
         [struct((depth_count // 2, 4, block, rows_y), F32)] * 2,
         [pltpu.VMEM((8, rows_y, 128), F32)],
-    )(*lights, *total)
+    )(lights[0][0], *lights[1], *total, mx, my, *near[0], corner[0][1], partial[1], shaded[0])
     level = 0
     while True:
         theirs = lax.ppermute(given, "depth", [(i, i ^ 1 << level) for i in range(depth_count)])

time: 22.3 us -> 23.2 us (1.040)
  the two profiles are of different devices: /device:TPU:18 before, /device:TPU:0 now
where the time goes in v7:
time: 23.2 us; the launch traced here: 23.1 us
  starting transfers between devices  11.6 us (50%)
  Pallas kernels  7.92 us (34%)
  waiting for transfers between devices  3.48 us (15%)
    ppermute x6, starting transfers between devices, swap(): return lax.ppermute(piece, axes, swaps(counts, x_round, y_round))  9.95 us
    ppermute x2, waiting for transfers between devices, per_device(): lax.ppermute(given, 'depth', [(i, i ^ 1 << level) for i in range(depth_co...  3.44 us
    pallas_call x2, Pallas kernels, per_device(): call(functools.partial(cells_kernel, rim, bumps, g), f'cells{g}', [VMEM]...  2.25 us
    ppermute x2, starting transfers between devices, per_device(): lax.ppermute(given, 'depth', [(i, i ^ 1 << level) for i in range(depth_co...  1.63 us
    pallas_call x2, Pallas kernels, per_device(): call(functools.partial(own_kernel, rim, h, early), f'own{h}', [VMEM] * (6...  1.54 us
    pallas_call x1, Pallas kernels, per_device(): call(functools.partial(first_kernel, rim, rounds), 'first', [HBM] * (1 +...  1.31 us
    pallas_call x1, Pallas kernels, per_device(): call(functools.partial(last_kernel, rim, depth_count), 'last', [VMEM] * 1...  0.7 us
    pallas_call x2, Pallas kernels, per_device(): call(functools.partial(merge_kernel, level), f'merge{level}', [VMEM] * 3,...  0.63 us
  transfers between devices with their start and end apart: 8, of which 2 were waited for; matrix products, arithmetic and copies ran while one was open for 0% of the time, Pallas kernels for 23%

profile of v7, /device:TPU:0, one launch (start us, length us, event | category | flops | bytes accessed | tf_op | source)
XLA Modules:
  0.0 23.1 jit_solution(11869753714141028530)
XLA Ops:
  0.0 1.3 %first.1 = (f32[2,2,16,16,256]{4,3,2,1,0:T(8,128)S(1)}, bf16[2,16,16,256]{3,2,1,0:T(8,128)(2,1)S(1)}, bf16[2,16,16,256]{3,2,1,0:T(8,128)(2,1)S(1)}, bf16[16,16,2...) custom-call(f32[32,32,256]{2,1,0:T(8,128)} %density.1, ...), custom_call_target="tpu_custom_call" | custom-call | tf_op jit(solution)/shard_map/first/pallas_call | solution.py:348
  1.3 3.0 %collective-permute-start = (bf16[16,16,256]{2,1,0:T(8,128)(2,1)S(1)}, bf16[16,16,256]{2,1,0:T(8,128)(2,1)S(1)}, u32[]{:S(2)}, u32[]{:S(2)}) collective-permute-start(bf16[16,16,256]{2,1,0:T(8,128)(2,1)S(1)} %get-tuple-element.47), channel_id=1, source_target_pairs={{0,1},{2,3},{4,5},{6,7},{8,9},{10,11},{12,13},{14,15},{16,17},{18,... | collective-permute-start | bytes 393224 | tf_op jit(solution)/shard_map/ppermute | solution.py:340
  4.4 3.1 %collective-permute-start.3 = (bf16[2,16,16,256]{3,2,1,0:T(8,128)(2,1)S(1)}, bf16[2,16,16,256]{3,2,1,0:T(8,128)(2,1)S(1)}, u32[]{:S(2)}, u32[]{:S(2)}) collective-permute-start(bf16[2,16,16,256]{3,2,1,0:T(8,128)(2,1)S(1)} %get-tuple-element.55.xs0), channel_id=1, source_target_pairs={{0,2},{1,3},{4,6},{5,7},{8,10},{9,11},{12,14},{13,15},{16,18},{17,... | collective-permute-start | bytes 786440 | tf_op jit(solution)/shard_map/ppermute | solution.py:340
  7.5 0.3 %prepare.1 = (f32[8,24,128]{2,1,0:T(8,128)S(1)}, s32[2,2,8,128]{3,2,1,0:T(8,128)S(1)}, s32[4,8,32]{2,1,0:T(8,128)S(1)}) custom-call(f32[4,8]{1,0:T(4,128)S(1)} %get-tuple-element.37.centre, f32[4,8]{1,0:T(4,128)S(1)} %get-tuple-element.38.width, f32[3,4,8]{2,1,0:T(4,128)S(1)} %get-tuple-element.39.colour, f32[4,8]{1,0:T(4,128)S(1)} %get-tuple-element.40.opacity, ...), custom_call_target="tpu_custom_call" | custom-call | tf_op jit(solution)/shard_map/prepare/pallas_call | solution.py:361
  7.8 1.1 %cells1.1 = (f32[3,2,16,16,256]{4,3,2,1,0:T(8,128)S(1)}, f32[16,128]{1,0:T(8,128)S(1)}) custom-call(f32[2,2,16,16,256]{4,3,2,1,0:T(8,128)S(1)} %get-tuple-element.49.held, f32[8,24,128]{2,1,0:T(8,128)S(1)} %get-tuple-element.50.table, s32[2,2,8,128]{3,2,1,0:T(8,128)S(1)} %get-tuple-element.51.signs), custom_call_target="tpu_custom_call" | custom-call | flops 262144 | bytes 262144 | tf_op jit(solution)/shard_map/cells1/pallas_call | solution.py:378
  8.9 0.7 %collective-permute-start.1 = (bf16[16,16,256]{2,1,0:T(8,128)(2,1)S(1)}, bf16[16,16,256]{2,1,0:T(8,128)(2,1)S(1)}, u32[]{:S(2)}, u32[]{:S(2)}) collective-permute-start(bf16[16,16,256]{2,1,0:T(8,128)(2,1)S(1)} %get-tuple-element.53), channel_id=1, source_target_pairs={{0,1},{2,3},{4,5},{6,7},{8,9},{10,11},{12,13},{14,15},{16,17},{18,... | collective-permute-start | bytes 393224 | tf_op jit(solution)/shard_map/ppermute | solution.py:340
  9.6 0.0 collective-permute-start.5
  9.6 3.1 %collective-permute-start.2 = (bf16[16,16,256]{2,1,0:T(8,128)(2,1)S(1)}, bf16[16,16,256]{2,1,0:T(8,128)(2,1)S(1)}, u32[]{:S(2)}, u32[]{:S(2)}) collective-permute-start(bf16[16,16,256]{2,1,0:T(8,128)(2,1)S(1)} %collective-permute-done.refs_2_.refs_7_), channel_id=1, source_target_pairs={{0,2},{1,3},{4,6},{5,7},{8,10},{9,11},{12,14},{13,15},{16,18},{17,... | collective-permute-start | bytes 393224 | tf_op jit(solution)/shard_map/ppermute | solution.py:340
  12.7 1.1 %cells0.1 = (f32[3,2,16,16,256]{4,3,2,1,0:T(8,128)S(1)}, f32[16,128]{1,0:T(8,128)S(1)}) custom-call(f32[2,2,16,16,256]{4,3,2,1,0:T(8,128)S(1)} %get-tuple-element.49.held, f32[8,24,128]{2,1,0:T(8,128)S(1)} %get-tuple-element.50.table, s32[2,2,8,128]{3,2,1,0:T(8,128)S(1)} %get-tuple-element.51.signs), custom_call_target="tpu_custom_call" | custom-call | flops 26214400000 | bytes 2621440000 | tf_op jit(solution)/shard_map/cells0/pallas_call | solution.py:378
  13.8 0.6 %matrices.1 = (bf16[256,768]{1,0:T(8,128)(2,1)S(1)}, bf16[256,768]{1,0:T(8,128)(2,1)S(1)}) custom-call(bf16[2,33]{1,0:T(2,128)(2,1)S(1)} %get-tuple-element.44.taps), custom_call_target="tpu_custom_call" | custom-call | tf_op jit(solution)/shard_map/matrices/pallas_call | solution.py:369
  14.4 0.0 collective-permute-done.4.halo
  14.4 0.8 %own1.1 = (f32[3,16,128]{2,1,0:T(8,128)S(1)}, f32[1,256,256]{2,1,0:T(8,128)S(1)}) custom-call(bf16[256,768]{1,0:T(8,128)(2,1)S(1)} %get-tuple-element.45.mx.refs_0_.refs_5_, bf16[256,768]{1,0:T(8,128)(2,1)S(1)} %get-tuple-element.46.my.refs_1_.refs_6_, bf16[2,16,16,256]{3,2,1,0:T(8,128)(2,1)S(1)} %get-tuple-element.55.xs0, ...), custom_call_target="tpu_custom_call" | custom-call | tf_op jit(solution)/shard_map/own1/pallas_call | solution.py:404
  15.2 0.0 collective-permute-done.3.halo
  15.2 0.8 %own0.1 = (f32[3,16,128]{2,1,0:T(8,128)S(1)}, f32[1,256,256]{2,1,0:T(8,128)S(1)}) custom-call(bf16[256,768]{1,0:T(8,128)(2,1)S(1)} %get-tuple-element.45.mx.refs_0_.refs_5_, bf16[256,768]{1,0:T(8,128)(2,1)S(1)} %get-tuple-element.46.my.refs_1_.refs_6_, bf16[2,16,16,256]{3,2,1,0:T(8,128)(2,1)S(1)} %get-tuple-element.55.xs0, ...), custom_call_target="tpu_custom_call" | custom-call | tf_op jit(solution)/shard_map/own0/pallas_call | solution.py:404
  16.0 0.0 collective-permute-done.1.refs_3_.refs_8_
  16.0 0.0 collective-permute-done.2.refs_4_
  16.1 0.6 %late00.1.refs_0_ = f32[3,16,128]{2,1,0:T(8,128)S(1)} custom-call(bf16[256,768]{1,0:T(8,128)(2,1)S(1)} %get-tuple-element.45.mx.refs_0_.refs_5_, bf16[256,768]{1,0:T(8,128)(2,1)S(1)} %get-tuple-element.46.my.refs_1_.refs_6_, bf16[16,16,256]{2,1,0:T(8,128)(2,1)S(1)} %collective-permute-done.refs_2_.refs_7_, ...), custom_call_target="tpu_custom_call" | custom-call | tf_op jit(solution)/shard_map/late00/pallas_call | solution.py:415
  16.7 0.0 collective-permute-done.5.refs_9_
  16.7 0.7 %last.1 = (f32[2,4,8,32]{3,2,1,0:T(8,128)S(1)}, f32[2,4,8,32]{3,2,1,0:T(8,128)S(1)}) custom-call(f32[3,16,128]{2,1,0:T(8,128)S(1)} %late00.1.refs_0_, f32[3,16,128]{2,1,0:T(8,128)S(1)} %get-tuple-element.60.refs_1_, f32[3,16,128]{2,1,0:T(8,128)S(1)} %get-tuple-element.61.refs_2_, f32[16,128]{1,0:T(8,128)S(1)} %get-tuple-element.62.refs_3_, ...), custom_call_target="tpu_custom_call" | custom-call | tf_op jit(solution)/shard_map/last/pallas_call | solution.py:418
  17.4 0.1 collective-permute-start.6
  17.5 1.2 %collective-permute-done.6.theirs = f32[2,4,8,32]{3,2,1,0:T(8,128)S(1)} collective-permute-done((f32[2,4,8,32]{3,2,1,0:T(8,128)S(1)}, f32[2,4,8,32]{3,2,1,0:T(8,128)S(1)}, u32[]{:S(2)}, u32[]{:S(2)}) %collective-permute-start.6) | collective-permute-done | bytes 8224 | tf_op jit(solution)/shard_map/ppermute | solution.py:427
  18.7 1.6 %collective-permute-start.7 = (f32[1,4,8,32]{3,2,1,0:T(8,128)S(1)}, f32[1,4,8,32]{3,2,1,0:T(8,128)S(1)}, u32[]{:S(2)}, u32[]{:S(2)}) collective-permute-start(f32[1,4,8,32]{3,2,1,0:T(8,128)S(1)} %get-tuple-element.68), channel_id=1, source_target_pairs={{0,16},{8,24},{16,0},{24,8},{1,17},{9,25},{17,1},{25,9},{2,18},{10... | collective-permute-start | bytes 12296 | tf_op jit(solution)/shard_map/ppermute | solution.py:427
  20.2 2.2 %collective-permute-done.7.theirs = f32[1,4,8,32]{3,2,1,0:T(8,128)S(1)} collective-permute-done((f32[1,4,8,32]{3,2,1,0:T(8,128)S(1)}, f32[1,4,8,32]{3,2,1,0:T(8,128)S(1)}, u32[]{:S(2)}, u32[]{:S(2)}) %collective-permute-start.7) | collective-permute-done | bytes 4128 | tf_op jit(solution)/shard_map/ppermute | solution.py:427
  22.5 0.6 %merge1.1 = f32[4,1,1,8,32]{4,3,2,1,0:T(8,128)} custom-call(s32[4,8,32]{2,1,0:T(8,128)S(1)} %get-tuple-element.43.order_map, f32[1,4,8,32]{3,2,1,0:T(8,128)S(1)} %get-tuple-element.67.kept, f32[1,4,8,32]{3,2,1,0:T(8,128)S(1)} %collective-permute-done.7.theirs), custom_call_target="tpu_custom_call" | custom-call | tf_op jit(solution)/shard_map/merge1/pallas_call | solution.py:430
  (3 shorter events, 0.0 us)
Async XLA Ops:
  1.3 7.6 %collective-permute-start = (bf16[16,16,256]{2,1,0:T(8,128)(2,1)S(1)}, bf16[16,16,256]{2,1,0:T(8,128)(2,1)S(1)}, u32[]{:S(2)}, u32[]{:S(2)}) collective-permute-start(bf16[16,16,256]{2,1,0:T(8,128)(2,1)S(1)} %get-tuple-element.47), channel_id=1, source_target_pairs={{0,1},{2,3},{4,5},{6,7},{8,9},{10,11},{12,13},{14,15},{16,17},{18,... | collective-permute-start | bytes 393224 | tf_op jit(solution)/shard_map/ppermute | solution.py:340
  4.3 10.1 %collective-permute-start.4 = (bf16[2,16,16,256]{3,2,1,0:T(8,128)(2,1)S(1)}, bf16[2,16,16,256]{3,2,1,0:T(8,128)(2,1)S(1)}, u32[]{:S(2)}, u32[]{:S(2)}) collective-permute-start(bf16[2,16,16,256]{3,2,1,0:T(8,128)(2,1)S(1)} %get-tuple-element.56.xs1), channel_id=1, source_target_pairs={{2,4},{3,5},{10,12},{11,13},{18,20},{19,21},{26,28},{27,29},{0,8},... | collective-permute-start | bytes 786440 | tf_op jit(solution)/shard_map/ppermute | solution.py:340
  4.4 10.9 %collective-permute-start.3 = (bf16[2,16,16,256]{3,2,1,0:T(8,128)(2,1)S(1)}, bf16[2,16,16,256]{3,2,1,0:T(8,128)(2,1)S(1)}, u32[]{:S(2)}, u32[]{:S(2)}) collective-permute-start(bf16[2,16,16,256]{3,2,1,0:T(8,128)(2,1)S(1)} %get-tuple-element.55.xs0), channel_id=1, source_target_pairs={{0,2},{1,3},{4,6},{5,7},{8,10},{9,11},{12,14},{13,15},{16,18},{17,... | collective-permute-start | bytes 786440 | tf_op jit(solution)/shard_map/ppermute | solution.py:340
  8.9 7.1 %collective-permute-start.1 = (bf16[16,16,256]{2,1,0:T(8,128)(2,1)S(1)}, bf16[16,16,256]{2,1,0:T(8,128)(2,1)S(1)}, u32[]{:S(2)}, u32[]{:S(2)}) collective-permute-start(bf16[16,16,256]{2,1,0:T(8,128)(2,1)S(1)} %get-tuple-element.53), channel_id=1, source_target_pairs={{0,1},{2,3},{4,5},{6,7},{8,9},{10,11},{12,13},{14,15},{16,17},{18,... | collective-permute-start | bytes 393224 | tf_op jit(solution)/shard_map/ppermute | solution.py:340
  9.6 7.1 %collective-permute-start.5 = (bf16[16,16,256]{2,1,0:T(8,128)(2,1)S(1)}, bf16[16,16,256]{2,1,0:T(8,128)(2,1)S(1)}, u32[]{:S(2)}, u32[]{:S(2)}) collective-permute-start(bf16[16,16,256]{2,1,0:T(8,128)(2,1)S(1)} %get-tuple-element.53), channel_id=1, source_target_pairs={{2,5},{3,4},{10,13},{11,12},{18,21},{19,20},{26,29},{27,28},{0,8},... | collective-permute-start | bytes 393224 | tf_op jit(solution)/shard_map/ppermute | solution.py:340
  9.6 6.5 %collective-permute-start.2 = (bf16[16,16,256]{2,1,0:T(8,128)(2,1)S(1)}, bf16[16,16,256]{2,1,0:T(8,128)(2,1)S(1)}, u32[]{:S(2)}, u32[]{:S(2)}) collective-permute-start(bf16[16,16,256]{2,1,0:T(8,128)(2,1)S(1)} %collective-permute-done.refs_2_.refs_7_), channel_id=1, source_target_pairs={{0,2},{1,3},{4,6},{5,7},{8,10},{9,11},{12,14},{13,15},{16,18},{17,... | collective-permute-start | bytes 393224 | tf_op jit(solution)/shard_map/ppermute | solution.py:340
  17.4 1.3 %collective-permute-start.6 = (f32[2,4,8,32]{3,2,1,0:T(8,128)S(1)}, f32[2,4,8,32]{3,2,1,0:T(8,128)S(1)}, u32[]{:S(2)}, u32[]{:S(2)}) collective-permute-start(f32[2,4,8,32]{3,2,1,0:T(8,128)S(1)} %get-tuple-element.66), channel_id=1, source_target_pairs={{0,8},{8,0},{16,24},{24,16},{1,9},{9,1},{17,25},{25,17},{2,10},{10... | collective-permute-start | bytes 24584 | tf_op jit(solution)/shard_map/ppermute | solution.py:427
  18.7 3.8 %collective-permute-start.7 = (f32[1,4,8,32]{3,2,1,0:T(8,128)S(1)}, f32[1,4,8,32]{3,2,1,0:T(8,128)S(1)}, u32[]{:S(2)}, u32[]{:S(2)}) collective-permute-start(f32[1,4,8,32]{3,2,1,0:T(8,128)S(1)} %get-tuple-element.68), channel_id=1, source_target_pairs={{0,16},{8,24},{16,0},{24,8},{1,17},{9,25},{17,1},{25,9},{2,18},{10... | collective-permute-start | bytes 12296 | tf_op jit(solution)/shard_map/ppermute | solution.py:427

commit v8 on v7

--- a/solution.py
+++ b/solution.py
@@ -237,46 +237,52 @@
     return [rays(shade * shaded[c, h], place.half[h] * rim, lane) for c in range(3)]
 
 
-def own_kernel(rim, h, early, mx, my, xs0, xs1, halo, *refs):
+def own_kernel(rim, early, mx, my, xs0, xs1, halo0, halo1, *refs):
     place = Place()
     size = rim * rim
-    s, e = (blur_x(place, rim, mx, h, [xs0[g], xs1[g]], halo[g]) for g in range(2))
-    cells = jnp.concatenate([e, s], axis=0)
-    partial = refs[-1]
-    partial[0] = dot(my[:, :2 * size], cells)
-    other = dot(my[:, size:], cells)
-    if not early:
-        partial[1] = other
-        return
-    shaded, out, partial = refs
-    for c, part in enumerate(lit(place, rim, other, shaded, h)):
+    if early:
+        shaded, out, partial = refs
+    else:
+        partial, = refs
+    for h, halo in enumerate((halo0, halo1)):
+        s, e = (blur_x(place, rim, mx, h, [xs0[g], xs1[g]], halo[g]) for g in range(2))
+        cells = jnp.concatenate([e, s], axis=0)
+        partial[0, h] = dot(my[:, :2 * size], cells)
+        other = dot(my[:, size:], cells)
+        if not early:
+            partial[1, h] = other
+            continue
+        for c, part in enumerate(lit(place, rim, other, shaded, h)):
+            out[c] = part if h == 0 else out[c] + part
+
+
+def late(rim, g, mx, my, near0, partial, near1, halo0, halo1, shaded):
+    place = Place()
+    size = rim * rim
+    block = my[:, 2 * size:] if g == 0 else my[:, :size]
+    acc = None
+    for h, halo in enumerate((halo0, halo1)):
+        across = blur_x(place, rim, mx, h, [near0[...], near1[...]], halo[...])
+        across = jnp.where(place.has_y[g], across, jnp.zeros_like(across))
+        part = lit(place, rim, partial[g, h] + dot(block, across), shaded, h)
+        acc = part if h == 0 else [a + b for a, b in zip(acc, part)]
+    return acc
+
+
+def late_kernel(rim, g, *refs):
+    *refs, out = refs
+    for c, part in enumerate(late(rim, g, *refs)):
         out[c] = part
 
 
-def late(rim, g, h, mx, my, near0, near1, halo, partial, shaded):
-    place = Place()
-    size = rim * rim
-    across = blur_x(place, rim, mx, h, [near0[...], near1[...]], halo[...])
-    across = jnp.where(place.has_y[g], across, jnp.zeros_like(across))
-    block = my[:, 2 * size:] if g == 0 else my[:, :size]
-    return lit(place, rim, partial[g] + dot(block, across), shaded, h)
-
-
-def late_kernel(rim, g, h, *refs):
-    *refs, out = refs
-    for c, part in enumerate(late(rim, g, h, *refs)):
-        out[c] = part
-
-
 def last_kernel(rim, depth_count, *refs):
-    (light_s, light_e0, light_e1, total0, total1), refs = refs[:5], refs[5:]
-    refs, (kept, given, img) = refs[:7], refs[7:]
+    refs, (light_e, total0, total1, kept, given, img) = refs[:8], refs[8:]
     place = Place()
     rows = 2 * rim
     at_s, at_e = group_rows(place, rim, 0), group_rows(place, rim, 1)
-    for c, part in enumerate(late(rim, 0, 1, *refs)):
-        img[c, at_s, :] = light_s[c] + part
-        img[c, at_e, :] = light_e0[c] + light_e1[c]
+    for c, part in enumerate(late(rim, 0, *refs)):
+        img[c, at_s, :] = part
+        img[c, at_e, :] = light_e[c]
     img[3, at_s, :] = jnp.exp2(total0[...])
     img[3, at_e, :] = jnp.exp2(total1[...])
     for c in range(4):
@@ -390,38 +396,35 @@
 
     corner = [[None, None] for r in range(rounds)]
     for r in range(rounds):
+        near[r][1] = swap(strips[2 * r + 1], None, r)
         strip, arrived, total[1] = lax.optimization_barrier(
             (strips[2 * r + 1], near[r][0], total[1])
         )
         corner[r] = [swap(arrived, 0, None), swap(strip, 1, r)]
-        near[r][1] = swap(strip, None, r)
 
     early = rounds < 2
     colours = struct((3, rim, 128), F32)
-    partial, lights = [None, None], [[None, None], [None, None]]
-    for h in range(2):
-        unlit = struct((2 - early, size, rows_z), F32)
-        results = call(
-            functools.partial(own_kernel, rim, h, early),
-            f"own{h}",
-            [VMEM] * (6 if early else 5),
-            [colours, unlit] if early else [unlit],
-        )(mx, my, xs0, xs1, halo_x[h], *([shaded[1]] if early else []))
-        partial[h] = results[-1]
-        if early:
-            lights[1][h] = results[0]
-    for g in range(rounds):
-        for h in range(2 if g == 1 else 1):
-            lights[g][h] = call(
-                functools.partial(late_kernel, rim, g, h), f"late{g}{h}", [VMEM] * 7, colours
-            )(mx, my, *near[g], corner[g][h], partial[h], shaded[g])
+    unlit = struct((2 - early, 2, size, rows_z), F32)
+    results = call(
+        functools.partial(own_kernel, rim, early),
+        "own",
+        [VMEM] * (7 if early else 6),
+        [colours, unlit] if early else [unlit],
+    )(mx, my, xs0, xs1, *halo_x, *([shaded[1]] if early else []))
+    partial = results[-1]
+    if early:
+        light = results[0]
+    else:
+        light = call(functools.partial(late_kernel, rim, 1), "late", [VMEM] * 8, colours)(
+            mx, my, near[1][0], partial, near[1][1], *corner[1], shaded[1]
+        )
     kept, given = call(
         functools.partial(last_kernel, rim, depth_count),
         "last",
-        [VMEM] * 12,
+        [VMEM] * 11,
         [struct((depth_count // 2, 4, block, rows_y), F32)] * 2,
         [pltpu.VMEM((8, rows_y, 128), F32)],
-    )(lights[0][0], *lights[1], *total, mx, my, *near[0], corner[0][1], partial[1], shaded[0])
+    )(mx, my, near[0][0], partial, near[0][1], *corner[0], shaded[0], light, *total)
     level = 0
     while True:
         theirs = lax.ppermute(given, "depth", [(i, i ^ 1 << level) for i in range(depth_count)])

time: 23.2 us -> 22.2 us (0.957); the launches traced: 23.1 us -> 21.8 us
  starting transfers between devices: 11.6 us -> 9.96 us
  waiting for transfers between devices: 3.48 us -> 4.24 us
  Pallas kernels: 7.92 us -> 7.52 us
    ppermute x6, starting transfers between devices: 9.95 us -> 8.33 us  [swap(): return lax.ppermute(piece, axes, swaps(counts, x_round, y_round))]
    pallas_call x3 -> x1, Pallas kernels: 2.15 us -> 1.24 us  [per_device(): call(functools.partial(own_kernel, rim, early), 'own', [VMEM] * (7 if ear...]
    ppermute x6, waiting for transfers between devices: 0.03 us -> 0.8 us  [swap(): return lax.ppermute(piece, axes, swaps(counts, x_round, y_round))]
    pallas_call x1, Pallas kernels: 0.7 us -> 1.16 us  [per_device(): call(functools.partial(last_kernel, rim, depth_count), 'last', [VMEM] * 1...]
  transfers between devices with their start and end apart: 8 -> 8, of which waited for: 2 -> 4; matrix products, arithmetic and copies ran while one was open for 0% -> 0% of each run, Pallas kernels for 23% -> 20%
where the time goes in v8:
time: 22.2 us; the launch traced here: 21.8 us
  starting transfers between devices  9.96 us (45%)
  Pallas kernels  7.52 us (34%)
  waiting for transfers between devices  4.24 us (19%)
    ppermute x6, starting transfers between devices, swap(): return lax.ppermute(piece, axes, swaps(counts, x_round, y_round))  8.33 us
    ppermute x2, waiting for transfers between devices, per_device(): lax.ppermute(given, 'depth', [(i, i ^ 1 << level) for i in range(depth_co...  3.44 us
    pallas_call x2, Pallas kernels, per_device(): call(functools.partial(cells_kernel, rim, bumps, g), f'cells{g}', [VMEM]...  2.31 us
    ppermute x2, starting transfers between devices, per_device(): lax.ppermute(given, 'depth', [(i, i ^ 1 << level) for i in range(depth_co...  1.63 us
    pallas_call x1, Pallas kernels, per_device(): call(functools.partial(first_kernel, rim, rounds), 'first', [HBM] * (1 +...  1.31 us
    pallas_call x1, Pallas kernels, per_device(): call(functools.partial(own_kernel, rim, early), 'own', [VMEM] * (7 if ear...  1.24 us
    pallas_call x1, Pallas kernels, per_device(): call(functools.partial(last_kernel, rim, depth_count), 'last', [VMEM] * 1...  1.16 us
    ppermute x6, waiting for transfers between devices, swap(): return lax.ppermute(piece, axes, swaps(counts, x_round, y_round))  0.8 us
  transfers between devices with their start and end apart: 8, of which 4 were waited for; matrix products, arithmetic and copies ran while one was open for 0% of the time, Pallas kernels for 20%

profile of v8, /device:TPU:0, one launch (start us, length us, event | category | flops | bytes accessed | tf_op | source)
XLA Modules:
  0.0 21.8 jit_solution(13504433821198815839)
XLA Ops:
  0.0 1.3 %first.1 = (f32[2,2,16,16,256]{4,3,2,1,0:T(8,128)S(1)}, bf16[2,16,16,256]{3,2,1,0:T(8,128)(2,1)S(1)}, bf16[2,16,16,256]{3,2,1,0:T(8,128)(2,1)S(1)}, bf16[16,16,2...) custom-call(f32[32,32,256]{2,1,0:T(8,128)} %density.1, ...), custom_call_target="tpu_custom_call" | custom-call | tf_op jit(solution)/shard_map/first/pallas_call | solution.py:354
  1.3 3.0 %collective-permute-start = (bf16[16,16,256]{2,1,0:T(8,128)(2,1)S(1)}, bf16[16,16,256]{2,1,0:T(8,128)(2,1)S(1)}, u32[]{:S(2)}, u32[]{:S(2)}) collective-permute-start(bf16[16,16,256]{2,1,0:T(8,128)(2,1)S(1)} %get-tuple-element.45), channel_id=1, source_target_pairs={{0,1},{2,3},{4,5},{6,7},{8,9},{10,11},{12,13},{14,15},{16,17},{18,... | collective-permute-start | bytes 393224 | tf_op jit(solution)/shard_map/ppermute | solution.py:346
  4.3 1.6 %collective-permute-start.1 = (bf16[2,16,16,256]{3,2,1,0:T(8,128)(2,1)S(1)}, bf16[2,16,16,256]{3,2,1,0:T(8,128)(2,1)S(1)}, u32[]{:S(2)}, u32[]{:S(2)}) collective-permute-start(bf16[2,16,16,256]{3,2,1,0:T(8,128)(2,1)S(1)} %get-tuple-element.46.xs0), channel_id=1, source_target_pairs={{0,2},{1,3},{4,6},{5,7},{8,10},{9,11},{12,14},{13,15},{16,18},{17,... | collective-permute-start | bytes 786440 | tf_op jit(solution)/shard_map/ppermute | solution.py:346
  5.9 0.0 collective-permute-start.2
  5.9 0.5 %collective-permute-start.3 = (bf16[16,16,256]{2,1,0:T(8,128)(2,1)S(1)}, bf16[16,16,256]{2,1,0:T(8,128)(2,1)S(1)}, u32[]{:S(2)}, u32[]{:S(2)}) collective-permute-start(bf16[16,16,256]{2,1,0:T(8,128)(2,1)S(1)} %get-tuple-element.56), channel_id=1, source_target_pairs={{0,1},{2,3},{4,5},{6,7},{8,9},{10,11},{12,13},{14,15},{16,17},{18,... | collective-permute-start | bytes 393224 | tf_op jit(solution)/shard_map/ppermute | solution.py:346
  6.4 0.3 %prepare.1 = (f32[8,24,128]{2,1,0:T(8,128)S(1)}, s32[2,2,8,128]{3,2,1,0:T(8,128)S(1)}, s32[4,8,32]{2,1,0:T(8,128)S(1)}) custom-call(f32[4,8]{1,0:T(4,128)S(1)} %get-tuple-element.35.centre, f32[4,8]{1,0:T(4,128)S(1)} %get-tuple-element.36.width, f32[3,4,8]{2,1,0:T(4,128)S(1)} %get-tuple-element.37.colour, f32[4,8]{1,0:T(4,128)S(1)} %get-tuple-element.38.opacity, ...), custom_call_target="tpu_custom_call" | custom-call | tf_op jit(solution)/shard_map/prepare/pallas_call | solution.py:367
  6.7 1.2 %cells1.1 = (f32[3,2,16,16,256]{4,3,2,1,0:T(8,128)S(1)}, f32[16,128]{1,0:T(8,128)S(1)}) custom-call(f32[2,2,16,16,256]{4,3,2,1,0:T(8,128)S(1)} %get-tuple-element.48.held, f32[8,24,128]{2,1,0:T(8,128)S(1)} %get-tuple-element.49.table, s32[2,2,8,128]{3,2,1,0:T(8,128)S(1)} %get-tuple-element.50.signs), custom_call_target="tpu_custom_call" | custom-call | flops 262144 | bytes 262144 | tf_op jit(solution)/shard_map/cells1/pallas_call | solution.py:384
  7.9 0.0 collective-permute-done.refs_2_
  7.9 3.2 %collective-permute-start.4 = (bf16[16,16,256]{2,1,0:T(8,128)(2,1)S(1)}, bf16[16,16,256]{2,1,0:T(8,128)(2,1)S(1)}, u32[]{:S(2)}, u32[]{:S(2)}) collective-permute-start(bf16[16,16,256]{2,1,0:T(8,128)(2,1)S(1)} %collective-permute-done.refs_2_), channel_id=1, source_target_pairs={{0,2},{1,3},{4,6},{5,7},{8,10},{9,11},{12,14},{13,15},{16,18},{17,... | collective-permute-start | bytes 393224 | tf_op jit(solution)/shard_map/ppermute | solution.py:346
  11.1 0.0 collective-permute-start.5
  11.1 1.2 %cells0.1 = (f32[3,2,16,16,256]{4,3,2,1,0:T(8,128)S(1)}, f32[16,128]{1,0:T(8,128)S(1)}) custom-call(f32[2,2,16,16,256]{4,3,2,1,0:T(8,128)S(1)} %get-tuple-element.48.held, f32[8,24,128]{2,1,0:T(8,128)S(1)} %get-tuple-element.49.table, s32[2,2,8,128]{3,2,1,0:T(8,128)S(1)} %get-tuple-element.50.signs), custom_call_target="tpu_custom_call" | custom-call | flops 26214400000 | bytes 2621440000 | tf_op jit(solution)/shard_map/cells0/pallas_call | solution.py:384
  12.3 0.6 %matrices.1 = (bf16[256,768]{1,0:T(8,128)(2,1)S(1)}, bf16[256,768]{1,0:T(8,128)(2,1)S(1)}) custom-call(bf16[2,33]{1,0:T(2,128)(2,1)S(1)} %get-tuple-element.42.taps), custom_call_target="tpu_custom_call" | custom-call | tf_op jit(solution)/shard_map/matrices/pallas_call | solution.py:375
  12.9 0.5 %collective-permute-done.1.halo0 = bf16[2,16,16,256]{3,2,1,0:T(8,128)(2,1)S(1)} collective-permute-done((bf16[2,16,16,256]{3,2,1,0:T(8,128)(2,1)S(1)}, bf16[2,16,16,256]{3,2,1,0:T(8,128)(2,1)S(1)}, u32[]{:S(2)}, u32[]{:S(2)}) %collective-permute-start.1) | collective-permute-done | bytes 262176 | tf_op jit(solution)/shard_map/ppermute | solution.py:346
  13.4 0.0 collective-permute-done.2.halo1
  13.4 1.2 %own.1 = (f32[3,16,128]{2,1,0:T(8,128)S(1)}, f32[1,2,256,256]{3,2,1,0:T(8,128)S(1)}) custom-call(bf16[256,768]{1,0:T(8,128)(2,1)S(1)} %get-tuple-element.43.mx.refs_0_, bf16[256,768]{1,0:T(8,128)(2,1)S(1)} %get-tuple-element.44.my.refs_1_, bf16[2,16,16,256]{3,2,1,0:T(8,128)(2,1)S(1)} %get-tuple-element.46.xs0, ...), custom_call_target="tpu_custom_call" | custom-call | tf_op jit(solution)/shard_map/own/pallas_call | solution.py:408
  14.6 0.0 collective-permute-done.3.refs_4_
  14.7 0.3 %collective-permute-done.4.refs_5_ = bf16[16,16,256]{2,1,0:T(8,128)(2,1)S(1)} collective-permute-done((bf16[16,16,256]{2,1,0:T(8,128)(2,1)S(1)}, bf16[16,16,256]{2,1,0:T(8,128)(2,1)S(1)}, u32[]{:S(2)}, u32[]{:S(2)}) %collective-permute-start.4) | collective-permute-done | bytes 131104 | tf_op jit(solution)/shard_map/ppermute | solution.py:346
  14.9 0.0 collective-permute-done.5.refs_6_
  14.9 1.2 %last.1 = (f32[2,4,8,32]{3,2,1,0:T(8,128)S(1)}, f32[2,4,8,32]{3,2,1,0:T(8,128)S(1)}) custom-call(bf16[256,768]{1,0:T(8,128)(2,1)S(1)} %get-tuple-element.43.mx.refs_0_, bf16[256,768]{1,0:T(8,128)(2,1)S(1)} %get-tuple-element.44.my.refs_1_, bf16[16,16,256]{2,1,0:T(8,128)(2,1)S(1)} %collective-permute-done.refs_2_, ...), custom_call_target="tpu_custom_call" | custom-call | tf_op jit(solution)/shard_map/last/pallas_call | solution.py:421
  16.1 0.1 collective-permute-start.6
  16.2 1.2 %collective-permute-done.6.theirs = f32[2,4,8,32]{3,2,1,0:T(8,128)S(1)} collective-permute-done((f32[2,4,8,32]{3,2,1,0:T(8,128)S(1)}, f32[2,4,8,32]{3,2,1,0:T(8,128)S(1)}, u32[]{:S(2)}, u32[]{:S(2)}) %collective-permute-start.6) | collective-permute-done | bytes 8224 | tf_op jit(solution)/shard_map/ppermute | solution.py:430
  17.4 1.6 %collective-permute-start.7 = (f32[1,4,8,32]{3,2,1,0:T(8,128)S(1)}, f32[1,4,8,32]{3,2,1,0:T(8,128)S(1)}, u32[]{:S(2)}, u32[]{:S(2)}) collective-permute-start(f32[1,4,8,32]{3,2,1,0:T(8,128)S(1)} %get-tuple-element.64), channel_id=1, source_target_pairs={{0,16},{8,24},{16,0},{24,8},{1,17},{9,25},{17,1},{25,9},{2,18},{10... | collective-permute-start | bytes 12296 | tf_op jit(solution)/shard_map/ppermute | solution.py:430
  18.9 2.2 %collective-permute-done.7.theirs = f32[1,4,8,32]{3,2,1,0:T(8,128)S(1)} collective-permute-done((f32[1,4,8,32]{3,2,1,0:T(8,128)S(1)}, f32[1,4,8,32]{3,2,1,0:T(8,128)S(1)}, u32[]{:S(2)}, u32[]{:S(2)}) %collective-permute-start.7) | collective-permute-done | bytes 4128 | tf_op jit(solution)/shard_map/ppermute | solution.py:430
  21.2 0.6 %merge1.1 = f32[4,1,1,8,32]{4,3,2,1,0:T(8,128)} custom-call(s32[4,8,32]{2,1,0:T(8,128)S(1)} %get-tuple-element.41.order_map, f32[1,4,8,32]{3,2,1,0:T(8,128)S(1)} %get-tuple-element.63.kept, f32[1,4,8,32]{3,2,1,0:T(8,128)S(1)} %collective-permute-done.7.theirs), custom_call_target="tpu_custom_call" | custom-call | tf_op jit(solution)/shard_map/merge1/pallas_call | solution.py:433
  (1 shorter events, 0.0 us)
Async XLA Ops:
  1.3 6.6 %collective-permute-start = (bf16[16,16,256]{2,1,0:T(8,128)(2,1)S(1)}, bf16[16,16,256]{2,1,0:T(8,128)(2,1)S(1)}, u32[]{:S(2)}, u32[]{:S(2)}) collective-permute-start(bf16[16,16,256]{2,1,0:T(8,128)(2,1)S(1)} %get-tuple-element.45), channel_id=1, source_target_pairs={{0,1},{2,3},{4,5},{6,7},{8,9},{10,11},{12,13},{14,15},{16,17},{18,... | collective-permute-start | bytes 393224 | tf_op jit(solution)/shard_map/ppermute | solution.py:346
  4.3 9.0 %collective-permute-start.1 = (bf16[2,16,16,256]{3,2,1,0:T(8,128)(2,1)S(1)}, bf16[2,16,16,256]{3,2,1,0:T(8,128)(2,1)S(1)}, u32[]{:S(2)}, u32[]{:S(2)}) collective-permute-start(bf16[2,16,16,256]{3,2,1,0:T(8,128)(2,1)S(1)} %get-tuple-element.46.xs0), channel_id=1, source_target_pairs={{0,2},{1,3},{4,6},{5,7},{8,10},{9,11},{12,14},{13,15},{16,18},{17,... | collective-permute-start | bytes 786440 | tf_op jit(solution)/shard_map/ppermute | solution.py:346
  5.9 7.5 %collective-permute-start.2 = (bf16[2,16,16,256]{3,2,1,0:T(8,128)(2,1)S(1)}, bf16[2,16,16,256]{3,2,1,0:T(8,128)(2,1)S(1)}, u32[]{:S(2)}, u32[]{:S(2)}) collective-permute-start(bf16[2,16,16,256]{3,2,1,0:T(8,128)(2,1)S(1)} %get-tuple-element.47.xs1), channel_id=1, source_target_pairs={{2,4},{3,5},{10,12},{11,13},{18,20},{19,21},{26,28},{27,29},{0,8},... | collective-permute-start | bytes 786440 | tf_op jit(solution)/shard_map/ppermute | solution.py:346
  5.9 8.7 %collective-permute-start.3 = (bf16[16,16,256]{2,1,0:T(8,128)(2,1)S(1)}, bf16[16,16,256]{2,1,0:T(8,128)(2,1)S(1)}, u32[]{:S(2)}, u32[]{:S(2)}) collective-permute-start(bf16[16,16,256]{2,1,0:T(8,128)(2,1)S(1)} %get-tuple-element.56), channel_id=1, source_target_pairs={{0,1},{2,3},{4,5},{6,7},{8,9},{10,11},{12,13},{14,15},{16,17},{18,... | collective-permute-start | bytes 393224 | tf_op jit(solution)/shard_map/ppermute | solution.py:346
  7.9 7.0 %collective-permute-start.4 = (bf16[16,16,256]{2,1,0:T(8,128)(2,1)S(1)}, bf16[16,16,256]{2,1,0:T(8,128)(2,1)S(1)}, u32[]{:S(2)}, u32[]{:S(2)}) collective-permute-start(bf16[16,16,256]{2,1,0:T(8,128)(2,1)S(1)} %collective-permute-done.refs_2_), channel_id=1, source_target_pairs={{0,2},{1,3},{4,6},{5,7},{8,10},{9,11},{12,14},{13,15},{16,18},{17,... | collective-permute-start | bytes 393224 | tf_op jit(solution)/shard_map/ppermute | solution.py:346
  11.1 3.8 %collective-permute-start.5 = (bf16[16,16,256]{2,1,0:T(8,128)(2,1)S(1)}, bf16[16,16,256]{2,1,0:T(8,128)(2,1)S(1)}, u32[]{:S(2)}, u32[]{:S(2)}) collective-permute-start(bf16[16,16,256]{2,1,0:T(8,128)(2,1)S(1)} %get-tuple-element.56), channel_id=1, source_target_pairs={{2,5},{3,4},{10,13},{11,12},{18,21},{19,20},{26,29},{27,28},{0,8},... | collective-permute-start | bytes 393224 | tf_op jit(solution)/shard_map/ppermute | solution.py:346
  16.1 1.3 %collective-permute-start.6 = (f32[2,4,8,32]{3,2,1,0:T(8,128)S(1)}, f32[2,4,8,32]{3,2,1,0:T(8,128)S(1)}, u32[]{:S(2)}, u32[]{:S(2)}) collective-permute-start(f32[2,4,8,32]{3,2,1,0:T(8,128)S(1)} %get-tuple-element.62), channel_id=1, source_target_pairs={{0,8},{8,0},{16,24},{24,16},{1,9},{9,1},{17,25},{25,17},{2,10},{10... | collective-permute-start | bytes 24584 | tf_op jit(solution)/shard_map/ppermute | solution.py:430
  17.4 3.8 %collective-permute-start.7 = (f32[1,4,8,32]{3,2,1,0:T(8,128)S(1)}, f32[1,4,8,32]{3,2,1,0:T(8,128)S(1)}, u32[]{:S(2)}, u32[]{:S(2)}) collective-permute-start(f32[1,4,8,32]{3,2,1,0:T(8,128)S(1)} %get-tuple-element.64), channel_id=1, source_target_pairs={{0,16},{8,24},{16,0},{24,8},{1,17},{9,25},{17,1},{25,9},{2,18},{10... | collective-permute-start | bytes 12296 | tf_op jit(solution)/shard_map/ppermute | solution.py:430

commit v9 on v8

--- a/solution.py
+++ b/solution.py
@@ -372,13 +372,6 @@
         + [struct((depth_count, block, rows_y), jnp.int32)],
     )(*tables[1:])
     halo_x = [swap(cells, h, None) for h, cells in enumerate((xs0, xs1))]
-    mx, my = call(
-        functools.partial(matrices_kernel, rim),
-        "matrices",
-        [VMEM],
-        [struct((size, 3 * size), BF16)] * 2,
-        [pltpu.VMEM((8, 128), F32)],
-    )(tables[0])
     shaded, total = [None, None], [None, None]
     for g in (1, 0):
         shaded[g], total[g] = call(
@@ -388,8 +381,8 @@
             [struct((3, 2, rim, rim, rows_z), F32), struct((rim, 128), F32)],
             [pltpu.VMEM((2, size, rows_z), F32), pltpu.VMEM((3, 2, size, rows_z), F32)],
             cost_estimate=pl.CostEstimate(
-                flops=density.size * (100000 if g == 0 else 1),
-                bytes_accessed=density.size * (10000 if g == 0 else 1),
+                flops=density.size,
+                bytes_accessed=density.size,
                 transcendentals=density.size * 3,
             ),
         )(held, table, signs)
@@ -397,10 +390,21 @@
     corner = [[None, None] for r in range(rounds)]
     for r in range(rounds):
         near[r][1] = swap(strips[2 * r + 1], None, r)
-        strip, arrived, total[1] = lax.optimization_barrier(
-            (strips[2 * r + 1], near[r][0], total[1])
-        )
-        corner[r] = [swap(arrived, 0, None), swap(strip, 1, r)]
+        strip, table = lax.optimization_barrier((strips[2 * r + 1], table))
+        corner[r][1] = swap(strip, 1, r)
+        arrived, total[0] = lax.optimization_barrier((near[r][0], total[0]))
+        corner[r][0] = swap(arrived, 0, None)
+    taps, total[0] = lax.optimization_barrier((tables[0], total[0]))
+    mx, my = call(
+        functools.partial(matrices_kernel, rim),
+        "matrices",
+        [VMEM],
+        [struct((size, 3 * size), BF16)] * 2,
+        [pltpu.VMEM((8, 128), F32)],
+        cost_estimate=pl.CostEstimate(
+            flops=density.size * 100000, bytes_accessed=density.size * 10000, transcendentals=0
+        ),
+    )(taps)
 
     early = rounds < 2
     colours = struct((3, rim, 128), F32)

time: 22.2 us -> 23.2 us (1.045); the launches traced: 21.8 us -> 23.1 us
  starting transfers between devices: 9.96 us -> 11 us
  waiting for transfers between devices: 4.24 us -> 4.49 us
    ppermute x6, starting transfers between devices: 8.33 us -> 9.36 us  [swap(): return lax.ppermute(piece, axes, swaps(counts, x_round, y_round))]
    ppermute x6, waiting for transfers between devices: 0.8 us -> 1.05 us  [swap(): return lax.ppermute(piece, axes, swaps(counts, x_round, y_round))]
  transfers between devices with their start and end apart: 8 -> 8, of which waited for: 4 -> 3; matrix products, arithmetic and copies ran while one was open for 0% -> 0% of each run, Pallas kernels for 20% -> 19%
where the time goes in v9:
time: 23.2 us; the launch traced here: 23.1 us
  starting transfers between devices  11 us (47%)
  Pallas kernels  7.52 us (32%)
  waiting for transfers between devices  4.49 us (19%)
    ppermute x6, starting transfers between devices, swap(): return lax.ppermute(piece, axes, swaps(counts, x_round, y_round))  9.36 us
    ppermute x2, waiting for transfers between devices, per_device(): lax.ppermute(given, 'depth', [(i, i ^ 1 << level) for i in range(depth_co...  3.44 us
    pallas_call x2, Pallas kernels, per_device(): call(functools.partial(cells_kernel, rim, bumps, g), f'cells{g}', [VMEM]...  2.31 us
    ppermute x2, starting transfers between devices, per_device(): lax.ppermute(given, 'depth', [(i, i ^ 1 << level) for i in range(depth_co...  1.63 us
    pallas_call x1, Pallas kernels, per_device(): call(functools.partial(first_kernel, rim, rounds), 'first', [HBM] * (1 +...  1.31 us
    pallas_call x1, Pallas kernels, per_device(): call(functools.partial(own_kernel, rim, early), 'own', [VMEM] * (7 if ear...  1.24 us
    pallas_call x1, Pallas kernels, per_device(): call(functools.partial(last_kernel, rim, depth_count), 'last', [VMEM] * 1...  1.16 us
    ppermute x6, waiting for transfers between devices, swap(): return lax.ppermute(piece, axes, swaps(counts, x_round, y_round))  1.05 us
  transfers between devices with their start and end apart: 8, of which 3 were waited for; matrix products, arithmetic and copies ran while one was open for 0% of the time, Pallas kernels for 19%

profile of v9, /device:TPU:0, one launch (start us, length us, event | category | flops | bytes accessed | tf_op | source)
XLA Modules:
  0.0 23.1 jit_solution(5520966869159527890)
XLA Ops:
  0.0 1.3 %first.1 = (f32[2,2,16,16,256]{4,3,2,1,0:T(8,128)S(1)}, bf16[2,16,16,256]{3,2,1,0:T(8,128)(2,1)S(1)}, bf16[2,16,16,256]{3,2,1,0:T(8,128)(2,1)S(1)}, bf16[16,16,2...) custom-call(f32[32,32,256]{2,1,0:T(8,128)} %density.1, ...), custom_call_target="tpu_custom_call" | custom-call | tf_op jit(solution)/shard_map/first/pallas_call | solution.py:354
  1.3 3.0 %collective-permute-start = (bf16[16,16,256]{2,1,0:T(8,128)(2,1)S(1)}, bf16[16,16,256]{2,1,0:T(8,128)(2,1)S(1)}, u32[]{:S(2)}, u32[]{:S(2)}) collective-permute-start(bf16[16,16,256]{2,1,0:T(8,128)(2,1)S(1)} %get-tuple-element.45), channel_id=1, source_target_pairs={{0,1},{2,3},{4,5},{6,7},{8,9},{10,11},{12,13},{14,15},{16,17},{18,... | collective-permute-start | bytes 393224 | tf_op jit(solution)/shard_map/ppermute | solution.py:346
  4.3 1.6 %collective-permute-start.1 = (bf16[2,16,16,256]{3,2,1,0:T(8,128)(2,1)S(1)}, bf16[2,16,16,256]{3,2,1,0:T(8,128)(2,1)S(1)}, u32[]{:S(2)}, u32[]{:S(2)}) collective-permute-start(bf16[2,16,16,256]{3,2,1,0:T(8,128)(2,1)S(1)} %get-tuple-element.54.xs0), channel_id=1, source_target_pairs={{0,2},{1,3},{4,6},{5,7},{8,10},{9,11},{12,14},{13,15},{16,18},{17,... | collective-permute-start | bytes 786440 | tf_op jit(solution)/shard_map/ppermute | solution.py:346
  5.9 0.0 collective-permute-start.2
  5.9 0.5 %collective-permute-start.3 = (bf16[16,16,256]{2,1,0:T(8,128)(2,1)S(1)}, bf16[16,16,256]{2,1,0:T(8,128)(2,1)S(1)}, u32[]{:S(2)}, u32[]{:S(2)}) collective-permute-start(bf16[16,16,256]{2,1,0:T(8,128)(2,1)S(1)} %get-tuple-element.60), channel_id=1, source_target_pairs={{0,1},{2,3},{4,5},{6,7},{8,9},{10,11},{12,13},{14,15},{16,17},{18,... | collective-permute-start | bytes 393224 | tf_op jit(solution)/shard_map/ppermute | solution.py:346
  6.4 0.3 %prepare.1 = (f32[8,24,128]{2,1,0:T(8,128)S(1)}, s32[2,2,8,128]{3,2,1,0:T(8,128)S(1)}, s32[4,8,32]{2,1,0:T(8,128)S(1)}) custom-call(f32[4,8]{1,0:T(4,128)S(1)} %get-tuple-element.37.centre, f32[4,8]{1,0:T(4,128)S(1)} %get-tuple-element.38.width, f32[3,4,8]{2,1,0:T(4,128)S(1)} %get-tuple-element.39.colour, f32[4,8]{1,0:T(4,128)S(1)} %get-tuple-element.40.opacity, ...), custom_call_target="tpu_custom_call" | custom-call | tf_op jit(solution)/shard_map/prepare/pallas_call | solution.py:367
  6.7 0.3 %collective-permute-start.5 = (bf16[16,16,256]{2,1,0:T(8,128)(2,1)S(1)}, bf16[16,16,256]{2,1,0:T(8,128)(2,1)S(1)}, u32[]{:S(2)}, u32[]{:S(2)}) collective-permute-start(bf16[16,16,256]{2,1,0:T(8,128)(2,1)S(1)} %get-tuple-element.60), channel_id=1, source_target_pairs={{2,5},{3,4},{10,13},{11,12},{18,21},{19,20},{26,29},{27,28},{0,8},... | collective-permute-start | bytes 393224 | tf_op jit(solution)/shard_map/ppermute | solution.py:346
  7.0 1.2 %cells1.1 = (f32[3,2,16,16,256]{4,3,2,1,0:T(8,128)S(1)}, f32[16,128]{1,0:T(8,128)S(1)}) custom-call(f32[2,2,16,16,256]{4,3,2,1,0:T(8,128)S(1)} %get-tuple-element.46.held, f32[8,24,128]{2,1,0:T(8,128)S(1)} %get-tuple-element.47.table, s32[2,2,8,128]{3,2,1,0:T(8,128)S(1)} %get-tuple-element.48.signs), custom_call_target="tpu_custom_call" | custom-call | flops 262144 | bytes 262144 | tf_op jit(solution)/shard_map/cells1/pallas_call | solution.py:377
  8.2 1.2 %cells0.1 = (f32[3,2,16,16,256]{4,3,2,1,0:T(8,128)S(1)}, f32[16,128]{1,0:T(8,128)S(1)}) custom-call(f32[2,2,16,16,256]{4,3,2,1,0:T(8,128)S(1)} %get-tuple-element.46.held, f32[8,24,128]{2,1,0:T(8,128)S(1)} %get-tuple-element.47.table, s32[2,2,8,128]{3,2,1,0:T(8,128)S(1)} %get-tuple-element.48.signs), custom_call_target="tpu_custom_call" | custom-call | flops 262144 | bytes 262144 | tf_op jit(solution)/shard_map/cells0/pallas_call | solution.py:377
  9.3 0.0 collective-permute-done.refs_2_
  9.3 3.9 %collective-permute-start.4 = (bf16[16,16,256]{2,1,0:T(8,128)(2,1)S(1)}, bf16[16,16,256]{2,1,0:T(8,128)(2,1)S(1)}, u32[]{:S(2)}, u32[]{:S(2)}) collective-permute-start(bf16[16,16,256]{2,1,0:T(8,128)(2,1)S(1)} %collective-permute-done.refs_2_), channel_id=1, source_target_pairs={{0,2},{1,3},{4,6},{5,7},{8,10},{9,11},{12,14},{13,15},{16,18},{17,... | collective-permute-start | bytes 393224 | tf_op jit(solution)/shard_map/ppermute | solution.py:346
  13.3 0.6 %matrices.1 = (bf16[256,768]{1,0:T(8,128)(2,1)S(1)}, bf16[256,768]{1,0:T(8,128)(2,1)S(1)}) custom-call(bf16[2,33]{1,0:T(2,128)(2,1)S(1)} %get-tuple-element.51.taps), custom_call_target="tpu_custom_call" | custom-call | flops 26214400000 | bytes 2621440000 | tf_op jit(solution)/shard_map/matrices/pallas_call | solution.py:398
  13.9 0.0 collective-permute-done.1.halo0
  13.9 0.0 collective-permute-done.2.halo1
  13.9 1.2 %own.1 = (f32[3,16,128]{2,1,0:T(8,128)S(1)}, f32[1,2,256,256]{3,2,1,0:T(8,128)S(1)}) custom-call(bf16[256,768]{1,0:T(8,128)(2,1)S(1)} %get-tuple-element.52.mx.refs_0_, bf16[256,768]{1,0:T(8,128)(2,1)S(1)} %get-tuple-element.53.my.refs_1_, bf16[2,16,16,256]{3,2,1,0:T(8,128)(2,1)S(1)} %get-tuple-element.54.xs0, ...), custom_call_target="tpu_custom_call" | custom-call | tf_op jit(solution)/shard_map/own/pallas_call | solution.py:412
  15.2 0.0 collective-permute-done.5.refs_6_
  15.2 0.0 collective-permute-done.3.refs_4_
  15.2 1.0 %collective-permute-done.4.refs_5_ = bf16[16,16,256]{2,1,0:T(8,128)(2,1)S(1)} collective-permute-done((bf16[16,16,256]{2,1,0:T(8,128)(2,1)S(1)}, bf16[16,16,256]{2,1,0:T(8,128)(2,1)S(1)}, u32[]{:S(2)}, u32[]{:S(2)}) %collective-permute-start.4) | collective-permute-done | bytes 131104 | tf_op jit(solution)/shard_map/ppermute | solution.py:346
  16.2 1.2 %last.1 = (f32[2,4,8,32]{3,2,1,0:T(8,128)S(1)}, f32[2,4,8,32]{3,2,1,0:T(8,128)S(1)}) custom-call(bf16[256,768]{1,0:T(8,128)(2,1)S(1)} %get-tuple-element.52.mx.refs_0_, bf16[256,768]{1,0:T(8,128)(2,1)S(1)} %get-tuple-element.53.my.refs_1_, bf16[16,16,256]{2,1,0:T(8,128)(2,1)S(1)} %collective-permute-done.refs_2_, ...), custom_call_target="tpu_custom_call" | custom-call | tf_op jit(solution)/shard_map/last/pallas_call | solution.py:425
  17.4 0.1 collective-permute-start.6
  17.5 1.2 %collective-permute-done.6.theirs = f32[2,4,8,32]{3,2,1,0:T(8,128)S(1)} collective-permute-done((f32[2,4,8,32]{3,2,1,0:T(8,128)S(1)}, f32[2,4,8,32]{3,2,1,0:T(8,128)S(1)}, u32[]{:S(2)}, u32[]{:S(2)}) %collective-permute-start.6) | collective-permute-done | bytes 8224 | tf_op jit(solution)/shard_map/ppermute | solution.py:434
  18.7 1.6 %collective-permute-start.7 = (f32[1,4,8,32]{3,2,1,0:T(8,128)S(1)}, f32[1,4,8,32]{3,2,1,0:T(8,128)S(1)}, u32[]{:S(2)}, u32[]{:S(2)}) collective-permute-start(f32[1,4,8,32]{3,2,1,0:T(8,128)S(1)} %get-tuple-element.68), channel_id=1, source_target_pairs={{0,16},{8,24},{16,0},{24,8},{1,17},{9,25},{17,1},{25,9},{2,18},{10... | collective-permute-start | bytes 12296 | tf_op jit(solution)/shard_map/ppermute | solution.py:434
  20.2 2.2 %collective-permute-done.7.theirs = f32[1,4,8,32]{3,2,1,0:T(8,128)S(1)} collective-permute-done((f32[1,4,8,32]{3,2,1,0:T(8,128)S(1)}, f32[1,4,8,32]{3,2,1,0:T(8,128)S(1)}, u32[]{:S(2)}, u32[]{:S(2)}) %collective-permute-start.7) | collective-permute-done | bytes 4128 | tf_op jit(solution)/shard_map/ppermute | solution.py:434
  22.5 0.6 %merge1.1 = f32[4,1,1,8,32]{4,3,2,1,0:T(8,128)} custom-call(s32[4,8,32]{2,1,0:T(8,128)S(1)} %get-tuple-element.43.order_map, f32[1,4,8,32]{3,2,1,0:T(8,128)S(1)} %get-tuple-element.67.kept, f32[1,4,8,32]{3,2,1,0:T(8,128)S(1)} %collective-permute-done.7.theirs), custom_call_target="tpu_custom_call" | custom-call | tf_op jit(solution)/shard_map/merge1/pallas_call | solution.py:437
  (1 shorter events, 0.0 us)
Async XLA Ops:
  1.3 8.0 %collective-permute-start = (bf16[16,16,256]{2,1,0:T(8,128)(2,1)S(1)}, bf16[16,16,256]{2,1,0:T(8,128)(2,1)S(1)}, u32[]{:S(2)}, u32[]{:S(2)}) collective-permute-start(bf16[16,16,256]{2,1,0:T(8,128)(2,1)S(1)} %get-tuple-element.45), channel_id=1, source_target_pairs={{0,1},{2,3},{4,5},{6,7},{8,9},{10,11},{12,13},{14,15},{16,17},{18,... | collective-permute-start | bytes 393224 | tf_op jit(solution)/shard_map/ppermute | solution.py:346
  4.3 9.6 %collective-permute-start.1 = (bf16[2,16,16,256]{3,2,1,0:T(8,128)(2,1)S(1)}, bf16[2,16,16,256]{3,2,1,0:T(8,128)(2,1)S(1)}, u32[]{:S(2)}, u32[]{:S(2)}) collective-permute-start(bf16[2,16,16,256]{3,2,1,0:T(8,128)(2,1)S(1)} %get-tuple-element.54.xs0), channel_id=1, source_target_pairs={{0,2},{1,3},{4,6},{5,7},{8,10},{9,11},{12,14},{13,15},{16,18},{17,... | collective-permute-start | bytes 786440 | tf_op jit(solution)/shard_map/ppermute | solution.py:346
  5.9 8.0 %collective-permute-start.2 = (bf16[2,16,16,256]{3,2,1,0:T(8,128)(2,1)S(1)}, bf16[2,16,16,256]{3,2,1,0:T(8,128)(2,1)S(1)}, u32[]{:S(2)}, u32[]{:S(2)}) collective-permute-start(bf16[2,16,16,256]{3,2,1,0:T(8,128)(2,1)S(1)} %get-tuple-element.55.xs1), channel_id=1, source_target_pairs={{2,4},{3,5},{10,12},{11,13},{18,20},{19,21},{26,28},{27,29},{0,8},... | collective-permute-start | bytes 786440 | tf_op jit(solution)/shard_map/ppermute | solution.py:346
  5.9 9.2 %collective-permute-start.3 = (bf16[16,16,256]{2,1,0:T(8,128)(2,1)S(1)}, bf16[16,16,256]{2,1,0:T(8,128)(2,1)S(1)}, u32[]{:S(2)}, u32[]{:S(2)}) collective-permute-start(bf16[16,16,256]{2,1,0:T(8,128)(2,1)S(1)} %get-tuple-element.60), channel_id=1, source_target_pairs={{0,1},{2,3},{4,5},{6,7},{8,9},{10,11},{12,13},{14,15},{16,17},{18,... | collective-permute-start | bytes 393224 | tf_op jit(solution)/shard_map/ppermute | solution.py:346
  6.7 8.5 %collective-permute-start.5 = (bf16[16,16,256]{2,1,0:T(8,128)(2,1)S(1)}, bf16[16,16,256]{2,1,0:T(8,128)(2,1)S(1)}, u32[]{:S(2)}, u32[]{:S(2)}) collective-permute-start(bf16[16,16,256]{2,1,0:T(8,128)(2,1)S(1)} %get-tuple-element.60), channel_id=1, source_target_pairs={{2,5},{3,4},{10,13},{11,12},{18,21},{19,20},{26,29},{27,28},{0,8},... | collective-permute-start | bytes 393224 | tf_op jit(solution)/shard_map/ppermute | solution.py:346
  9.3 6.9 %collective-permute-start.4 = (bf16[16,16,256]{2,1,0:T(8,128)(2,1)S(1)}, bf16[16,16,256]{2,1,0:T(8,128)(2,1)S(1)}, u32[]{:S(2)}, u32[]{:S(2)}) collective-permute-start(bf16[16,16,256]{2,1,0:T(8,128)(2,1)S(1)} %collective-permute-done.refs_2_), channel_id=1, source_target_pairs={{0,2},{1,3},{4,6},{5,7},{8,10},{9,11},{12,14},{13,15},{16,18},{17,... | collective-permute-start | bytes 393224 | tf_op jit(solution)/shard_map/ppermute | solution.py:346
  17.4 1.3 %collective-permute-start.6 = (f32[2,4,8,32]{3,2,1,0:T(8,128)S(1)}, f32[2,4,8,32]{3,2,1,0:T(8,128)S(1)}, u32[]{:S(2)}, u32[]{:S(2)}) collective-permute-start(f32[2,4,8,32]{3,2,1,0:T(8,128)S(1)} %get-tuple-element.66), channel_id=1, source_target_pairs={{0,8},{8,0},{16,24},{24,16},{1,9},{9,1},{17,25},{25,17},{2,10},{10... | collective-permute-start | bytes 24584 | tf_op jit(solution)/shard_map/ppermute | solution.py:434
  18.7 3.8 %collective-permute-start.7 = (f32[1,4,8,32]{3,2,1,0:T(8,128)S(1)}, f32[1,4,8,32]{3,2,1,0:T(8,128)S(1)}, u32[]{:S(2)}, u32[]{:S(2)}) collective-permute-start(f32[1,4,8,32]{3,2,1,0:T(8,128)S(1)} %get-tuple-element.68), channel_id=1, source_target_pairs={{0,16},{8,24},{16,0},{24,8},{1,17},{9,25},{17,1},{25,9},{2,18},{10... | collective-permute-start | bytes 12296 | tf_op jit(solution)/shard_map/ppermute | solution.py:434

commit v10 on v8

--- a/solution.py
+++ b/solution.py
@@ -70,29 +70,34 @@
 
 def first_kernel(rim, rounds, density, *refs):
     place = Place()
-    n_tables = (len(refs) - 4 - 2 * rounds) // 2
-    tables, refs = refs[:n_tables], refs[n_tables:]
+    tables, refs = refs[:7], refs[7:]
     held, xs, refs = refs[0], refs[1:3], refs[3:]
     strips, refs = refs[:2 * rounds], refs[2 * rounds:]
-    tables_out, sems = refs[:n_tables], refs[n_tables]
+    mx, my, table, signs, order_map, *local_tables, padded, sems = refs
     copies = []
+    for i, (src, dst) in enumerate(zip(tables, local_tables)):
+        copies.append(pltpu.make_async_copy(src, dst, sems.at[4 + i]))
+    parts = []
     for g in range(2):
         for h in range(2):
             rows = density.at[half_rows(place, rim, h), group_rows(place, rim, g), :]
-            copies.append(pltpu.make_async_copy(rows, held.at[g, h], sems.at[2 * g + h]))
-    for i, (src, dst) in enumerate(zip(tables, tables_out)):
-        copies.append(pltpu.make_async_copy(src, dst, sems.at[4 + i]))
+            parts.append(pltpu.make_async_copy(rows, held.at[g, h], sems.at[2 * g + h]))
+    for copy in copies + parts:
+        copy.start()
     for copy in copies:
-        copy.start()
+        copy.wait()
+    taps, *local_tables = local_tables
+    padded[...] = jnp.zeros(padded.shape, F32)
+    padded[0:2, 0:taps.shape[1]] = taps[...].astype(F32)
+    mx[...], my[...] = blur_matrices(rim, place, padded[...])
+    look_up(rim, place, *local_tables, table, signs, order_map)
     for g in range(2):
         for h in range(2):
-            copies[2 * g + h].wait()
+            parts[2 * g + h].wait()
             coarse = held[g, h].astype(BF16)
             xs[h][g] = coarse
             if g < rounds:
                 strips[2 * g + h][...] = coarse
-    for copy in copies[4:]:
-        copy.wait()
 
 
 def toeplitz(taps, rim):
@@ -127,16 +132,9 @@
     return parts
 
 
-def matrices_kernel(rim, taps, mx, my, padded):
-    padded[...] = jnp.zeros(padded.shape, F32)
-    padded[0:2, 0:taps.shape[1]] = taps[...].astype(F32)
-    mx[...], my[...] = blur_matrices(rim, Place(), padded[...])
-
-
-def prepare_kernel(
-    rim, centre, width, colour, opacity, brick_tf, view_order, table, signs, order_map
+def look_up(
+    rim, place, centre, width, colour, opacity, brick_tf, view_order, table, signs, order_map
 ):
-    place = Place()
     wide = width[...]
     rows = [centre[...], (-LOG2E) / (wide * wide), opacity[...] * (-LOG2E)]
     rows += [colour[c] * 0.5 for c in range(3)]
@@ -244,9 +242,13 @@
         shaded, out, partial = refs
     else:
         partial, = refs
-    for h, halo in enumerate((halo0, halo1)):
-        s, e = (blur_x(place, rim, mx, h, [xs0[g], xs1[g]], halo[g]) for g in range(2))
-        cells = jnp.concatenate([e, s], axis=0)
+    halos = (halo0, halo1)
+    across = [
+        [blur_x(place, rim, mx, h, [xs0[g], xs1[g]], halos[h][g]) for h in range(2)]
+        for g in range(2)
+    ]
+    for h in range(2):
+        cells = jnp.concatenate([across[1][h], across[0][h]], axis=0)
         partial[0, h] = dot(my[:, :2 * size], cells)
         other = dot(my[:, size:], cells)
         if not early:
@@ -260,13 +262,14 @@
     place = Place()
     size = rim * rim
     block = my[:, 2 * size:] if g == 0 else my[:, :size]
-    acc = None
-    for h, halo in enumerate((halo0, halo1)):
-        across = blur_x(place, rim, mx, h, [near0[...], near1[...]], halo[...])
-        across = jnp.where(place.has_y[g], across, jnp.zeros_like(across))
-        part = lit(place, rim, partial[g, h] + dot(block, across), shaded, h)
-        acc = part if h == 0 else [a + b for a, b in zip(acc, part)]
-    return acc
+    across = [
+        blur_x(place, rim, mx, h, [near0[...], near1[...]], halo[...])
+        for h, halo in enumerate((halo0, halo1))
+    ]
+    across = [jnp.where(place.has_y[g], cells, jnp.zeros_like(cells)) for cells in across]
+    occlusion = [partial[g, h] + dot(block, across[h]) for h in range(2)]
+    lights = [lit(place, rim, occlusion[h], shaded, h) for h in range(2)]
+    return [a + b for a, b in zip(*lights)]
 
 
 def late_kernel(rim, g, *refs):
@@ -351,34 +354,23 @@
     )
     piece = struct((rim, rim, rows_z), BF16)
     both = struct((2, rim, rim, rows_z), BF16)
+    bricks = rows_z // 128
     held, xs0, xs1, *refs = call(
         functools.partial(first_kernel, rim, rounds),
         "first",
         [HBM] * (1 + len(tables)),
         [struct((2, 2, rim, rim, rows_z), F32), both, both]
         + [piece] * (2 * rounds)
-        + [struct(t.shape, t.dtype) for t in tables],
-        [pltpu.SemaphoreType.DMA((4 + len(tables),))],
+        + [struct((size, 3 * size), BF16)] * 2
+        + [struct((4 * bricks, 6 * bumps, 128), F32), struct((2, 2, 8, 128), jnp.int32)]
+        + [struct((depth_count, block, rows_y), jnp.int32)],
+        [pltpu.VMEM(t.shape, t.dtype) for t in tables]
+        + [pltpu.VMEM((8, 128), F32), pltpu.SemaphoreType.DMA((4 + len(tables),))],
     )(in_hbm(density), *[in_hbm(t) for t in tables])
-    strips, tables = refs[:2 * rounds], refs[2 * rounds:]
+    strips, (mx, my, table, signs, order_map) = refs[:2 * rounds], refs[2 * rounds:]
     near = [[swap(strips[2 * r], None, r), None] for r in range(rounds)]
 
-    bricks = rows_z // 128
-    table, signs, order_map = call(
-        functools.partial(prepare_kernel, rim),
-        "prepare",
-        [VMEM] * (len(tables) - 1),
-        [struct((4 * bricks, 6 * bumps, 128), F32), struct((2, 2, 8, 128), jnp.int32)]
-        + [struct((depth_count, block, rows_y), jnp.int32)],
-    )(*tables[1:])
     halo_x = [swap(cells, h, None) for h, cells in enumerate((xs0, xs1))]
-    mx, my = call(
-        functools.partial(matrices_kernel, rim),
-        "matrices",
-        [VMEM],
-        [struct((size, 3 * size), BF16)] * 2,
-        [pltpu.VMEM((8, 128), F32)],
-    )(tables[0])
     shaded, total = [None, None], [None, None]
     for g in (1, 0):
         shaded[g], total[g] = call(
@@ -389,7 +381,7 @@
             [pltpu.VMEM((2, size, rows_z), F32), pltpu.VMEM((3, 2, size, rows_z), F32)],
             cost_estimate=pl.CostEstimate(
                 flops=density.size * (100000 if g == 0 else 1),
-                bytes_accessed=density.size * (10000 if g == 0 else 1),
+                bytes_accessed=density.size,
                 transcendentals=density.size * 3,
             ),
         )(held, table, signs)

time: 22.2 us -> 22.3 us (level)
  waiting for transfers between devices: 4.24 us -> 5.6 us
  Pallas kernels: 7.52 us -> 6.48 us
  starting transfers between devices: 9.96 us -> 9.69 us
    ppermute x6, waiting for transfers between devices: 0.8 us -> 2.16 us  [swap(): return lax.ppermute(piece, axes, swaps(counts, x_round, y_round))]
    pallas_call x2 -> x0, Pallas kernels: 0.88 us -> none  [the longest x1 0.62 us: per_device(): call(functools.partial(matrices_kernel, rim), 'matrices', [VMEM], [struct...]
    pallas_call x1, Pallas kernels: 1.31 us -> 1.6 us  [per_device(): call(functools.partial(first_kernel, rim, rounds), 'first', [HBM] * (1 +...]
    ppermute x6, starting transfers between devices: 8.33 us -> 8.06 us  [swap(): return lax.ppermute(piece, axes, swaps(counts, x_round, y_round))]
    pallas_call x1, Pallas kernels: 1.16 us -> 0.9 us  [per_device(): call(functools.partial(last_kernel, rim, depth_count), 'last', [VMEM] * 1...]
  transfers between devices with their start and end apart: 8 -> 8, of which waited for: 4 -> 5; matrix products, arithmetic and copies ran while one was open for 0% -> 0% of each run, Pallas kernels for 20% -> 15%
where the time goes in v10:
time: 22.3 us; the launch traced here: 21.8 us
  starting transfers between devices  9.69 us (43%)
  Pallas kernels  6.48 us (29%)
  waiting for transfers between devices  5.6 us (25%)
    ppermute x6, starting transfers between devices, swap(): return lax.ppermute(piece, axes, swaps(counts, x_round, y_round))  8.06 us
    ppermute x2, waiting for transfers between devices, per_device(): lax.ppermute(given, 'depth', [(i, i ^ 1 << level) for i in range(depth_co...  3.44 us
    pallas_call x2, Pallas kernels, per_device(): call(functools.partial(cells_kernel, rim, bumps, g), f'cells{g}', [VMEM]...  2.25 us
    ppermute x6, waiting for transfers between devices, swap(): return lax.ppermute(piece, axes, swaps(counts, x_round, y_round))  2.16 us
    ppermute x2, starting transfers between devices, per_device(): lax.ppermute(given, 'depth', [(i, i ^ 1 << level) for i in range(depth_co...  1.63 us
    pallas_call x1, Pallas kernels, per_device(): call(functools.partial(first_kernel, rim, rounds), 'first', [HBM] * (1 +...  1.6 us
    pallas_call x1, Pallas kernels, per_device(): call(functools.partial(own_kernel, rim, early), 'own', [VMEM] * (7 if ear...  1.11 us
    pallas_call x1, Pallas kernels, per_device(): call(functools.partial(last_kernel, rim, depth_count), 'last', [VMEM] * 1...  0.9 us
  transfers between devices with their start and end apart: 8, of which 5 were waited for; matrix products, arithmetic and copies ran while one was open for 0% of the time, Pallas kernels for 15%

profile of v10, /device:TPU:0, one launch (start us, length us, event | category | flops | bytes accessed | tf_op | source)
XLA Modules:
  0.0 21.8 jit_solution(15388743537119014373)
XLA Ops:
  0.0 1.6 %first.1 = (f32[2,2,16,16,256]{4,3,2,1,0:T(8,128)S(1)}, bf16[2,16,16,256]{3,2,1,0:T(8,128)(2,1)S(1)}, bf16[2,16,16,256]{3,2,1,0:T(8,128)(2,1)S(1)}, bf16[16,16,2...) custom-call(f32[32,32,256]{2,1,0:T(8,128)} %density.1, ...), custom_call_target="tpu_custom_call" | custom-call | tf_op jit(solution)/shard_map/first/pallas_call | solution.py:358
  1.6 3.0 %collective-permute-start = (bf16[16,16,256]{2,1,0:T(8,128)(2,1)S(1)}, bf16[16,16,256]{2,1,0:T(8,128)(2,1)S(1)}, u32[]{:S(2)}, u32[]{:S(2)}) collective-permute-start(bf16[16,16,256]{2,1,0:T(8,128)(2,1)S(1)} %get-tuple-element.31), channel_id=1, source_target_pairs={{0,1},{2,3},{4,5},{6,7},{8,9},{10,11},{12,13},{14,15},{16,17},{18,... | collective-permute-start | bytes 393224 | tf_op jit(solution)/shard_map/ppermute | solution.py:349
  4.6 1.6 %collective-permute-start.1 = (bf16[2,16,16,256]{3,2,1,0:T(8,128)(2,1)S(1)}, bf16[2,16,16,256]{3,2,1,0:T(8,128)(2,1)S(1)}, u32[]{:S(2)}, u32[]{:S(2)}) collective-permute-start(bf16[2,16,16,256]{3,2,1,0:T(8,128)(2,1)S(1)} %get-tuple-element.32.xs0), channel_id=1, source_target_pairs={{0,2},{1,3},{4,6},{5,7},{8,10},{9,11},{12,14},{13,15},{16,18},{17,... | collective-permute-start | bytes 786440 | tf_op jit(solution)/shard_map/ppermute | solution.py:349
  6.2 0.0 collective-permute-start.2
  6.2 0.5 %collective-permute-start.3 = (bf16[16,16,256]{2,1,0:T(8,128)(2,1)S(1)}, bf16[16,16,256]{2,1,0:T(8,128)(2,1)S(1)}, u32[]{:S(2)}, u32[]{:S(2)}) collective-permute-start(bf16[16,16,256]{2,1,0:T(8,128)(2,1)S(1)} %get-tuple-element.42), channel_id=1, source_target_pairs={{0,1},{2,3},{4,5},{6,7},{8,9},{10,11},{12,13},{14,15},{16,17},{18,... | collective-permute-start | bytes 393224 | tf_op jit(solution)/shard_map/ppermute | solution.py:349
  6.7 1.1 %cells1.1 = (f32[3,2,16,16,256]{4,3,2,1,0:T(8,128)S(1)}, f32[16,128]{1,0:T(8,128)S(1)}) custom-call(f32[2,2,16,16,256]{4,3,2,1,0:T(8,128)S(1)} %get-tuple-element.34.held, f32[8,24,128]{2,1,0:T(8,128)S(1)} %get-tuple-element.35.table, s32[2,2,8,128]{3,2,1,0:T(8,128)S(1)} %get-tuple-element.36.signs), custom_call_target="tpu_custom_call" | custom-call | flops 262144 | bytes 262144 | tf_op jit(solution)/shard_map/cells1/pallas_call | solution.py:376
  7.9 0.3 %collective-permute-done.refs_2_ = bf16[16,16,256]{2,1,0:T(8,128)(2,1)S(1)} collective-permute-done((bf16[16,16,256]{2,1,0:T(8,128)(2,1)S(1)}, bf16[16,16,256]{2,1,0:T(8,128)(2,1)S(1)}, u32[]{:S(2)}, u32[]{:S(2)}) %collective-permute-start) | collective-permute-done | bytes 131104 | tf_op jit(solution)/shard_map/ppermute | solution.py:349
  8.1 2.9 %collective-permute-start.4 = (bf16[16,16,256]{2,1,0:T(8,128)(2,1)S(1)}, bf16[16,16,256]{2,1,0:T(8,128)(2,1)S(1)}, u32[]{:S(2)}, u32[]{:S(2)}) collective-permute-start(bf16[16,16,256]{2,1,0:T(8,128)(2,1)S(1)} %collective-permute-done.refs_2_), channel_id=1, source_target_pairs={{0,2},{1,3},{4,6},{5,7},{8,10},{9,11},{12,14},{13,15},{16,18},{17,... | collective-permute-start | bytes 393224 | tf_op jit(solution)/shard_map/ppermute | solution.py:349
  11.1 0.0 collective-permute-start.5
  11.1 1.1 %cells0.1 = (f32[3,2,16,16,256]{4,3,2,1,0:T(8,128)S(1)}, f32[16,128]{1,0:T(8,128)S(1)}) custom-call(f32[2,2,16,16,256]{4,3,2,1,0:T(8,128)S(1)} %get-tuple-element.34.held, f32[8,24,128]{2,1,0:T(8,128)S(1)} %get-tuple-element.35.table, s32[2,2,8,128]{3,2,1,0:T(8,128)S(1)} %get-tuple-element.36.signs), custom_call_target="tpu_custom_call" | custom-call | flops 26214400000 | bytes 262144 | tf_op jit(solution)/shard_map/cells0/pallas_call | solution.py:376
  12.2 1.6 %collective-permute-done.1.halo0 = bf16[2,16,16,256]{3,2,1,0:T(8,128)(2,1)S(1)} collective-permute-done((bf16[2,16,16,256]{3,2,1,0:T(8,128)(2,1)S(1)}, bf16[2,16,16,256]{3,2,1,0:T(8,128)(2,1)S(1)}, u32[]{:S(2)}, u32[]{:S(2)}) %collective-permute-start.1) | collective-permute-done | bytes 262176 | tf_op jit(solution)/shard_map/ppermute | solution.py:349
  13.8 0.0 collective-permute-done.2.halo1
  13.8 1.1 %own.1 = (f32[3,16,128]{2,1,0:T(8,128)S(1)}, f32[1,2,256,256]{3,2,1,0:T(8,128)S(1)}) custom-call(bf16[256,768]{1,0:T(8,128)(2,1)S(1)} %get-tuple-element.29.mx.refs_0_, bf16[256,768]{1,0:T(8,128)(2,1)S(1)} %get-tuple-element.30.my.refs_1_, bf16[2,16,16,256]{3,2,1,0:T(8,128)(2,1)S(1)} %get-tuple-element.32.xs0, ...), custom_call_target="tpu_custom_call" | custom-call | tf_op jit(solution)/shard_map/own/pallas_call | solution.py:400
  14.9 0.0 collective-permute-done.3.refs_4_
  14.9 0.3 %collective-permute-done.4.refs_5_ = bf16[16,16,256]{2,1,0:T(8,128)(2,1)S(1)} collective-permute-done((bf16[16,16,256]{2,1,0:T(8,128)(2,1)S(1)}, bf16[16,16,256]{2,1,0:T(8,128)(2,1)S(1)}, u32[]{:S(2)}, u32[]{:S(2)}) %collective-permute-start.4) | collective-permute-done | bytes 131104 | tf_op jit(solution)/shard_map/ppermute | solution.py:349
  15.2 0.0 collective-permute-done.5.refs_6_
  15.2 0.9 %last.1 = (f32[2,4,8,32]{3,2,1,0:T(8,128)S(1)}, f32[2,4,8,32]{3,2,1,0:T(8,128)S(1)}) custom-call(bf16[256,768]{1,0:T(8,128)(2,1)S(1)} %get-tuple-element.29.mx.refs_0_, bf16[256,768]{1,0:T(8,128)(2,1)S(1)} %get-tuple-element.30.my.refs_1_, bf16[16,16,256]{2,1,0:T(8,128)(2,1)S(1)} %collective-permute-done.refs_2_, ...), custom_call_target="tpu_custom_call" | custom-call | tf_op jit(solution)/shard_map/last/pallas_call | solution.py:413
  16.1 0.1 collective-permute-start.6
  16.2 1.2 %collective-permute-done.6.theirs = f32[2,4,8,32]{3,2,1,0:T(8,128)S(1)} collective-permute-done((f32[2,4,8,32]{3,2,1,0:T(8,128)S(1)}, f32[2,4,8,32]{3,2,1,0:T(8,128)S(1)}, u32[]{:S(2)}, u32[]{:S(2)}) %collective-permute-start.6) | collective-permute-done | bytes 8224 | tf_op jit(solution)/shard_map/ppermute | solution.py:422
  17.4 1.6 %collective-permute-start.7 = (f32[1,4,8,32]{3,2,1,0:T(8,128)S(1)}, f32[1,4,8,32]{3,2,1,0:T(8,128)S(1)}, u32[]{:S(2)}, u32[]{:S(2)}) collective-permute-start(f32[1,4,8,32]{3,2,1,0:T(8,128)S(1)} %get-tuple-element.50), channel_id=1, source_target_pairs={{0,16},{8,24},{16,0},{24,8},{1,17},{9,25},{17,1},{25,9},{2,18},{10... | collective-permute-start | bytes 12296 | tf_op jit(solution)/shard_map/ppermute | solution.py:422
  19.0 2.2 %collective-permute-done.7.theirs = f32[1,4,8,32]{3,2,1,0:T(8,128)S(1)} collective-permute-done((f32[1,4,8,32]{3,2,1,0:T(8,128)S(1)}, f32[1,4,8,32]{3,2,1,0:T(8,128)S(1)}, u32[]{:S(2)}, u32[]{:S(2)}) %collective-permute-start.7) | collective-permute-done | bytes 4128 | tf_op jit(solution)/shard_map/ppermute | solution.py:422
  21.2 0.6 %merge1.1 = f32[4,1,1,8,32]{4,3,2,1,0:T(8,128)} custom-call(s32[4,8,32]{2,1,0:T(8,128)S(1)} %get-tuple-element.28.order_map, f32[1,4,8,32]{3,2,1,0:T(8,128)S(1)} %get-tuple-element.49.kept, f32[1,4,8,32]{3,2,1,0:T(8,128)S(1)} %collective-permute-done.7.theirs), custom_call_target="tpu_custom_call" | custom-call | tf_op jit(solution)/shard_map/merge1/pallas_call | solution.py:425
  (1 shorter events, 0.0 us)
Async XLA Ops:
  1.6 6.5 %collective-permute-start = (bf16[16,16,256]{2,1,0:T(8,128)(2,1)S(1)}, bf16[16,16,256]{2,1,0:T(8,128)(2,1)S(1)}, u32[]{:S(2)}, u32[]{:S(2)}) collective-permute-start(bf16[16,16,256]{2,1,0:T(8,128)(2,1)S(1)} %get-tuple-element.31), channel_id=1, source_target_pairs={{0,1},{2,3},{4,5},{6,7},{8,9},{10,11},{12,13},{14,15},{16,17},{18,... | collective-permute-start | bytes 393224 | tf_op jit(solution)/shard_map/ppermute | solution.py:349
  4.6 9.2 %collective-permute-start.1 = (bf16[2,16,16,256]{3,2,1,0:T(8,128)(2,1)S(1)}, bf16[2,16,16,256]{3,2,1,0:T(8,128)(2,1)S(1)}, u32[]{:S(2)}, u32[]{:S(2)}) collective-permute-start(bf16[2,16,16,256]{3,2,1,0:T(8,128)(2,1)S(1)} %get-tuple-element.32.xs0), channel_id=1, source_target_pairs={{0,2},{1,3},{4,6},{5,7},{8,10},{9,11},{12,14},{13,15},{16,18},{17,... | collective-permute-start | bytes 786440 | tf_op jit(solution)/shard_map/ppermute | solution.py:349
  6.2 7.6 %collective-permute-start.2 = (bf16[2,16,16,256]{3,2,1,0:T(8,128)(2,1)S(1)}, bf16[2,16,16,256]{3,2,1,0:T(8,128)(2,1)S(1)}, u32[]{:S(2)}, u32[]{:S(2)}) collective-permute-start(bf16[2,16,16,256]{3,2,1,0:T(8,128)(2,1)S(1)} %get-tuple-element.33.xs1), channel_id=1, source_target_pairs={{2,4},{3,5},{10,12},{11,13},{18,20},{19,21},{26,28},{27,29},{0,8},... | collective-permute-start | bytes 786440 | tf_op jit(solution)/shard_map/ppermute | solution.py:349
  6.2 8.7 %collective-permute-start.3 = (bf16[16,16,256]{2,1,0:T(8,128)(2,1)S(1)}, bf16[16,16,256]{2,1,0:T(8,128)(2,1)S(1)}, u32[]{:S(2)}, u32[]{:S(2)}) collective-permute-start(bf16[16,16,256]{2,1,0:T(8,128)(2,1)S(1)} %get-tuple-element.42), channel_id=1, source_target_pairs={{0,1},{2,3},{4,5},{6,7},{8,9},{10,11},{12,13},{14,15},{16,17},{18,... | collective-permute-start | bytes 393224 | tf_op jit(solution)/shard_map/ppermute | solution.py:349
  8.1 7.1 %collective-permute-start.4 = (bf16[16,16,256]{2,1,0:T(8,128)(2,1)S(1)}, bf16[16,16,256]{2,1,0:T(8,128)(2,1)S(1)}, u32[]{:S(2)}, u32[]{:S(2)}) collective-permute-start(bf16[16,16,256]{2,1,0:T(8,128)(2,1)S(1)} %collective-permute-done.refs_2_), channel_id=1, source_target_pairs={{0,2},{1,3},{4,6},{5,7},{8,10},{9,11},{12,14},{13,15},{16,18},{17,... | collective-permute-start | bytes 393224 | tf_op jit(solution)/shard_map/ppermute | solution.py:349
  11.1 4.1 %collective-permute-start.5 = (bf16[16,16,256]{2,1,0:T(8,128)(2,1)S(1)}, bf16[16,16,256]{2,1,0:T(8,128)(2,1)S(1)}, u32[]{:S(2)}, u32[]{:S(2)}) collective-permute-start(bf16[16,16,256]{2,1,0:T(8,128)(2,1)S(1)} %get-tuple-element.42), channel_id=1, source_target_pairs={{2,5},{3,4},{10,13},{11,12},{18,21},{19,20},{26,29},{27,28},{0,8},... | collective-permute-start | bytes 393224 | tf_op jit(solution)/shard_map/ppermute | solution.py:349
  16.1 1.3 %collective-permute-start.6 = (f32[2,4,8,32]{3,2,1,0:T(8,128)S(1)}, f32[2,4,8,32]{3,2,1,0:T(8,128)S(1)}, u32[]{:S(2)}, u32[]{:S(2)}) collective-permute-start(f32[2,4,8,32]{3,2,1,0:T(8,128)S(1)} %get-tuple-element.48), channel_id=1, source_target_pairs={{0,8},{8,0},{16,24},{24,16},{1,9},{9,1},{17,25},{25,17},{2,10},{10... | collective-permute-start | bytes 24584 | tf_op jit(solution)/shard_map/ppermute | solution.py:422
  17.4 3.8 %collective-permute-start.7 = (f32[1,4,8,32]{3,2,1,0:T(8,128)S(1)}, f32[1,4,8,32]{3,2,1,0:T(8,128)S(1)}, u32[]{:S(2)}, u32[]{:S(2)}) collective-permute-start(f32[1,4,8,32]{3,2,1,0:T(8,128)S(1)} %get-tuple-element.50), channel_id=1, source_target_pairs={{0,16},{8,24},{16,0},{24,8},{1,17},{9,25},{17,1},{25,9},{2,18},{10... | collective-permute-start | bytes 12296 | tf_op jit(solution)/shard_map/ppermute | solution.py:422

commit v11 on v8

--- a/solution.py
+++ b/solution.py
@@ -244,9 +244,13 @@
         shaded, out, partial = refs
     else:
         partial, = refs
-    for h, halo in enumerate((halo0, halo1)):
-        s, e = (blur_x(place, rim, mx, h, [xs0[g], xs1[g]], halo[g]) for g in range(2))
-        cells = jnp.concatenate([e, s], axis=0)
+    halos = (halo0, halo1)
+    across = [
+        [blur_x(place, rim, mx, h, [xs0[g], xs1[g]], halos[h][g]) for h in range(2)]
+        for g in range(2)
+    ]
+    for h in range(2):
+        cells = jnp.concatenate([across[1][h], across[0][h]], axis=0)
         partial[0, h] = dot(my[:, :2 * size], cells)
         other = dot(my[:, size:], cells)
         if not early:
@@ -260,13 +264,14 @@
     place = Place()
     size = rim * rim
     block = my[:, 2 * size:] if g == 0 else my[:, :size]
-    acc = None
-    for h, halo in enumerate((halo0, halo1)):
-        across = blur_x(place, rim, mx, h, [near0[...], near1[...]], halo[...])
-        across = jnp.where(place.has_y[g], across, jnp.zeros_like(across))
-        part = lit(place, rim, partial[g, h] + dot(block, across), shaded, h)
-        acc = part if h == 0 else [a + b for a, b in zip(acc, part)]
-    return acc
+    across = [
+        blur_x(place, rim, mx, h, [near0[...], near1[...]], halo[...])
+        for h, halo in enumerate((halo0, halo1))
+    ]
+    across = [jnp.where(place.has_y[g], cells, jnp.zeros_like(cells)) for cells in across]
+    occlusion = [partial[g, h] + dot(block, across[h]) for h in range(2)]
+    lights = [lit(place, rim, occlusion[h], shaded, h) for h in range(2)]
+    return [a + b for a, b in zip(*lights)]
 
 
 def late_kernel(rim, g, *refs):

time: 22.2 us -> 22 us (level)
  Pallas kernels: 7.52 us -> 7.12 us
    pallas_call x1, Pallas kernels: 1.16 us -> 0.9 us  [per_device(): call(functools.partial(last_kernel, rim, depth_count), 'last', [VMEM] * 1...]
where the time goes in v11:
time: 22 us; the launch traced here: 21.5 us
  starting transfers between devices  9.96 us (45%)
  Pallas kernels  7.12 us (32%)
  waiting for transfers between devices  4.38 us (20%)
    ppermute x6, starting transfers between devices, swap(): return lax.ppermute(piece, axes, swaps(counts, x_round, y_round))  8.33 us
    ppermute x2, waiting for transfers between devices, per_device(): lax.ppermute(given, 'depth', [(i, i ^ 1 << level) for i in range(depth_co...  3.44 us
    pallas_call x2, Pallas kernels, per_device(): call(functools.partial(cells_kernel, rim, bumps, g), f'cells{g}', [VMEM]...  2.31 us
    ppermute x2, starting transfers between devices, per_device(): lax.ppermute(given, 'depth', [(i, i ^ 1 << level) for i in range(depth_co...  1.63 us
    pallas_call x1, Pallas kernels, per_device(): call(functools.partial(first_kernel, rim, rounds), 'first', [HBM] * (1 +...  1.31 us
    pallas_call x1, Pallas kernels, per_device(): call(functools.partial(own_kernel, rim, early), 'own', [VMEM] * (7 if ear...  1.1 us
    ppermute x6, waiting for transfers between devices, swap(): return lax.ppermute(piece, axes, swaps(counts, x_round, y_round))  0.93 us
    pallas_call x1, Pallas kernels, per_device(): call(functools.partial(last_kernel, rim, depth_count), 'last', [VMEM] * 1...  0.9 us
  transfers between devices with their start and end apart: 8, of which 4 were waited for; matrix products, arithmetic and copies ran while one was open for 0% of the time, Pallas kernels for 20%

profile of v11, /device:TPU:0, one launch (start us, length us, event | category | flops | bytes accessed | tf_op | source)
XLA Modules:
  0.0 21.5 jit_solution(1342695699128451310)
XLA Ops:
  0.0 1.3 %first.1 = (f32[2,2,16,16,256]{4,3,2,1,0:T(8,128)S(1)}, bf16[2,16,16,256]{3,2,1,0:T(8,128)(2,1)S(1)}, bf16[2,16,16,256]{3,2,1,0:T(8,128)(2,1)S(1)}, bf16[16,16,2...) custom-call(f32[32,32,256]{2,1,0:T(8,128)} %density.1, ...), custom_call_target="tpu_custom_call" | custom-call | tf_op jit(solution)/shard_map/first/pallas_call | solution.py:359
  1.3 3.0 %collective-permute-start = (bf16[16,16,256]{2,1,0:T(8,128)(2,1)S(1)}, bf16[16,16,256]{2,1,0:T(8,128)(2,1)S(1)}, u32[]{:S(2)}, u32[]{:S(2)}) collective-permute-start(bf16[16,16,256]{2,1,0:T(8,128)(2,1)S(1)} %get-tuple-element.45), channel_id=1, source_target_pairs={{0,1},{2,3},{4,5},{6,7},{8,9},{10,11},{12,13},{14,15},{16,17},{18,... | collective-permute-start | bytes 393224 | tf_op jit(solution)/shard_map/ppermute | solution.py:351
  4.3 1.6 %collective-permute-start.1 = (bf16[2,16,16,256]{3,2,1,0:T(8,128)(2,1)S(1)}, bf16[2,16,16,256]{3,2,1,0:T(8,128)(2,1)S(1)}, u32[]{:S(2)}, u32[]{:S(2)}) collective-permute-start(bf16[2,16,16,256]{3,2,1,0:T(8,128)(2,1)S(1)} %get-tuple-element.46.xs0), channel_id=1, source_target_pairs={{0,2},{1,3},{4,6},{5,7},{8,10},{9,11},{12,14},{13,15},{16,18},{17,... | collective-permute-start | bytes 786440 | tf_op jit(solution)/shard_map/ppermute | solution.py:351
  5.9 0.0 collective-permute-start.2
  5.9 0.5 %collective-permute-start.3 = (bf16[16,16,256]{2,1,0:T(8,128)(2,1)S(1)}, bf16[16,16,256]{2,1,0:T(8,128)(2,1)S(1)}, u32[]{:S(2)}, u32[]{:S(2)}) collective-permute-start(bf16[16,16,256]{2,1,0:T(8,128)(2,1)S(1)} %get-tuple-element.56), channel_id=1, source_target_pairs={{0,1},{2,3},{4,5},{6,7},{8,9},{10,11},{12,13},{14,15},{16,17},{18,... | collective-permute-start | bytes 393224 | tf_op jit(solution)/shard_map/ppermute | solution.py:351
  6.4 0.3 %prepare.1 = (f32[8,24,128]{2,1,0:T(8,128)S(1)}, s32[2,2,8,128]{3,2,1,0:T(8,128)S(1)}, s32[4,8,32]{2,1,0:T(8,128)S(1)}) custom-call(f32[4,8]{1,0:T(4,128)S(1)} %get-tuple-element.35.centre, f32[4,8]{1,0:T(4,128)S(1)} %get-tuple-element.36.width, f32[3,4,8]{2,1,0:T(4,128)S(1)} %get-tuple-element.37.colour, f32[4,8]{1,0:T(4,128)S(1)} %get-tuple-element.38.opacity, ...), custom_call_target="tpu_custom_call" | custom-call | tf_op jit(solution)/shard_map/prepare/pallas_call | solution.py:372
  6.7 1.2 %cells1.1 = (f32[3,2,16,16,256]{4,3,2,1,0:T(8,128)S(1)}, f32[16,128]{1,0:T(8,128)S(1)}) custom-call(f32[2,2,16,16,256]{4,3,2,1,0:T(8,128)S(1)} %get-tuple-element.48.held, f32[8,24,128]{2,1,0:T(8,128)S(1)} %get-tuple-element.49.table, s32[2,2,8,128]{3,2,1,0:T(8,128)S(1)} %get-tuple-element.50.signs), custom_call_target="tpu_custom_call" | custom-call | flops 262144 | bytes 262144 | tf_op jit(solution)/shard_map/cells1/pallas_call | solution.py:389
  7.9 0.0 collective-permute-done.refs_2_
  7.9 3.2 %collective-permute-start.4 = (bf16[16,16,256]{2,1,0:T(8,128)(2,1)S(1)}, bf16[16,16,256]{2,1,0:T(8,128)(2,1)S(1)}, u32[]{:S(2)}, u32[]{:S(2)}) collective-permute-start(bf16[16,16,256]{2,1,0:T(8,128)(2,1)S(1)} %collective-permute-done.refs_2_), channel_id=1, source_target_pairs={{0,2},{1,3},{4,6},{5,7},{8,10},{9,11},{12,14},{13,15},{16,18},{17,... | collective-permute-start | bytes 393224 | tf_op jit(solution)/shard_map/ppermute | solution.py:351
  11.1 0.0 collective-permute-start.5
  11.1 1.2 %cells0.1 = (f32[3,2,16,16,256]{4,3,2,1,0:T(8,128)S(1)}, f32[16,128]{1,0:T(8,128)S(1)}) custom-call(f32[2,2,16,16,256]{4,3,2,1,0:T(8,128)S(1)} %get-tuple-element.48.held, f32[8,24,128]{2,1,0:T(8,128)S(1)} %get-tuple-element.49.table, s32[2,2,8,128]{3,2,1,0:T(8,128)S(1)} %get-tuple-element.50.signs), custom_call_target="tpu_custom_call" | custom-call | flops 26214400000 | bytes 2621440000 | tf_op jit(solution)/shard_map/cells0/pallas_call | solution.py:389
  12.3 0.6 %matrices.1 = (bf16[256,768]{1,0:T(8,128)(2,1)S(1)}, bf16[256,768]{1,0:T(8,128)(2,1)S(1)}) custom-call(bf16[2,33]{1,0:T(2,128)(2,1)S(1)} %get-tuple-element.42.taps), custom_call_target="tpu_custom_call" | custom-call | tf_op jit(solution)/shard_map/matrices/pallas_call | solution.py:380
  12.9 0.5 %collective-permute-done.1.halo0 = bf16[2,16,16,256]{3,2,1,0:T(8,128)(2,1)S(1)} collective-permute-done((bf16[2,16,16,256]{3,2,1,0:T(8,128)(2,1)S(1)}, bf16[2,16,16,256]{3,2,1,0:T(8,128)(2,1)S(1)}, u32[]{:S(2)}, u32[]{:S(2)}) %collective-permute-start.1) | collective-permute-done | bytes 262176 | tf_op jit(solution)/shard_map/ppermute | solution.py:351
  13.4 0.0 collective-permute-done.2.halo1
  13.4 1.1 %own.1 = (f32[3,16,128]{2,1,0:T(8,128)S(1)}, f32[1,2,256,256]{3,2,1,0:T(8,128)S(1)}) custom-call(bf16[256,768]{1,0:T(8,128)(2,1)S(1)} %get-tuple-element.43.mx.refs_0_, bf16[256,768]{1,0:T(8,128)(2,1)S(1)} %get-tuple-element.44.my.refs_1_, bf16[2,16,16,256]{3,2,1,0:T(8,128)(2,1)S(1)} %get-tuple-element.46.xs0, ...), custom_call_target="tpu_custom_call" | custom-call | tf_op jit(solution)/shard_map/own/pallas_call | solution.py:413
  14.5 0.0 collective-permute-done.3.refs_4_
  14.5 0.4 %collective-permute-done.4.refs_5_ = bf16[16,16,256]{2,1,0:T(8,128)(2,1)S(1)} collective-permute-done((bf16[16,16,256]{2,1,0:T(8,128)(2,1)S(1)}, bf16[16,16,256]{2,1,0:T(8,128)(2,1)S(1)}, u32[]{:S(2)}, u32[]{:S(2)}) %collective-permute-start.4) | collective-permute-done | bytes 131104 | tf_op jit(solution)/shard_map/ppermute | solution.py:351
  14.9 0.0 collective-permute-done.5.refs_6_
  14.9 0.9 %last.1 = (f32[2,4,8,32]{3,2,1,0:T(8,128)S(1)}, f32[2,4,8,32]{3,2,1,0:T(8,128)S(1)}) custom-call(bf16[256,768]{1,0:T(8,128)(2,1)S(1)} %get-tuple-element.43.mx.refs_0_, bf16[256,768]{1,0:T(8,128)(2,1)S(1)} %get-tuple-element.44.my.refs_1_, bf16[16,16,256]{2,1,0:T(8,128)(2,1)S(1)} %collective-permute-done.refs_2_, ...), custom_call_target="tpu_custom_call" | custom-call | tf_op jit(solution)/shard_map/last/pallas_call | solution.py:426
  15.8 0.1 collective-permute-start.6
  15.9 1.2 %collective-permute-done.6.theirs = f32[2,4,8,32]{3,2,1,0:T(8,128)S(1)} collective-permute-done((f32[2,4,8,32]{3,2,1,0:T(8,128)S(1)}, f32[2,4,8,32]{3,2,1,0:T(8,128)S(1)}, u32[]{:S(2)}, u32[]{:S(2)}) %collective-permute-start.6) | collective-permute-done | bytes 8224 | tf_op jit(solution)/shard_map/ppermute | solution.py:435
  17.1 1.6 %collective-permute-start.7 = (f32[1,4,8,32]{3,2,1,0:T(8,128)S(1)}, f32[1,4,8,32]{3,2,1,0:T(8,128)S(1)}, u32[]{:S(2)}, u32[]{:S(2)}) collective-permute-start(f32[1,4,8,32]{3,2,1,0:T(8,128)S(1)} %get-tuple-element.64), channel_id=1, source_target_pairs={{0,16},{8,24},{16,0},{24,8},{1,17},{9,25},{17,1},{25,9},{2,18},{10... | collective-permute-start | bytes 12296 | tf_op jit(solution)/shard_map/ppermute | solution.py:435
  18.7 2.2 %collective-permute-done.7.theirs = f32[1,4,8,32]{3,2,1,0:T(8,128)S(1)} collective-permute-done((f32[1,4,8,32]{3,2,1,0:T(8,128)S(1)}, f32[1,4,8,32]{3,2,1,0:T(8,128)S(1)}, u32[]{:S(2)}, u32[]{:S(2)}) %collective-permute-start.7) | collective-permute-done | bytes 4128 | tf_op jit(solution)/shard_map/ppermute | solution.py:435
  20.9 0.6 %merge1.1 = f32[4,1,1,8,32]{4,3,2,1,0:T(8,128)} custom-call(s32[4,8,32]{2,1,0:T(8,128)S(1)} %get-tuple-element.41.order_map, f32[1,4,8,32]{3,2,1,0:T(8,128)S(1)} %get-tuple-element.63.kept, f32[1,4,8,32]{3,2,1,0:T(8,128)S(1)} %collective-permute-done.7.theirs), custom_call_target="tpu_custom_call" | custom-call | tf_op jit(solution)/shard_map/merge1/pallas_call | solution.py:438
  (1 shorter events, 0.0 us)
Async XLA Ops:
  1.3 6.6 %collective-permute-start = (bf16[16,16,256]{2,1,0:T(8,128)(2,1)S(1)}, bf16[16,16,256]{2,1,0:T(8,128)(2,1)S(1)}, u32[]{:S(2)}, u32[]{:S(2)}) collective-permute-start(bf16[16,16,256]{2,1,0:T(8,128)(2,1)S(1)} %get-tuple-element.45), channel_id=1, source_target_pairs={{0,1},{2,3},{4,5},{6,7},{8,9},{10,11},{12,13},{14,15},{16,17},{18,... | collective-permute-start | bytes 393224 | tf_op jit(solution)/shard_map/ppermute | solution.py:351
  4.3 9.0 %collective-permute-start.1 = (bf16[2,16,16,256]{3,2,1,0:T(8,128)(2,1)S(1)}, bf16[2,16,16,256]{3,2,1,0:T(8,128)(2,1)S(1)}, u32[]{:S(2)}, u32[]{:S(2)}) collective-permute-start(bf16[2,16,16,256]{3,2,1,0:T(8,128)(2,1)S(1)} %get-tuple-element.46.xs0), channel_id=1, source_target_pairs={{0,2},{1,3},{4,6},{5,7},{8,10},{9,11},{12,14},{13,15},{16,18},{17,... | collective-permute-start | bytes 786440 | tf_op jit(solution)/shard_map/ppermute | solution.py:351
  5.9 7.5 %collective-permute-start.2 = (bf16[2,16,16,256]{3,2,1,0:T(8,128)(2,1)S(1)}, bf16[2,16,16,256]{3,2,1,0:T(8,128)(2,1)S(1)}, u32[]{:S(2)}, u32[]{:S(2)}) collective-permute-start(bf16[2,16,16,256]{3,2,1,0:T(8,128)(2,1)S(1)} %get-tuple-element.47.xs1), channel_id=1, source_target_pairs={{2,4},{3,5},{10,12},{11,13},{18,20},{19,21},{26,28},{27,29},{0,8},... | collective-permute-start | bytes 786440 | tf_op jit(solution)/shard_map/ppermute | solution.py:351
  5.9 8.6 %collective-permute-start.3 = (bf16[16,16,256]{2,1,0:T(8,128)(2,1)S(1)}, bf16[16,16,256]{2,1,0:T(8,128)(2,1)S(1)}, u32[]{:S(2)}, u32[]{:S(2)}) collective-permute-start(bf16[16,16,256]{2,1,0:T(8,128)(2,1)S(1)} %get-tuple-element.56), channel_id=1, source_target_pairs={{0,1},{2,3},{4,5},{6,7},{8,9},{10,11},{12,13},{14,15},{16,17},{18,... | collective-permute-start | bytes 393224 | tf_op jit(solution)/shard_map/ppermute | solution.py:351
  7.9 7.0 %collective-permute-start.4 = (bf16[16,16,256]{2,1,0:T(8,128)(2,1)S(1)}, bf16[16,16,256]{2,1,0:T(8,128)(2,1)S(1)}, u32[]{:S(2)}, u32[]{:S(2)}) collective-permute-start(bf16[16,16,256]{2,1,0:T(8,128)(2,1)S(1)} %collective-permute-done.refs_2_), channel_id=1, source_target_pairs={{0,2},{1,3},{4,6},{5,7},{8,10},{9,11},{12,14},{13,15},{16,18},{17,... | collective-permute-start | bytes 393224 | tf_op jit(solution)/shard_map/ppermute | solution.py:351
  11.1 3.8 %collective-permute-start.5 = (bf16[16,16,256]{2,1,0:T(8,128)(2,1)S(1)}, bf16[16,16,256]{2,1,0:T(8,128)(2,1)S(1)}, u32[]{:S(2)}, u32[]{:S(2)}) collective-permute-start(bf16[16,16,256]{2,1,0:T(8,128)(2,1)S(1)} %get-tuple-element.56), channel_id=1, source_target_pairs={{2,5},{3,4},{10,13},{11,12},{18,21},{19,20},{26,29},{27,28},{0,8},... | collective-permute-start | bytes 393224 | tf_op jit(solution)/shard_map/ppermute | solution.py:351
  15.8 1.3 %collective-permute-start.6 = (f32[2,4,8,32]{3,2,1,0:T(8,128)S(1)}, f32[2,4,8,32]{3,2,1,0:T(8,128)S(1)}, u32[]{:S(2)}, u32[]{:S(2)}) collective-permute-start(f32[2,4,8,32]{3,2,1,0:T(8,128)S(1)} %get-tuple-element.62), channel_id=1, source_target_pairs={{0,8},{8,0},{16,24},{24,16},{1,9},{9,1},{17,25},{25,17},{2,10},{10... | collective-permute-start | bytes 24584 | tf_op jit(solution)/shard_map/ppermute | solution.py:435
  17.1 3.8 %collective-permute-start.7 = (f32[1,4,8,32]{3,2,1,0:T(8,128)S(1)}, f32[1,4,8,32]{3,2,1,0:T(8,128)S(1)}, u32[]{:S(2)}, u32[]{:S(2)}) collective-permute-start(f32[1,4,8,32]{3,2,1,0:T(8,128)S(1)} %get-tuple-element.64), channel_id=1, source_target_pairs={{0,16},{8,24},{16,0},{24,8},{1,17},{9,25},{17,1},{25,9},{2,18},{10... | collective-permute-start | bytes 12296 | tf_op jit(solution)/shard_map/ppermute | solution.py:435

commit v12 on v8

--- a/solution.py
+++ b/solution.py
@@ -23,25 +23,20 @@
     return [(i, i + 1) for i in range(shift, count - 1, 2)]
 
 
-def swaps(counts, x_round, y_round):
+def swaps(counts, axis, shift):
     depth_count, count_x, count_y = counts
     index = lambda d, x, y: (d * count_x + x) * count_y + y
-    stay = lambda count: [(i, i) for i in range(count)]
-    pairs_x = stay(count_x) if x_round is None else line_pairs(count_x, x_round)
-    pairs_y = stay(count_y) if y_round is None else line_pairs(count_y, y_round)
-    ends = {((a, c), (b, e)) for a, b in pairs_x for c, e in pairs_y}
-    if x_round is not None and y_round is not None:
-        ends |= {((a, e), (b, c)) for a, b in pairs_x for c, e in pairs_y}
-    used = {end for pair in ends for end in pair}
     pairs = []
-    for d in range(depth_count):
-        pairs += [(index(d, *a), index(d, *b)) for a, b in sorted(ends)]
     for x in range(count_x):
         for y in range(count_y):
-            if (x, y) not in used:
+            ends = [p for p in line_pairs(counts[axis], shift) if (x, y)[axis - 1] in p]
+            if not ends:
                 pairs += [
                     (index(d, x, y), index(d + 1, x, y)) for d in range(0, depth_count - 1, 2)
                 ]
+            elif (x, y)[axis - 1] == ends[0][0]:
+                other = (ends[0][1], y) if axis == 1 else (x, ends[0][1])
+                pairs += [(index(d, x, y), index(d, *other)) for d in range(depth_count)]
     return pairs + [(b, a) for a, b in pairs]
 
 
@@ -68,13 +63,11 @@
     return pl.ds(place.half[h] * rim, rim)
 
 
-def first_kernel(rim, rounds, density, *refs):
-    place = Place()
-    n_tables = (len(refs) - 4 - 2 * rounds) // 2
-    tables, refs = refs[:n_tables], refs[n_tables:]
-    held, xs, refs = refs[0], refs[1:3], refs[3:]
-    strips, refs = refs[:2 * rounds], refs[2 * rounds:]
-    tables_out, sems = refs[:n_tables], refs[n_tables]
+def first_kernel(rim, density, *refs):
+    place = Place()
+    n_tables = (len(refs) - 6) // 2
+    tables, held, coarse = refs[:n_tables], refs[n_tables], refs[n_tables + 1:n_tables + 5]
+    tables_out, sems = refs[n_tables + 5:-1], refs[-1]
     copies = []
     for g in range(2):
         for h in range(2):
@@ -87,10 +80,7 @@
     for g in range(2):
         for h in range(2):
             copies[2 * g + h].wait()
-            coarse = held[g, h].astype(BF16)
-            xs[h][g] = coarse
-            if g < rounds:
-                strips[2 * g + h][...] = coarse
+            coarse[2 * g + h][...] = held[g, h].astype(BF16)
     for copy in copies[4:]:
         copy.wait()
 
@@ -237,36 +227,45 @@
     return [rays(shade * shaded[c, h], place.half[h] * rim, lane) for c in range(3)]
 
 
-def own_kernel(rim, early, mx, my, xs0, xs1, halo0, halo1, *refs):
+def strip_kernel(rim, h, mx, near0, near1, halo, out):
+    across = blur_x(Place(), rim, mx, h, [near0[...], near1[...]], halo[...])
+    out[...] = across.reshape(out.shape)
+
+
+def own_kernel(rim, early, mx, my, near0, near1, halo0, halo1, strip0, strip1, *refs):
     place = Place()
     size = rim * rim
+    across = [
+        blur_x(place, rim, mx, h, [near0[...], near1[...]], halo[...])
+        for h, halo in enumerate((halo0, halo1))
+    ]
     if early:
         shaded, out, partial = refs
     else:
-        partial, = refs
-    for h, halo in enumerate((halo0, halo1)):
-        s, e = (blur_x(place, rim, mx, h, [xs0[g], xs1[g]], halo[g]) for g in range(2))
-        cells = jnp.concatenate([e, s], axis=0)
+        partial, *others = refs
+    for h, strip in enumerate((strip0, strip1)):
+        cells = jnp.concatenate([across[h], strip[...].reshape(size, strip.shape[2])], axis=0)
         partial[0, h] = dot(my[:, :2 * size], cells)
         other = dot(my[:, size:], cells)
         if not early:
+            others[h][...] = across[h].reshape(strip.shape)
             partial[1, h] = other
             continue
         for c, part in enumerate(lit(place, rim, other, shaded, h)):
             out[c] = part if h == 0 else out[c] + part
 
 
-def late(rim, g, mx, my, near0, partial, near1, halo0, halo1, shaded):
+def late(rim, g, my, partial, halo0, halo1, shaded):
     place = Place()
     size = rim * rim
     block = my[:, 2 * size:] if g == 0 else my[:, :size]
-    acc = None
+    occlusion = []
     for h, halo in enumerate((halo0, halo1)):
-        across = blur_x(place, rim, mx, h, [near0[...], near1[...]], halo[...])
-        across = jnp.where(place.has_y[g], across, jnp.zeros_like(across))
-        part = lit(place, rim, partial[g, h] + dot(block, across), shaded, h)
-        acc = part if h == 0 else [a + b for a, b in zip(acc, part)]
-    return acc
+        cells = halo[...].reshape(size, halo.shape[2])
+        cells = jnp.where(place.has_y[g], cells, jnp.zeros_like(cells))
+        occlusion.append(partial[g, h] + dot(block, cells))
+    lights = [lit(place, rim, occlusion[h], shaded, h) for h in range(2)]
+    return [a + b for a, b in zip(*lights)]
 
 
 def late_kernel(rim, g, *refs):
@@ -276,7 +275,7 @@
 
 
 def last_kernel(rim, depth_count, *refs):
-    refs, (light_e, total0, total1, kept, given, img) = refs[:8], refs[8:]
+    refs, (light_e, total0, total1, kept, given, img) = refs[:5], refs[5:]
     place = Place()
     rows = 2 * rim
     at_s, at_e = group_rows(place, rim, 0), group_rows(place, rim, 1)
@@ -342,27 +341,24 @@
     block = rows_x // depth_count
     rounds = sum(1 for shift in range(2) if line_pairs(count_y, shift))
 
-    def swap(piece, x_round, y_round):
-        return lax.ppermute(piece, axes, swaps(counts, x_round, y_round))
+    def swap(piece, axis, shift):
+        return lax.ppermute(piece, axes, swaps(counts, axis, shift))
 
     in_hbm = lambda array: pltpu.with_memory_space_constraint(array, pltpu.HBM)
     tables = (
         kernel_taps, tf_centre.T, tf_width.T, tf_color.T, tf_opacity.T, brick_tf, view_order
     )
     piece = struct((rim, rim, rows_z), BF16)
-    both = struct((2, rim, rim, rows_z), BF16)
-    held, xs0, xs1, *refs = call(
-        functools.partial(first_kernel, rim, rounds),
+    held, *refs = call(
+        functools.partial(first_kernel, rim),
         "first",
         [HBM] * (1 + len(tables)),
-        [struct((2, 2, rim, rim, rows_z), F32), both, both]
-        + [piece] * (2 * rounds)
+        [struct((2, 2, rim, rim, rows_z), F32)]
+        + [piece] * 4
         + [struct(t.shape, t.dtype) for t in tables],
         [pltpu.SemaphoreType.DMA((4 + len(tables),))],
     )(in_hbm(density), *[in_hbm(t) for t in tables])
-    strips, tables = refs[:2 * rounds], refs[2 * rounds:]
-    near = [[swap(strips[2 * r], None, r), None] for r in range(rounds)]
-
+    coarse, tables = [refs[0:2], refs[2:4]], refs[4:]
     bricks = rows_z // 128
     table, signs, order_map = call(
         functools.partial(prepare_kernel, rim),
@@ -371,7 +367,7 @@
         [struct((4 * bricks, 6 * bumps, 128), F32), struct((2, 2, 8, 128), jnp.int32)]
         + [struct((depth_count, block, rows_y), jnp.int32)],
     )(*tables[1:])
-    halo_x = [swap(cells, h, None) for h, cells in enumerate((xs0, xs1))]
+    halo_x = [[swap(coarse[0][h], 1, h) for h in range(2)], None]
     mx, my = call(
         functools.partial(matrices_kernel, rim),
         "matrices",
@@ -389,42 +385,46 @@
             [pltpu.VMEM((2, size, rows_z), F32), pltpu.VMEM((3, 2, size, rows_z), F32)],
             cost_estimate=pl.CostEstimate(
                 flops=density.size * (100000 if g == 0 else 1),
-                bytes_accessed=density.size * (10000 if g == 0 else 1),
+                bytes_accessed=density.size,
                 transcendentals=density.size * 3,
             ),
         )(held, table, signs)
 
-    corner = [[None, None] for r in range(rounds)]
-    for r in range(rounds):
-        near[r][1] = swap(strips[2 * r + 1], None, r)
-        strip, arrived, total[1] = lax.optimization_barrier(
-            (strips[2 * r + 1], near[r][0], total[1])
+    strips, halo_y = [], []
+    for h in range(2):
+        if h == 0:
+            mx, total[1] = lax.optimization_barrier((mx, total[1]))
+        strip = call(functools.partial(strip_kernel, rim, h), f"strip{h}", [VMEM] * 4, piece)(
+            mx, *coarse[0], halo_x[0][h]
         )
-        corner[r] = [swap(arrived, 0, None), swap(strip, 1, r)]
-
+        strips.append(strip)
+        halo_y.append(swap(strip, 2, 0))
+        if h == 0:
+            pieces = lax.optimization_barrier((*coarse[1], strip))
+            halo_x[1] = [swap(pieces[n], 1, n) for n in range(2)]
     early = rounds < 2
     colours = struct((3, rim, 128), F32)
     unlit = struct((2 - early, 2, size, rows_z), F32)
     results = call(
         functools.partial(own_kernel, rim, early),
         "own",
-        [VMEM] * (7 if early else 6),
-        [colours, unlit] if early else [unlit],
-    )(mx, my, xs0, xs1, *halo_x, *([shaded[1]] if early else []))
-    partial = results[-1]
+        [VMEM] * (9 if early else 8),
+        [colours, unlit] if early else [unlit, piece, piece],
+    )(mx, my, *coarse[1], *halo_x[1], *strips, *([shaded[1]] if early else []))
     if early:
-        light = results[0]
+        light, partial = results
     else:
-        light = call(functools.partial(late_kernel, rim, 1), "late", [VMEM] * 8, colours)(
-            mx, my, near[1][0], partial, near[1][1], *corner[1], shaded[1]
+        partial, *others = results
+        light = call(functools.partial(late_kernel, rim, 1), "late", [VMEM] * 5, colours)(
+            my, partial, *[swap(strip, 2, 1) for strip in others], shaded[1]
         )
     kept, given = call(
         functools.partial(last_kernel, rim, depth_count),
         "last",
-        [VMEM] * 11,
+        [VMEM] * 8,
         [struct((depth_count // 2, 4, block, rows_y), F32)] * 2,
         [pltpu.VMEM((8, rows_y, 128), F32)],
-    )(mx, my, near[0][0], partial, near[0][1], *corner[0], shaded[0], light, *total)
+    )(my, partial, *halo_y, shaded[0], light, *total)
     level = 0
     while True:
         theirs = lax.ppermute(given, "depth", [(i, i ^ 1 << level) for i in range(depth_count)])

time: 22.2 us -> 24.2 us (1.090); the launches traced: 21.8 us -> 24.1 us
  waiting for transfers between devices: 4.24 us -> 8.21 us
  starting transfers between devices: 9.96 us -> 8.62 us
  Pallas kernels: 7.52 us -> 7.14 us
    ppermute x6, waiting for transfers between devices: 0.8 us -> 4.77 us  [swap(): return lax.ppermute(piece, axes, swaps(counts, axis, shift))]
    ppermute x6, starting transfers between devices: 8.33 us -> 6.99 us  [swap(): return lax.ppermute(piece, axes, swaps(counts, axis, shift))]
    pallas_call x3 -> x5, Pallas kernels: 3.71 us -> 3.33 us  [the longest x1 1.31 us: per_device(): call(functools.partial(first_kernel, rim), 'first', [HBM] * (1 + len(tabl...]
  transfers between devices with their start and end apart: 8 -> 8, of which waited for: 4 -> 5; matrix products, arithmetic and copies ran while one was open for 0% -> 0% of each run, Pallas kernels for 20% -> 19%
where the time goes in v12:
time: 24.2 us; the launch traced here: 24.1 us
  starting transfers between devices  8.62 us (36%)
  waiting for transfers between devices  8.21 us (34%)
  Pallas kernels  7.14 us (30%)
    ppermute x6, starting transfers between devices, swap(): return lax.ppermute(piece, axes, swaps(counts, axis, shift))  6.99 us
    ppermute x6, waiting for transfers between devices, swap(): return lax.ppermute(piece, axes, swaps(counts, axis, shift))  4.77 us
    ppermute x2, waiting for transfers between devices, per_device(): lax.ppermute(given, 'depth', [(i, i ^ 1 << level) for i in range(depth_co...  3.44 us
    pallas_call x2, Pallas kernels, per_device(): call(functools.partial(cells_kernel, rim, bumps, g), f'cells{g}', [VMEM]...  2.31 us
    ppermute x2, starting transfers between devices, per_device(): lax.ppermute(given, 'depth', [(i, i ^ 1 << level) for i in range(depth_co...  1.63 us
    pallas_call x1, Pallas kernels, per_device(): call(functools.partial(first_kernel, rim), 'first', [HBM] * (1 + len(tabl...  1.31 us
    pallas_call x1, Pallas kernels, per_device(): call(functools.partial(own_kernel, rim, early), 'own', [VMEM] * (9 if ear...  0.9 us
    pallas_call x2, Pallas kernels, per_device(): call(functools.partial(merge_kernel, level), f'merge{level}', [VMEM] * 3,...  0.63 us
  transfers between devices with their start and end apart: 8, of which 5 were waited for; matrix products, arithmetic and copies ran while one was open for 0% of the time, Pallas kernels for 19%

profile of v12, /device:TPU:0, one launch (start us, length us, event | category | flops | bytes accessed | tf_op | source)
XLA Modules:
  0.0 24.1 jit_solution(16253705370496927457)
XLA Ops:
  0.0 1.3 %first.1 = (f32[2,2,16,16,256]{4,3,2,1,0:T(8,128)S(1)}, bf16[16,16,256]{2,1,0:T(8,128)(2,1)S(1)}, bf16[16,16,256]{2,1,0:T(8,128)(2,1)S(1)}, bf16[16,16,256]{2,1,...) custom-call(f32[32,32,256]{2,1,0:T(8,128)} %density.1, ...), custom_call_target="tpu_custom_call" | custom-call | tf_op jit(solution)/shard_map/first/pallas_call | solution.py:352
  1.3 3.1 %collective-permute-start = (bf16[16,16,256]{2,1,0:T(8,128)(2,1)S(1)}, bf16[16,16,256]{2,1,0:T(8,128)(2,1)S(1)}, u32[]{:S(2)}, u32[]{:S(2)}) collective-permute-start(bf16[16,16,256]{2,1,0:T(8,128)(2,1)S(1)} %get-tuple-element.53.near0), channel_id=1, source_target_pairs={{0,2},{8,10},{16,18},{24,26},{1,3},{9,11},{17,19},{25,27},{4,6},{1... | collective-permute-start | bytes 393224 | tf_op jit(solution)/shard_map/ppermute | solution.py:345
  4.4 0.0 collective-permute-start.3
  4.4 0.3 %prepare.1 = (f32[8,24,128]{2,1,0:T(8,128)S(1)}, s32[2,2,8,128]{3,2,1,0:T(8,128)S(1)}, s32[4,8,32]{2,1,0:T(8,128)S(1)}) custom-call(f32[4,8]{1,0:T(4,128)S(1)} %get-tuple-element.36.centre, f32[4,8]{1,0:T(4,128)S(1)} %get-tuple-element.37.width, f32[3,4,8]{2,1,0:T(4,128)S(1)} %get-tuple-element.38.colour, f32[4,8]{1,0:T(4,128)S(1)} %get-tuple-element.39.opacity, ...), custom_call_target="tpu_custom_call" | custom-call | tf_op jit(solution)/shard_map/prepare/pallas_call | solution.py:363
  4.7 1.2 %cells1.1 = (f32[3,2,16,16,256]{4,3,2,1,0:T(8,128)S(1)}, f32[16,128]{1,0:T(8,128)S(1)}) custom-call(f32[2,2,16,16,256]{4,3,2,1,0:T(8,128)S(1)} %get-tuple-element.46.held, f32[8,24,128]{2,1,0:T(8,128)S(1)} %get-tuple-element.47.table, s32[2,2,8,128]{3,2,1,0:T(8,128)S(1)} %get-tuple-element.48.signs), custom_call_target="tpu_custom_call" | custom-call | flops 262144 | bytes 262144 | tf_op jit(solution)/shard_map/cells1/pallas_call | solution.py:380
  5.8 0.6 %matrices.1 = (bf16[256,768]{1,0:T(8,128)(2,1)S(1)}, bf16[256,768]{1,0:T(8,128)(2,1)S(1)}) custom-call(bf16[2,33]{1,0:T(2,128)(2,1)S(1)} %get-tuple-element.43.taps), custom_call_target="tpu_custom_call" | custom-call | tf_op jit(solution)/shard_map/matrices/pallas_call | solution.py:371
  6.5 1.4 %collective-permute-done.halo = bf16[16,16,256]{2,1,0:T(8,128)(2,1)S(1)} collective-permute-done((bf16[16,16,256]{2,1,0:T(8,128)(2,1)S(1)}, bf16[16,16,256]{2,1,0:T(8,128)(2,1)S(1)}, u32[]{:S(2)}, u32[]{:S(2)}) %collective-permute-start) | collective-permute-done | bytes 131104 | tf_op jit(solution)/shard_map/ppermute | solution.py:345
  7.9 0.3 %strip0.1 = bf16[16,16,256]{2,1,0:T(8,128)(2,1)S(1)} custom-call(bf16[256,768]{1,0:T(8,128)(2,1)S(1)} %get-tuple-element.50.mx, bf16[16,16,256]{2,1,0:T(8,128)(2,1)S(1)} %get-tuple-element.53.near0, bf16[16,16,256]{2,1,0:T(8,128)(2,1)S(1)} %get-tuple-element.54.near1, bf16[16,16,256]{2,1,0:T(8,128)(2,1)S(1)} %collective-permute-done.halo), custom_call_target="tpu_custom_call" | custom-call | tf_op jit(solution)/shard_map/strip0/pallas_call | solution.py:397
  8.2 1.7 %collective-permute-start.4 = (bf16[16,16,256]{2,1,0:T(8,128)(2,1)S(1)}, bf16[16,16,256]{2,1,0:T(8,128)(2,1)S(1)}, u32[]{:S(2)}, u32[]{:S(2)}) collective-permute-start(bf16[16,16,256]{2,1,0:T(8,128)(2,1)S(1)} %strip0.1), channel_id=1, source_target_pairs={{0,1},{8,9},{16,17},{24,25},{2,3},{10,11},{18,19},{26,27},{4,5},{1... | collective-permute-start | bytes 393224 | tf_op jit(solution)/shard_map/ppermute | solution.py:345
  9.9 1.6 %collective-permute-start.1 = (bf16[16,16,256]{2,1,0:T(8,128)(2,1)S(1)}, bf16[16,16,256]{2,1,0:T(8,128)(2,1)S(1)}, u32[]{:S(2)}, u32[]{:S(2)}) collective-permute-start(bf16[16,16,256]{2,1,0:T(8,128)(2,1)S(1)} %get-tuple-element.55.near0), channel_id=1, source_target_pairs={{0,2},{8,10},{16,18},{24,26},{1,3},{9,11},{17,19},{25,27},{4,6},{1... | collective-permute-start | bytes 393224 | tf_op jit(solution)/shard_map/ppermute | solution.py:345
  11.5 0.3 %strip1.1 = bf16[16,16,256]{2,1,0:T(8,128)(2,1)S(1)} custom-call(bf16[256,768]{1,0:T(8,128)(2,1)S(1)} %get-tuple-element.50.mx, bf16[16,16,256]{2,1,0:T(8,128)(2,1)S(1)} %get-tuple-element.53.near0, bf16[16,16,256]{2,1,0:T(8,128)(2,1)S(1)} %get-tuple-element.54.near1, bf16[16,16,256]{2,1,0:T(8,128)(2,1)S(1)} %collective-permute-done.3.halo), custom_call_target="tpu_custom_call" | custom-call | tf_op jit(solution)/shard_map/strip1/pallas_call | solution.py:397
  11.8 0.6 %collective-permute-start.5 = (bf16[16,16,256]{2,1,0:T(8,128)(2,1)S(1)}, bf16[16,16,256]{2,1,0:T(8,128)(2,1)S(1)}, u32[]{:S(2)}, u32[]{:S(2)}) collective-permute-start(bf16[16,16,256]{2,1,0:T(8,128)(2,1)S(1)} %strip1.1), channel_id=1, source_target_pairs={{0,1},{8,9},{16,17},{24,25},{2,3},{10,11},{18,19},{26,27},{4,5},{1... | collective-permute-start | bytes 393224 | tf_op jit(solution)/shard_map/ppermute | solution.py:345
  12.4 1.2 %cells0.1 = (f32[3,2,16,16,256]{4,3,2,1,0:T(8,128)S(1)}, f32[16,128]{1,0:T(8,128)S(1)}) custom-call(f32[2,2,16,16,256]{4,3,2,1,0:T(8,128)S(1)} %get-tuple-element.46.held, f32[8,24,128]{2,1,0:T(8,128)S(1)} %get-tuple-element.47.table, s32[2,2,8,128]{3,2,1,0:T(8,128)S(1)} %get-tuple-element.48.signs), custom_call_target="tpu_custom_call" | custom-call | flops 26214400000 | bytes 262144 | tf_op jit(solution)/shard_map/cells0/pallas_call | solution.py:380
  13.5 1.4 %collective-permute-done.1.halo0 = bf16[16,16,256]{2,1,0:T(8,128)(2,1)S(1)} collective-permute-done((bf16[16,16,256]{2,1,0:T(8,128)(2,1)S(1)}, bf16[16,16,256]{2,1,0:T(8,128)(2,1)S(1)}, u32[]{:S(2)}, u32[]{:S(2)}) %collective-permute-start.1) | collective-permute-done | bytes 131104 | tf_op jit(solution)/shard_map/ppermute | solution.py:345
  14.9 0.0 collective-permute-done.2.halo1
  14.9 0.9 %own.1 = (f32[3,16,128]{2,1,0:T(8,128)S(1)}, f32[1,2,256,256]{3,2,1,0:T(8,128)S(1)}) custom-call(bf16[256,768]{1,0:T(8,128)(2,1)S(1)} %get-tuple-element.50.mx, bf16[256,768]{1,0:T(8,128)(2,1)S(1)} %get-tuple-element.44.my.refs_0_, bf16[16,16,256]{2,1,0:T(8,128)(2,1)S(1)} %get-tuple-element.55.near0, bf16[16,16,256]{2,1,0:T(8,128)(2,1)S(1)} %get-tuple-element.56.near1, ...), custom_call_target="tpu_custom_call" | custom-call | tf_op jit(solution)/shard_map/own/pallas_call | solution.py:408
  15.8 0.0 collective-permute-done.4.refs_2_
  15.8 2.0 %collective-permute-done.5.refs_3_ = bf16[16,16,256]{2,1,0:T(8,128)(2,1)S(1)} collective-permute-done((bf16[16,16,256]{2,1,0:T(8,128)(2,1)S(1)}, bf16[16,16,256]{2,1,0:T(8,128)(2,1)S(1)}, u32[]{:S(2)}, u32[]{:S(2)}) %collective-permute-start.5) | collective-permute-done | bytes 131104 | tf_op jit(solution)/shard_map/ppermute | solution.py:345
  17.8 0.6 %last.1 = (f32[2,4,8,32]{3,2,1,0:T(8,128)S(1)}, f32[2,4,8,32]{3,2,1,0:T(8,128)S(1)}) custom-call(bf16[256,768]{1,0:T(8,128)(2,1)S(1)} %get-tuple-element.44.my.refs_0_, f32[1,2,256,256]{3,2,1,0:T(8,128)S(1)} %get-tuple-element.58.refs_1_, bf16[16,16,256]{2,1,0:T(8,128)(2,1)S(1)} %collective-permute-done.4.refs_2_, ...), custom_call_target="tpu_custom_call" | custom-call | tf_op jit(solution)/shard_map/last/pallas_call | solution.py:421
  18.3 0.1 collective-permute-start.6
  18.4 1.2 %collective-permute-done.6.theirs = f32[2,4,8,32]{3,2,1,0:T(8,128)S(1)} collective-permute-done((f32[2,4,8,32]{3,2,1,0:T(8,128)S(1)}, f32[2,4,8,32]{3,2,1,0:T(8,128)S(1)}, u32[]{:S(2)}, u32[]{:S(2)}) %collective-permute-start.6) | collective-permute-done | bytes 8224 | tf_op jit(solution)/shard_map/ppermute | solution.py:430
  19.6 1.6 %collective-permute-start.7 = (f32[1,4,8,32]{3,2,1,0:T(8,128)S(1)}, f32[1,4,8,32]{3,2,1,0:T(8,128)S(1)}, u32[]{:S(2)}, u32[]{:S(2)}) collective-permute-start(f32[1,4,8,32]{3,2,1,0:T(8,128)S(1)} %get-tuple-element.66), channel_id=1, source_target_pairs={{0,16},{8,24},{16,0},{24,8},{1,17},{9,25},{17,1},{25,9},{2,18},{10... | collective-permute-start | bytes 12296 | tf_op jit(solution)/shard_map/ppermute | solution.py:430
  21.2 2.2 %collective-permute-done.7.theirs = f32[1,4,8,32]{3,2,1,0:T(8,128)S(1)} collective-permute-done((f32[1,4,8,32]{3,2,1,0:T(8,128)S(1)}, f32[1,4,8,32]{3,2,1,0:T(8,128)S(1)}, u32[]{:S(2)}, u32[]{:S(2)}) %collective-permute-start.7) | collective-permute-done | bytes 4128 | tf_op jit(solution)/shard_map/ppermute | solution.py:430
  23.4 0.6 %merge1.1 = f32[4,1,1,8,32]{4,3,2,1,0:T(8,128)} custom-call(s32[4,8,32]{2,1,0:T(8,128)S(1)} %get-tuple-element.42.order_map, f32[1,4,8,32]{3,2,1,0:T(8,128)S(1)} %get-tuple-element.65.kept, f32[1,4,8,32]{3,2,1,0:T(8,128)S(1)} %collective-permute-done.7.theirs), custom_call_target="tpu_custom_call" | custom-call | tf_op jit(solution)/shard_map/merge1/pallas_call | solution.py:433
  (3 shorter events, 0.0 us)
Async XLA Ops:
  1.3 6.6 %collective-permute-start = (bf16[16,16,256]{2,1,0:T(8,128)(2,1)S(1)}, bf16[16,16,256]{2,1,0:T(8,128)(2,1)S(1)}, u32[]{:S(2)}, u32[]{:S(2)}) collective-permute-start(bf16[16,16,256]{2,1,0:T(8,128)(2,1)S(1)} %get-tuple-element.53.near0), channel_id=1, source_target_pairs={{0,2},{8,10},{16,18},{24,26},{1,3},{9,11},{17,19},{25,27},{4,6},{1... | collective-permute-start | bytes 393224 | tf_op jit(solution)/shard_map/ppermute | solution.py:345
  4.4 7.1 %collective-permute-start.3 = (bf16[16,16,256]{2,1,0:T(8,128)(2,1)S(1)}, bf16[16,16,256]{2,1,0:T(8,128)(2,1)S(1)}, u32[]{:S(2)}, u32[]{:S(2)}) collective-permute-start(bf16[16,16,256]{2,1,0:T(8,128)(2,1)S(1)} %get-tuple-element.54.near1), channel_id=1, source_target_pairs={{0,8},{16,24},{1,9},{17,25},{2,4},{10,12},{18,20},{26,28},{3,5},{1... | collective-permute-start | bytes 393224 | tf_op jit(solution)/shard_map/ppermute | solution.py:345
  8.2 7.6 %collective-permute-start.4 = (bf16[16,16,256]{2,1,0:T(8,128)(2,1)S(1)}, bf16[16,16,256]{2,1,0:T(8,128)(2,1)S(1)}, u32[]{:S(2)}, u32[]{:S(2)}) collective-permute-start(bf16[16,16,256]{2,1,0:T(8,128)(2,1)S(1)} %strip0.1), channel_id=1, source_target_pairs={{0,1},{8,9},{16,17},{24,25},{2,3},{10,11},{18,19},{26,27},{4,5},{1... | collective-permute-start | bytes 393224 | tf_op jit(solution)/shard_map/ppermute | solution.py:345
  9.9 5.0 %collective-permute-start.1 = (bf16[16,16,256]{2,1,0:T(8,128)(2,1)S(1)}, bf16[16,16,256]{2,1,0:T(8,128)(2,1)S(1)}, u32[]{:S(2)}, u32[]{:S(2)}) collective-permute-start(bf16[16,16,256]{2,1,0:T(8,128)(2,1)S(1)} %get-tuple-element.55.near0), channel_id=1, source_target_pairs={{0,2},{8,10},{16,18},{24,26},{1,3},{9,11},{17,19},{25,27},{4,6},{1... | collective-permute-start | bytes 393224 | tf_op jit(solution)/shard_map/ppermute | solution.py:345
  11.5 3.4 %collective-permute-start.2 = (bf16[16,16,256]{2,1,0:T(8,128)(2,1)S(1)}, bf16[16,16,256]{2,1,0:T(8,128)(2,1)S(1)}, u32[]{:S(2)}, u32[]{:S(2)}) collective-permute-start(bf16[16,16,256]{2,1,0:T(8,128)(2,1)S(1)} %get-tuple-element.56.near1), channel_id=1, source_target_pairs={{0,8},{16,24},{1,9},{17,25},{2,4},{10,12},{18,20},{26,28},{3,5},{1... | collective-permute-start | bytes 393224 | tf_op jit(solution)/shard_map/ppermute | solution.py:345
  11.8 6.0 %collective-permute-start.5 = (bf16[16,16,256]{2,1,0:T(8,128)(2,1)S(1)}, bf16[16,16,256]{2,1,0:T(8,128)(2,1)S(1)}, u32[]{:S(2)}, u32[]{:S(2)}) collective-permute-start(bf16[16,16,256]{2,1,0:T(8,128)(2,1)S(1)} %strip1.1), channel_id=1, source_target_pairs={{0,1},{8,9},{16,17},{24,25},{2,3},{10,11},{18,19},{26,27},{4,5},{1... | collective-permute-start | bytes 393224 | tf_op jit(solution)/shard_map/ppermute | solution.py:345
  18.3 1.3 %collective-permute-start.6 = (f32[2,4,8,32]{3,2,1,0:T(8,128)S(1)}, f32[2,4,8,32]{3,2,1,0:T(8,128)S(1)}, u32[]{:S(2)}, u32[]{:S(2)}) collective-permute-start(f32[2,4,8,32]{3,2,1,0:T(8,128)S(1)} %get-tuple-element.64), channel_id=1, source_target_pairs={{0,8},{8,0},{16,24},{24,16},{1,9},{9,1},{17,25},{25,17},{2,10},{10... | collective-permute-start | bytes 24584 | tf_op jit(solution)/shard_map/ppermute | solution.py:430
  19.6 3.8 %collective-permute-start.7 = (f32[1,4,8,32]{3,2,1,0:T(8,128)S(1)}, f32[1,4,8,32]{3,2,1,0:T(8,128)S(1)}, u32[]{:S(2)}, u32[]{:S(2)}) collective-permute-start(f32[1,4,8,32]{3,2,1,0:T(8,128)S(1)} %get-tuple-element.66), channel_id=1, source_target_pairs={{0,16},{8,24},{16,0},{24,8},{1,17},{9,25},{17,1},{25,9},{2,18},{10... | collective-permute-start | bytes 12296 | tf_op jit(solution)/shard_map/ppermute | solution.py:430

commit v13 on v12

--- a/solution.py
+++ b/solution.py
@@ -232,7 +232,7 @@
     out[...] = across.reshape(out.shape)
 
 
-def own_kernel(rim, early, mx, my, near0, near1, halo0, halo1, strip0, strip1, *refs):
+def own_kernel(rim, early, strip0, strip1, mx, my, near0, near1, halo0, halo1, *refs):
     place = Place()
     size = rim * rim
     across = [
@@ -367,7 +367,7 @@
         [struct((4 * bricks, 6 * bumps, 128), F32), struct((2, 2, 8, 128), jnp.int32)]
         + [struct((depth_count, block, rows_y), jnp.int32)],
     )(*tables[1:])
-    halo_x = [[swap(coarse[0][h], 1, h) for h in range(2)], None]
+    halo_x = [[swap(coarse[g][h], 1, h) for h in range(2)] for g in range(2)]
     mx, my = call(
         functools.partial(matrices_kernel, rim),
         "matrices",
@@ -399,9 +399,6 @@
         )
         strips.append(strip)
         halo_y.append(swap(strip, 2, 0))
-        if h == 0:
-            pieces = lax.optimization_barrier((*coarse[1], strip))
-            halo_x[1] = [swap(pieces[n], 1, n) for n in range(2)]
     early = rounds < 2
     colours = struct((3, rim, 128), F32)
     unlit = struct((2 - early, 2, size, rows_z), F32)
@@ -410,7 +407,7 @@
         "own",
         [VMEM] * (9 if early else 8),
         [colours, unlit] if early else [unlit, piece, piece],
-    )(mx, my, *coarse[1], *halo_x[1], *strips, *([shaded[1]] if early else []))
+    )(*strips, mx, my, *coarse[1], *halo_x[1], *([shaded[1]] if early else []))
     if early:
         light, partial = results
     else:

time: 24.2 us -> 25.1 us (1.037)
  starting transfers between devices: 8.62 us -> 10 us
  waiting for transfers between devices: 8.21 us -> 7.71 us
    ppermute x6, starting transfers between devices: 6.99 us -> 8.4 us  [swap(): return lax.ppermute(piece, axes, swaps(counts, axis, shift))]
    ppermute x6, waiting for transfers between devices: 4.77 us -> 4.27 us  [swap(): return lax.ppermute(piece, axes, swaps(counts, axis, shift))]
  transfers between devices with their start and end apart: 8 -> 8, of which waited for: 5 -> 4; matrix products, arithmetic and copies ran while one was open for 0% -> 0% of each run, Pallas kernels for 19% -> 19%
where the time goes in v13:
time: 25.1 us; the launch traced here: 25 us
  starting transfers between devices  10 us (40%)
  waiting for transfers between devices  7.71 us (31%)
  Pallas kernels  7.14 us (28%)
    ppermute x6, starting transfers between devices, swap(): return lax.ppermute(piece, axes, swaps(counts, axis, shift))  8.4 us
    ppermute x6, waiting for transfers between devices, swap(): return lax.ppermute(piece, axes, swaps(counts, axis, shift))  4.27 us
    ppermute x2, waiting for transfers between devices, per_device(): lax.ppermute(given, 'depth', [(i, i ^ 1 << level) for i in range(depth_co...  3.44 us
    pallas_call x2, Pallas kernels, per_device(): call(functools.partial(cells_kernel, rim, bumps, g), f'cells{g}', [VMEM]...  2.31 us
    ppermute x2, starting transfers between devices, per_device(): lax.ppermute(given, 'depth', [(i, i ^ 1 << level) for i in range(depth_co...  1.63 us
    pallas_call x1, Pallas kernels, per_device(): call(functools.partial(first_kernel, rim), 'first', [HBM] * (1 + len(tabl...  1.31 us
    pallas_call x1, Pallas kernels, per_device(): call(functools.partial(own_kernel, rim, early), 'own', [VMEM] * (9 if ear...  0.9 us
    pallas_call x2, Pallas kernels, per_device(): call(functools.partial(merge_kernel, level), f'merge{level}', [VMEM] * 3,...  0.63 us
  transfers between devices with their start and end apart: 8, of which 4 were waited for; matrix products, arithmetic and copies ran while one was open for 0% of the time, Pallas kernels for 19%

profile of v13, /device:TPU:0, one launch (start us, length us, event | category | flops | bytes accessed | tf_op | source)
XLA Modules:
  0.0 25.0 jit_solution(9827588419668427018)
XLA Ops:
  0.0 1.3 %first.1 = (f32[2,2,16,16,256]{4,3,2,1,0:T(8,128)S(1)}, bf16[16,16,256]{2,1,0:T(8,128)(2,1)S(1)}, bf16[16,16,256]{2,1,0:T(8,128)(2,1)S(1)}, bf16[16,16,256]{2,1,...) custom-call(f32[32,32,256]{2,1,0:T(8,128)} %density.1, ...), custom_call_target="tpu_custom_call" | custom-call | tf_op jit(solution)/shard_map/first/pallas_call | solution.py:352
  1.3 3.1 %collective-permute-start = (bf16[16,16,256]{2,1,0:T(8,128)(2,1)S(1)}, bf16[16,16,256]{2,1,0:T(8,128)(2,1)S(1)}, u32[]{:S(2)}, u32[]{:S(2)}) collective-permute-start(bf16[16,16,256]{2,1,0:T(8,128)(2,1)S(1)} %get-tuple-element.49.near0), channel_id=1, source_target_pairs={{0,2},{8,10},{16,18},{24,26},{1,3},{9,11},{17,19},{25,27},{4,6},{1... | collective-permute-start | bytes 393224 | tf_op jit(solution)/shard_map/ppermute | solution.py:345
  4.4 0.0 collective-permute-start.1
  4.4 3.1 %collective-permute-start.2 = (bf16[16,16,256]{2,1,0:T(8,128)(2,1)S(1)}, bf16[16,16,256]{2,1,0:T(8,128)(2,1)S(1)}, u32[]{:S(2)}, u32[]{:S(2)}) collective-permute-start(bf16[16,16,256]{2,1,0:T(8,128)(2,1)S(1)} %get-tuple-element.51.near0), channel_id=1, source_target_pairs={{0,2},{8,10},{16,18},{24,26},{1,3},{9,11},{17,19},{25,27},{4,6},{1... | collective-permute-start | bytes 393224 | tf_op jit(solution)/shard_map/ppermute | solution.py:345
  7.6 0.3 %prepare.1 = (f32[8,24,128]{2,1,0:T(8,128)S(1)}, s32[2,2,8,128]{3,2,1,0:T(8,128)S(1)}, s32[4,8,32]{2,1,0:T(8,128)S(1)}) custom-call(f32[4,8]{1,0:T(4,128)S(1)} %get-tuple-element.34.centre, f32[4,8]{1,0:T(4,128)S(1)} %get-tuple-element.35.width, f32[3,4,8]{2,1,0:T(4,128)S(1)} %get-tuple-element.36.colour, f32[4,8]{1,0:T(4,128)S(1)} %get-tuple-element.37.opacity, ...), custom_call_target="tpu_custom_call" | custom-call | tf_op jit(solution)/shard_map/prepare/pallas_call | solution.py:363
  7.8 1.2 %cells1.1 = (f32[3,2,16,16,256]{4,3,2,1,0:T(8,128)S(1)}, f32[16,128]{1,0:T(8,128)S(1)}) custom-call(f32[2,2,16,16,256]{4,3,2,1,0:T(8,128)S(1)} %get-tuple-element.44.held, f32[8,24,128]{2,1,0:T(8,128)S(1)} %get-tuple-element.45.table, s32[2,2,8,128]{3,2,1,0:T(8,128)S(1)} %get-tuple-element.46.signs), custom_call_target="tpu_custom_call" | custom-call | flops 262144 | bytes 262144 | tf_op jit(solution)/shard_map/cells1/pallas_call | solution.py:380
  9.0 0.6 %matrices.1 = (bf16[256,768]{1,0:T(8,128)(2,1)S(1)}, bf16[256,768]{1,0:T(8,128)(2,1)S(1)}) custom-call(bf16[2,33]{1,0:T(2,128)(2,1)S(1)} %get-tuple-element.41.taps), custom_call_target="tpu_custom_call" | custom-call | tf_op jit(solution)/shard_map/matrices/pallas_call | solution.py:371
  9.6 0.3 %strip0.1 = bf16[16,16,256]{2,1,0:T(8,128)(2,1)S(1)} custom-call(bf16[256,768]{1,0:T(8,128)(2,1)S(1)} %get-tuple-element.48.mx, bf16[16,16,256]{2,1,0:T(8,128)(2,1)S(1)} %get-tuple-element.49.near0, bf16[16,16,256]{2,1,0:T(8,128)(2,1)S(1)} %get-tuple-element.50.near1, bf16[16,16,256]{2,1,0:T(8,128)(2,1)S(1)} %collective-permute-done.halo), custom_call_target="tpu_custom_call" | custom-call | tf_op jit(solution)/shard_map/strip0/pallas_call | solution.py:397
  9.9 1.6 %collective-permute-start.4 = (bf16[16,16,256]{2,1,0:T(8,128)(2,1)S(1)}, bf16[16,16,256]{2,1,0:T(8,128)(2,1)S(1)}, u32[]{:S(2)}, u32[]{:S(2)}) collective-permute-start(bf16[16,16,256]{2,1,0:T(8,128)(2,1)S(1)} %strip0.1), channel_id=1, source_target_pairs={{0,1},{8,9},{16,17},{24,25},{2,3},{10,11},{18,19},{26,27},{4,5},{1... | collective-permute-start | bytes 393224 | tf_op jit(solution)/shard_map/ppermute | solution.py:345
  11.5 0.0 collective-permute-done.1.halo
  11.5 0.3 %strip1.1 = bf16[16,16,256]{2,1,0:T(8,128)(2,1)S(1)} custom-call(bf16[256,768]{1,0:T(8,128)(2,1)S(1)} %get-tuple-element.48.mx, bf16[16,16,256]{2,1,0:T(8,128)(2,1)S(1)} %get-tuple-element.49.near0, bf16[16,16,256]{2,1,0:T(8,128)(2,1)S(1)} %get-tuple-element.50.near1, bf16[16,16,256]{2,1,0:T(8,128)(2,1)S(1)} %collective-permute-done.1.halo), custom_call_target="tpu_custom_call" | custom-call | tf_op jit(solution)/shard_map/strip1/pallas_call | solution.py:397
  11.8 0.6 %collective-permute-start.5 = (bf16[16,16,256]{2,1,0:T(8,128)(2,1)S(1)}, bf16[16,16,256]{2,1,0:T(8,128)(2,1)S(1)}, u32[]{:S(2)}, u32[]{:S(2)}) collective-permute-start(bf16[16,16,256]{2,1,0:T(8,128)(2,1)S(1)} %strip1.1), channel_id=1, source_target_pairs={{0,1},{8,9},{16,17},{24,25},{2,3},{10,11},{18,19},{26,27},{4,5},{1... | collective-permute-start | bytes 393224 | tf_op jit(solution)/shard_map/ppermute | solution.py:345
  12.4 1.2 %cells0.1 = (f32[3,2,16,16,256]{4,3,2,1,0:T(8,128)S(1)}, f32[16,128]{1,0:T(8,128)S(1)}) custom-call(f32[2,2,16,16,256]{4,3,2,1,0:T(8,128)S(1)} %get-tuple-element.44.held, f32[8,24,128]{2,1,0:T(8,128)S(1)} %get-tuple-element.45.table, s32[2,2,8,128]{3,2,1,0:T(8,128)S(1)} %get-tuple-element.46.signs), custom_call_target="tpu_custom_call" | custom-call | flops 26214400000 | bytes 262144 | tf_op jit(solution)/shard_map/cells0/pallas_call | solution.py:380
  13.5 0.0 collective-permute-done.2.halo0
  13.5 0.0 collective-permute-done.3.halo1
  13.5 0.9 %own.1 = (f32[3,16,128]{2,1,0:T(8,128)S(1)}, f32[1,2,256,256]{3,2,1,0:T(8,128)S(1)}) custom-call(bf16[16,16,256]{2,1,0:T(8,128)(2,1)S(1)} %strip0.1, bf16[16,16,256]{2,1,0:T(8,128)(2,1)S(1)} %strip1.1, bf16[256,768]{1,0:T(8,128)(2,1)S(1)} %get-tuple-element.48.mx, bf16[256,768]{1,0:T(8,128)(2,1)S(1)} %get-tuple-element.42.my.refs_0_, ...), custom_call_target="tpu_custom_call" | custom-call | tf_op jit(solution)/shard_map/own/pallas_call | solution.py:405
  14.4 1.8 %collective-permute-done.4.refs_2_ = bf16[16,16,256]{2,1,0:T(8,128)(2,1)S(1)} collective-permute-done((bf16[16,16,256]{2,1,0:T(8,128)(2,1)S(1)}, bf16[16,16,256]{2,1,0:T(8,128)(2,1)S(1)}, u32[]{:S(2)}, u32[]{:S(2)}) %collective-permute-start.4) | collective-permute-done | bytes 131104 | tf_op jit(solution)/shard_map/ppermute | solution.py:345
  16.3 2.4 %collective-permute-done.5.refs_3_ = bf16[16,16,256]{2,1,0:T(8,128)(2,1)S(1)} collective-permute-done((bf16[16,16,256]{2,1,0:T(8,128)(2,1)S(1)}, bf16[16,16,256]{2,1,0:T(8,128)(2,1)S(1)}, u32[]{:S(2)}, u32[]{:S(2)}) %collective-permute-start.5) | collective-permute-done | bytes 131104 | tf_op jit(solution)/shard_map/ppermute | solution.py:345
  18.7 0.6 %last.1 = (f32[2,4,8,32]{3,2,1,0:T(8,128)S(1)}, f32[2,4,8,32]{3,2,1,0:T(8,128)S(1)}) custom-call(bf16[256,768]{1,0:T(8,128)(2,1)S(1)} %get-tuple-element.42.my.refs_0_, f32[1,2,256,256]{3,2,1,0:T(8,128)S(1)} %get-tuple-element.54.refs_1_, bf16[16,16,256]{2,1,0:T(8,128)(2,1)S(1)} %collective-permute-done.4.refs_2_, ...), custom_call_target="tpu_custom_call" | custom-call | tf_op jit(solution)/shard_map/last/pallas_call | solution.py:418
  19.3 0.1 collective-permute-start.6
  19.4 1.2 %collective-permute-done.6.theirs = f32[2,4,8,32]{3,2,1,0:T(8,128)S(1)} collective-permute-done((f32[2,4,8,32]{3,2,1,0:T(8,128)S(1)}, f32[2,4,8,32]{3,2,1,0:T(8,128)S(1)}, u32[]{:S(2)}, u32[]{:S(2)}) %collective-permute-start.6) | collective-permute-done | bytes 8224 | tf_op jit(solution)/shard_map/ppermute | solution.py:427
  20.6 1.6 %collective-permute-start.7 = (f32[1,4,8,32]{3,2,1,0:T(8,128)S(1)}, f32[1,4,8,32]{3,2,1,0:T(8,128)S(1)}, u32[]{:S(2)}, u32[]{:S(2)}) collective-permute-start(f32[1,4,8,32]{3,2,1,0:T(8,128)S(1)} %get-tuple-element.62), channel_id=1, source_target_pairs={{0,16},{8,24},{16,0},{24,8},{1,17},{9,25},{17,1},{25,9},{2,18},{10... | collective-permute-start | bytes 12296 | tf_op jit(solution)/shard_map/ppermute | solution.py:427
  22.1 2.2 %collective-permute-done.7.theirs = f32[1,4,8,32]{3,2,1,0:T(8,128)S(1)} collective-permute-done((f32[1,4,8,32]{3,2,1,0:T(8,128)S(1)}, f32[1,4,8,32]{3,2,1,0:T(8,128)S(1)}, u32[]{:S(2)}, u32[]{:S(2)}) %collective-permute-start.7) | collective-permute-done | bytes 4128 | tf_op jit(solution)/shard_map/ppermute | solution.py:427
  24.4 0.6 %merge1.1 = f32[4,1,1,8,32]{4,3,2,1,0:T(8,128)} custom-call(s32[4,8,32]{2,1,0:T(8,128)S(1)} %get-tuple-element.40.order_map, f32[1,4,8,32]{3,2,1,0:T(8,128)S(1)} %get-tuple-element.61.kept, f32[1,4,8,32]{3,2,1,0:T(8,128)S(1)} %collective-permute-done.7.theirs), custom_call_target="tpu_custom_call" | custom-call | tf_op jit(solution)/shard_map/merge1/pallas_call | solution.py:430
  (3 shorter events, 0.0 us)
Async XLA Ops:
  1.3 8.3 %collective-permute-start = (bf16[16,16,256]{2,1,0:T(8,128)(2,1)S(1)}, bf16[16,16,256]{2,1,0:T(8,128)(2,1)S(1)}, u32[]{:S(2)}, u32[]{:S(2)}) collective-permute-start(bf16[16,16,256]{2,1,0:T(8,128)(2,1)S(1)} %get-tuple-element.49.near0), channel_id=1, source_target_pairs={{0,2},{8,10},{16,18},{24,26},{1,3},{9,11},{17,19},{25,27},{4,6},{1... | collective-permute-start | bytes 393224 | tf_op jit(solution)/shard_map/ppermute | solution.py:345
  4.4 7.1 %collective-permute-start.1 = (bf16[16,16,256]{2,1,0:T(8,128)(2,1)S(1)}, bf16[16,16,256]{2,1,0:T(8,128)(2,1)S(1)}, u32[]{:S(2)}, u32[]{:S(2)}) collective-permute-start(bf16[16,16,256]{2,1,0:T(8,128)(2,1)S(1)} %get-tuple-element.50.near1), channel_id=1, source_target_pairs={{0,8},{16,24},{1,9},{17,25},{2,4},{10,12},{18,20},{26,28},{3,5},{1... | collective-permute-start | bytes 393224 | tf_op jit(solution)/shard_map/ppermute | solution.py:345
  4.4 9.1 %collective-permute-start.2 = (bf16[16,16,256]{2,1,0:T(8,128)(2,1)S(1)}, bf16[16,16,256]{2,1,0:T(8,128)(2,1)S(1)}, u32[]{:S(2)}, u32[]{:S(2)}) collective-permute-start(bf16[16,16,256]{2,1,0:T(8,128)(2,1)S(1)} %get-tuple-element.51.near0), channel_id=1, source_target_pairs={{0,2},{8,10},{16,18},{24,26},{1,3},{9,11},{17,19},{25,27},{4,6},{1... | collective-permute-start | bytes 393224 | tf_op jit(solution)/shard_map/ppermute | solution.py:345
  7.6 6.0 %collective-permute-start.3 = (bf16[16,16,256]{2,1,0:T(8,128)(2,1)S(1)}, bf16[16,16,256]{2,1,0:T(8,128)(2,1)S(1)}, u32[]{:S(2)}, u32[]{:S(2)}) collective-permute-start(bf16[16,16,256]{2,1,0:T(8,128)(2,1)S(1)} %get-tuple-element.52.near1), channel_id=1, source_target_pairs={{0,8},{16,24},{1,9},{17,25},{2,4},{10,12},{18,20},{26,28},{3,5},{1... | collective-permute-start | bytes 393224 | tf_op jit(solution)/shard_map/ppermute | solution.py:345
  9.9 6.4 %collective-permute-start.4 = (bf16[16,16,256]{2,1,0:T(8,128)(2,1)S(1)}, bf16[16,16,256]{2,1,0:T(8,128)(2,1)S(1)}, u32[]{:S(2)}, u32[]{:S(2)}) collective-permute-start(bf16[16,16,256]{2,1,0:T(8,128)(2,1)S(1)} %strip0.1), channel_id=1, source_target_pairs={{0,1},{8,9},{16,17},{24,25},{2,3},{10,11},{18,19},{26,27},{4,5},{1... | collective-permute-start | bytes 393224 | tf_op jit(solution)/shard_map/ppermute | solution.py:345
  11.8 6.9 %collective-permute-start.5 = (bf16[16,16,256]{2,1,0:T(8,128)(2,1)S(1)}, bf16[16,16,256]{2,1,0:T(8,128)(2,1)S(1)}, u32[]{:S(2)}, u32[]{:S(2)}) collective-permute-start(bf16[16,16,256]{2,1,0:T(8,128)(2,1)S(1)} %strip1.1), channel_id=1, source_target_pairs={{0,1},{8,9},{16,17},{24,25},{2,3},{10,11},{18,19},{26,27},{4,5},{1... | collective-permute-start | bytes 393224 | tf_op jit(solution)/shard_map/ppermute | solution.py:345
  19.3 1.3 %collective-permute-start.6 = (f32[2,4,8,32]{3,2,1,0:T(8,128)S(1)}, f32[2,4,8,32]{3,2,1,0:T(8,128)S(1)}, u32[]{:S(2)}, u32[]{:S(2)}) collective-permute-start(f32[2,4,8,32]{3,2,1,0:T(8,128)S(1)} %get-tuple-element.60), channel_id=1, source_target_pairs={{0,8},{8,0},{16,24},{24,16},{1,9},{9,1},{17,25},{25,17},{2,10},{10... | collective-permute-start | bytes 24584 | tf_op jit(solution)/shard_map/ppermute | solution.py:427
  20.6 3.8 %collective-permute-start.7 = (f32[1,4,8,32]{3,2,1,0:T(8,128)S(1)}, f32[1,4,8,32]{3,2,1,0:T(8,128)S(1)}, u32[]{:S(2)}, u32[]{:S(2)}) collective-permute-start(f32[1,4,8,32]{3,2,1,0:T(8,128)S(1)} %get-tuple-element.62), channel_id=1, source_target_pairs={{0,16},{8,24},{16,0},{24,8},{1,17},{9,25},{17,1},{25,9},{2,18},{10... | collective-permute-start | bytes 12296 | tf_op jit(solution)/shard_map/ppermute | solution.py:427

commit v14 on v13

--- a/solution.py
+++ b/solution.py
@@ -232,7 +232,7 @@
     out[...] = across.reshape(out.shape)
 
 
-def own_kernel(rim, early, strip0, strip1, mx, my, near0, near1, halo0, halo1, *refs):
+def own_kernel(rim, early, strip0, halo0, strip1, halo1, mx, my, near0, near1, *refs):
     place = Place()
     size = rim * rim
     across = [
@@ -375,6 +375,17 @@
         [struct((size, 3 * size), BF16)] * 2,
         [pltpu.VMEM((8, 128), F32)],
     )(tables[0])
+    strips, halo_y = [], []
+    for h in range(2):
+        if h == 1:
+            mx, halo_x[1][0] = lax.optimization_barrier((mx, halo_x[1][0]))
+        strip = call(functools.partial(strip_kernel, rim, h), f"strip{h}", [VMEM] * 4, piece)(
+            mx, *coarse[0], halo_x[0][h]
+        )
+        strips.append(strip)
+        halo_y.append(swap(strip, 2, 0))
+    table, first = lax.optimization_barrier((table, strips[0]))
+    strips[0] = first
     shaded, total = [None, None], [None, None]
     for g in (1, 0):
         shaded[g], total[g] = call(
@@ -390,15 +401,6 @@
             ),
         )(held, table, signs)
 
-    strips, halo_y = [], []
-    for h in range(2):
-        if h == 0:
-            mx, total[1] = lax.optimization_barrier((mx, total[1]))
-        strip = call(functools.partial(strip_kernel, rim, h), f"strip{h}", [VMEM] * 4, piece)(
-            mx, *coarse[0], halo_x[0][h]
-        )
-        strips.append(strip)
-        halo_y.append(swap(strip, 2, 0))
     early = rounds < 2
     colours = struct((3, rim, 128), F32)
     unlit = struct((2 - early, 2, size, rows_z), F32)
@@ -407,7 +409,9 @@
         "own",
         [VMEM] * (9 if early else 8),
         [colours, unlit] if early else [unlit, piece, piece],
-    )(*strips, mx, my, *coarse[1], *halo_x[1], *([shaded[1]] if early else []))
+    )(
+        strips[0], halo_x[1][0], strips[1], halo_x[1][1], mx, my, *coarse[1], *([shaded[1]] if early else [])
+    )
     if early:
         light, partial = results
     else:

time: 25.1 us -> 23.3 us (0.928)
  starting transfers between devices: 10 us -> 8.89 us
  waiting for transfers between devices: 7.71 us -> 7.07 us
    ppermute x6, starting transfers between devices: 8.4 us -> 7.12 us  [swap(): return lax.ppermute(piece, axes, swaps(counts, axis, shift))]
    ppermute x6, waiting for transfers between devices: 4.27 us -> 3.76 us  [swap(): return lax.ppermute(piece, axes, swaps(counts, axis, shift))]
  transfers between devices with their start and end apart: 8 -> 8, of which waited for: 4 -> 4; matrix products, arithmetic and copies ran while one was open for 0% -> 0% of each run, Pallas kernels for 19% -> 20%
where the time goes in v14:
time: 23.3 us; the launch traced here: 23.1 us
  starting transfers between devices  8.89 us (38%)
  Pallas kernels  7.09 us (30%)
  waiting for transfers between devices  7.07 us (30%)
    ppermute x6, starting transfers between devices, swap(): return lax.ppermute(piece, axes, swaps(counts, axis, shift))  7.12 us
    ppermute x6, waiting for transfers between devices, swap(): return lax.ppermute(piece, axes, swaps(counts, axis, shift))  3.76 us
    ppermute x2, waiting for transfers between devices, per_device(): lax.ppermute(given, 'depth', [(i, i ^ 1 << level) for i in range(depth_co...  3.3 us
    pallas_call x2, Pallas kernels, per_device(): call(functools.partial(cells_kernel, rim, bumps, g), f'cells{g}', [VMEM]...  2.25 us
    ppermute x2, starting transfers between devices, per_device(): lax.ppermute(given, 'depth', [(i, i ^ 1 << level) for i in range(depth_co...  1.77 us
    pallas_call x1, Pallas kernels, per_device(): call(functools.partial(first_kernel, rim), 'first', [HBM] * (1 + len(tabl...  1.31 us
    pallas_call x1, Pallas kernels, per_device(): call(functools.partial(own_kernel, rim, early), 'own', [VMEM] * (9 if ear...  0.9 us
    pallas_call x2, Pallas kernels, per_device(): call(functools.partial(merge_kernel, level), f'merge{level}', [VMEM] * 3,...  0.63 us
  transfers between devices with their start and end apart: 8, of which 4 were waited for; matrix products, arithmetic and copies ran while one was open for 0% of the time, Pallas kernels for 20%

profile of v14, /device:TPU:0, one launch (start us, length us, event | category | flops | bytes accessed | tf_op | source)
XLA Modules:
  0.0 23.1 jit_solution(5164952041439103158)
XLA Ops:
  0.0 1.3 %first.1 = (f32[2,2,16,16,256]{4,3,2,1,0:T(8,128)S(1)}, bf16[16,16,256]{2,1,0:T(8,128)(2,1)S(1)}, bf16[16,16,256]{2,1,0:T(8,128)(2,1)S(1)}, bf16[16,16,256]{2,1,...) custom-call(f32[32,32,256]{2,1,0:T(8,128)} %density.1, ...), custom_call_target="tpu_custom_call" | custom-call | tf_op jit(solution)/shard_map/first/pallas_call | solution.py:352
  1.3 3.1 %collective-permute-start = (bf16[16,16,256]{2,1,0:T(8,128)(2,1)S(1)}, bf16[16,16,256]{2,1,0:T(8,128)(2,1)S(1)}, u32[]{:S(2)}, u32[]{:S(2)}) collective-permute-start(bf16[16,16,256]{2,1,0:T(8,128)(2,1)S(1)} %get-tuple-element.47.near0), channel_id=1, source_target_pairs={{0,2},{8,10},{16,18},{24,26},{1,3},{9,11},{17,19},{25,27},{4,6},{1... | collective-permute-start | bytes 393224 | tf_op jit(solution)/shard_map/ppermute | solution.py:345
  4.4 0.1 collective-permute-start.1
  4.5 0.0 collective-permute-start.2
  4.5 0.5 %collective-permute-start.3 = (bf16[16,16,256]{2,1,0:T(8,128)(2,1)S(1)}, bf16[16,16,256]{2,1,0:T(8,128)(2,1)S(1)}, u32[]{:S(2)}, u32[]{:S(2)}) collective-permute-start(bf16[16,16,256]{2,1,0:T(8,128)(2,1)S(1)} %get-tuple-element.53.near1), channel_id=1, source_target_pairs={{0,8},{16,24},{1,9},{17,25},{2,4},{10,12},{18,20},{26,28},{3,5},{1... | collective-permute-start | bytes 393224 | tf_op jit(solution)/shard_map/ppermute | solution.py:345
  5.0 0.6 %matrices.1 = (bf16[256,768]{1,0:T(8,128)(2,1)S(1)}, bf16[256,768]{1,0:T(8,128)(2,1)S(1)}) custom-call(bf16[2,33]{1,0:T(2,128)(2,1)S(1)} %get-tuple-element.43.taps), custom_call_target="tpu_custom_call" | custom-call | tf_op jit(solution)/shard_map/matrices/pallas_call | solution.py:371
  5.6 0.3 %prepare.1 = (f32[8,24,128]{2,1,0:T(8,128)S(1)}, s32[2,2,8,128]{3,2,1,0:T(8,128)S(1)}, s32[4,8,32]{2,1,0:T(8,128)S(1)}) custom-call(f32[4,8]{1,0:T(4,128)S(1)} %get-tuple-element.36.centre, f32[4,8]{1,0:T(4,128)S(1)} %get-tuple-element.37.width, f32[3,4,8]{2,1,0:T(4,128)S(1)} %get-tuple-element.38.colour, f32[4,8]{1,0:T(4,128)S(1)} %get-tuple-element.39.opacity, ...), custom_call_target="tpu_custom_call" | custom-call | tf_op jit(solution)/shard_map/prepare/pallas_call | solution.py:363
  5.9 2.8 %collective-permute-done.halo = bf16[16,16,256]{2,1,0:T(8,128)(2,1)S(1)} collective-permute-done((bf16[16,16,256]{2,1,0:T(8,128)(2,1)S(1)}, bf16[16,16,256]{2,1,0:T(8,128)(2,1)S(1)}, u32[]{:S(2)}, u32[]{:S(2)}) %collective-permute-start) | collective-permute-done | bytes 131104 | tf_op jit(solution)/shard_map/ppermute | solution.py:345
  8.7 0.3 %strip0.1 = bf16[16,16,256]{2,1,0:T(8,128)(2,1)S(1)} custom-call(bf16[256,768]{1,0:T(8,128)(2,1)S(1)} %get-tuple-element.52.mx, bf16[16,16,256]{2,1,0:T(8,128)(2,1)S(1)} %get-tuple-element.47.near0, bf16[16,16,256]{2,1,0:T(8,128)(2,1)S(1)} %get-tuple-element.48.near1, bf16[16,16,256]{2,1,0:T(8,128)(2,1)S(1)} %collective-permute-done.halo), custom_call_target="tpu_custom_call" | custom-call | tf_op jit(solution)/shard_map/strip0/pallas_call | solution.py:382
  9.0 2.1 %collective-permute-start.4 = (bf16[16,16,256]{2,1,0:T(8,128)(2,1)S(1)}, bf16[16,16,256]{2,1,0:T(8,128)(2,1)S(1)}, u32[]{:S(2)}, u32[]{:S(2)}) collective-permute-start(bf16[16,16,256]{2,1,0:T(8,128)(2,1)S(1)} %strip0.1), channel_id=1, source_target_pairs={{0,1},{8,9},{16,17},{24,25},{2,3},{10,11},{18,19},{26,27},{4,5},{1... | collective-permute-start | bytes 393224 | tf_op jit(solution)/shard_map/ppermute | solution.py:345
  11.1 0.0 collective-permute-done.1.halo0
  11.1 0.3 %strip1.1 = bf16[16,16,256]{2,1,0:T(8,128)(2,1)S(1)} custom-call(bf16[256,768]{1,0:T(8,128)(2,1)S(1)} %get-tuple-element.52.mx, bf16[16,16,256]{2,1,0:T(8,128)(2,1)S(1)} %get-tuple-element.47.near0, bf16[16,16,256]{2,1,0:T(8,128)(2,1)S(1)} %get-tuple-element.48.near1, bf16[16,16,256]{2,1,0:T(8,128)(2,1)S(1)} %collective-permute-done.2.halo), custom_call_target="tpu_custom_call" | custom-call | tf_op jit(solution)/shard_map/strip1/pallas_call | solution.py:382
  11.4 1.4 %collective-permute-start.5 = (bf16[16,16,256]{2,1,0:T(8,128)(2,1)S(1)}, bf16[16,16,256]{2,1,0:T(8,128)(2,1)S(1)}, u32[]{:S(2)}, u32[]{:S(2)}) collective-permute-start(bf16[16,16,256]{2,1,0:T(8,128)(2,1)S(1)} %strip1.1), channel_id=1, source_target_pairs={{0,1},{8,9},{16,17},{24,25},{2,3},{10,11},{18,19},{26,27},{4,5},{1... | collective-permute-start | bytes 393224 | tf_op jit(solution)/shard_map/ppermute | solution.py:345
  12.7 1.1 %cells0.1 = (f32[3,2,16,16,256]{4,3,2,1,0:T(8,128)S(1)}, f32[16,128]{1,0:T(8,128)S(1)}) custom-call(f32[2,2,16,16,256]{4,3,2,1,0:T(8,128)S(1)} %get-tuple-element.54.held, f32[8,24,128]{2,1,0:T(8,128)S(1)} %get-tuple-element.55.table, s32[2,2,8,128]{3,2,1,0:T(8,128)S(1)} %get-tuple-element.56.signs), custom_call_target="tpu_custom_call" | custom-call | flops 26214400000 | bytes 262144 | tf_op jit(solution)/shard_map/cells0/pallas_call | solution.py:391
  13.9 1.1 %cells1.1 = (f32[3,2,16,16,256]{4,3,2,1,0:T(8,128)S(1)}, f32[16,128]{1,0:T(8,128)S(1)}) custom-call(f32[2,2,16,16,256]{4,3,2,1,0:T(8,128)S(1)} %get-tuple-element.54.held, f32[8,24,128]{2,1,0:T(8,128)S(1)} %get-tuple-element.55.table, s32[2,2,8,128]{3,2,1,0:T(8,128)S(1)} %get-tuple-element.56.signs), custom_call_target="tpu_custom_call" | custom-call | flops 262144 | bytes 262144 | tf_op jit(solution)/shard_map/cells1/pallas_call | solution.py:391
  15.0 0.0 collective-permute-done.3.halo1
  15.0 0.9 %own.1 = (f32[3,16,128]{2,1,0:T(8,128)S(1)}, f32[1,2,256,256]{3,2,1,0:T(8,128)S(1)}) custom-call(bf16[16,16,256]{2,1,0:T(8,128)(2,1)S(1)} %strip0.1, bf16[16,16,256]{2,1,0:T(8,128)(2,1)S(1)} %collective-permute-done.1.halo0, bf16[16,16,256]{2,1,0:T(8,128)(2,1)S(1)} %strip1.1, bf16[16,16,256]{2,1,0:T(8,128)(2,1)S(1)} %collective-permute-done.3.halo1, ...), custom_call_target="tpu_custom_call" | custom-call | tf_op jit(solution)/shard_map/own/pallas_call | solution.py:407
  15.9 0.9 %collective-permute-done.5.refs_3_ = bf16[16,16,256]{2,1,0:T(8,128)(2,1)S(1)} collective-permute-done((bf16[16,16,256]{2,1,0:T(8,128)(2,1)S(1)}, bf16[16,16,256]{2,1,0:T(8,128)(2,1)S(1)}, u32[]{:S(2)}, u32[]{:S(2)}) %collective-permute-start.5) | collective-permute-done | bytes 131104 | tf_op jit(solution)/shard_map/ppermute | solution.py:345
  16.9 0.6 %last.1 = (f32[2,4,8,32]{3,2,1,0:T(8,128)S(1)}, f32[2,4,8,32]{3,2,1,0:T(8,128)S(1)}) custom-call(bf16[256,768]{1,0:T(8,128)(2,1)S(1)} %get-tuple-element.44.my.refs_0_, f32[1,2,256,256]{3,2,1,0:T(8,128)S(1)} %get-tuple-element.58.refs_1_, bf16[16,16,256]{2,1,0:T(8,128)(2,1)S(1)} %collective-permute-done.4.refs_2_, ...), custom_call_target="tpu_custom_call" | custom-call | tf_op jit(solution)/shard_map/last/pallas_call | solution.py:422
  17.4 0.1 collective-permute-start.6
  17.5 1.2 %collective-permute-done.6.theirs = f32[2,4,8,32]{3,2,1,0:T(8,128)S(1)} collective-permute-done((f32[2,4,8,32]{3,2,1,0:T(8,128)S(1)}, f32[2,4,8,32]{3,2,1,0:T(8,128)S(1)}, u32[]{:S(2)}, u32[]{:S(2)}) %collective-permute-start.6) | collective-permute-done | bytes 8224 | tf_op jit(solution)/shard_map/ppermute | solution.py:431
  18.7 1.7 %collective-permute-start.7 = (f32[1,4,8,32]{3,2,1,0:T(8,128)S(1)}, f32[1,4,8,32]{3,2,1,0:T(8,128)S(1)}, u32[]{:S(2)}, u32[]{:S(2)}) collective-permute-start(f32[1,4,8,32]{3,2,1,0:T(8,128)S(1)} %get-tuple-element.66), channel_id=1, source_target_pairs={{0,16},{8,24},{16,0},{24,8},{1,17},{9,25},{17,1},{25,9},{2,18},{10... | collective-permute-start | bytes 12296 | tf_op jit(solution)/shard_map/ppermute | solution.py:431
  20.4 2.1 %collective-permute-done.7.theirs = f32[1,4,8,32]{3,2,1,0:T(8,128)S(1)} collective-permute-done((f32[1,4,8,32]{3,2,1,0:T(8,128)S(1)}, f32[1,4,8,32]{3,2,1,0:T(8,128)S(1)}, u32[]{:S(2)}, u32[]{:S(2)}) %collective-permute-start.7) | collective-permute-done | bytes 4128 | tf_op jit(solution)/shard_map/ppermute | solution.py:431
  22.5 0.6 %merge1.1 = f32[4,1,1,8,32]{4,3,2,1,0:T(8,128)} custom-call(s32[4,8,32]{2,1,0:T(8,128)S(1)} %get-tuple-element.42.order_map, f32[1,4,8,32]{3,2,1,0:T(8,128)S(1)} %get-tuple-element.65.kept, f32[1,4,8,32]{3,2,1,0:T(8,128)S(1)} %collective-permute-done.7.theirs), custom_call_target="tpu_custom_call" | custom-call | tf_op jit(solution)/shard_map/merge1/pallas_call | solution.py:434
  (3 shorter events, 0.0 us)
Async XLA Ops:
  1.3 7.4 %collective-permute-start = (bf16[16,16,256]{2,1,0:T(8,128)(2,1)S(1)}, bf16[16,16,256]{2,1,0:T(8,128)(2,1)S(1)}, u32[]{:S(2)}, u32[]{:S(2)}) collective-permute-start(bf16[16,16,256]{2,1,0:T(8,128)(2,1)S(1)} %get-tuple-element.47.near0), channel_id=1, source_target_pairs={{0,2},{8,10},{16,18},{24,26},{1,3},{9,11},{17,19},{25,27},{4,6},{1... | collective-permute-start | bytes 393224 | tf_op jit(solution)/shard_map/ppermute | solution.py:345
  4.4 6.7 %collective-permute-start.1 = (bf16[16,16,256]{2,1,0:T(8,128)(2,1)S(1)}, bf16[16,16,256]{2,1,0:T(8,128)(2,1)S(1)}, u32[]{:S(2)}, u32[]{:S(2)}) collective-permute-start(bf16[16,16,256]{2,1,0:T(8,128)(2,1)S(1)} %get-tuple-element.50.near0), channel_id=1, source_target_pairs={{0,2},{8,10},{16,18},{24,26},{1,3},{9,11},{17,19},{25,27},{4,6},{1... | collective-permute-start | bytes 393224 | tf_op jit(solution)/shard_map/ppermute | solution.py:345
  4.5 6.6 %collective-permute-start.2 = (bf16[16,16,256]{2,1,0:T(8,128)(2,1)S(1)}, bf16[16,16,256]{2,1,0:T(8,128)(2,1)S(1)}, u32[]{:S(2)}, u32[]{:S(2)}) collective-permute-start(bf16[16,16,256]{2,1,0:T(8,128)(2,1)S(1)} %get-tuple-element.48.near1), channel_id=1, source_target_pairs={{0,8},{16,24},{1,9},{17,25},{2,4},{10,12},{18,20},{26,28},{3,5},{1... | collective-permute-start | bytes 393224 | tf_op jit(solution)/shard_map/ppermute | solution.py:345
  4.5 10.5 %collective-permute-start.3 = (bf16[16,16,256]{2,1,0:T(8,128)(2,1)S(1)}, bf16[16,16,256]{2,1,0:T(8,128)(2,1)S(1)}, u32[]{:S(2)}, u32[]{:S(2)}) collective-permute-start(bf16[16,16,256]{2,1,0:T(8,128)(2,1)S(1)} %get-tuple-element.53.near1), channel_id=1, source_target_pairs={{0,8},{16,24},{1,9},{17,25},{2,4},{10,12},{18,20},{26,28},{3,5},{1... | collective-permute-start | bytes 393224 | tf_op jit(solution)/shard_map/ppermute | solution.py:345
  9.0 6.9 %collective-permute-start.4 = (bf16[16,16,256]{2,1,0:T(8,128)(2,1)S(1)}, bf16[16,16,256]{2,1,0:T(8,128)(2,1)S(1)}, u32[]{:S(2)}, u32[]{:S(2)}) collective-permute-start(bf16[16,16,256]{2,1,0:T(8,128)(2,1)S(1)} %strip0.1), channel_id=1, source_target_pairs={{0,1},{8,9},{16,17},{24,25},{2,3},{10,11},{18,19},{26,27},{4,5},{1... | collective-permute-start | bytes 393224 | tf_op jit(solution)/shard_map/ppermute | solution.py:345
  11.4 5.5 %collective-permute-start.5 = (bf16[16,16,256]{2,1,0:T(8,128)(2,1)S(1)}, bf16[16,16,256]{2,1,0:T(8,128)(2,1)S(1)}, u32[]{:S(2)}, u32[]{:S(2)}) collective-permute-start(bf16[16,16,256]{2,1,0:T(8,128)(2,1)S(1)} %strip1.1), channel_id=1, source_target_pairs={{0,1},{8,9},{16,17},{24,25},{2,3},{10,11},{18,19},{26,27},{4,5},{1... | collective-permute-start | bytes 393224 | tf_op jit(solution)/shard_map/ppermute | solution.py:345
  17.4 1.3 %collective-permute-start.6 = (f32[2,4,8,32]{3,2,1,0:T(8,128)S(1)}, f32[2,4,8,32]{3,2,1,0:T(8,128)S(1)}, u32[]{:S(2)}, u32[]{:S(2)}) collective-permute-start(f32[2,4,8,32]{3,2,1,0:T(8,128)S(1)} %get-tuple-element.64), channel_id=1, source_target_pairs={{0,8},{8,0},{16,24},{24,16},{1,9},{9,1},{17,25},{25,17},{2,10},{10... | collective-permute-start | bytes 24584 | tf_op jit(solution)/shard_map/ppermute | solution.py:431
  18.7 3.8 %collective-permute-start.7 = (f32[1,4,8,32]{3,2,1,0:T(8,128)S(1)}, f32[1,4,8,32]{3,2,1,0:T(8,128)S(1)}, u32[]{:S(2)}, u32[]{:S(2)}) collective-permute-start(f32[1,4,8,32]{3,2,1,0:T(8,128)S(1)} %get-tuple-element.66), channel_id=1, source_target_pairs={{0,16},{8,24},{16,0},{24,8},{1,17},{9,25},{17,1},{25,9},{2,18},{10... | collective-permute-start | bytes 12296 | tf_op jit(solution)/shard_map/ppermute | solution.py:431

commit v15 on v14

--- a/solution.py
+++ b/solution.py
@@ -367,7 +367,7 @@
         [struct((4 * bricks, 6 * bumps, 128), F32), struct((2, 2, 8, 128), jnp.int32)]
         + [struct((depth_count, block, rows_y), jnp.int32)],
     )(*tables[1:])
-    halo_x = [[swap(coarse[g][h], 1, h) for h in range(2)] for g in range(2)]
+    halo_x = [[swap(coarse[0][h], 1, h) for h in range(2)], None]
     mx, my = call(
         functools.partial(matrices_kernel, rim),
         "matrices",
@@ -375,10 +375,10 @@
         [struct((size, 3 * size), BF16)] * 2,
         [pltpu.VMEM((8, 128), F32)],
     )(tables[0])
+    *others, table, mx = lax.optimization_barrier((*coarse[1], table, mx))
+    halo_x[1] = [swap(others[h], 1, h) for h in range(2)]
     strips, halo_y = [], []
     for h in range(2):
-        if h == 1:
-            mx, halo_x[1][0] = lax.optimization_barrier((mx, halo_x[1][0]))
         strip = call(functools.partial(strip_kernel, rim, h), f"strip{h}", [VMEM] * 4, piece)(
             mx, *coarse[0], halo_x[0][h]
         )

time: 23.3 us -> 24 us (1.030)
  starting transfers between devices: 8.89 us -> 10.1 us
  waiting for transfers between devices: 7.07 us -> 6.59 us
    ppermute x6, starting transfers between devices: 7.12 us -> 8.46 us  [swap(): return lax.ppermute(piece, axes, swaps(counts, axis, shift))]
    ppermute x6, waiting for transfers between devices: 3.76 us -> 3.16 us  [swap(): return lax.ppermute(piece, axes, swaps(counts, axis, shift))]
  transfers between devices with their start and end apart: 8 -> 8, of which waited for: 4 -> 4; matrix products, arithmetic and copies ran while one was open for 0% -> 0% of each run, Pallas kernels for 20% -> 19%
where the time goes in v15:
time: 24 us; the launch traced here: 23.9 us
  starting transfers between devices  10.1 us (42%)
  Pallas kernels  7.09 us (30%)
  waiting for transfers between devices  6.59 us (27%)
    ppermute x6, starting transfers between devices, swap(): return lax.ppermute(piece, axes, swaps(counts, axis, shift))  8.46 us
    ppermute x2, waiting for transfers between devices, per_device(): lax.ppermute(given, 'depth', [(i, i ^ 1 << level) for i in range(depth_co...  3.43 us
    ppermute x6, waiting for transfers between devices, swap(): return lax.ppermute(piece, axes, swaps(counts, axis, shift))  3.16 us
    pallas_call x2, Pallas kernels, per_device(): call(functools.partial(cells_kernel, rim, bumps, g), f'cells{g}', [VMEM]...  2.25 us
    ppermute x2, starting transfers between devices, per_device(): lax.ppermute(given, 'depth', [(i, i ^ 1 << level) for i in range(depth_co...  1.64 us
    pallas_call x1, Pallas kernels, per_device(): call(functools.partial(first_kernel, rim), 'first', [HBM] * (1 + len(tabl...  1.31 us
    pallas_call x1, Pallas kernels, per_device(): call(functools.partial(own_kernel, rim, early), 'own', [VMEM] * (9 if ear...  0.9 us
    pallas_call x2, Pallas kernels, per_device(): call(functools.partial(merge_kernel, level), f'merge{level}', [VMEM] * 3,...  0.63 us
  transfers between devices with their start and end apart: 8, of which 4 were waited for; matrix products, arithmetic and copies ran while one was open for 0% of the time, Pallas kernels for 19%

profile of v15, /device:TPU:0, one launch (start us, length us, event | category | flops | bytes accessed | tf_op | source)
XLA Modules:
  0.0 23.9 jit_solution(3052741353793447873)
XLA Ops:
  0.0 1.3 %first.1 = (f32[2,2,16,16,256]{4,3,2,1,0:T(8,128)S(1)}, bf16[16,16,256]{2,1,0:T(8,128)(2,1)S(1)}, bf16[16,16,256]{2,1,0:T(8,128)(2,1)S(1)}, bf16[16,16,256]{2,1,...) custom-call(f32[32,32,256]{2,1,0:T(8,128)} %density.1, ...), custom_call_target="tpu_custom_call" | custom-call | tf_op jit(solution)/shard_map/first/pallas_call | solution.py:352
  1.3 3.1 %collective-permute-start = (bf16[16,16,256]{2,1,0:T(8,128)(2,1)S(1)}, bf16[16,16,256]{2,1,0:T(8,128)(2,1)S(1)}, u32[]{:S(2)}, u32[]{:S(2)}) collective-permute-start(bf16[16,16,256]{2,1,0:T(8,128)(2,1)S(1)} %get-tuple-element.53.near0), channel_id=1, source_target_pairs={{0,2},{8,10},{16,18},{24,26},{1,3},{9,11},{17,19},{25,27},{4,6},{1... | collective-permute-start | bytes 393224 | tf_op jit(solution)/shard_map/ppermute | solution.py:345
  4.4 0.0 collective-permute-start.2
  4.4 0.6 %matrices.1 = (bf16[256,768]{1,0:T(8,128)(2,1)S(1)}, bf16[256,768]{1,0:T(8,128)(2,1)S(1)}) custom-call(bf16[2,33]{1,0:T(2,128)(2,1)S(1)} %get-tuple-element.45.taps), custom_call_target="tpu_custom_call" | custom-call | tf_op jit(solution)/shard_map/matrices/pallas_call | solution.py:371
  5.0 0.3 %prepare.1 = (f32[8,24,128]{2,1,0:T(8,128)S(1)}, s32[2,2,8,128]{3,2,1,0:T(8,128)S(1)}, s32[4,8,32]{2,1,0:T(8,128)S(1)}) custom-call(f32[4,8]{1,0:T(4,128)S(1)} %get-tuple-element.38.centre, f32[4,8]{1,0:T(4,128)S(1)} %get-tuple-element.39.width, f32[3,4,8]{2,1,0:T(4,128)S(1)} %get-tuple-element.40.colour, f32[4,8]{1,0:T(4,128)S(1)} %get-tuple-element.41.opacity, ...), custom_call_target="tpu_custom_call" | custom-call | tf_op jit(solution)/shard_map/prepare/pallas_call | solution.py:363
  5.3 3.2 %collective-permute-start.1 = (bf16[16,16,256]{2,1,0:T(8,128)(2,1)S(1)}, bf16[16,16,256]{2,1,0:T(8,128)(2,1)S(1)}, u32[]{:S(2)}, u32[]{:S(2)}) collective-permute-start(bf16[16,16,256]{2,1,0:T(8,128)(2,1)S(1)} %get-tuple-element.56.near0), channel_id=1, source_target_pairs={{0,2},{8,10},{16,18},{24,26},{1,3},{9,11},{17,19},{25,27},{4,6},{1... | collective-permute-start | bytes 393224 | tf_op jit(solution)/shard_map/ppermute | solution.py:345
  8.5 0.0 collective-permute-start.3
  8.5 0.0 collective-permute-done.halo
  8.5 0.3 %strip0.1 = bf16[16,16,256]{2,1,0:T(8,128)(2,1)S(1)} custom-call(bf16[256,768]{1,0:T(8,128)(2,1)S(1)} %get-tuple-element.52.mx, bf16[16,16,256]{2,1,0:T(8,128)(2,1)S(1)} %get-tuple-element.53.near0, bf16[16,16,256]{2,1,0:T(8,128)(2,1)S(1)} %get-tuple-element.54.near1, bf16[16,16,256]{2,1,0:T(8,128)(2,1)S(1)} %collective-permute-done.halo), custom_call_target="tpu_custom_call" | custom-call | tf_op jit(solution)/shard_map/strip0/pallas_call | solution.py:382
  8.8 1.6 %collective-permute-start.4 = (bf16[16,16,256]{2,1,0:T(8,128)(2,1)S(1)}, bf16[16,16,256]{2,1,0:T(8,128)(2,1)S(1)}, u32[]{:S(2)}, u32[]{:S(2)}) collective-permute-start(bf16[16,16,256]{2,1,0:T(8,128)(2,1)S(1)} %strip0.1), channel_id=1, source_target_pairs={{0,1},{8,9},{16,17},{24,25},{2,3},{10,11},{18,19},{26,27},{4,5},{1... | collective-permute-start | bytes 393224 | tf_op jit(solution)/shard_map/ppermute | solution.py:345
  10.4 0.0 collective-permute-done.2.halo
  10.4 0.3 %strip1.1 = bf16[16,16,256]{2,1,0:T(8,128)(2,1)S(1)} custom-call(bf16[256,768]{1,0:T(8,128)(2,1)S(1)} %get-tuple-element.52.mx, bf16[16,16,256]{2,1,0:T(8,128)(2,1)S(1)} %get-tuple-element.53.near0, bf16[16,16,256]{2,1,0:T(8,128)(2,1)S(1)} %get-tuple-element.54.near1, bf16[16,16,256]{2,1,0:T(8,128)(2,1)S(1)} %collective-permute-done.2.halo), custom_call_target="tpu_custom_call" | custom-call | tf_op jit(solution)/shard_map/strip1/pallas_call | solution.py:382
  10.7 0.6 %collective-permute-start.5 = (bf16[16,16,256]{2,1,0:T(8,128)(2,1)S(1)}, bf16[16,16,256]{2,1,0:T(8,128)(2,1)S(1)}, u32[]{:S(2)}, u32[]{:S(2)}) collective-permute-start(bf16[16,16,256]{2,1,0:T(8,128)(2,1)S(1)} %strip1.1), channel_id=1, source_target_pairs={{0,1},{8,9},{16,17},{24,25},{2,3},{10,11},{18,19},{26,27},{4,5},{1... | collective-permute-start | bytes 393224 | tf_op jit(solution)/shard_map/ppermute | solution.py:345
  11.3 1.1 %cells0.1 = (f32[3,2,16,16,256]{4,3,2,1,0:T(8,128)S(1)}, f32[16,128]{1,0:T(8,128)S(1)}) custom-call(f32[2,2,16,16,256]{4,3,2,1,0:T(8,128)S(1)} %get-tuple-element.58.held, f32[8,24,128]{2,1,0:T(8,128)S(1)} %get-tuple-element.59.table, s32[2,2,8,128]{3,2,1,0:T(8,128)S(1)} %get-tuple-element.60.signs), custom_call_target="tpu_custom_call" | custom-call | flops 26214400000 | bytes 262144 | tf_op jit(solution)/shard_map/cells0/pallas_call | solution.py:391
  12.4 1.1 %cells1.1 = (f32[3,2,16,16,256]{4,3,2,1,0:T(8,128)S(1)}, f32[16,128]{1,0:T(8,128)S(1)}) custom-call(f32[2,2,16,16,256]{4,3,2,1,0:T(8,128)S(1)} %get-tuple-element.58.held, f32[8,24,128]{2,1,0:T(8,128)S(1)} %get-tuple-element.59.table, s32[2,2,8,128]{3,2,1,0:T(8,128)S(1)} %get-tuple-element.60.signs), custom_call_target="tpu_custom_call" | custom-call | flops 262144 | bytes 262144 | tf_op jit(solution)/shard_map/cells1/pallas_call | solution.py:391
  13.5 0.9 %own.1 = (f32[3,16,128]{2,1,0:T(8,128)S(1)}, f32[1,2,256,256]{3,2,1,0:T(8,128)S(1)}) custom-call(bf16[16,16,256]{2,1,0:T(8,128)(2,1)S(1)} %strip0.1, bf16[16,16,256]{2,1,0:T(8,128)(2,1)S(1)} %collective-permute-done.1.halo0, bf16[16,16,256]{2,1,0:T(8,128)(2,1)S(1)} %strip1.1, bf16[16,16,256]{2,1,0:T(8,128)(2,1)S(1)} %collective-permute-done.3.halo1, ...), custom_call_target="tpu_custom_call" | custom-call | tf_op jit(solution)/shard_map/own/pallas_call | solution.py:407
  14.4 0.7 %collective-permute-done.4.refs_2_ = bf16[16,16,256]{2,1,0:T(8,128)(2,1)S(1)} collective-permute-done((bf16[16,16,256]{2,1,0:T(8,128)(2,1)S(1)}, bf16[16,16,256]{2,1,0:T(8,128)(2,1)S(1)}, u32[]{:S(2)}, u32[]{:S(2)}) %collective-permute-start.4) | collective-permute-done | bytes 131104 | tf_op jit(solution)/shard_map/ppermute | solution.py:345
  15.2 2.4 %collective-permute-done.5.refs_3_ = bf16[16,16,256]{2,1,0:T(8,128)(2,1)S(1)} collective-permute-done((bf16[16,16,256]{2,1,0:T(8,128)(2,1)S(1)}, bf16[16,16,256]{2,1,0:T(8,128)(2,1)S(1)}, u32[]{:S(2)}, u32[]{:S(2)}) %collective-permute-start.5) | collective-permute-done | bytes 131104 | tf_op jit(solution)/shard_map/ppermute | solution.py:345
  17.6 0.6 %last.1 = (f32[2,4,8,32]{3,2,1,0:T(8,128)S(1)}, f32[2,4,8,32]{3,2,1,0:T(8,128)S(1)}) custom-call(bf16[256,768]{1,0:T(8,128)(2,1)S(1)} %get-tuple-element.46.my.refs_0_, f32[1,2,256,256]{3,2,1,0:T(8,128)S(1)} %get-tuple-element.62.refs_1_, bf16[16,16,256]{2,1,0:T(8,128)(2,1)S(1)} %collective-permute-done.4.refs_2_, ...), custom_call_target="tpu_custom_call" | custom-call | tf_op jit(solution)/shard_map/last/pallas_call | solution.py:422
  18.2 0.1 collective-permute-start.6
  18.2 1.2 %collective-permute-done.6.theirs = f32[2,4,8,32]{3,2,1,0:T(8,128)S(1)} collective-permute-done((f32[2,4,8,32]{3,2,1,0:T(8,128)S(1)}, f32[2,4,8,32]{3,2,1,0:T(8,128)S(1)}, u32[]{:S(2)}, u32[]{:S(2)}) %collective-permute-start.6) | collective-permute-done | bytes 8224 | tf_op jit(solution)/shard_map/ppermute | solution.py:431
  19.4 1.6 %collective-permute-start.7 = (f32[1,4,8,32]{3,2,1,0:T(8,128)S(1)}, f32[1,4,8,32]{3,2,1,0:T(8,128)S(1)}, u32[]{:S(2)}, u32[]{:S(2)}) collective-permute-start(f32[1,4,8,32]{3,2,1,0:T(8,128)S(1)} %get-tuple-element.70), channel_id=1, source_target_pairs={{0,16},{8,24},{16,0},{24,8},{1,17},{9,25},{17,1},{25,9},{2,18},{10... | collective-permute-start | bytes 12296 | tf_op jit(solution)/shard_map/ppermute | solution.py:431
  21.0 2.2 %collective-permute-done.7.theirs = f32[1,4,8,32]{3,2,1,0:T(8,128)S(1)} collective-permute-done((f32[1,4,8,32]{3,2,1,0:T(8,128)S(1)}, f32[1,4,8,32]{3,2,1,0:T(8,128)S(1)}, u32[]{:S(2)}, u32[]{:S(2)}) %collective-permute-start.7) | collective-permute-done | bytes 4128 | tf_op jit(solution)/shard_map/ppermute | solution.py:431
  23.3 0.6 %merge1.1 = f32[4,1,1,8,32]{4,3,2,1,0:T(8,128)} custom-call(s32[4,8,32]{2,1,0:T(8,128)S(1)} %get-tuple-element.44.order_map, f32[1,4,8,32]{3,2,1,0:T(8,128)S(1)} %get-tuple-element.69.kept, f32[1,4,8,32]{3,2,1,0:T(8,128)S(1)} %collective-permute-done.7.theirs), custom_call_target="tpu_custom_call" | custom-call | tf_op jit(solution)/shard_map/merge1/pallas_call | solution.py:434
  (3 shorter events, 0.0 us)
Async XLA Ops:
  1.3 7.2 %collective-permute-start = (bf16[16,16,256]{2,1,0:T(8,128)(2,1)S(1)}, bf16[16,16,256]{2,1,0:T(8,128)(2,1)S(1)}, u32[]{:S(2)}, u32[]{:S(2)}) collective-permute-start(bf16[16,16,256]{2,1,0:T(8,128)(2,1)S(1)} %get-tuple-element.53.near0), channel_id=1, source_target_pairs={{0,2},{8,10},{16,18},{24,26},{1,3},{9,11},{17,19},{25,27},{4,6},{1... | collective-permute-start | bytes 393224 | tf_op jit(solution)/shard_map/ppermute | solution.py:345
  4.4 6.0 %collective-permute-start.2 = (bf16[16,16,256]{2,1,0:T(8,128)(2,1)S(1)}, bf16[16,16,256]{2,1,0:T(8,128)(2,1)S(1)}, u32[]{:S(2)}, u32[]{:S(2)}) collective-permute-start(bf16[16,16,256]{2,1,0:T(8,128)(2,1)S(1)} %get-tuple-element.54.near1), channel_id=1, source_target_pairs={{0,8},{16,24},{1,9},{17,25},{2,4},{10,12},{18,20},{26,28},{3,5},{1... | collective-permute-start | bytes 393224 | tf_op jit(solution)/shard_map/ppermute | solution.py:345
  5.3 8.2 %collective-permute-start.1 = (bf16[16,16,256]{2,1,0:T(8,128)(2,1)S(1)}, bf16[16,16,256]{2,1,0:T(8,128)(2,1)S(1)}, u32[]{:S(2)}, u32[]{:S(2)}) collective-permute-start(bf16[16,16,256]{2,1,0:T(8,128)(2,1)S(1)} %get-tuple-element.56.near0), channel_id=1, source_target_pairs={{0,2},{8,10},{16,18},{24,26},{1,3},{9,11},{17,19},{25,27},{4,6},{1... | collective-permute-start | bytes 393224 | tf_op jit(solution)/shard_map/ppermute | solution.py:345
  8.5 5.0 %collective-permute-start.3 = (bf16[16,16,256]{2,1,0:T(8,128)(2,1)S(1)}, bf16[16,16,256]{2,1,0:T(8,128)(2,1)S(1)}, u32[]{:S(2)}, u32[]{:S(2)}) collective-permute-start(bf16[16,16,256]{2,1,0:T(8,128)(2,1)S(1)} %get-tuple-element.57.near1), channel_id=1, source_target_pairs={{0,8},{16,24},{1,9},{17,25},{2,4},{10,12},{18,20},{26,28},{3,5},{1... | collective-permute-start | bytes 393224 | tf_op jit(solution)/shard_map/ppermute | solution.py:345
  8.8 6.4 %collective-permute-start.4 = (bf16[16,16,256]{2,1,0:T(8,128)(2,1)S(1)}, bf16[16,16,256]{2,1,0:T(8,128)(2,1)S(1)}, u32[]{:S(2)}, u32[]{:S(2)}) collective-permute-start(bf16[16,16,256]{2,1,0:T(8,128)(2,1)S(1)} %strip0.1), channel_id=1, source_target_pairs={{0,1},{8,9},{16,17},{24,25},{2,3},{10,11},{18,19},{26,27},{4,5},{1... | collective-permute-start | bytes 393224 | tf_op jit(solution)/shard_map/ppermute | solution.py:345
  10.7 6.9 %collective-permute-start.5 = (bf16[16,16,256]{2,1,0:T(8,128)(2,1)S(1)}, bf16[16,16,256]{2,1,0:T(8,128)(2,1)S(1)}, u32[]{:S(2)}, u32[]{:S(2)}) collective-permute-start(bf16[16,16,256]{2,1,0:T(8,128)(2,1)S(1)} %strip1.1), channel_id=1, source_target_pairs={{0,1},{8,9},{16,17},{24,25},{2,3},{10,11},{18,19},{26,27},{4,5},{1... | collective-permute-start | bytes 393224 | tf_op jit(solution)/shard_map/ppermute | solution.py:345
  18.2 1.3 %collective-permute-start.6 = (f32[2,4,8,32]{3,2,1,0:T(8,128)S(1)}, f32[2,4,8,32]{3,2,1,0:T(8,128)S(1)}, u32[]{:S(2)}, u32[]{:S(2)}) collective-permute-start(f32[2,4,8,32]{3,2,1,0:T(8,128)S(1)} %get-tuple-element.68), channel_id=1, source_target_pairs={{0,8},{8,0},{16,24},{24,16},{1,9},{9,1},{17,25},{25,17},{2,10},{10... | collective-permute-start | bytes 24584 | tf_op jit(solution)/shard_map/ppermute | solution.py:431
  19.4 3.8 %collective-permute-start.7 = (f32[1,4,8,32]{3,2,1,0:T(8,128)S(1)}, f32[1,4,8,32]{3,2,1,0:T(8,128)S(1)}, u32[]{:S(2)}, u32[]{:S(2)}) collective-permute-start(f32[1,4,8,32]{3,2,1,0:T(8,128)S(1)} %get-tuple-element.70), channel_id=1, source_target_pairs={{0,16},{8,24},{16,0},{24,8},{1,17},{9,25},{17,1},{25,9},{2,18},{10... | collective-permute-start | bytes 12296 | tf_op jit(solution)/shard_map/ppermute | solution.py:431

commit v16 on v15

--- a/solution.py
+++ b/solution.py
@@ -43,12 +43,12 @@
 class Place:
     def __init__(self):
         self.depth = lax.axis_index("depth")
-        self.half, self.has_x = self.sides("sx")
-        self.group, self.has_y = self.sides("sy")
-
-    def sides(self, axis):
+        self.half, self.has_x = self.sides("sx", 1)
+        self.group, self.has_y = self.sides("sy", 0)
+
+    def sides(self, axis, shift):
         at, last = lax.axis_index(axis), lax.axis_size(axis) - 1
-        parity = lax.rem(at, 2)
+        parity = lax.rem(at + shift, 2)
         upper, lower = at < last, at > 0
         order = (1 - parity, parity)
         either = lambda side: jnp.where(side == 1, upper.astype(jnp.int32), lower.astype(jnp.int32))
@@ -367,7 +367,7 @@
         [struct((4 * bricks, 6 * bumps, 128), F32), struct((2, 2, 8, 128), jnp.int32)]
         + [struct((depth_count, block, rows_y), jnp.int32)],
     )(*tables[1:])
-    halo_x = [[swap(coarse[0][h], 1, h) for h in range(2)], None]
+    halo_x = [[swap(coarse[0][h], 1, 1 - h) for h in range(2)], None]
     mx, my = call(
         functools.partial(matrices_kernel, rim),
         "matrices",
@@ -376,7 +376,7 @@
         [pltpu.VMEM((8, 128), F32)],
     )(tables[0])
     *others, table, mx = lax.optimization_barrier((*coarse[1], table, mx))
-    halo_x[1] = [swap(others[h], 1, h) for h in range(2)]
+    halo_x[1] = [swap(others[h], 1, 1 - h) for h in range(2)]
     strips, halo_y = [], []
     for h in range(2):
         strip = call(functools.partial(strip_kernel, rim, h), f"strip{h}", [VMEM] * 4, piece)(

time: 24 us -> 23.2 us (0.967)
  waiting for transfers between devices: 6.59 us -> 5.68 us
    ppermute x6, waiting for transfers between devices: 3.16 us -> 2.25 us  [swap(): return lax.ppermute(piece, axes, swaps(counts, axis, shift))]
  transfers between devices with their start and end apart: 8 -> 8, of which waited for: 4 -> 4; matrix products, arithmetic and copies ran while one was open for 0% -> 0% of each run, Pallas kernels for 19% -> 20%
where the time goes in v16:
time: 23.2 us; the launch traced here: 23 us
  starting transfers between devices  10.2 us (44%)
  Pallas kernels  7.08 us (31%)
  waiting for transfers between devices  5.68 us (24%)
    ppermute x6, starting transfers between devices, swap(): return lax.ppermute(piece, axes, swaps(counts, axis, shift))  8.54 us
    ppermute x2, waiting for transfers between devices, per_device(): lax.ppermute(given, 'depth', [(i, i ^ 1 << level) for i in range(depth_co...  3.43 us
    ppermute x6, waiting for transfers between devices, swap(): return lax.ppermute(piece, axes, swaps(counts, axis, shift))  2.25 us
    pallas_call x2, Pallas kernels, per_device(): call(functools.partial(cells_kernel, rim, bumps, g), f'cells{g}', [VMEM]...  2.25 us
    ppermute x2, starting transfers between devices, per_device(): lax.ppermute(given, 'depth', [(i, i ^ 1 << level) for i in range(depth_co...  1.64 us
    pallas_call x1, Pallas kernels, per_device(): call(functools.partial(first_kernel, rim), 'first', [HBM] * (1 + len(tabl...  1.31 us
    pallas_call x1, Pallas kernels, per_device(): call(functools.partial(own_kernel, rim, early), 'own', [VMEM] * (9 if ear...  0.9 us
    pallas_call x2, Pallas kernels, per_device(): call(functools.partial(merge_kernel, level), f'merge{level}', [VMEM] * 3,...  0.63 us
  transfers between devices with their start and end apart: 8, of which 4 were waited for; matrix products, arithmetic and copies ran while one was open for 0% of the time, Pallas kernels for 20%

profile of v16, /device:TPU:0, one launch (start us, length us, event | category | flops | bytes accessed | tf_op | source)
XLA Modules:
  0.0 23.0 jit_solution(1080974501586025910)
XLA Ops:
  0.0 1.3 %first.1 = (f32[2,2,16,16,256]{4,3,2,1,0:T(8,128)S(1)}, bf16[16,16,256]{2,1,0:T(8,128)(2,1)S(1)}, bf16[16,16,256]{2,1,0:T(8,128)(2,1)S(1)}, bf16[16,16,256]{2,1,...) custom-call(f32[32,32,256]{2,1,0:T(8,128)} %density.1, ...), custom_call_target="tpu_custom_call" | custom-call | tf_op jit(solution)/shard_map/first/pallas_call | solution.py:352
  1.3 0.5 %collective-permute-start = (bf16[16,16,256]{2,1,0:T(8,128)(2,1)S(1)}, bf16[16,16,256]{2,1,0:T(8,128)(2,1)S(1)}, u32[]{:S(2)}, u32[]{:S(2)}) collective-permute-start(bf16[16,16,256]{2,1,0:T(8,128)(2,1)S(1)} %get-tuple-element.53.near0), channel_id=1, source_target_pairs={{0,8},{16,24},{1,9},{17,25},{2,4},{10,12},{18,20},{26,28},{3,5},{1... | collective-permute-start | bytes 393224 | tf_op jit(solution)/shard_map/ppermute | solution.py:345
  1.8 4.1 %collective-permute-start.2 = (bf16[16,16,256]{2,1,0:T(8,128)(2,1)S(1)}, bf16[16,16,256]{2,1,0:T(8,128)(2,1)S(1)}, u32[]{:S(2)}, u32[]{:S(2)}) collective-permute-start(bf16[16,16,256]{2,1,0:T(8,128)(2,1)S(1)} %get-tuple-element.54.near1), channel_id=1, source_target_pairs={{0,2},{8,10},{16,18},{24,26},{1,3},{9,11},{17,19},{25,27},{4,6},{1... | collective-permute-start | bytes 393224 | tf_op jit(solution)/shard_map/ppermute | solution.py:345
  6.0 0.6 %matrices.1 = (bf16[256,768]{1,0:T(8,128)(2,1)S(1)}, bf16[256,768]{1,0:T(8,128)(2,1)S(1)}) custom-call(bf16[2,33]{1,0:T(2,128)(2,1)S(1)} %get-tuple-element.45.taps), custom_call_target="tpu_custom_call" | custom-call | tf_op jit(solution)/shard_map/matrices/pallas_call | solution.py:371
  6.6 0.3 %prepare.1 = (f32[8,24,128]{2,1,0:T(8,128)S(1)}, s32[2,2,8,128]{3,2,1,0:T(8,128)S(1)}, s32[4,8,32]{2,1,0:T(8,128)S(1)}) custom-call(f32[4,8]{1,0:T(4,128)S(1)} %get-tuple-element.38.centre, f32[4,8]{1,0:T(4,128)S(1)} %get-tuple-element.39.width, f32[3,4,8]{2,1,0:T(4,128)S(1)} %get-tuple-element.40.colour, f32[4,8]{1,0:T(4,128)S(1)} %get-tuple-element.41.opacity, ...), custom_call_target="tpu_custom_call" | custom-call | tf_op jit(solution)/shard_map/prepare/pallas_call | solution.py:363
  6.9 0.1 collective-permute-start.1
  7.0 1.6 %collective-permute-start.3 = (bf16[16,16,256]{2,1,0:T(8,128)(2,1)S(1)}, bf16[16,16,256]{2,1,0:T(8,128)(2,1)S(1)}, u32[]{:S(2)}, u32[]{:S(2)}) collective-permute-start(bf16[16,16,256]{2,1,0:T(8,128)(2,1)S(1)} %get-tuple-element.57.near1), channel_id=1, source_target_pairs={{0,2},{8,10},{16,18},{24,26},{1,3},{9,11},{17,19},{25,27},{4,6},{1... | collective-permute-start | bytes 393224 | tf_op jit(solution)/shard_map/ppermute | solution.py:345
  8.6 0.3 %strip0.1 = bf16[16,16,256]{2,1,0:T(8,128)(2,1)S(1)} custom-call(bf16[256,768]{1,0:T(8,128)(2,1)S(1)} %get-tuple-element.52.mx, bf16[16,16,256]{2,1,0:T(8,128)(2,1)S(1)} %get-tuple-element.53.near0, bf16[16,16,256]{2,1,0:T(8,128)(2,1)S(1)} %get-tuple-element.54.near1, bf16[16,16,256]{2,1,0:T(8,128)(2,1)S(1)} %collective-permute-done.halo), custom_call_target="tpu_custom_call" | custom-call | tf_op jit(solution)/shard_map/strip0/pallas_call | solution.py:382
  8.9 1.6 %collective-permute-start.4 = (bf16[16,16,256]{2,1,0:T(8,128)(2,1)S(1)}, bf16[16,16,256]{2,1,0:T(8,128)(2,1)S(1)}, u32[]{:S(2)}, u32[]{:S(2)}) collective-permute-start(bf16[16,16,256]{2,1,0:T(8,128)(2,1)S(1)} %strip0.1), channel_id=1, source_target_pairs={{0,1},{8,9},{16,17},{24,25},{2,3},{10,11},{18,19},{26,27},{4,5},{1... | collective-permute-start | bytes 393224 | tf_op jit(solution)/shard_map/ppermute | solution.py:345
  10.5 0.0 collective-permute-done.2.halo
  10.5 0.3 %strip1.1 = bf16[16,16,256]{2,1,0:T(8,128)(2,1)S(1)} custom-call(bf16[256,768]{1,0:T(8,128)(2,1)S(1)} %get-tuple-element.52.mx, bf16[16,16,256]{2,1,0:T(8,128)(2,1)S(1)} %get-tuple-element.53.near0, bf16[16,16,256]{2,1,0:T(8,128)(2,1)S(1)} %get-tuple-element.54.near1, bf16[16,16,256]{2,1,0:T(8,128)(2,1)S(1)} %collective-permute-done.2.halo), custom_call_target="tpu_custom_call" | custom-call | tf_op jit(solution)/shard_map/strip1/pallas_call | solution.py:382
  10.8 0.6 %collective-permute-start.5 = (bf16[16,16,256]{2,1,0:T(8,128)(2,1)S(1)}, bf16[16,16,256]{2,1,0:T(8,128)(2,1)S(1)}, u32[]{:S(2)}, u32[]{:S(2)}) collective-permute-start(bf16[16,16,256]{2,1,0:T(8,128)(2,1)S(1)} %strip1.1), channel_id=1, source_target_pairs={{0,1},{8,9},{16,17},{24,25},{2,3},{10,11},{18,19},{26,27},{4,5},{1... | collective-permute-start | bytes 393224 | tf_op jit(solution)/shard_map/ppermute | solution.py:345
  11.3 1.1 %cells0.1 = (f32[3,2,16,16,256]{4,3,2,1,0:T(8,128)S(1)}, f32[16,128]{1,0:T(8,128)S(1)}) custom-call(f32[2,2,16,16,256]{4,3,2,1,0:T(8,128)S(1)} %get-tuple-element.58.held, f32[8,24,128]{2,1,0:T(8,128)S(1)} %get-tuple-element.59.table, s32[2,2,8,128]{3,2,1,0:T(8,128)S(1)} %get-tuple-element.60.signs), custom_call_target="tpu_custom_call" | custom-call | flops 26214400000 | bytes 262144 | tf_op jit(solution)/shard_map/cells0/pallas_call | solution.py:391
  12.5 1.1 %cells1.1 = (f32[3,2,16,16,256]{4,3,2,1,0:T(8,128)S(1)}, f32[16,128]{1,0:T(8,128)S(1)}) custom-call(f32[2,2,16,16,256]{4,3,2,1,0:T(8,128)S(1)} %get-tuple-element.58.held, f32[8,24,128]{2,1,0:T(8,128)S(1)} %get-tuple-element.59.table, s32[2,2,8,128]{3,2,1,0:T(8,128)S(1)} %get-tuple-element.60.signs), custom_call_target="tpu_custom_call" | custom-call | flops 262144 | bytes 262144 | tf_op jit(solution)/shard_map/cells1/pallas_call | solution.py:391
  13.6 0.0 collective-permute-done.3.halo1
  13.6 0.9 %own.1 = (f32[3,16,128]{2,1,0:T(8,128)S(1)}, f32[1,2,256,256]{3,2,1,0:T(8,128)S(1)}) custom-call(bf16[16,16,256]{2,1,0:T(8,128)(2,1)S(1)} %strip0.1, bf16[16,16,256]{2,1,0:T(8,128)(2,1)S(1)} %collective-permute-done.1.halo0, bf16[16,16,256]{2,1,0:T(8,128)(2,1)S(1)} %strip1.1, bf16[16,16,256]{2,1,0:T(8,128)(2,1)S(1)} %collective-permute-done.3.halo1, ...), custom_call_target="tpu_custom_call" | custom-call | tf_op jit(solution)/shard_map/own/pallas_call | solution.py:407
  14.5 0.7 %collective-permute-done.4.refs_2_ = bf16[16,16,256]{2,1,0:T(8,128)(2,1)S(1)} collective-permute-done((bf16[16,16,256]{2,1,0:T(8,128)(2,1)S(1)}, bf16[16,16,256]{2,1,0:T(8,128)(2,1)S(1)}, u32[]{:S(2)}, u32[]{:S(2)}) %collective-permute-start.4) | collective-permute-done | bytes 131104 | tf_op jit(solution)/shard_map/ppermute | solution.py:345
  15.2 1.6 %collective-permute-done.5.refs_3_ = bf16[16,16,256]{2,1,0:T(8,128)(2,1)S(1)} collective-permute-done((bf16[16,16,256]{2,1,0:T(8,128)(2,1)S(1)}, bf16[16,16,256]{2,1,0:T(8,128)(2,1)S(1)}, u32[]{:S(2)}, u32[]{:S(2)}) %collective-permute-start.5) | collective-permute-done | bytes 131104 | tf_op jit(solution)/shard_map/ppermute | solution.py:345
  16.8 0.6 %last.1 = (f32[2,4,8,32]{3,2,1,0:T(8,128)S(1)}, f32[2,4,8,32]{3,2,1,0:T(8,128)S(1)}) custom-call(bf16[256,768]{1,0:T(8,128)(2,1)S(1)} %get-tuple-element.46.my.refs_0_, f32[1,2,256,256]{3,2,1,0:T(8,128)S(1)} %get-tuple-element.62.refs_1_, bf16[16,16,256]{2,1,0:T(8,128)(2,1)S(1)} %collective-permute-done.4.refs_2_, ...), custom_call_target="tpu_custom_call" | custom-call | tf_op jit(solution)/shard_map/last/pallas_call | solution.py:422
  17.3 0.1 collective-permute-start.6
  17.4 1.2 %collective-permute-done.6.theirs = f32[2,4,8,32]{3,2,1,0:T(8,128)S(1)} collective-permute-done((f32[2,4,8,32]{3,2,1,0:T(8,128)S(1)}, f32[2,4,8,32]{3,2,1,0:T(8,128)S(1)}, u32[]{:S(2)}, u32[]{:S(2)}) %collective-permute-start.6) | collective-permute-done | bytes 8224 | tf_op jit(solution)/shard_map/ppermute | solution.py:431
  18.6 1.6 %collective-permute-start.7 = (f32[1,4,8,32]{3,2,1,0:T(8,128)S(1)}, f32[1,4,8,32]{3,2,1,0:T(8,128)S(1)}, u32[]{:S(2)}, u32[]{:S(2)}) collective-permute-start(f32[1,4,8,32]{3,2,1,0:T(8,128)S(1)} %get-tuple-element.70), channel_id=1, source_target_pairs={{0,16},{8,24},{16,0},{24,8},{1,17},{9,25},{17,1},{25,9},{2,18},{10... | collective-permute-start | bytes 12296 | tf_op jit(solution)/shard_map/ppermute | solution.py:431
  20.2 2.2 %collective-permute-done.7.theirs = f32[1,4,8,32]{3,2,1,0:T(8,128)S(1)} collective-permute-done((f32[1,4,8,32]{3,2,1,0:T(8,128)S(1)}, f32[1,4,8,32]{3,2,1,0:T(8,128)S(1)}, u32[]{:S(2)}, u32[]{:S(2)}) %collective-permute-start.7) | collective-permute-done | bytes 4128 | tf_op jit(solution)/shard_map/ppermute | solution.py:431
  22.4 0.6 %merge1.1 = f32[4,1,1,8,32]{4,3,2,1,0:T(8,128)} custom-call(s32[4,8,32]{2,1,0:T(8,128)S(1)} %get-tuple-element.44.order_map, f32[1,4,8,32]{3,2,1,0:T(8,128)S(1)} %get-tuple-element.69.kept, f32[1,4,8,32]{3,2,1,0:T(8,128)S(1)} %collective-permute-done.7.theirs), custom_call_target="tpu_custom_call" | custom-call | tf_op jit(solution)/shard_map/merge1/pallas_call | solution.py:434
  (3 shorter events, 0.0 us)
Async XLA Ops:
  1.3 7.3 %collective-permute-start = (bf16[16,16,256]{2,1,0:T(8,128)(2,1)S(1)}, bf16[16,16,256]{2,1,0:T(8,128)(2,1)S(1)}, u32[]{:S(2)}, u32[]{:S(2)}) collective-permute-start(bf16[16,16,256]{2,1,0:T(8,128)(2,1)S(1)} %get-tuple-element.53.near0), channel_id=1, source_target_pairs={{0,8},{16,24},{1,9},{17,25},{2,4},{10,12},{18,20},{26,28},{3,5},{1... | collective-permute-start | bytes 393224 | tf_op jit(solution)/shard_map/ppermute | solution.py:345
  1.8 8.6 %collective-permute-start.2 = (bf16[16,16,256]{2,1,0:T(8,128)(2,1)S(1)}, bf16[16,16,256]{2,1,0:T(8,128)(2,1)S(1)}, u32[]{:S(2)}, u32[]{:S(2)}) collective-permute-start(bf16[16,16,256]{2,1,0:T(8,128)(2,1)S(1)} %get-tuple-element.54.near1), channel_id=1, source_target_pairs={{0,2},{8,10},{16,18},{24,26},{1,3},{9,11},{17,19},{25,27},{4,6},{1... | collective-permute-start | bytes 393224 | tf_op jit(solution)/shard_map/ppermute | solution.py:345
  6.9 6.7 %collective-permute-start.1 = (bf16[16,16,256]{2,1,0:T(8,128)(2,1)S(1)}, bf16[16,16,256]{2,1,0:T(8,128)(2,1)S(1)}, u32[]{:S(2)}, u32[]{:S(2)}) collective-permute-start(bf16[16,16,256]{2,1,0:T(8,128)(2,1)S(1)} %get-tuple-element.56.near0), channel_id=1, source_target_pairs={{0,8},{16,24},{1,9},{17,25},{2,4},{10,12},{18,20},{26,28},{3,5},{1... | collective-permute-start | bytes 393224 | tf_op jit(solution)/shard_map/ppermute | solution.py:345
  7.0 6.6 %collective-permute-start.3 = (bf16[16,16,256]{2,1,0:T(8,128)(2,1)S(1)}, bf16[16,16,256]{2,1,0:T(8,128)(2,1)S(1)}, u32[]{:S(2)}, u32[]{:S(2)}) collective-permute-start(bf16[16,16,256]{2,1,0:T(8,128)(2,1)S(1)} %get-tuple-element.57.near1), channel_id=1, source_target_pairs={{0,2},{8,10},{16,18},{24,26},{1,3},{9,11},{17,19},{25,27},{4,6},{1... | collective-permute-start | bytes 393224 | tf_op jit(solution)/shard_map/ppermute | solution.py:345
  8.9 6.3 %collective-permute-start.4 = (bf16[16,16,256]{2,1,0:T(8,128)(2,1)S(1)}, bf16[16,16,256]{2,1,0:T(8,128)(2,1)S(1)}, u32[]{:S(2)}, u32[]{:S(2)}) collective-permute-start(bf16[16,16,256]{2,1,0:T(8,128)(2,1)S(1)} %strip0.1), channel_id=1, source_target_pairs={{0,1},{8,9},{16,17},{24,25},{2,3},{10,11},{18,19},{26,27},{4,5},{1... | collective-permute-start | bytes 393224 | tf_op jit(solution)/shard_map/ppermute | solution.py:345
  10.8 6.0 %collective-permute-start.5 = (bf16[16,16,256]{2,1,0:T(8,128)(2,1)S(1)}, bf16[16,16,256]{2,1,0:T(8,128)(2,1)S(1)}, u32[]{:S(2)}, u32[]{:S(2)}) collective-permute-start(bf16[16,16,256]{2,1,0:T(8,128)(2,1)S(1)} %strip1.1), channel_id=1, source_target_pairs={{0,1},{8,9},{16,17},{24,25},{2,3},{10,11},{18,19},{26,27},{4,5},{1... | collective-permute-start | bytes 393224 | tf_op jit(solution)/shard_map/ppermute | solution.py:345
  17.3 1.3 %collective-permute-start.6 = (f32[2,4,8,32]{3,2,1,0:T(8,128)S(1)}, f32[2,4,8,32]{3,2,1,0:T(8,128)S(1)}, u32[]{:S(2)}, u32[]{:S(2)}) collective-permute-start(f32[2,4,8,32]{3,2,1,0:T(8,128)S(1)} %get-tuple-element.68), channel_id=1, source_target_pairs={{0,8},{8,0},{16,24},{24,16},{1,9},{9,1},{17,25},{25,17},{2,10},{10... | collective-permute-start | bytes 24584 | tf_op jit(solution)/shard_map/ppermute | solution.py:431
  18.6 3.8 %collective-permute-start.7 = (f32[1,4,8,32]{3,2,1,0:T(8,128)S(1)}, f32[1,4,8,32]{3,2,1,0:T(8,128)S(1)}, u32[]{:S(2)}, u32[]{:S(2)}) collective-permute-start(f32[1,4,8,32]{3,2,1,0:T(8,128)S(1)} %get-tuple-element.70), channel_id=1, source_target_pairs={{0,16},{8,24},{16,0},{24,8},{1,17},{9,25},{17,1},{25,9},{2,18},{10... | collective-permute-start | bytes 12296 | tf_op jit(solution)/shard_map/ppermute | solution.py:431

commit v17 on v16

--- a/solution.py
+++ b/solution.py
@@ -65,24 +65,29 @@
 
 def first_kernel(rim, density, *refs):
     place = Place()
-    n_tables = (len(refs) - 6) // 2
-    tables, held, coarse = refs[:n_tables], refs[n_tables], refs[n_tables + 1:n_tables + 5]
-    tables_out, sems = refs[n_tables + 5:-1], refs[-1]
+    tables, held, coarse, refs = refs[:7], refs[7], refs[8:12], refs[12:]
+    mx, my, table, signs, order_map, *local_tables, padded, sems = refs
     copies = []
+    for i, (src, dst) in enumerate(zip(tables, local_tables)):
+        copies.append(pltpu.make_async_copy(src, dst, sems.at[4 + i]))
+    parts = []
     for g in range(2):
         for h in range(2):
             rows = density.at[half_rows(place, rim, h), group_rows(place, rim, g), :]
-            copies.append(pltpu.make_async_copy(rows, held.at[g, h], sems.at[2 * g + h]))
-    for i, (src, dst) in enumerate(zip(tables, tables_out)):
-        copies.append(pltpu.make_async_copy(src, dst, sems.at[4 + i]))
+            parts.append(pltpu.make_async_copy(rows, held.at[g, h], sems.at[2 * g + h]))
+    for copy in copies + parts:
+        copy.start()
     for copy in copies:
-        copy.start()
+        copy.wait()
+    taps, *local_tables = local_tables
+    padded[...] = jnp.zeros(padded.shape, F32)
+    padded[0:2, 0:taps.shape[1]] = taps[...].astype(F32)
+    mx[...], my[...] = blur_matrices(rim, place, padded[...])
+    look_up(rim, place, *local_tables, table, signs, order_map)
     for g in range(2):
         for h in range(2):
-            copies[2 * g + h].wait()
+            parts[2 * g + h].wait()
             coarse[2 * g + h][...] = held[g, h].astype(BF16)
-    for copy in copies[4:]:
-        copy.wait()
 
 
 def toeplitz(taps, rim):
@@ -117,16 +122,9 @@
     return parts
 
 
-def matrices_kernel(rim, taps, mx, my, padded):
-    padded[...] = jnp.zeros(padded.shape, F32)
-    padded[0:2, 0:taps.shape[1]] = taps[...].astype(F32)
-    mx[...], my[...] = blur_matrices(rim, Place(), padded[...])
-
-
-def prepare_kernel(
-    rim, centre, width, colour, opacity, brick_tf, view_order, table, signs, order_map
+def look_up(
+    rim, place, centre, width, colour, opacity, brick_tf, view_order, table, signs, order_map
 ):
-    place = Place()
     wide = width[...]
     rows = [centre[...], (-LOG2E) / (wide * wide), opacity[...] * (-LOG2E)]
     rows += [colour[c] * 0.5 for c in range(3)]
@@ -232,7 +230,7 @@
     out[...] = across.reshape(out.shape)
 
 
-def own_kernel(rim, early, strip0, halo0, strip1, halo1, mx, my, near0, near1, *refs):
+def own_kernel(rim, early, strip0, halo1, strip1, halo0, mx, my, near0, near1, *refs):
     place = Place()
     size = rim * rim
     across = [
@@ -349,34 +347,21 @@
         kernel_taps, tf_centre.T, tf_width.T, tf_color.T, tf_opacity.T, brick_tf, view_order
     )
     piece = struct((rim, rim, rows_z), BF16)
+    bricks = rows_z // 128
     held, *refs = call(
         functools.partial(first_kernel, rim),
         "first",
         [HBM] * (1 + len(tables)),
         [struct((2, 2, rim, rim, rows_z), F32)]
         + [piece] * 4
-        + [struct(t.shape, t.dtype) for t in tables],
-        [pltpu.SemaphoreType.DMA((4 + len(tables),))],
+        + [struct((size, 3 * size), BF16)] * 2
+        + [struct((4 * bricks, 6 * bumps, 128), F32), struct((2, 2, 8, 128), jnp.int32)]
+        + [struct((depth_count, block, rows_y), jnp.int32)],
+        [pltpu.VMEM(t.shape, t.dtype) for t in tables]
+        + [pltpu.VMEM((8, 128), F32), pltpu.SemaphoreType.DMA((4 + len(tables),))],
     )(in_hbm(density), *[in_hbm(t) for t in tables])
-    coarse, tables = [refs[0:2], refs[2:4]], refs[4:]
-    bricks = rows_z // 128
-    table, signs, order_map = call(
-        functools.partial(prepare_kernel, rim),
-        "prepare",
-        [VMEM] * (len(tables) - 1),
-        [struct((4 * bricks, 6 * bumps, 128), F32), struct((2, 2, 8, 128), jnp.int32)]
-        + [struct((depth_count, block, rows_y), jnp.int32)],
-    )(*tables[1:])
-    halo_x = [[swap(coarse[0][h], 1, 1 - h) for h in range(2)], None]
-    mx, my = call(
-        functools.partial(matrices_kernel, rim),
-        "matrices",
-        [VMEM],
-        [struct((size, 3 * size), BF16)] * 2,
-        [pltpu.VMEM((8, 128), F32)],
-    )(tables[0])
-    *others, table, mx = lax.optimization_barrier((*coarse[1], table, mx))
-    halo_x[1] = [swap(others[h], 1, 1 - h) for h in range(2)]
+    coarse, (mx, my, table, signs, order_map) = [refs[0:2], refs[2:4]], refs[4:]
+    halo_x = [[swap(coarse[g][h], 1, 1 - h) for h in range(2)] for g in range(2)]
     strips, halo_y = [], []
     for h in range(2):
         strip = call(functools.partial(strip_kernel, rim, h), f"strip{h}", [VMEM] * 4, piece)(
@@ -410,7 +395,7 @@
         [VMEM] * (9 if early else 8),
         [colours, unlit] if early else [unlit, piece, piece],
     )(
-        strips[0], halo_x[1][0], strips[1], halo_x[1][1], mx, my, *coarse[1], *([shaded[1]] if early else [])
+        strips[0], halo_x[1][1], strips[1], halo_x[1][0], mx, my, *coarse[1], *([shaded[1]] if early else [])
     )
     if early:
         light, partial = results

time: 23.2 us -> 22.4 us (0.966)
  starting transfers between devices: 10.2 us -> 9.5 us
  Pallas kernels: 7.08 us -> 6.55 us
  waiting for transfers between devices: 5.68 us -> 6.08 us
    pallas_call x2 -> x0, Pallas kernels: 0.88 us -> none  [the longest x1 0.62 us: per_device(): call(functools.partial(matrices_kernel, rim), 'matrices', [VMEM], [struct...]
    ppermute x6, starting transfers between devices: 8.54 us -> 7.86 us  [swap(): return lax.ppermute(piece, axes, swaps(counts, axis, shift))]
    ppermute x6, waiting for transfers between devices: 2.25 us -> 2.65 us  [swap(): return lax.ppermute(piece, axes, swaps(counts, axis, shift))]
    pallas_call x1, Pallas kernels: 1.31 us -> 1.6 us  [per_device(): call(functools.partial(first_kernel, rim), 'first', [HBM] * (1 + len(tabl...]
  transfers between devices with their start and end apart: 8 -> 8, of which waited for: 4 -> 4; matrix products, arithmetic and copies ran while one was open for 0% -> 0% of each run, Pallas kernels for 20% -> 17%
where the time goes in v17:
time: 22.4 us; the launch traced here: 22.2 us
  starting transfers between devices  9.5 us (42%)
  Pallas kernels  6.55 us (29%)
  waiting for transfers between devices  6.08 us (27%)
    ppermute x6, starting transfers between devices, swap(): return lax.ppermute(piece, axes, swaps(counts, axis, shift))  7.86 us
    ppermute x2, waiting for transfers between devices, per_device(): lax.ppermute(given, 'depth', [(i, i ^ 1 << level) for i in range(depth_co...  3.43 us
    ppermute x6, waiting for transfers between devices, swap(): return lax.ppermute(piece, axes, swaps(counts, axis, shift))  2.65 us
    pallas_call x2, Pallas kernels, per_device(): call(functools.partial(cells_kernel, rim, bumps, g), f'cells{g}', [VMEM]...  2.31 us
    ppermute x2, starting transfers between devices, per_device(): lax.ppermute(given, 'depth', [(i, i ^ 1 << level) for i in range(depth_co...  1.64 us
    pallas_call x1, Pallas kernels, per_device(): call(functools.partial(first_kernel, rim), 'first', [HBM] * (1 + len(tabl...  1.6 us
    pallas_call x1, Pallas kernels, per_device(): call(functools.partial(own_kernel, rim, early), 'own', [VMEM] * (9 if ear...  0.9 us
    pallas_call x2, Pallas kernels, per_device(): call(functools.partial(merge_kernel, level), f'merge{level}', [VMEM] * 3,...  0.63 us
  transfers between devices with their start and end apart: 8, of which 4 were waited for; matrix products, arithmetic and copies ran while one was open for 0% of the time, Pallas kernels for 17%

profile of v17, /device:TPU:0, one launch (start us, length us, event | category | flops | bytes accessed | tf_op | source)
XLA Modules:
  0.0 22.2 jit_solution(12398675284994794559)
XLA Ops:
  0.0 1.6 %first.1 = (f32[2,2,16,16,256]{4,3,2,1,0:T(8,128)S(1)}, bf16[16,16,256]{2,1,0:T(8,128)(2,1)S(1)}, bf16[16,16,256]{2,1,0:T(8,128)(2,1)S(1)}, bf16[16,16,256]{2,1,...) custom-call(f32[32,32,256]{2,1,0:T(8,128)} %density.1, ...), custom_call_target="tpu_custom_call" | custom-call | tf_op jit(solution)/shard_map/first/pallas_call | solution.py:351
  1.6 0.5 %collective-permute-start = (bf16[16,16,256]{2,1,0:T(8,128)(2,1)S(1)}, bf16[16,16,256]{2,1,0:T(8,128)(2,1)S(1)}, u32[]{:S(2)}, u32[]{:S(2)}) collective-permute-start(bf16[16,16,256]{2,1,0:T(8,128)(2,1)S(1)} %get-tuple-element.31.near0), channel_id=1, source_target_pairs={{0,8},{16,24},{1,9},{17,25},{2,4},{10,12},{18,20},{26,28},{3,5},{1... | collective-permute-start | bytes 393224 | tf_op jit(solution)/shard_map/ppermute | solution.py:343
  2.1 4.1 %collective-permute-start.2 = (bf16[16,16,256]{2,1,0:T(8,128)(2,1)S(1)}, bf16[16,16,256]{2,1,0:T(8,128)(2,1)S(1)}, u32[]{:S(2)}, u32[]{:S(2)}) collective-permute-start(bf16[16,16,256]{2,1,0:T(8,128)(2,1)S(1)} %get-tuple-element.32.near1), channel_id=1, source_target_pairs={{0,2},{8,10},{16,18},{24,26},{1,3},{9,11},{17,19},{25,27},{4,6},{1... | collective-permute-start | bytes 393224 | tf_op jit(solution)/shard_map/ppermute | solution.py:343
  6.3 0.0 collective-permute-start.1
  6.3 0.0 collective-permute-start.3
  6.3 0.0 collective-permute-done.halo
  6.3 0.3 %strip0.1 = bf16[16,16,256]{2,1,0:T(8,128)(2,1)S(1)} custom-call(bf16[256,768]{1,0:T(8,128)(2,1)S(1)} %get-tuple-element.30.mx, bf16[16,16,256]{2,1,0:T(8,128)(2,1)S(1)} %get-tuple-element.31.near0, bf16[16,16,256]{2,1,0:T(8,128)(2,1)S(1)} %get-tuple-element.32.near1, bf16[16,16,256]{2,1,0:T(8,128)(2,1)S(1)} %collective-permute-done.halo), custom_call_target="tpu_custom_call" | custom-call | tf_op jit(solution)/shard_map/strip0/pallas_call | solution.py:367
  6.6 1.6 %collective-permute-start.4 = (bf16[16,16,256]{2,1,0:T(8,128)(2,1)S(1)}, bf16[16,16,256]{2,1,0:T(8,128)(2,1)S(1)}, u32[]{:S(2)}, u32[]{:S(2)}) collective-permute-start(bf16[16,16,256]{2,1,0:T(8,128)(2,1)S(1)} %strip0.1), channel_id=1, source_target_pairs={{0,1},{8,9},{16,17},{24,25},{2,3},{10,11},{18,19},{26,27},{4,5},{1... | collective-permute-start | bytes 393224 | tf_op jit(solution)/shard_map/ppermute | solution.py:343
  8.2 2.5 %collective-permute-done.2.halo = bf16[16,16,256]{2,1,0:T(8,128)(2,1)S(1)} collective-permute-done((bf16[16,16,256]{2,1,0:T(8,128)(2,1)S(1)}, bf16[16,16,256]{2,1,0:T(8,128)(2,1)S(1)}, u32[]{:S(2)}, u32[]{:S(2)}) %collective-permute-start.2) | collective-permute-done | bytes 131104 | tf_op jit(solution)/shard_map/ppermute | solution.py:343
  10.6 0.3 %strip1.1 = bf16[16,16,256]{2,1,0:T(8,128)(2,1)S(1)} custom-call(bf16[256,768]{1,0:T(8,128)(2,1)S(1)} %get-tuple-element.30.mx, bf16[16,16,256]{2,1,0:T(8,128)(2,1)S(1)} %get-tuple-element.31.near0, bf16[16,16,256]{2,1,0:T(8,128)(2,1)S(1)} %get-tuple-element.32.near1, bf16[16,16,256]{2,1,0:T(8,128)(2,1)S(1)} %collective-permute-done.2.halo), custom_call_target="tpu_custom_call" | custom-call | tf_op jit(solution)/shard_map/strip1/pallas_call | solution.py:367
  10.9 1.6 %collective-permute-start.5 = (bf16[16,16,256]{2,1,0:T(8,128)(2,1)S(1)}, bf16[16,16,256]{2,1,0:T(8,128)(2,1)S(1)}, u32[]{:S(2)}, u32[]{:S(2)}) collective-permute-start(bf16[16,16,256]{2,1,0:T(8,128)(2,1)S(1)} %strip1.1), channel_id=1, source_target_pairs={{0,1},{8,9},{16,17},{24,25},{2,3},{10,11},{18,19},{26,27},{4,5},{1... | collective-permute-start | bytes 393224 | tf_op jit(solution)/shard_map/ppermute | solution.py:343
  12.5 1.2 %cells0.1 = (f32[3,2,16,16,256]{4,3,2,1,0:T(8,128)S(1)}, f32[16,128]{1,0:T(8,128)S(1)}) custom-call(f32[2,2,16,16,256]{4,3,2,1,0:T(8,128)S(1)} %get-tuple-element.36.held, f32[8,24,128]{2,1,0:T(8,128)S(1)} %get-tuple-element.37.table, s32[2,2,8,128]{3,2,1,0:T(8,128)S(1)} %get-tuple-element.38.signs), custom_call_target="tpu_custom_call" | custom-call | flops 26214400000 | bytes 262144 | tf_op jit(solution)/shard_map/cells0/pallas_call | solution.py:376
  13.7 1.2 %cells1.1 = (f32[3,2,16,16,256]{4,3,2,1,0:T(8,128)S(1)}, f32[16,128]{1,0:T(8,128)S(1)}) custom-call(f32[2,2,16,16,256]{4,3,2,1,0:T(8,128)S(1)} %get-tuple-element.36.held, f32[8,24,128]{2,1,0:T(8,128)S(1)} %get-tuple-element.37.table, s32[2,2,8,128]{3,2,1,0:T(8,128)S(1)} %get-tuple-element.38.signs), custom_call_target="tpu_custom_call" | custom-call | flops 262144 | bytes 262144 | tf_op jit(solution)/shard_map/cells1/pallas_call | solution.py:376
  14.8 0.0 collective-permute-done.1.halo1
  14.8 0.0 collective-permute-done.3.halo0
  14.8 0.9 %own.1 = (f32[3,16,128]{2,1,0:T(8,128)S(1)}, f32[1,2,256,256]{3,2,1,0:T(8,128)S(1)}) custom-call(bf16[16,16,256]{2,1,0:T(8,128)(2,1)S(1)} %strip0.1, bf16[16,16,256]{2,1,0:T(8,128)(2,1)S(1)} %collective-permute-done.1.halo1, bf16[16,16,256]{2,1,0:T(8,128)(2,1)S(1)} %strip1.1, bf16[16,16,256]{2,1,0:T(8,128)(2,1)S(1)} %collective-permute-done.3.halo0, ...), custom_call_target="tpu_custom_call" | custom-call | tf_op jit(solution)/shard_map/own/pallas_call | solution.py:392
  15.7 0.0 collective-permute-done.4.refs_2_
  15.8 0.2 collective-permute-done.5.refs_3_
  15.9 0.6 %last.1 = (f32[2,4,8,32]{3,2,1,0:T(8,128)S(1)}, f32[2,4,8,32]{3,2,1,0:T(8,128)S(1)}) custom-call(bf16[256,768]{1,0:T(8,128)(2,1)S(1)} %get-tuple-element.28.my.refs_0_, f32[1,2,256,256]{3,2,1,0:T(8,128)S(1)} %get-tuple-element.40.refs_1_, bf16[16,16,256]{2,1,0:T(8,128)(2,1)S(1)} %collective-permute-done.4.refs_2_, ...), custom_call_target="tpu_custom_call" | custom-call | tf_op jit(solution)/shard_map/last/pallas_call | solution.py:407
  16.5 0.1 collective-permute-start.6
  16.6 1.2 %collective-permute-done.6.theirs = f32[2,4,8,32]{3,2,1,0:T(8,128)S(1)} collective-permute-done((f32[2,4,8,32]{3,2,1,0:T(8,128)S(1)}, f32[2,4,8,32]{3,2,1,0:T(8,128)S(1)}, u32[]{:S(2)}, u32[]{:S(2)}) %collective-permute-start.6) | collective-permute-done | bytes 8224 | tf_op jit(solution)/shard_map/ppermute | solution.py:416
  17.8 1.6 %collective-permute-start.7 = (f32[1,4,8,32]{3,2,1,0:T(8,128)S(1)}, f32[1,4,8,32]{3,2,1,0:T(8,128)S(1)}, u32[]{:S(2)}, u32[]{:S(2)}) collective-permute-start(f32[1,4,8,32]{3,2,1,0:T(8,128)S(1)} %get-tuple-element.48), channel_id=1, source_target_pairs={{0,16},{8,24},{16,0},{24,8},{1,17},{9,25},{17,1},{25,9},{2,18},{10... | collective-permute-start | bytes 12296 | tf_op jit(solution)/shard_map/ppermute | solution.py:416
  19.4 2.2 %collective-permute-done.7.theirs = f32[1,4,8,32]{3,2,1,0:T(8,128)S(1)} collective-permute-done((f32[1,4,8,32]{3,2,1,0:T(8,128)S(1)}, f32[1,4,8,32]{3,2,1,0:T(8,128)S(1)}, u32[]{:S(2)}, u32[]{:S(2)}) %collective-permute-start.7) | collective-permute-done | bytes 4128 | tf_op jit(solution)/shard_map/ppermute | solution.py:416
  21.6 0.6 %merge1.1 = f32[4,1,1,8,32]{4,3,2,1,0:T(8,128)} custom-call(s32[4,8,32]{2,1,0:T(8,128)S(1)} %get-tuple-element.27.order_map, f32[1,4,8,32]{3,2,1,0:T(8,128)S(1)} %get-tuple-element.47.kept, f32[1,4,8,32]{3,2,1,0:T(8,128)S(1)} %collective-permute-done.7.theirs), custom_call_target="tpu_custom_call" | custom-call | tf_op jit(solution)/shard_map/merge1/pallas_call | solution.py:419
  (1 shorter events, 0.0 us)
Async XLA Ops:
  1.6 4.7 %collective-permute-start = (bf16[16,16,256]{2,1,0:T(8,128)(2,1)S(1)}, bf16[16,16,256]{2,1,0:T(8,128)(2,1)S(1)}, u32[]{:S(2)}, u32[]{:S(2)}) collective-permute-start(bf16[16,16,256]{2,1,0:T(8,128)(2,1)S(1)} %get-tuple-element.31.near0), channel_id=1, source_target_pairs={{0,8},{16,24},{1,9},{17,25},{2,4},{10,12},{18,20},{26,28},{3,5},{1... | collective-permute-start | bytes 393224 | tf_op jit(solution)/shard_map/ppermute | solution.py:343
  2.1 8.5 %collective-permute-start.2 = (bf16[16,16,256]{2,1,0:T(8,128)(2,1)S(1)}, bf16[16,16,256]{2,1,0:T(8,128)(2,1)S(1)}, u32[]{:S(2)}, u32[]{:S(2)}) collective-permute-start(bf16[16,16,256]{2,1,0:T(8,128)(2,1)S(1)} %get-tuple-element.32.near1), channel_id=1, source_target_pairs={{0,2},{8,10},{16,18},{24,26},{1,3},{9,11},{17,19},{25,27},{4,6},{1... | collective-permute-start | bytes 393224 | tf_op jit(solution)/shard_map/ppermute | solution.py:343
  6.3 8.5 %collective-permute-start.1 = (bf16[16,16,256]{2,1,0:T(8,128)(2,1)S(1)}, bf16[16,16,256]{2,1,0:T(8,128)(2,1)S(1)}, u32[]{:S(2)}, u32[]{:S(2)}) collective-permute-start(bf16[16,16,256]{2,1,0:T(8,128)(2,1)S(1)} %get-tuple-element.34.near1), channel_id=1, source_target_pairs={{0,2},{8,10},{16,18},{24,26},{1,3},{9,11},{17,19},{25,27},{4,6},{1... | collective-permute-start | bytes 393224 | tf_op jit(solution)/shard_map/ppermute | solution.py:343
  6.3 8.5 %collective-permute-start.3 = (bf16[16,16,256]{2,1,0:T(8,128)(2,1)S(1)}, bf16[16,16,256]{2,1,0:T(8,128)(2,1)S(1)}, u32[]{:S(2)}, u32[]{:S(2)}) collective-permute-start(bf16[16,16,256]{2,1,0:T(8,128)(2,1)S(1)} %get-tuple-element.35.near0), channel_id=1, source_target_pairs={{0,8},{16,24},{1,9},{17,25},{2,4},{10,12},{18,20},{26,28},{3,5},{1... | collective-permute-start | bytes 393224 | tf_op jit(solution)/shard_map/ppermute | solution.py:343
  6.6 9.2 %collective-permute-start.4 = (bf16[16,16,256]{2,1,0:T(8,128)(2,1)S(1)}, bf16[16,16,256]{2,1,0:T(8,128)(2,1)S(1)}, u32[]{:S(2)}, u32[]{:S(2)}) collective-permute-start(bf16[16,16,256]{2,1,0:T(8,128)(2,1)S(1)} %strip0.1), channel_id=1, source_target_pairs={{0,1},{8,9},{16,17},{24,25},{2,3},{10,11},{18,19},{26,27},{4,5},{1... | collective-permute-start | bytes 393224 | tf_op jit(solution)/shard_map/ppermute | solution.py:343
  10.9 5.0 %collective-permute-start.5 = (bf16[16,16,256]{2,1,0:T(8,128)(2,1)S(1)}, bf16[16,16,256]{2,1,0:T(8,128)(2,1)S(1)}, u32[]{:S(2)}, u32[]{:S(2)}) collective-permute-start(bf16[16,16,256]{2,1,0:T(8,128)(2,1)S(1)} %strip1.1), channel_id=1, source_target_pairs={{0,1},{8,9},{16,17},{24,25},{2,3},{10,11},{18,19},{26,27},{4,5},{1... | collective-permute-start | bytes 393224 | tf_op jit(solution)/shard_map/ppermute | solution.py:343
  16.5 1.3 %collective-permute-start.6 = (f32[2,4,8,32]{3,2,1,0:T(8,128)S(1)}, f32[2,4,8,32]{3,2,1,0:T(8,128)S(1)}, u32[]{:S(2)}, u32[]{:S(2)}) collective-permute-start(f32[2,4,8,32]{3,2,1,0:T(8,128)S(1)} %get-tuple-element.46), channel_id=1, source_target_pairs={{0,8},{8,0},{16,24},{24,16},{1,9},{9,1},{17,25},{25,17},{2,10},{10... | collective-permute-start | bytes 24584 | tf_op jit(solution)/shard_map/ppermute | solution.py:416
  17.8 3.8 %collective-permute-start.7 = (f32[1,4,8,32]{3,2,1,0:T(8,128)S(1)}, f32[1,4,8,32]{3,2,1,0:T(8,128)S(1)}, u32[]{:S(2)}, u32[]{:S(2)}) collective-permute-start(f32[1,4,8,32]{3,2,1,0:T(8,128)S(1)} %get-tuple-element.48), channel_id=1, source_target_pairs={{0,16},{8,24},{16,0},{24,8},{1,17},{9,25},{17,1},{25,9},{2,18},{10... | collective-permute-start | bytes 12296 | tf_op jit(solution)/shard_map/ppermute | solution.py:416

commit v18 on v17

--- a/solution.py
+++ b/solution.py
@@ -43,7 +43,7 @@
 class Place:
     def __init__(self):
         self.depth = lax.axis_index("depth")
-        self.half, self.has_x = self.sides("sx", 1)
+        self.half, self.has_x = self.sides("sx", 0)
         self.group, self.has_y = self.sides("sy", 0)
 
     def sides(self, axis, shift):
@@ -230,7 +230,7 @@
     out[...] = across.reshape(out.shape)
 
 
-def own_kernel(rim, early, strip0, halo1, strip1, halo0, mx, my, near0, near1, *refs):
+def own_kernel(rim, early, strip0, halo0, strip1, halo1, mx, my, near0, near1, *refs):
     place = Place()
     size = rim * rim
     across = [
@@ -361,7 +361,7 @@
         + [pltpu.VMEM((8, 128), F32), pltpu.SemaphoreType.DMA((4 + len(tables),))],
     )(in_hbm(density), *[in_hbm(t) for t in tables])
     coarse, (mx, my, table, signs, order_map) = [refs[0:2], refs[2:4]], refs[4:]
-    halo_x = [[swap(coarse[g][h], 1, 1 - h) for h in range(2)] for g in range(2)]
+    halo_x = [[swap(coarse[g][h], 1, h) for h in range(2)] for g in range(2)]
     strips, halo_y = [], []
     for h in range(2):
         strip = call(functools.partial(strip_kernel, rim, h), f"strip{h}", [VMEM] * 4, piece)(
@@ -395,7 +395,7 @@
         [VMEM] * (9 if early else 8),
         [colours, unlit] if early else [unlit, piece, piece],
     )(
-        strips[0], halo_x[1][1], strips[1], halo_x[1][0], mx, my, *coarse[1], *([shaded[1]] if early else [])
+        strips[0], halo_x[1][0], strips[1], halo_x[1][1], mx, my, *coarse[1], *([shaded[1]] if early else [])
     )
     if early:
         light, partial = results

time: 22.4 us -> 23.3 us (1.040)
  starting transfers between devices: 9.5 us -> 10 us
  waiting for transfers between devices: 6.08 us -> 6.55 us
    ppermute x6, starting transfers between devices: 7.86 us -> 8.4 us  [swap(): return lax.ppermute(piece, axes, swaps(counts, axis, shift))]
    ppermute x6, waiting for transfers between devices: 2.65 us -> 3.1 us  [swap(): return lax.ppermute(piece, axes, swaps(counts, axis, shift))]
  transfers between devices with their start and end apart: 8 -> 8, of which waited for: 4 -> 5; matrix products, arithmetic and copies ran while one was open for 0% -> 0% of each run, Pallas kernels for 17% -> 16%
where the time goes in v18:
time: 23.3 us; the launch traced here: 23.2 us
  starting transfers between devices  10 us (43%)
  Pallas kernels  6.55 us (28%)
  waiting for transfers between devices  6.55 us (28%)
    ppermute x6, starting transfers between devices, swap(): return lax.ppermute(piece, axes, swaps(counts, axis, shift))  8.4 us
    ppermute x2, waiting for transfers between devices, per_device(): lax.ppermute(given, 'depth', [(i, i ^ 1 << level) for i in range(depth_co...  3.44 us
    ppermute x6, waiting for transfers between devices, swap(): return lax.ppermute(piece, axes, swaps(counts, axis, shift))  3.1 us
    pallas_call x2, Pallas kernels, per_device(): call(functools.partial(cells_kernel, rim, bumps, g), f'cells{g}', [VMEM]...  2.31 us
    ppermute x2, starting transfers between devices, per_device(): lax.ppermute(given, 'depth', [(i, i ^ 1 << level) for i in range(depth_co...  1.63 us
    pallas_call x1, Pallas kernels, per_device(): call(functools.partial(first_kernel, rim), 'first', [HBM] * (1 + len(tabl...  1.6 us
    pallas_call x1, Pallas kernels, per_device(): call(functools.partial(own_kernel, rim, early), 'own', [VMEM] * (9 if ear...  0.9 us
    pallas_call x2, Pallas kernels, per_device(): call(functools.partial(merge_kernel, level), f'merge{level}', [VMEM] * 3,...  0.63 us
  transfers between devices with their start and end apart: 8, of which 5 were waited for; matrix products, arithmetic and copies ran while one was open for 0% of the time, Pallas kernels for 16%

profile of v18, /device:TPU:0, one launch (start us, length us, event | category | flops | bytes accessed | tf_op | source)
XLA Modules:
  0.0 23.2 jit_solution(3600197747703807144)
XLA Ops:
  0.0 1.6 %first.1 = (f32[2,2,16,16,256]{4,3,2,1,0:T(8,128)S(1)}, bf16[16,16,256]{2,1,0:T(8,128)(2,1)S(1)}, bf16[16,16,256]{2,1,0:T(8,128)(2,1)S(1)}, bf16[16,16,256]{2,1,...) custom-call(f32[32,32,256]{2,1,0:T(8,128)} %density.1, ...), custom_call_target="tpu_custom_call" | custom-call | tf_op jit(solution)/shard_map/first/pallas_call | solution.py:351
  1.6 3.1 %collective-permute-start = (bf16[16,16,256]{2,1,0:T(8,128)(2,1)S(1)}, bf16[16,16,256]{2,1,0:T(8,128)(2,1)S(1)}, u32[]{:S(2)}, u32[]{:S(2)}) collective-permute-start(bf16[16,16,256]{2,1,0:T(8,128)(2,1)S(1)} %get-tuple-element.31.near0), channel_id=1, source_target_pairs={{0,2},{8,10},{16,18},{24,26},{1,3},{9,11},{17,19},{25,27},{4,6},{1... | collective-permute-start | bytes 393224 | tf_op jit(solution)/shard_map/ppermute | solution.py:343
  4.7 0.0 collective-permute-start.2
  4.7 3.1 %collective-permute-start.1 = (bf16[16,16,256]{2,1,0:T(8,128)(2,1)S(1)}, bf16[16,16,256]{2,1,0:T(8,128)(2,1)S(1)}, u32[]{:S(2)}, u32[]{:S(2)}) collective-permute-start(bf16[16,16,256]{2,1,0:T(8,128)(2,1)S(1)} %get-tuple-element.34.near0), channel_id=1, source_target_pairs={{0,2},{8,10},{16,18},{24,26},{1,3},{9,11},{17,19},{25,27},{4,6},{1... | collective-permute-start | bytes 393224 | tf_op jit(solution)/shard_map/ppermute | solution.py:343
  7.8 0.0 collective-permute-start.3
  7.8 0.5 %collective-permute-done.halo = bf16[16,16,256]{2,1,0:T(8,128)(2,1)S(1)} collective-permute-done((bf16[16,16,256]{2,1,0:T(8,128)(2,1)S(1)}, bf16[16,16,256]{2,1,0:T(8,128)(2,1)S(1)}, u32[]{:S(2)}, u32[]{:S(2)}) %collective-permute-start) | collective-permute-done | bytes 131104 | tf_op jit(solution)/shard_map/ppermute | solution.py:343
  8.3 0.3 %strip0.1 = bf16[16,16,256]{2,1,0:T(8,128)(2,1)S(1)} custom-call(bf16[256,768]{1,0:T(8,128)(2,1)S(1)} %get-tuple-element.30.mx, bf16[16,16,256]{2,1,0:T(8,128)(2,1)S(1)} %get-tuple-element.31.near0, bf16[16,16,256]{2,1,0:T(8,128)(2,1)S(1)} %get-tuple-element.32.near1, bf16[16,16,256]{2,1,0:T(8,128)(2,1)S(1)} %collective-permute-done.halo), custom_call_target="tpu_custom_call" | custom-call | tf_op jit(solution)/shard_map/strip0/pallas_call | solution.py:367
  8.6 1.9 %collective-permute-start.4 = (bf16[16,16,256]{2,1,0:T(8,128)(2,1)S(1)}, bf16[16,16,256]{2,1,0:T(8,128)(2,1)S(1)}, u32[]{:S(2)}, u32[]{:S(2)}) collective-permute-start(bf16[16,16,256]{2,1,0:T(8,128)(2,1)S(1)} %strip0.1), channel_id=1, source_target_pairs={{0,1},{8,9},{16,17},{24,25},{2,3},{10,11},{18,19},{26,27},{4,5},{1... | collective-permute-start | bytes 393224 | tf_op jit(solution)/shard_map/ppermute | solution.py:343
  10.6 0.0 collective-permute-done.2.halo
  10.6 0.3 %strip1.1 = bf16[16,16,256]{2,1,0:T(8,128)(2,1)S(1)} custom-call(bf16[256,768]{1,0:T(8,128)(2,1)S(1)} %get-tuple-element.30.mx, bf16[16,16,256]{2,1,0:T(8,128)(2,1)S(1)} %get-tuple-element.31.near0, bf16[16,16,256]{2,1,0:T(8,128)(2,1)S(1)} %get-tuple-element.32.near1, bf16[16,16,256]{2,1,0:T(8,128)(2,1)S(1)} %collective-permute-done.2.halo), custom_call_target="tpu_custom_call" | custom-call | tf_op jit(solution)/shard_map/strip1/pallas_call | solution.py:367
  10.8 0.2 collective-permute-start.5
  11.1 1.2 %cells0.1 = (f32[3,2,16,16,256]{4,3,2,1,0:T(8,128)S(1)}, f32[16,128]{1,0:T(8,128)S(1)}) custom-call(f32[2,2,16,16,256]{4,3,2,1,0:T(8,128)S(1)} %get-tuple-element.36.held, f32[8,24,128]{2,1,0:T(8,128)S(1)} %get-tuple-element.37.table, s32[2,2,8,128]{3,2,1,0:T(8,128)S(1)} %get-tuple-element.38.signs), custom_call_target="tpu_custom_call" | custom-call | flops 26214400000 | bytes 262144 | tf_op jit(solution)/shard_map/cells0/pallas_call | solution.py:376
  12.2 1.2 %cells1.1 = (f32[3,2,16,16,256]{4,3,2,1,0:T(8,128)S(1)}, f32[16,128]{1,0:T(8,128)S(1)}) custom-call(f32[2,2,16,16,256]{4,3,2,1,0:T(8,128)S(1)} %get-tuple-element.36.held, f32[8,24,128]{2,1,0:T(8,128)S(1)} %get-tuple-element.37.table, s32[2,2,8,128]{3,2,1,0:T(8,128)S(1)} %get-tuple-element.38.signs), custom_call_target="tpu_custom_call" | custom-call | flops 262144 | bytes 262144 | tf_op jit(solution)/shard_map/cells1/pallas_call | solution.py:376
  13.4 0.0 collective-permute-done.1.halo0
  13.4 0.0 collective-permute-done.3.halo1
  13.4 0.9 %own.1 = (f32[3,16,128]{2,1,0:T(8,128)S(1)}, f32[1,2,256,256]{3,2,1,0:T(8,128)S(1)}) custom-call(bf16[16,16,256]{2,1,0:T(8,128)(2,1)S(1)} %strip0.1, bf16[16,16,256]{2,1,0:T(8,128)(2,1)S(1)} %collective-permute-done.1.halo0, bf16[16,16,256]{2,1,0:T(8,128)(2,1)S(1)} %strip1.1, bf16[16,16,256]{2,1,0:T(8,128)(2,1)S(1)} %collective-permute-done.3.halo1, ...), custom_call_target="tpu_custom_call" | custom-call | tf_op jit(solution)/shard_map/own/pallas_call | solution.py:392
  14.3 0.7 %collective-permute-done.4.refs_2_ = bf16[16,16,256]{2,1,0:T(8,128)(2,1)S(1)} collective-permute-done((bf16[16,16,256]{2,1,0:T(8,128)(2,1)S(1)}, bf16[16,16,256]{2,1,0:T(8,128)(2,1)S(1)}, u32[]{:S(2)}, u32[]{:S(2)}) %collective-permute-start.4) | collective-permute-done | bytes 131104 | tf_op jit(solution)/shard_map/ppermute | solution.py:343
  15.0 1.9 %collective-permute-done.5.refs_3_ = bf16[16,16,256]{2,1,0:T(8,128)(2,1)S(1)} collective-permute-done((bf16[16,16,256]{2,1,0:T(8,128)(2,1)S(1)}, bf16[16,16,256]{2,1,0:T(8,128)(2,1)S(1)}, u32[]{:S(2)}, u32[]{:S(2)}) %collective-permute-start.5) | collective-permute-done | bytes 131104 | tf_op jit(solution)/shard_map/ppermute | solution.py:343
  16.9 0.6 %last.1 = (f32[2,4,8,32]{3,2,1,0:T(8,128)S(1)}, f32[2,4,8,32]{3,2,1,0:T(8,128)S(1)}) custom-call(bf16[256,768]{1,0:T(8,128)(2,1)S(1)} %get-tuple-element.28.my.refs_0_, f32[1,2,256,256]{3,2,1,0:T(8,128)S(1)} %get-tuple-element.40.refs_1_, bf16[16,16,256]{2,1,0:T(8,128)(2,1)S(1)} %collective-permute-done.4.refs_2_, ...), custom_call_target="tpu_custom_call" | custom-call | tf_op jit(solution)/shard_map/last/pallas_call | solution.py:407
  17.5 0.1 collective-permute-start.6
  17.6 1.2 %collective-permute-done.6.theirs = f32[2,4,8,32]{3,2,1,0:T(8,128)S(1)} collective-permute-done((f32[2,4,8,32]{3,2,1,0:T(8,128)S(1)}, f32[2,4,8,32]{3,2,1,0:T(8,128)S(1)}, u32[]{:S(2)}, u32[]{:S(2)}) %collective-permute-start.6) | collective-permute-done | bytes 8224 | tf_op jit(solution)/shard_map/ppermute | solution.py:416
  18.8 1.6 %collective-permute-start.7 = (f32[1,4,8,32]{3,2,1,0:T(8,128)S(1)}, f32[1,4,8,32]{3,2,1,0:T(8,128)S(1)}, u32[]{:S(2)}, u32[]{:S(2)}) collective-permute-start(f32[1,4,8,32]{3,2,1,0:T(8,128)S(1)} %get-tuple-element.48), channel_id=1, source_target_pairs={{0,16},{8,24},{16,0},{24,8},{1,17},{9,25},{17,1},{25,9},{2,18},{10... | collective-permute-start | bytes 12296 | tf_op jit(solution)/shard_map/ppermute | solution.py:416
  20.3 2.2 %collective-permute-done.7.theirs = f32[1,4,8,32]{3,2,1,0:T(8,128)S(1)} collective-permute-done((f32[1,4,8,32]{3,2,1,0:T(8,128)S(1)}, f32[1,4,8,32]{3,2,1,0:T(8,128)S(1)}, u32[]{:S(2)}, u32[]{:S(2)}) %collective-permute-start.7) | collective-permute-done | bytes 4128 | tf_op jit(solution)/shard_map/ppermute | solution.py:416
  22.6 0.6 %merge1.1 = f32[4,1,1,8,32]{4,3,2,1,0:T(8,128)} custom-call(s32[4,8,32]{2,1,0:T(8,128)S(1)} %get-tuple-element.27.order_map, f32[1,4,8,32]{3,2,1,0:T(8,128)S(1)} %get-tuple-element.47.kept, f32[1,4,8,32]{3,2,1,0:T(8,128)S(1)} %collective-permute-done.7.theirs), custom_call_target="tpu_custom_call" | custom-call | tf_op jit(solution)/shard_map/merge1/pallas_call | solution.py:419
  (1 shorter events, 0.0 us)
Async XLA Ops:
  1.6 6.7 %collective-permute-start = (bf16[16,16,256]{2,1,0:T(8,128)(2,1)S(1)}, bf16[16,16,256]{2,1,0:T(8,128)(2,1)S(1)}, u32[]{:S(2)}, u32[]{:S(2)}) collective-permute-start(bf16[16,16,256]{2,1,0:T(8,128)(2,1)S(1)} %get-tuple-element.31.near0), channel_id=1, source_target_pairs={{0,2},{8,10},{16,18},{24,26},{1,3},{9,11},{17,19},{25,27},{4,6},{1... | collective-permute-start | bytes 393224 | tf_op jit(solution)/shard_map/ppermute | solution.py:343
  4.7 5.9 %collective-permute-start.2 = (bf16[16,16,256]{2,1,0:T(8,128)(2,1)S(1)}, bf16[16,16,256]{2,1,0:T(8,128)(2,1)S(1)}, u32[]{:S(2)}, u32[]{:S(2)}) collective-permute-start(bf16[16,16,256]{2,1,0:T(8,128)(2,1)S(1)} %get-tuple-element.32.near1), channel_id=1, source_target_pairs={{0,8},{16,24},{1,9},{17,25},{2,4},{10,12},{18,20},{26,28},{3,5},{1... | collective-permute-start | bytes 393224 | tf_op jit(solution)/shard_map/ppermute | solution.py:343
  4.7 8.7 %collective-permute-start.1 = (bf16[16,16,256]{2,1,0:T(8,128)(2,1)S(1)}, bf16[16,16,256]{2,1,0:T(8,128)(2,1)S(1)}, u32[]{:S(2)}, u32[]{:S(2)}) collective-permute-start(bf16[16,16,256]{2,1,0:T(8,128)(2,1)S(1)} %get-tuple-element.34.near0), channel_id=1, source_target_pairs={{0,2},{8,10},{16,18},{24,26},{1,3},{9,11},{17,19},{25,27},{4,6},{1... | collective-permute-start | bytes 393224 | tf_op jit(solution)/shard_map/ppermute | solution.py:343
  7.8 5.6 %collective-permute-start.3 = (bf16[16,16,256]{2,1,0:T(8,128)(2,1)S(1)}, bf16[16,16,256]{2,1,0:T(8,128)(2,1)S(1)}, u32[]{:S(2)}, u32[]{:S(2)}) collective-permute-start(bf16[16,16,256]{2,1,0:T(8,128)(2,1)S(1)} %get-tuple-element.35.near1), channel_id=1, source_target_pairs={{0,8},{16,24},{1,9},{17,25},{2,4},{10,12},{18,20},{26,28},{3,5},{1... | collective-permute-start | bytes 393224 | tf_op jit(solution)/shard_map/ppermute | solution.py:343
  8.6 6.4 %collective-permute-start.4 = (bf16[16,16,256]{2,1,0:T(8,128)(2,1)S(1)}, bf16[16,16,256]{2,1,0:T(8,128)(2,1)S(1)}, u32[]{:S(2)}, u32[]{:S(2)}) collective-permute-start(bf16[16,16,256]{2,1,0:T(8,128)(2,1)S(1)} %strip0.1), channel_id=1, source_target_pairs={{0,1},{8,9},{16,17},{24,25},{2,3},{10,11},{18,19},{26,27},{4,5},{1... | collective-permute-start | bytes 393224 | tf_op jit(solution)/shard_map/ppermute | solution.py:343
  10.8 6.1 %collective-permute-start.5 = (bf16[16,16,256]{2,1,0:T(8,128)(2,1)S(1)}, bf16[16,16,256]{2,1,0:T(8,128)(2,1)S(1)}, u32[]{:S(2)}, u32[]{:S(2)}) collective-permute-start(bf16[16,16,256]{2,1,0:T(8,128)(2,1)S(1)} %strip1.1), channel_id=1, source_target_pairs={{0,1},{8,9},{16,17},{24,25},{2,3},{10,11},{18,19},{26,27},{4,5},{1... | collective-permute-start | bytes 393224 | tf_op jit(solution)/shard_map/ppermute | solution.py:343
  17.5 1.3 %collective-permute-start.6 = (f32[2,4,8,32]{3,2,1,0:T(8,128)S(1)}, f32[2,4,8,32]{3,2,1,0:T(8,128)S(1)}, u32[]{:S(2)}, u32[]{:S(2)}) collective-permute-start(f32[2,4,8,32]{3,2,1,0:T(8,128)S(1)} %get-tuple-element.46), channel_id=1, source_target_pairs={{0,8},{8,0},{16,24},{24,16},{1,9},{9,1},{17,25},{25,17},{2,10},{10... | collective-permute-start | bytes 24584 | tf_op jit(solution)/shard_map/ppermute | solution.py:416
  18.8 3.8 %collective-permute-start.7 = (f32[1,4,8,32]{3,2,1,0:T(8,128)S(1)}, f32[1,4,8,32]{3,2,1,0:T(8,128)S(1)}, u32[]{:S(2)}, u32[]{:S(2)}) collective-permute-start(f32[1,4,8,32]{3,2,1,0:T(8,128)S(1)} %get-tuple-element.48), channel_id=1, source_target_pairs={{0,16},{8,24},{16,0},{24,8},{1,17},{9,25},{17,1},{25,9},{2,18},{10... | collective-permute-start | bytes 12296 | tf_op jit(solution)/shard_map/ppermute | solution.py:416

commit v19 on v11

--- a/solution.py
+++ b/solution.py
@@ -129,7 +129,7 @@
 
 def matrices_kernel(rim, taps, mx, my, padded):
     padded[...] = jnp.zeros(padded.shape, F32)
-    padded[0:2, 0:taps.shape[1]] = taps[...].astype(F32)
+    padded[0:2, 0:taps.shape[1]] = taps[...]
     mx[...], my[...] = blur_matrices(rim, Place(), padded[...])
 
 
@@ -351,9 +351,7 @@
         return lax.ppermute(piece, axes, swaps(counts, x_round, y_round))
 
     in_hbm = lambda array: pltpu.with_memory_space_constraint(array, pltpu.HBM)
-    tables = (
-        kernel_taps, tf_centre.T, tf_width.T, tf_color.T, tf_opacity.T, brick_tf, view_order
-    )
+    tables = (tf_centre.T, tf_width.T, tf_color.T, tf_opacity.T, brick_tf, view_order)
     piece = struct((rim, rim, rows_z), BF16)
     both = struct((2, rim, rim, rows_z), BF16)
     held, xs0, xs1, *refs = call(
@@ -372,10 +370,10 @@
     table, signs, order_map = call(
         functools.partial(prepare_kernel, rim),
         "prepare",
-        [VMEM] * (len(tables) - 1),
+        [VMEM] * len(tables),
         [struct((4 * bricks, 6 * bumps, 128), F32), struct((2, 2, 8, 128), jnp.int32)]
         + [struct((depth_count, block, rows_y), jnp.int32)],
-    )(*tables[1:])
+    )(*tables)
     halo_x = [swap(cells, h, None) for h, cells in enumerate((xs0, xs1))]
     mx, my = call(
         functools.partial(matrices_kernel, rim),
@@ -383,7 +381,7 @@
         [VMEM],
         [struct((size, 3 * size), BF16)] * 2,
         [pltpu.VMEM((8, 128), F32)],
-    )(tables[0])
+    )(kernel_taps.astype(F32))
     shaded, total = [None, None], [None, None]
     for g in (1, 0):
         shaded[g], total[g] = call(

time: 22 us -> 22 us (level)
  no operation moved by 1% of the time
where the time goes in v19:
time: 22 us; the launch traced here: 21.5 us
  starting transfers between devices  9.97 us (45%)
  Pallas kernels  7.11 us (32%)
  waiting for transfers between devices  4.34 us (20%)
    ppermute x6, starting transfers between devices, swap(): return lax.ppermute(piece, axes, swaps(counts, x_round, y_round))  8.34 us
    ppermute x2, waiting for transfers between devices, per_device(): lax.ppermute(given, 'depth', [(i, i ^ 1 << level) for i in range(depth_co...  3.44 us
    pallas_call x2, Pallas kernels, per_device(): call(functools.partial(cells_kernel, rim, bumps, g), f'cells{g}', [VMEM]...  2.31 us
    ppermute x2, starting transfers between devices, per_device(): lax.ppermute(given, 'depth', [(i, i ^ 1 << level) for i in range(depth_co...  1.63 us
    pallas_call x1, Pallas kernels, per_device(): call(functools.partial(first_kernel, rim, rounds), 'first', [HBM] * (1 +...  1.3 us
    pallas_call x1, Pallas kernels, per_device(): call(functools.partial(own_kernel, rim, early), 'own', [VMEM] * (7 if ear...  1.1 us
    pallas_call x1, Pallas kernels, per_device(): call(functools.partial(last_kernel, rim, depth_count), 'last', [VMEM] * 1...  0.9 us
    ppermute x6, waiting for transfers between devices, swap(): return lax.ppermute(piece, axes, swaps(counts, x_round, y_round))  0.9 us
  transfers between devices with their start and end apart: 8, of which 4 were waited for; matrix products, arithmetic and copies ran while one was open for 0% of the time, Pallas kernels for 20%

profile of v19, /device:TPU:0, one launch (start us, length us, event | category | flops | bytes accessed | tf_op | source)
XLA Modules:
  0.0 21.5 jit_solution(7113220198112111796)
XLA Ops:
  0.0 1.3 %first.1 = (f32[2,2,16,16,256]{4,3,2,1,0:T(8,128)S(1)}, bf16[2,16,16,256]{3,2,1,0:T(8,128)(2,1)S(1)}, bf16[2,16,16,256]{3,2,1,0:T(8,128)(2,1)S(1)}, bf16[16,16,2...) custom-call(f32[32,32,256]{2,1,0:T(8,128)} %density.1, ...), custom_call_target="tpu_custom_call" | custom-call | tf_op jit(solution)/shard_map/first/pallas_call | solution.py:357
  1.3 3.0 %collective-permute-start = (bf16[16,16,256]{2,1,0:T(8,128)(2,1)S(1)}, bf16[16,16,256]{2,1,0:T(8,128)(2,1)S(1)}, u32[]{:S(2)}, u32[]{:S(2)}) collective-permute-start(bf16[16,16,256]{2,1,0:T(8,128)(2,1)S(1)} %get-tuple-element.43), channel_id=1, source_target_pairs={{0,1},{2,3},{4,5},{6,7},{8,9},{10,11},{12,13},{14,15},{16,17},{18,... | collective-permute-start | bytes 393224 | tf_op jit(solution)/shard_map/ppermute | solution.py:351
  4.3 1.6 %collective-permute-start.1 = (bf16[2,16,16,256]{3,2,1,0:T(8,128)(2,1)S(1)}, bf16[2,16,16,256]{3,2,1,0:T(8,128)(2,1)S(1)}, u32[]{:S(2)}, u32[]{:S(2)}) collective-permute-start(bf16[2,16,16,256]{3,2,1,0:T(8,128)(2,1)S(1)} %get-tuple-element.44.xs0), channel_id=1, source_target_pairs={{0,2},{1,3},{4,6},{5,7},{8,10},{9,11},{12,14},{13,15},{16,18},{17,... | collective-permute-start | bytes 786440 | tf_op jit(solution)/shard_map/ppermute | solution.py:351
  5.9 0.0 collective-permute-start.2
  5.9 0.5 %collective-permute-start.3 = (bf16[16,16,256]{2,1,0:T(8,128)(2,1)S(1)}, bf16[16,16,256]{2,1,0:T(8,128)(2,1)S(1)}, u32[]{:S(2)}, u32[]{:S(2)}) collective-permute-start(bf16[16,16,256]{2,1,0:T(8,128)(2,1)S(1)} %get-tuple-element.54), channel_id=1, source_target_pairs={{0,1},{2,3},{4,5},{6,7},{8,9},{10,11},{12,13},{14,15},{16,17},{18,... | collective-permute-start | bytes 393224 | tf_op jit(solution)/shard_map/ppermute | solution.py:351
  6.4 0.3 %prepare.1 = (f32[8,24,128]{2,1,0:T(8,128)S(1)}, s32[2,2,8,128]{3,2,1,0:T(8,128)S(1)}, s32[4,8,32]{2,1,0:T(8,128)S(1)}) custom-call(f32[4,8]{1,0:T(4,128)S(1)} %get-tuple-element.34.centre, f32[4,8]{1,0:T(4,128)S(1)} %get-tuple-element.35.width, f32[3,4,8]{2,1,0:T(4,128)S(1)} %get-tuple-element.36.colour, f32[4,8]{1,0:T(4,128)S(1)} %get-tuple-element.37.opacity, ...), custom_call_target="tpu_custom_call" | custom-call | tf_op jit(solution)/shard_map/prepare/pallas_call | solution.py:370
  6.7 1.2 %cells1.1 = (f32[3,2,16,16,256]{4,3,2,1,0:T(8,128)S(1)}, f32[16,128]{1,0:T(8,128)S(1)}) custom-call(f32[2,2,16,16,256]{4,3,2,1,0:T(8,128)S(1)} %get-tuple-element.46.held, f32[8,24,128]{2,1,0:T(8,128)S(1)} %get-tuple-element.47.table, s32[2,2,8,128]{3,2,1,0:T(8,128)S(1)} %get-tuple-element.48.signs), custom_call_target="tpu_custom_call" | custom-call | flops 262144 | bytes 262144 | tf_op jit(solution)/shard_map/cells1/pallas_call | solution.py:387
  7.9 0.0 collective-permute-done.refs_2_
  7.9 0.0 copy-start
  7.9 3.2 %collective-permute-start.4 = (bf16[16,16,256]{2,1,0:T(8,128)(2,1)S(1)}, bf16[16,16,256]{2,1,0:T(8,128)(2,1)S(1)}, u32[]{:S(2)}, u32[]{:S(2)}) collective-permute-start(bf16[16,16,256]{2,1,0:T(8,128)(2,1)S(1)} %collective-permute-done.refs_2_), channel_id=1, source_target_pairs={{0,2},{1,3},{4,6},{5,7},{8,10},{9,11},{12,14},{13,15},{16,18},{17,... | collective-permute-start | bytes 393224 | tf_op jit(solution)/shard_map/ppermute | solution.py:351
  11.1 0.0 collective-permute-start.5
  11.1 1.2 %cells0.1 = (f32[3,2,16,16,256]{4,3,2,1,0:T(8,128)S(1)}, f32[16,128]{1,0:T(8,128)S(1)}) custom-call(f32[2,2,16,16,256]{4,3,2,1,0:T(8,128)S(1)} %get-tuple-element.46.held, f32[8,24,128]{2,1,0:T(8,128)S(1)} %get-tuple-element.47.table, s32[2,2,8,128]{3,2,1,0:T(8,128)S(1)} %get-tuple-element.48.signs), custom_call_target="tpu_custom_call" | custom-call | flops 26214400000 | bytes 2621440000 | tf_op jit(solution)/shard_map/cells0/pallas_call | solution.py:387
  12.3 0.6 %matrices.1 = (bf16[256,768]{1,0:T(8,128)(2,1)S(1)}, bf16[256,768]{1,0:T(8,128)(2,1)S(1)}) custom-call(f32[2,33]{1,0:T(2,128)S(1)} %convert_element_type.3.taps), custom_call_target="tpu_custom_call" | custom-call | tf_op jit(solution)/shard_map/matrices/pallas_call | solution.py:378
  12.9 0.5 %collective-permute-done.1.halo0 = bf16[2,16,16,256]{3,2,1,0:T(8,128)(2,1)S(1)} collective-permute-done((bf16[2,16,16,256]{3,2,1,0:T(8,128)(2,1)S(1)}, bf16[2,16,16,256]{3,2,1,0:T(8,128)(2,1)S(1)}, u32[]{:S(2)}, u32[]{:S(2)}) %collective-permute-start.1) | collective-permute-done | bytes 262176 | tf_op jit(solution)/shard_map/ppermute | solution.py:351
  13.4 0.0 collective-permute-done.2.halo1
  13.4 1.1 %own.1 = (f32[3,16,128]{2,1,0:T(8,128)S(1)}, f32[1,2,256,256]{3,2,1,0:T(8,128)S(1)}) custom-call(bf16[256,768]{1,0:T(8,128)(2,1)S(1)} %get-tuple-element.41.mx.refs_0_, bf16[256,768]{1,0:T(8,128)(2,1)S(1)} %get-tuple-element.42.my.refs_1_, bf16[2,16,16,256]{3,2,1,0:T(8,128)(2,1)S(1)} %get-tuple-element.44.xs0, ...), custom_call_target="tpu_custom_call" | custom-call | tf_op jit(solution)/shard_map/own/pallas_call | solution.py:411
  14.5 0.0 collective-permute-done.3.refs_4_
  14.5 0.4 %collective-permute-done.4.refs_5_ = bf16[16,16,256]{2,1,0:T(8,128)(2,1)S(1)} collective-permute-done((bf16[16,16,256]{2,1,0:T(8,128)(2,1)S(1)}, bf16[16,16,256]{2,1,0:T(8,128)(2,1)S(1)}, u32[]{:S(2)}, u32[]{:S(2)}) %collective-permute-start.4) | collective-permute-done | bytes 131104 | tf_op jit(solution)/shard_map/ppermute | solution.py:351
  14.9 0.9 %last.1 = (f32[2,4,8,32]{3,2,1,0:T(8,128)S(1)}, f32[2,4,8,32]{3,2,1,0:T(8,128)S(1)}) custom-call(bf16[256,768]{1,0:T(8,128)(2,1)S(1)} %get-tuple-element.41.mx.refs_0_, bf16[256,768]{1,0:T(8,128)(2,1)S(1)} %get-tuple-element.42.my.refs_1_, bf16[16,16,256]{2,1,0:T(8,128)(2,1)S(1)} %collective-permute-done.refs_2_, ...), custom_call_target="tpu_custom_call" | custom-call | tf_op jit(solution)/shard_map/last/pallas_call | solution.py:424
  15.8 0.1 collective-permute-start.6
  15.9 1.2 %collective-permute-done.6.theirs = f32[2,4,8,32]{3,2,1,0:T(8,128)S(1)} collective-permute-done((f32[2,4,8,32]{3,2,1,0:T(8,128)S(1)}, f32[2,4,8,32]{3,2,1,0:T(8,128)S(1)}, u32[]{:S(2)}, u32[]{:S(2)}) %collective-permute-start.6) | collective-permute-done | bytes 8224 | tf_op jit(solution)/shard_map/ppermute | solution.py:433
  17.1 1.6 %collective-permute-start.7 = (f32[1,4,8,32]{3,2,1,0:T(8,128)S(1)}, f32[1,4,8,32]{3,2,1,0:T(8,128)S(1)}, u32[]{:S(2)}, u32[]{:S(2)}) collective-permute-start(f32[1,4,8,32]{3,2,1,0:T(8,128)S(1)} %get-tuple-element.62), channel_id=1, source_target_pairs={{0,16},{8,24},{16,0},{24,8},{1,17},{9,25},{17,1},{25,9},{2,18},{10... | collective-permute-start | bytes 12296 | tf_op jit(solution)/shard_map/ppermute | solution.py:433
  18.7 2.2 %collective-permute-done.7.theirs = f32[1,4,8,32]{3,2,1,0:T(8,128)S(1)} collective-permute-done((f32[1,4,8,32]{3,2,1,0:T(8,128)S(1)}, f32[1,4,8,32]{3,2,1,0:T(8,128)S(1)}, u32[]{:S(2)}, u32[]{:S(2)}) %collective-permute-start.7) | collective-permute-done | bytes 4128 | tf_op jit(solution)/shard_map/ppermute | solution.py:433
  20.9 0.6 %merge1.1 = f32[4,1,1,8,32]{4,3,2,1,0:T(8,128)} custom-call(s32[4,8,32]{2,1,0:T(8,128)S(1)} %get-tuple-element.40.order_map, f32[1,4,8,32]{3,2,1,0:T(8,128)S(1)} %get-tuple-element.61.kept, f32[1,4,8,32]{3,2,1,0:T(8,128)S(1)} %collective-permute-done.7.theirs), custom_call_target="tpu_custom_call" | custom-call | tf_op jit(solution)/shard_map/merge1/pallas_call | solution.py:436
  (4 shorter events, 0.0 us)
Async XLA Ops:
  1.3 6.6 %collective-permute-start = (bf16[16,16,256]{2,1,0:T(8,128)(2,1)S(1)}, bf16[16,16,256]{2,1,0:T(8,128)(2,1)S(1)}, u32[]{:S(2)}, u32[]{:S(2)}) collective-permute-start(bf16[16,16,256]{2,1,0:T(8,128)(2,1)S(1)} %get-tuple-element.43), channel_id=1, source_target_pairs={{0,1},{2,3},{4,5},{6,7},{8,9},{10,11},{12,13},{14,15},{16,17},{18,... | collective-permute-start | bytes 393224 | tf_op jit(solution)/shard_map/ppermute | solution.py:351
  4.3 9.0 %collective-permute-start.1 = (bf16[2,16,16,256]{3,2,1,0:T(8,128)(2,1)S(1)}, bf16[2,16,16,256]{3,2,1,0:T(8,128)(2,1)S(1)}, u32[]{:S(2)}, u32[]{:S(2)}) collective-permute-start(bf16[2,16,16,256]{3,2,1,0:T(8,128)(2,1)S(1)} %get-tuple-element.44.xs0), channel_id=1, source_target_pairs={{0,2},{1,3},{4,6},{5,7},{8,10},{9,11},{12,14},{13,15},{16,18},{17,... | collective-permute-start | bytes 786440 | tf_op jit(solution)/shard_map/ppermute | solution.py:351
  5.9 7.5 %collective-permute-start.2 = (bf16[2,16,16,256]{3,2,1,0:T(8,128)(2,1)S(1)}, bf16[2,16,16,256]{3,2,1,0:T(8,128)(2,1)S(1)}, u32[]{:S(2)}, u32[]{:S(2)}) collective-permute-start(bf16[2,16,16,256]{3,2,1,0:T(8,128)(2,1)S(1)} %get-tuple-element.45.xs1), channel_id=1, source_target_pairs={{2,4},{3,5},{10,12},{11,13},{18,20},{19,21},{26,28},{27,29},{0,8},... | collective-permute-start | bytes 786440 | tf_op jit(solution)/shard_map/ppermute | solution.py:351
  5.9 8.6 %collective-permute-start.3 = (bf16[16,16,256]{2,1,0:T(8,128)(2,1)S(1)}, bf16[16,16,256]{2,1,0:T(8,128)(2,1)S(1)}, u32[]{:S(2)}, u32[]{:S(2)}) collective-permute-start(bf16[16,16,256]{2,1,0:T(8,128)(2,1)S(1)} %get-tuple-element.54), channel_id=1, source_target_pairs={{0,1},{2,3},{4,5},{6,7},{8,9},{10,11},{12,13},{14,15},{16,17},{18,... | collective-permute-start | bytes 393224 | tf_op jit(solution)/shard_map/ppermute | solution.py:351
  7.9 4.4 %copy-start = (bf16[2,33]{1,0:T(2,128)(2,1)S(1)}, bf16[2,33]{1,0:T(2,128)(2,1)}, u32[]{:S(2)}) copy-start(bf16[2,33]{1,0:T(2,128)(2,1)} %param.9) | copy-start | bytes 400
  7.9 7.0 %collective-permute-start.4 = (bf16[16,16,256]{2,1,0:T(8,128)(2,1)S(1)}, bf16[16,16,256]{2,1,0:T(8,128)(2,1)S(1)}, u32[]{:S(2)}, u32[]{:S(2)}) collective-permute-start(bf16[16,16,256]{2,1,0:T(8,128)(2,1)S(1)} %collective-permute-done.refs_2_), channel_id=1, source_target_pairs={{0,2},{1,3},{4,6},{5,7},{8,10},{9,11},{12,14},{13,15},{16,18},{17,... | collective-permute-start | bytes 393224 | tf_op jit(solution)/shard_map/ppermute | solution.py:351
  11.1 3.8 %collective-permute-start.5 = (bf16[16,16,256]{2,1,0:T(8,128)(2,1)S(1)}, bf16[16,16,256]{2,1,0:T(8,128)(2,1)S(1)}, u32[]{:S(2)}, u32[]{:S(2)}) collective-permute-start(bf16[16,16,256]{2,1,0:T(8,128)(2,1)S(1)} %get-tuple-element.54), channel_id=1, source_target_pairs={{2,5},{3,4},{10,13},{11,12},{18,21},{19,20},{26,29},{27,28},{0,8},... | collective-permute-start | bytes 393224 | tf_op jit(solution)/shard_map/ppermute | solution.py:351
  15.8 1.3 %collective-permute-start.6 = (f32[2,4,8,32]{3,2,1,0:T(8,128)S(1)}, f32[2,4,8,32]{3,2,1,0:T(8,128)S(1)}, u32[]{:S(2)}, u32[]{:S(2)}) collective-permute-start(f32[2,4,8,32]{3,2,1,0:T(8,128)S(1)} %get-tuple-element.60), channel_id=1, source_target_pairs={{0,8},{8,0},{16,24},{24,16},{1,9},{9,1},{17,25},{25,17},{2,10},{10... | collective-permute-start | bytes 24584 | tf_op jit(solution)/shard_map/ppermute | solution.py:433
  17.1 3.8 %collective-permute-start.7 = (f32[1,4,8,32]{3,2,1,0:T(8,128)S(1)}, f32[1,4,8,32]{3,2,1,0:T(8,128)S(1)}, u32[]{:S(2)}, u32[]{:S(2)}) collective-permute-start(f32[1,4,8,32]{3,2,1,0:T(8,128)S(1)} %get-tuple-element.62), channel_id=1, source_target_pairs={{0,16},{8,24},{16,0},{24,8},{1,17},{9,25},{17,1},{25,9},{2,18},{10... | collective-permute-start | bytes 12296 | tf_op jit(solution)/shard_map/ppermute | solution.py:433

commit v20 on v19

--- a/solution.py
+++ b/solution.py
@@ -260,15 +260,24 @@
             out[c] = part if h == 0 else out[c] + part
 
 
-def late(rim, g, mx, my, near0, partial, near1, halo0, halo1, shaded):
+def near_kernel(rim, mx, near0, order, near1, out):
+    size = rim * rim
+    cells = jnp.concatenate([r[...].reshape(size, r.shape[2]) for r in (near1, near0)], axis=0)
+    out[0] = dot(mx[:, :2 * size], cells)
+    out[1] = dot(mx[:, size:], cells)
+
+
+def late(rim, g, mx, my, blurred, partial, corner0, corner1, shaded):
     place = Place()
     size = rim * rim
     block = my[:, 2 * size:] if g == 0 else my[:, :size]
-    across = [
-        blur_x(place, rim, mx, h, [near0[...], near1[...]], halo[...])
-        for h, halo in enumerate((halo0, halo1))
-    ]
-    across = [jnp.where(place.has_y[g], cells, jnp.zeros_like(cells)) for cells in across]
+    across = []
+    for h, corner in enumerate((corner0, corner1)):
+        edge = corner[...].reshape(size, corner.shape[2])
+        edge = jnp.where(place.has_x[h], edge, jnp.zeros_like(edge))
+        beside = mx[:, 2 * size:] if h == 0 else mx[:, :size]
+        cells = (blurred[h] + dot(beside, edge)).astype(BF16)
+        across.append(jnp.where(place.has_y[g], cells, jnp.zeros_like(cells)))
     occlusion = [partial[g, h] + dot(block, across[h]) for h in range(2)]
     lights = [lit(place, rim, occlusion[h], shaded, h) for h in range(2)]
     return [a + b for a, b in zip(*lights)]
@@ -281,7 +290,7 @@
 
 
 def last_kernel(rim, depth_count, *refs):
-    refs, (light_e, total0, total1, kept, given, img) = refs[:8], refs[8:]
+    refs, (light_e, total0, total1, kept, given, img) = refs[:7], refs[7:]
     place = Place()
     rows = 2 * rim
     at_s, at_e = group_rows(place, rim, 0), group_rows(place, rim, 1)
@@ -415,19 +424,28 @@
         [colours, unlit] if early else [unlit],
     )(mx, my, xs0, xs1, *halo_x, *([shaded[1]] if early else []))
     partial = results[-1]
+    blurred = [
+        call(
+            functools.partial(near_kernel, rim),
+            f"near{r}",
+            [VMEM] * 4,
+            struct((2, size, rows_z), F32),
+        )(mx, near[r][0], partial, near[r][1])
+        for r in range(rounds)
+    ]
     if early:
         light = results[0]
     else:
-        light = call(functools.partial(late_kernel, rim, 1), "late", [VMEM] * 8, colours)(
-            mx, my, near[1][0], partial, near[1][1], *corner[1], shaded[1]
+        light = call(functools.partial(late_kernel, rim, 1), "late", [VMEM] * 7, colours)(
+            mx, my, blurred[1], partial, *corner[1], shaded[1]
         )
     kept, given = call(
         functools.partial(last_kernel, rim, depth_count),
         "last",
-        [VMEM] * 11,
+        [VMEM] * 10,
         [struct((depth_count // 2, 4, block, rows_y), F32)] * 2,
         [pltpu.VMEM((8, rows_y, 128), F32)],
-    )(mx, my, near[0][0], partial, near[0][1], *corner[0], shaded[0], light, *total)
+    )(mx, my, blurred[0], partial, *corner[0], shaded[0], light, *total)
     level = 0
     while True:
         theirs = lax.ppermute(given, "depth", [(i, i ^ 1 << level) for i in range(depth_count)])

time: 22 us -> 21.8 us (level)
  waiting for transfers between devices: 4.34 us -> 4.1 us
    pallas_call x0 -> x1, Pallas kernels: none -> 0.3 us  [per_device(): call(functools.partial(near_kernel, rim), f'near{r}', [VMEM] * 4, struct(...]
    ppermute x6, waiting for transfers between devices: 0.9 us -> 0.65 us  [swap(): return lax.ppermute(piece, axes, swaps(counts, x_round, y_round))]
  transfers between devices with their start and end apart: 8 -> 8, of which waited for: 4 -> 4; matrix products, arithmetic and copies ran while one was open for 0% -> 0% of each run, Pallas kernels for 20% -> 21%
where the time goes in v20:
time: 21.8 us; the launch traced here: 21.4 us
  starting transfers between devices  9.96 us (46%)
  Pallas kernels  7.21 us (33%)
  waiting for transfers between devices  4.1 us (19%)
    ppermute x6, starting transfers between devices, swap(): return lax.ppermute(piece, axes, swaps(counts, x_round, y_round))  8.33 us
    ppermute x2, waiting for transfers between devices, per_device(): lax.ppermute(given, 'depth', [(i, i ^ 1 << level) for i in range(depth_co...  3.44 us
    pallas_call x2, Pallas kernels, per_device(): call(functools.partial(cells_kernel, rim, bumps, g), f'cells{g}', [VMEM]...  2.25 us
    ppermute x2, starting transfers between devices, per_device(): lax.ppermute(given, 'depth', [(i, i ^ 1 << level) for i in range(depth_co...  1.63 us
    pallas_call x1, Pallas kernels, per_device(): call(functools.partial(first_kernel, rim, rounds), 'first', [HBM] * (1 +...  1.3 us
    pallas_call x1, Pallas kernels, per_device(): call(functools.partial(own_kernel, rim, early), 'own', [VMEM] * (7 if ear...  1.1 us
    pallas_call x1, Pallas kernels, per_device(): call(functools.partial(last_kernel, rim, depth_count), 'last', [VMEM] * 1...  0.76 us
    ppermute x6, waiting for transfers between devices, swap(): return lax.ppermute(piece, axes, swaps(counts, x_round, y_round))  0.65 us
  transfers between devices with their start and end apart: 8, of which 4 were waited for; matrix products, arithmetic and copies ran while one was open for 0% of the time, Pallas kernels for 21%

profile of v20, /device:TPU:0, one launch (start us, length us, event | category | flops | bytes accessed | tf_op | source)
XLA Modules:
  0.0 21.4 jit_solution(10299304806646466737)
XLA Ops:
  0.0 1.3 %first.1 = (f32[2,2,16,16,256]{4,3,2,1,0:T(8,128)S(1)}, bf16[2,16,16,256]{3,2,1,0:T(8,128)(2,1)S(1)}, bf16[2,16,16,256]{3,2,1,0:T(8,128)(2,1)S(1)}, bf16[16,16,2...) custom-call(f32[32,32,256]{2,1,0:T(8,128)} %density.1, ...), custom_call_target="tpu_custom_call" | custom-call | tf_op jit(solution)/shard_map/first/pallas_call | solution.py:366
  1.3 3.0 %collective-permute-start = (bf16[16,16,256]{2,1,0:T(8,128)(2,1)S(1)}, bf16[16,16,256]{2,1,0:T(8,128)(2,1)S(1)}, u32[]{:S(2)}, u32[]{:S(2)}) collective-permute-start(bf16[16,16,256]{2,1,0:T(8,128)(2,1)S(1)} %get-tuple-element.43), channel_id=1, source_target_pairs={{0,1},{2,3},{4,5},{6,7},{8,9},{10,11},{12,13},{14,15},{16,17},{18,... | collective-permute-start | bytes 393224 | tf_op jit(solution)/shard_map/ppermute | solution.py:360
  4.3 1.6 %collective-permute-start.1 = (bf16[2,16,16,256]{3,2,1,0:T(8,128)(2,1)S(1)}, bf16[2,16,16,256]{3,2,1,0:T(8,128)(2,1)S(1)}, u32[]{:S(2)}, u32[]{:S(2)}) collective-permute-start(bf16[2,16,16,256]{3,2,1,0:T(8,128)(2,1)S(1)} %get-tuple-element.44.xs0), channel_id=1, source_target_pairs={{0,2},{1,3},{4,6},{5,7},{8,10},{9,11},{12,14},{13,15},{16,18},{17,... | collective-permute-start | bytes 786440 | tf_op jit(solution)/shard_map/ppermute | solution.py:360
  5.9 0.5 %collective-permute-start.3 = (bf16[16,16,256]{2,1,0:T(8,128)(2,1)S(1)}, bf16[16,16,256]{2,1,0:T(8,128)(2,1)S(1)}, u32[]{:S(2)}, u32[]{:S(2)}) collective-permute-start(bf16[16,16,256]{2,1,0:T(8,128)(2,1)S(1)} %get-tuple-element.54), channel_id=1, source_target_pairs={{0,1},{2,3},{4,5},{6,7},{8,9},{10,11},{12,13},{14,15},{16,17},{18,... | collective-permute-start | bytes 393224 | tf_op jit(solution)/shard_map/ppermute | solution.py:360
  6.4 0.3 %prepare.1 = (f32[8,24,128]{2,1,0:T(8,128)S(1)}, s32[2,2,8,128]{3,2,1,0:T(8,128)S(1)}, s32[4,8,32]{2,1,0:T(8,128)S(1)}) custom-call(f32[4,8]{1,0:T(4,128)S(1)} %get-tuple-element.34.centre, f32[4,8]{1,0:T(4,128)S(1)} %get-tuple-element.35.width, f32[3,4,8]{2,1,0:T(4,128)S(1)} %get-tuple-element.36.colour, f32[4,8]{1,0:T(4,128)S(1)} %get-tuple-element.37.opacity, ...), custom_call_target="tpu_custom_call" | custom-call | tf_op jit(solution)/shard_map/prepare/pallas_call | solution.py:379
  6.7 1.1 %cells1.1 = (f32[3,2,16,16,256]{4,3,2,1,0:T(8,128)S(1)}, f32[16,128]{1,0:T(8,128)S(1)}) custom-call(f32[2,2,16,16,256]{4,3,2,1,0:T(8,128)S(1)} %get-tuple-element.46.held, f32[8,24,128]{2,1,0:T(8,128)S(1)} %get-tuple-element.47.table, s32[2,2,8,128]{3,2,1,0:T(8,128)S(1)} %get-tuple-element.48.signs), custom_call_target="tpu_custom_call" | custom-call | flops 262144 | bytes 262144 | tf_op jit(solution)/shard_map/cells1/pallas_call | solution.py:396
  7.8 0.0 collective-permute-done.near0
  7.8 0.0 copy-start
  7.8 3.2 %collective-permute-start.4 = (bf16[16,16,256]{2,1,0:T(8,128)(2,1)S(1)}, bf16[16,16,256]{2,1,0:T(8,128)(2,1)S(1)}, u32[]{:S(2)}, u32[]{:S(2)}) collective-permute-start(bf16[16,16,256]{2,1,0:T(8,128)(2,1)S(1)} %collective-permute-done.near0), channel_id=1, source_target_pairs={{0,2},{1,3},{4,6},{5,7},{8,10},{9,11},{12,14},{13,15},{16,18},{17,... | collective-permute-start | bytes 393224 | tf_op jit(solution)/shard_map/ppermute | solution.py:360
  11.1 0.0 collective-permute-start.5
  11.1 1.1 %cells0.1 = (f32[3,2,16,16,256]{4,3,2,1,0:T(8,128)S(1)}, f32[16,128]{1,0:T(8,128)S(1)}) custom-call(f32[2,2,16,16,256]{4,3,2,1,0:T(8,128)S(1)} %get-tuple-element.46.held, f32[8,24,128]{2,1,0:T(8,128)S(1)} %get-tuple-element.47.table, s32[2,2,8,128]{3,2,1,0:T(8,128)S(1)} %get-tuple-element.48.signs), custom_call_target="tpu_custom_call" | custom-call | flops 26214400000 | bytes 2621440000 | tf_op jit(solution)/shard_map/cells0/pallas_call | solution.py:396
  12.2 0.6 %matrices.1 = (bf16[256,768]{1,0:T(8,128)(2,1)S(1)}, bf16[256,768]{1,0:T(8,128)(2,1)S(1)}) custom-call(f32[2,33]{1,0:T(2,128)S(1)} %convert_element_type.3.taps), custom_call_target="tpu_custom_call" | custom-call | tf_op jit(solution)/shard_map/matrices/pallas_call | solution.py:387
  12.8 0.6 %collective-permute-done.1.halo0 = bf16[2,16,16,256]{3,2,1,0:T(8,128)(2,1)S(1)} collective-permute-done((bf16[2,16,16,256]{3,2,1,0:T(8,128)(2,1)S(1)}, bf16[2,16,16,256]{3,2,1,0:T(8,128)(2,1)S(1)}, u32[]{:S(2)}, u32[]{:S(2)}) %collective-permute-start.1) | collective-permute-done | bytes 262176 | tf_op jit(solution)/shard_map/ppermute | solution.py:360
  13.4 0.0 collective-permute-done.2.halo1
  13.4 1.1 %own.1 = (f32[3,16,128]{2,1,0:T(8,128)S(1)}, f32[1,2,256,256]{3,2,1,0:T(8,128)S(1)}) custom-call(bf16[256,768]{1,0:T(8,128)(2,1)S(1)} %get-tuple-element.41.mx.refs_0_, bf16[256,768]{1,0:T(8,128)(2,1)S(1)} %get-tuple-element.42.my.refs_1_, bf16[2,16,16,256]{3,2,1,0:T(8,128)(2,1)S(1)} %get-tuple-element.44.xs0, ...), custom_call_target="tpu_custom_call" | custom-call | tf_op jit(solution)/shard_map/own/pallas_call | solution.py:420
  14.5 0.0 collective-permute-done.3.near1
  14.5 0.3 %near0.1.refs_2_ = f32[2,256,256]{2,1,0:T(8,128)S(1)} custom-call(bf16[256,768]{1,0:T(8,128)(2,1)S(1)} %get-tuple-element.41.mx.refs_0_, bf16[16,16,256]{2,1,0:T(8,128)(2,1)S(1)} %collective-permute-done.near0, f32[1,2,256,256]{3,2,1,0:T(8,128)S(1)} %get-tuple-element.50.order.refs_3_, bf16[16,16,256]{2,1,0:T(8,128)(2,1)S(1)} %collective-permute-done.3.near1), custom_call_target="tpu_custom_call" | custom-call | tf_op jit(solution)/shard_map/near0/pallas_call | solution.py:428
  14.8 0.1 collective-permute-done.4.refs_4_
  14.9 0.8 %last.1 = (f32[2,4,8,32]{3,2,1,0:T(8,128)S(1)}, f32[2,4,8,32]{3,2,1,0:T(8,128)S(1)}) custom-call(bf16[256,768]{1,0:T(8,128)(2,1)S(1)} %get-tuple-element.41.mx.refs_0_, bf16[256,768]{1,0:T(8,128)(2,1)S(1)} %get-tuple-element.42.my.refs_1_, f32[2,256,256]{2,1,0:T(8,128)S(1)} %near0.1.refs_2_, f32[1,2,256,256]{3,2,1,0:T(8,128)S(1)} %get-tuple-element.50.order.refs_3_, ...), custom_call_target="tpu_custom_call" | custom-call | tf_op jit(solution)/shard_map/last/pallas_call | solution.py:442
  15.7 0.1 collective-permute-start.6
  15.8 1.2 %collective-permute-done.6.theirs = f32[2,4,8,32]{3,2,1,0:T(8,128)S(1)} collective-permute-done((f32[2,4,8,32]{3,2,1,0:T(8,128)S(1)}, f32[2,4,8,32]{3,2,1,0:T(8,128)S(1)}, u32[]{:S(2)}, u32[]{:S(2)}) %collective-permute-start.6) | collective-permute-done | bytes 8224 | tf_op jit(solution)/shard_map/ppermute | solution.py:451
  17.0 1.6 %collective-permute-start.7 = (f32[1,4,8,32]{3,2,1,0:T(8,128)S(1)}, f32[1,4,8,32]{3,2,1,0:T(8,128)S(1)}, u32[]{:S(2)}, u32[]{:S(2)}) collective-permute-start(f32[1,4,8,32]{3,2,1,0:T(8,128)S(1)} %get-tuple-element.62), channel_id=1, source_target_pairs={{0,16},{8,24},{16,0},{24,8},{1,17},{9,25},{17,1},{25,9},{2,18},{10... | collective-permute-start | bytes 12296 | tf_op jit(solution)/shard_map/ppermute | solution.py:451
  18.5 2.2 %collective-permute-done.7.theirs = f32[1,4,8,32]{3,2,1,0:T(8,128)S(1)} collective-permute-done((f32[1,4,8,32]{3,2,1,0:T(8,128)S(1)}, f32[1,4,8,32]{3,2,1,0:T(8,128)S(1)}, u32[]{:S(2)}, u32[]{:S(2)}) %collective-permute-start.7) | collective-permute-done | bytes 4128 | tf_op jit(solution)/shard_map/ppermute | solution.py:451
  20.8 0.6 %merge1.1 = f32[4,1,1,8,32]{4,3,2,1,0:T(8,128)} custom-call(s32[4,8,32]{2,1,0:T(8,128)S(1)} %get-tuple-element.40.order_map, f32[1,4,8,32]{3,2,1,0:T(8,128)S(1)} %get-tuple-element.61.kept, f32[1,4,8,32]{3,2,1,0:T(8,128)S(1)} %collective-permute-done.7.theirs), custom_call_target="tpu_custom_call" | custom-call | tf_op jit(solution)/shard_map/merge1/pallas_call | solution.py:454
  (5 shorter events, 0.0 us)
Async XLA Ops:
  1.3 6.5 %collective-permute-start = (bf16[16,16,256]{2,1,0:T(8,128)(2,1)S(1)}, bf16[16,16,256]{2,1,0:T(8,128)(2,1)S(1)}, u32[]{:S(2)}, u32[]{:S(2)}) collective-permute-start(bf16[16,16,256]{2,1,0:T(8,128)(2,1)S(1)} %get-tuple-element.43), channel_id=1, source_target_pairs={{0,1},{2,3},{4,5},{6,7},{8,9},{10,11},{12,13},{14,15},{16,17},{18,... | collective-permute-start | bytes 393224 | tf_op jit(solution)/shard_map/ppermute | solution.py:360
  4.3 9.1 %collective-permute-start.1 = (bf16[2,16,16,256]{3,2,1,0:T(8,128)(2,1)S(1)}, bf16[2,16,16,256]{3,2,1,0:T(8,128)(2,1)S(1)}, u32[]{:S(2)}, u32[]{:S(2)}) collective-permute-start(bf16[2,16,16,256]{3,2,1,0:T(8,128)(2,1)S(1)} %get-tuple-element.44.xs0), channel_id=1, source_target_pairs={{0,2},{1,3},{4,6},{5,7},{8,10},{9,11},{12,14},{13,15},{16,18},{17,... | collective-permute-start | bytes 786440 | tf_op jit(solution)/shard_map/ppermute | solution.py:360
  5.9 7.5 %collective-permute-start.2 = (bf16[2,16,16,256]{3,2,1,0:T(8,128)(2,1)S(1)}, bf16[2,16,16,256]{3,2,1,0:T(8,128)(2,1)S(1)}, u32[]{:S(2)}, u32[]{:S(2)}) collective-permute-start(bf16[2,16,16,256]{3,2,1,0:T(8,128)(2,1)S(1)} %get-tuple-element.45.xs1), channel_id=1, source_target_pairs={{2,4},{3,5},{10,12},{11,13},{18,20},{19,21},{26,28},{27,29},{0,8},... | collective-permute-start | bytes 786440 | tf_op jit(solution)/shard_map/ppermute | solution.py:360
  5.9 8.6 %collective-permute-start.3 = (bf16[16,16,256]{2,1,0:T(8,128)(2,1)S(1)}, bf16[16,16,256]{2,1,0:T(8,128)(2,1)S(1)}, u32[]{:S(2)}, u32[]{:S(2)}) collective-permute-start(bf16[16,16,256]{2,1,0:T(8,128)(2,1)S(1)} %get-tuple-element.54), channel_id=1, source_target_pairs={{0,1},{2,3},{4,5},{6,7},{8,9},{10,11},{12,13},{14,15},{16,17},{18,... | collective-permute-start | bytes 393224 | tf_op jit(solution)/shard_map/ppermute | solution.py:360
  7.8 4.4 %copy-start = (bf16[2,33]{1,0:T(2,128)(2,1)S(1)}, bf16[2,33]{1,0:T(2,128)(2,1)}, u32[]{:S(2)}) copy-start(bf16[2,33]{1,0:T(2,128)(2,1)} %param.9) | copy-start | bytes 400
  7.8 7.1 %collective-permute-start.4 = (bf16[16,16,256]{2,1,0:T(8,128)(2,1)S(1)}, bf16[16,16,256]{2,1,0:T(8,128)(2,1)S(1)}, u32[]{:S(2)}, u32[]{:S(2)}) collective-permute-start(bf16[16,16,256]{2,1,0:T(8,128)(2,1)S(1)} %collective-permute-done.near0), channel_id=1, source_target_pairs={{0,2},{1,3},{4,6},{5,7},{8,10},{9,11},{12,14},{13,15},{16,18},{17,... | collective-permute-start | bytes 393224 | tf_op jit(solution)/shard_map/ppermute | solution.py:360
  11.1 3.9 %collective-permute-start.5 = (bf16[16,16,256]{2,1,0:T(8,128)(2,1)S(1)}, bf16[16,16,256]{2,1,0:T(8,128)(2,1)S(1)}, u32[]{:S(2)}, u32[]{:S(2)}) collective-permute-start(bf16[16,16,256]{2,1,0:T(8,128)(2,1)S(1)} %get-tuple-element.54), channel_id=1, source_target_pairs={{2,5},{3,4},{10,13},{11,12},{18,21},{19,20},{26,29},{27,28},{0,8},... | collective-permute-start | bytes 393224 | tf_op jit(solution)/shard_map/ppermute | solution.py:360
  15.7 1.3 %collective-permute-start.6 = (f32[2,4,8,32]{3,2,1,0:T(8,128)S(1)}, f32[2,4,8,32]{3,2,1,0:T(8,128)S(1)}, u32[]{:S(2)}, u32[]{:S(2)}) collective-permute-start(f32[2,4,8,32]{3,2,1,0:T(8,128)S(1)} %get-tuple-element.60), channel_id=1, source_target_pairs={{0,8},{8,0},{16,24},{24,16},{1,9},{9,1},{17,25},{25,17},{2,10},{10... | collective-permute-start | bytes 24584 | tf_op jit(solution)/shard_map/ppermute | solution.py:451
  17.0 3.8 %collective-permute-start.7 = (f32[1,4,8,32]{3,2,1,0:T(8,128)S(1)}, f32[1,4,8,32]{3,2,1,0:T(8,128)S(1)}, u32[]{:S(2)}, u32[]{:S(2)}) collective-permute-start(f32[1,4,8,32]{3,2,1,0:T(8,128)S(1)} %get-tuple-element.62), channel_id=1, source_target_pairs={{0,16},{8,24},{16,0},{24,8},{1,17},{9,25},{17,1},{25,9},{2,18},{10... | collective-permute-start | bytes 12296 | tf_op jit(solution)/shard_map/ppermute | solution.py:451

commit v21 on v20

--- a/solution.py
+++ b/solution.py
@@ -70,20 +70,23 @@
 
 def first_kernel(rim, rounds, density, *refs):
     place = Place()
-    n_tables = (len(refs) - 4 - 2 * rounds) // 2
+    n_tables = (len(refs) - 7 - 2 * rounds) // 2
     tables, refs = refs[:n_tables], refs[n_tables:]
     held, xs, refs = refs[0], refs[1:3], refs[3:]
     strips, refs = refs[:2 * rounds], refs[2 * rounds:]
-    tables_out, sems = refs[:n_tables], refs[n_tables]
+    looked_up, local_tables, sems = refs[:3], refs[3:-1], refs[-1]
     copies = []
     for g in range(2):
         for h in range(2):
             rows = density.at[half_rows(place, rim, h), group_rows(place, rim, g), :]
             copies.append(pltpu.make_async_copy(rows, held.at[g, h], sems.at[2 * g + h]))
-    for i, (src, dst) in enumerate(zip(tables, tables_out)):
+    for i, (src, dst) in enumerate(zip(tables, local_tables)):
         copies.append(pltpu.make_async_copy(src, dst, sems.at[4 + i]))
-    for copy in copies:
+    for copy in copies[4:] + copies[:4]:
         copy.start()
+    for copy in copies[4:]:
+        copy.wait()
+    look_up(rim, place, *local_tables, *looked_up)
     for g in range(2):
         for h in range(2):
             copies[2 * g + h].wait()
@@ -91,8 +94,6 @@
             xs[h][g] = coarse
             if g < rounds:
                 strips[2 * g + h][...] = coarse
-    for copy in copies[4:]:
-        copy.wait()
 
 
 def toeplitz(taps, rim):
@@ -133,10 +134,9 @@
     mx[...], my[...] = blur_matrices(rim, Place(), padded[...])
 
 
-def prepare_kernel(
-    rim, centre, width, colour, opacity, brick_tf, view_order, table, signs, order_map
+def look_up(
+    rim, place, centre, width, colour, opacity, brick_tf, view_order, table, signs, order_map
 ):
-    place = Place()
     wide = width[...]
     rows = [centre[...], (-LOG2E) / (wide * wide), opacity[...] * (-LOG2E)]
     rows += [colour[c] * 0.5 for c in range(3)]
@@ -363,26 +363,21 @@
     tables = (tf_centre.T, tf_width.T, tf_color.T, tf_opacity.T, brick_tf, view_order)
     piece = struct((rim, rim, rows_z), BF16)
     both = struct((2, rim, rim, rows_z), BF16)
+    bricks = rows_z // 128
     held, xs0, xs1, *refs = call(
         functools.partial(first_kernel, rim, rounds),
         "first",
         [HBM] * (1 + len(tables)),
         [struct((2, 2, rim, rim, rows_z), F32), both, both]
         + [piece] * (2 * rounds)
-        + [struct(t.shape, t.dtype) for t in tables],
-        [pltpu.SemaphoreType.DMA((4 + len(tables),))],
+        + [struct((4 * bricks, 6 * bumps, 128), F32), struct((2, 2, 8, 128), jnp.int32)]
+        + [struct((depth_count, block, rows_y), jnp.int32)],
+        [pltpu.VMEM(t.shape, t.dtype) for t in tables]
+        + [pltpu.SemaphoreType.DMA((4 + len(tables),))],
     )(in_hbm(density), *[in_hbm(t) for t in tables])
-    strips, tables = refs[:2 * rounds], refs[2 * rounds:]
+    strips, (table, signs, order_map) = refs[:2 * rounds], refs[2 * rounds:]
     near = [[swap(strips[2 * r], None, r), None] for r in range(rounds)]
 
-    bricks = rows_z // 128
-    table, signs, order_map = call(
-        functools.partial(prepare_kernel, rim),
-        "prepare",
-        [VMEM] * len(tables),
-        [struct((4 * bricks, 6 * bumps, 128), F32), struct((2, 2, 8, 128), jnp.int32)]
-        + [struct((depth_count, block, rows_y), jnp.int32)],
-    )(*tables)
     halo_x = [swap(cells, h, None) for h, cells in enumerate((xs0, xs1))]
     mx, my = call(
         functools.partial(matrices_kernel, rim),

time: 21.8 us -> 21.9 us (level)
  waiting for transfers between devices: 4.1 us -> 4.67 us
  starting transfers between devices: 9.96 us -> 9.7 us
    ppermute x6, waiting for transfers between devices: 0.65 us -> 1.22 us  [swap(): return lax.ppermute(piece, axes, swaps(counts, x_round, y_round))]
    pallas_call x1 -> x0, Pallas kernels: 0.26 us -> none  [per_device(): call(functools.partial(prepare_kernel, rim), 'prepare', [VMEM] * len(tabl...]
    ppermute x6, starting transfers between devices: 8.33 us -> 8.08 us  [swap(): return lax.ppermute(piece, axes, swaps(counts, x_round, y_round))]
  transfers between devices with their start and end apart: 8 -> 8, of which waited for: 4 -> 4; matrix products, arithmetic and copies ran while one was open for 0% -> 0% of each run, Pallas kernels for 21% -> 20%
where the time goes in v21:
time: 21.9 us; the launch traced here: 21.5 us
  starting transfers between devices  9.7 us (44%)
  Pallas kernels  7.05 us (32%)
  waiting for transfers between devices  4.67 us (21%)
    ppermute x6, starting transfers between devices, swap(): return lax.ppermute(piece, axes, swaps(counts, x_round, y_round))  8.08 us
    ppermute x2, waiting for transfers between devices, per_device(): lax.ppermute(given, 'depth', [(i, i ^ 1 << level) for i in range(depth_co...  3.44 us
    pallas_call x2, Pallas kernels, per_device(): call(functools.partial(cells_kernel, rim, bumps, g), f'cells{g}', [VMEM]...  2.25 us
    ppermute x2, starting transfers between devices, per_device(): lax.ppermute(given, 'depth', [(i, i ^ 1 << level) for i in range(depth_co...  1.63 us
    pallas_call x1, Pallas kernels, per_device(): call(functools.partial(first_kernel, rim, rounds), 'first', [HBM] * (1 +...  1.38 us
    ppermute x6, waiting for transfers between devices, swap(): return lax.ppermute(piece, axes, swaps(counts, x_round, y_round))  1.22 us
    pallas_call x1, Pallas kernels, per_device(): call(functools.partial(own_kernel, rim, early), 'own', [VMEM] * (7 if ear...  1.1 us
    pallas_call x1, Pallas kernels, per_device(): call(functools.partial(last_kernel, rim, depth_count), 'last', [VMEM] * 1...  0.77 us
  transfers between devices with their start and end apart: 8, of which 4 were waited for; matrix products, arithmetic and copies ran while one was open for 0% of the time, Pallas kernels for 20%

profile of v21, /device:TPU:0, one launch (start us, length us, event | category | flops | bytes accessed | tf_op | source)
XLA Modules:
  0.0 21.5 jit_solution(17920533710938385308)
XLA Ops:
  0.0 1.4 %first.1 = (f32[2,2,16,16,256]{4,3,2,1,0:T(8,128)S(1)}, bf16[2,16,16,256]{3,2,1,0:T(8,128)(2,1)S(1)}, bf16[2,16,16,256]{3,2,1,0:T(8,128)(2,1)S(1)}, bf16[16,16,2...) custom-call(f32[32,32,256]{2,1,0:T(8,128)} %density.1, ...), custom_call_target="tpu_custom_call" | custom-call | tf_op jit(solution)/shard_map/first/pallas_call | solution.py:367
  1.4 3.0 %collective-permute-start = (bf16[16,16,256]{2,1,0:T(8,128)(2,1)S(1)}, bf16[16,16,256]{2,1,0:T(8,128)(2,1)S(1)}, u32[]{:S(2)}, u32[]{:S(2)}) collective-permute-start(bf16[16,16,256]{2,1,0:T(8,128)(2,1)S(1)} %get-tuple-element.31), channel_id=1, source_target_pairs={{0,1},{2,3},{4,5},{6,7},{8,9},{10,11},{12,13},{14,15},{16,17},{18,... | collective-permute-start | bytes 393224 | tf_op jit(solution)/shard_map/ppermute | solution.py:360
  4.4 1.6 %collective-permute-start.1 = (bf16[2,16,16,256]{3,2,1,0:T(8,128)(2,1)S(1)}, bf16[2,16,16,256]{3,2,1,0:T(8,128)(2,1)S(1)}, u32[]{:S(2)}, u32[]{:S(2)}) collective-permute-start(bf16[2,16,16,256]{3,2,1,0:T(8,128)(2,1)S(1)} %get-tuple-element.32.xs0), channel_id=1, source_target_pairs={{0,2},{1,3},{4,6},{5,7},{8,10},{9,11},{12,14},{13,15},{16,18},{17,... | collective-permute-start | bytes 786440 | tf_op jit(solution)/shard_map/ppermute | solution.py:360
  6.0 0.0 collective-permute-start.2
  6.0 0.5 %collective-permute-start.3 = (bf16[16,16,256]{2,1,0:T(8,128)(2,1)S(1)}, bf16[16,16,256]{2,1,0:T(8,128)(2,1)S(1)}, u32[]{:S(2)}, u32[]{:S(2)}) collective-permute-start(bf16[16,16,256]{2,1,0:T(8,128)(2,1)S(1)} %get-tuple-element.42), channel_id=1, source_target_pairs={{0,1},{2,3},{4,5},{6,7},{8,9},{10,11},{12,13},{14,15},{16,17},{18,... | collective-permute-start | bytes 393224 | tf_op jit(solution)/shard_map/ppermute | solution.py:360
  6.5 1.1 %cells1.1 = (f32[3,2,16,16,256]{4,3,2,1,0:T(8,128)S(1)}, f32[16,128]{1,0:T(8,128)S(1)}) custom-call(f32[2,2,16,16,256]{4,3,2,1,0:T(8,128)S(1)} %get-tuple-element.34.held, f32[8,24,128]{2,1,0:T(8,128)S(1)} %get-tuple-element.35.table, s32[2,2,8,128]{3,2,1,0:T(8,128)S(1)} %get-tuple-element.36.signs), custom_call_target="tpu_custom_call" | custom-call | flops 262144 | bytes 262144 | tf_op jit(solution)/shard_map/cells1/pallas_call | solution.py:391
  7.6 0.3 %collective-permute-done.near0 = bf16[16,16,256]{2,1,0:T(8,128)(2,1)S(1)} collective-permute-done((bf16[16,16,256]{2,1,0:T(8,128)(2,1)S(1)}, bf16[16,16,256]{2,1,0:T(8,128)(2,1)S(1)}, u32[]{:S(2)}, u32[]{:S(2)}) %collective-permute-start) | collective-permute-done | bytes 131104 | tf_op jit(solution)/shard_map/ppermute | solution.py:360
  7.9 3.0 %collective-permute-start.4 = (bf16[16,16,256]{2,1,0:T(8,128)(2,1)S(1)}, bf16[16,16,256]{2,1,0:T(8,128)(2,1)S(1)}, u32[]{:S(2)}, u32[]{:S(2)}) collective-permute-start(bf16[16,16,256]{2,1,0:T(8,128)(2,1)S(1)} %collective-permute-done.near0), channel_id=1, source_target_pairs={{0,2},{1,3},{4,6},{5,7},{8,10},{9,11},{12,14},{13,15},{16,18},{17,... | collective-permute-start | bytes 393224 | tf_op jit(solution)/shard_map/ppermute | solution.py:360
  10.9 0.0 collective-permute-start.5
  10.9 1.1 %cells0.1 = (f32[3,2,16,16,256]{4,3,2,1,0:T(8,128)S(1)}, f32[16,128]{1,0:T(8,128)S(1)}) custom-call(f32[2,2,16,16,256]{4,3,2,1,0:T(8,128)S(1)} %get-tuple-element.34.held, f32[8,24,128]{2,1,0:T(8,128)S(1)} %get-tuple-element.35.table, s32[2,2,8,128]{3,2,1,0:T(8,128)S(1)} %get-tuple-element.36.signs), custom_call_target="tpu_custom_call" | custom-call | flops 26214400000 | bytes 2621440000 | tf_op jit(solution)/shard_map/cells0/pallas_call | solution.py:391
  12.0 0.6 %matrices.1 = (bf16[256,768]{1,0:T(8,128)(2,1)S(1)}, bf16[256,768]{1,0:T(8,128)(2,1)S(1)}) custom-call(f32[2,33]{1,0:T(2,128)S(1)} %convert_element_type.3.taps), custom_call_target="tpu_custom_call" | custom-call | tf_op jit(solution)/shard_map/matrices/pallas_call | solution.py:382
  12.7 0.9 %collective-permute-done.1.halo0 = bf16[2,16,16,256]{3,2,1,0:T(8,128)(2,1)S(1)} collective-permute-done((bf16[2,16,16,256]{3,2,1,0:T(8,128)(2,1)S(1)}, bf16[2,16,16,256]{3,2,1,0:T(8,128)(2,1)S(1)}, u32[]{:S(2)}, u32[]{:S(2)}) %collective-permute-start.1) | collective-permute-done | bytes 262176 | tf_op jit(solution)/shard_map/ppermute | solution.py:360
  13.6 0.0 collective-permute-done.2.halo1
  13.6 1.1 %own.1 = (f32[3,16,128]{2,1,0:T(8,128)S(1)}, f32[1,2,256,256]{3,2,1,0:T(8,128)S(1)}) custom-call(bf16[256,768]{1,0:T(8,128)(2,1)S(1)} %get-tuple-element.29.mx.refs_0_, bf16[256,768]{1,0:T(8,128)(2,1)S(1)} %get-tuple-element.30.my.refs_1_, bf16[2,16,16,256]{3,2,1,0:T(8,128)(2,1)S(1)} %get-tuple-element.32.xs0, ...), custom_call_target="tpu_custom_call" | custom-call | tf_op jit(solution)/shard_map/own/pallas_call | solution.py:415
  14.7 0.0 collective-permute-done.3.near1
  14.7 0.3 %near0.1.refs_2_ = f32[2,256,256]{2,1,0:T(8,128)S(1)} custom-call(bf16[256,768]{1,0:T(8,128)(2,1)S(1)} %get-tuple-element.29.mx.refs_0_, bf16[16,16,256]{2,1,0:T(8,128)(2,1)S(1)} %collective-permute-done.near0, f32[1,2,256,256]{3,2,1,0:T(8,128)S(1)} %get-tuple-element.38.order.refs_3_, bf16[16,16,256]{2,1,0:T(8,128)(2,1)S(1)} %collective-permute-done.3.near1), custom_call_target="tpu_custom_call" | custom-call | tf_op jit(solution)/shard_map/near0/pallas_call | solution.py:423
  15.0 0.0 collective-permute-done.4.refs_4_
  15.0 0.0 collective-permute-done.5.refs_5_
  15.0 0.8 %last.1 = (f32[2,4,8,32]{3,2,1,0:T(8,128)S(1)}, f32[2,4,8,32]{3,2,1,0:T(8,128)S(1)}) custom-call(bf16[256,768]{1,0:T(8,128)(2,1)S(1)} %get-tuple-element.29.mx.refs_0_, bf16[256,768]{1,0:T(8,128)(2,1)S(1)} %get-tuple-element.30.my.refs_1_, f32[2,256,256]{2,1,0:T(8,128)S(1)} %near0.1.refs_2_, f32[1,2,256,256]{3,2,1,0:T(8,128)S(1)} %get-tuple-element.38.order.refs_3_, ...), custom_call_target="tpu_custom_call" | custom-call | tf_op jit(solution)/shard_map/last/pallas_call | solution.py:437
  15.8 0.1 collective-permute-start.6
  15.9 1.2 %collective-permute-done.6.theirs = f32[2,4,8,32]{3,2,1,0:T(8,128)S(1)} collective-permute-done((f32[2,4,8,32]{3,2,1,0:T(8,128)S(1)}, f32[2,4,8,32]{3,2,1,0:T(8,128)S(1)}, u32[]{:S(2)}, u32[]{:S(2)}) %collective-permute-start.6) | collective-permute-done | bytes 8224 | tf_op jit(solution)/shard_map/ppermute | solution.py:446
  17.1 1.6 %collective-permute-start.7 = (f32[1,4,8,32]{3,2,1,0:T(8,128)S(1)}, f32[1,4,8,32]{3,2,1,0:T(8,128)S(1)}, u32[]{:S(2)}, u32[]{:S(2)}) collective-permute-start(f32[1,4,8,32]{3,2,1,0:T(8,128)S(1)} %get-tuple-element.50), channel_id=1, source_target_pairs={{0,16},{8,24},{16,0},{24,8},{1,17},{9,25},{17,1},{25,9},{2,18},{10... | collective-permute-start | bytes 12296 | tf_op jit(solution)/shard_map/ppermute | solution.py:446
  18.7 2.2 %collective-permute-done.7.theirs = f32[1,4,8,32]{3,2,1,0:T(8,128)S(1)} collective-permute-done((f32[1,4,8,32]{3,2,1,0:T(8,128)S(1)}, f32[1,4,8,32]{3,2,1,0:T(8,128)S(1)}, u32[]{:S(2)}, u32[]{:S(2)}) %collective-permute-start.7) | collective-permute-done | bytes 4128 | tf_op jit(solution)/shard_map/ppermute | solution.py:446
  20.9 0.6 %merge1.1 = f32[4,1,1,8,32]{4,3,2,1,0:T(8,128)} custom-call(s32[4,8,32]{2,1,0:T(8,128)S(1)} %get-tuple-element.28.order_map, f32[1,4,8,32]{3,2,1,0:T(8,128)S(1)} %get-tuple-element.49.kept, f32[1,4,8,32]{3,2,1,0:T(8,128)S(1)} %collective-permute-done.7.theirs), custom_call_target="tpu_custom_call" | custom-call | tf_op jit(solution)/shard_map/merge1/pallas_call | solution.py:449
  (4 shorter events, 0.0 us)
Async XLA Ops:
  1.4 6.5 %collective-permute-start = (bf16[16,16,256]{2,1,0:T(8,128)(2,1)S(1)}, bf16[16,16,256]{2,1,0:T(8,128)(2,1)S(1)}, u32[]{:S(2)}, u32[]{:S(2)}) collective-permute-start(bf16[16,16,256]{2,1,0:T(8,128)(2,1)S(1)} %get-tuple-element.31), channel_id=1, source_target_pairs={{0,1},{2,3},{4,5},{6,7},{8,9},{10,11},{12,13},{14,15},{16,17},{18,... | collective-permute-start | bytes 393224 | tf_op jit(solution)/shard_map/ppermute | solution.py:360
  4.4 9.2 %collective-permute-start.1 = (bf16[2,16,16,256]{3,2,1,0:T(8,128)(2,1)S(1)}, bf16[2,16,16,256]{3,2,1,0:T(8,128)(2,1)S(1)}, u32[]{:S(2)}, u32[]{:S(2)}) collective-permute-start(bf16[2,16,16,256]{3,2,1,0:T(8,128)(2,1)S(1)} %get-tuple-element.32.xs0), channel_id=1, source_target_pairs={{0,2},{1,3},{4,6},{5,7},{8,10},{9,11},{12,14},{13,15},{16,18},{17,... | collective-permute-start | bytes 786440 | tf_op jit(solution)/shard_map/ppermute | solution.py:360
  6.0 7.6 %collective-permute-start.2 = (bf16[2,16,16,256]{3,2,1,0:T(8,128)(2,1)S(1)}, bf16[2,16,16,256]{3,2,1,0:T(8,128)(2,1)S(1)}, u32[]{:S(2)}, u32[]{:S(2)}) collective-permute-start(bf16[2,16,16,256]{3,2,1,0:T(8,128)(2,1)S(1)} %get-tuple-element.33.xs1), channel_id=1, source_target_pairs={{2,4},{3,5},{10,12},{11,13},{18,20},{19,21},{26,28},{27,29},{0,8},... | collective-permute-start | bytes 786440 | tf_op jit(solution)/shard_map/ppermute | solution.py:360
  6.0 8.7 %collective-permute-start.3 = (bf16[16,16,256]{2,1,0:T(8,128)(2,1)S(1)}, bf16[16,16,256]{2,1,0:T(8,128)(2,1)S(1)}, u32[]{:S(2)}, u32[]{:S(2)}) collective-permute-start(bf16[16,16,256]{2,1,0:T(8,128)(2,1)S(1)} %get-tuple-element.42), channel_id=1, source_target_pairs={{0,1},{2,3},{4,5},{6,7},{8,9},{10,11},{12,13},{14,15},{16,17},{18,... | collective-permute-start | bytes 393224 | tf_op jit(solution)/shard_map/ppermute | solution.py:360
  7.9 4.1 %copy-start = (bf16[2,33]{1,0:T(2,128)(2,1)S(1)}, bf16[2,33]{1,0:T(2,128)(2,1)}, u32[]{:S(2)}) copy-start(bf16[2,33]{1,0:T(2,128)(2,1)} %param.9) | copy-start | bytes 400
  7.9 7.1 %collective-permute-start.4 = (bf16[16,16,256]{2,1,0:T(8,128)(2,1)S(1)}, bf16[16,16,256]{2,1,0:T(8,128)(2,1)S(1)}, u32[]{:S(2)}, u32[]{:S(2)}) collective-permute-start(bf16[16,16,256]{2,1,0:T(8,128)(2,1)S(1)} %collective-permute-done.near0), channel_id=1, source_target_pairs={{0,2},{1,3},{4,6},{5,7},{8,10},{9,11},{12,14},{13,15},{16,18},{17,... | collective-permute-start | bytes 393224 | tf_op jit(solution)/shard_map/ppermute | solution.py:360
  10.9 4.2 %collective-permute-start.5 = (bf16[16,16,256]{2,1,0:T(8,128)(2,1)S(1)}, bf16[16,16,256]{2,1,0:T(8,128)(2,1)S(1)}, u32[]{:S(2)}, u32[]{:S(2)}) collective-permute-start(bf16[16,16,256]{2,1,0:T(8,128)(2,1)S(1)} %get-tuple-element.42), channel_id=1, source_target_pairs={{2,5},{3,4},{10,13},{11,12},{18,21},{19,20},{26,29},{27,28},{0,8},... | collective-permute-start | bytes 393224 | tf_op jit(solution)/shard_map/ppermute | solution.py:360
  15.8 1.3 %collective-permute-start.6 = (f32[2,4,8,32]{3,2,1,0:T(8,128)S(1)}, f32[2,4,8,32]{3,2,1,0:T(8,128)S(1)}, u32[]{:S(2)}, u32[]{:S(2)}) collective-permute-start(f32[2,4,8,32]{3,2,1,0:T(8,128)S(1)} %get-tuple-element.48), channel_id=1, source_target_pairs={{0,8},{8,0},{16,24},{24,16},{1,9},{9,1},{17,25},{25,17},{2,10},{10... | collective-permute-start | bytes 24584 | tf_op jit(solution)/shard_map/ppermute | solution.py:446
  17.1 3.8 %collective-permute-start.7 = (f32[1,4,8,32]{3,2,1,0:T(8,128)S(1)}, f32[1,4,8,32]{3,2,1,0:T(8,128)S(1)}, u32[]{:S(2)}, u32[]{:S(2)}) collective-permute-start(f32[1,4,8,32]{3,2,1,0:T(8,128)S(1)} %get-tuple-element.50), channel_id=1, source_target_pairs={{0,16},{8,24},{16,0},{24,8},{1,17},{9,25},{17,1},{25,9},{2,18},{10... | collective-permute-start | bytes 12296 | tf_op jit(solution)/shard_map/ppermute | solution.py:446

commit v22 on v21

--- a/solution.py
+++ b/solution.py
@@ -404,8 +404,8 @@
     corner = [[None, None] for r in range(rounds)]
     for r in range(rounds):
         near[r][1] = swap(strips[2 * r + 1], None, r)
-        strip, arrived, total[1] = lax.optimization_barrier(
-            (strips[2 * r + 1], near[r][0], total[1])
+        strip, arrived, mx, total[1] = lax.optimization_barrier(
+            (strips[2 * r + 1], near[r][0], mx, total[1])
         )
         corner[r] = [swap(arrived, 0, None), swap(strip, 1, r)]
 

time: 21.9 us -> 21.9 us (level)
  waiting for transfers between devices: 4.67 us -> 4.38 us
  starting transfers between devices: 9.7 us -> 9.96 us
    ppermute x6, waiting for transfers between devices: 1.22 us -> 0.94 us  [swap(): return lax.ppermute(piece, axes, swaps(counts, x_round, y_round))]
    ppermute x6, starting transfers between devices: 8.08 us -> 8.33 us  [swap(): return lax.ppermute(piece, axes, swaps(counts, x_round, y_round))]
where the time goes in v22:
time: 21.9 us; the launch traced here: 21.5 us
  starting transfers between devices  9.96 us (45%)
  Pallas kernels  7.05 us (32%)
  waiting for transfers between devices  4.38 us (20%)
    ppermute x6, starting transfers between devices, swap(): return lax.ppermute(piece, axes, swaps(counts, x_round, y_round))  8.33 us
    ppermute x2, waiting for transfers between devices, per_device(): lax.ppermute(given, 'depth', [(i, i ^ 1 << level) for i in range(depth_co...  3.44 us
    pallas_call x2, Pallas kernels, per_device(): call(functools.partial(cells_kernel, rim, bumps, g), f'cells{g}', [VMEM]...  2.25 us
    ppermute x2, starting transfers between devices, per_device(): lax.ppermute(given, 'depth', [(i, i ^ 1 << level) for i in range(depth_co...  1.63 us
    pallas_call x1, Pallas kernels, per_device(): call(functools.partial(first_kernel, rim, rounds), 'first', [HBM] * (1 +...  1.4 us
    pallas_call x1, Pallas kernels, per_device(): call(functools.partial(own_kernel, rim, early), 'own', [VMEM] * (7 if ear...  1.1 us
    ppermute x6, waiting for transfers between devices, swap(): return lax.ppermute(piece, axes, swaps(counts, x_round, y_round))  0.94 us
    pallas_call x1, Pallas kernels, per_device(): call(functools.partial(last_kernel, rim, depth_count), 'last', [VMEM] * 1...  0.76 us
  transfers between devices with their start and end apart: 8, of which 4 were waited for; matrix products, arithmetic and copies ran while one was open for 0% of the time, Pallas kernels for 20%

profile of v22, /device:TPU:0, one launch (start us, length us, event | category | flops | bytes accessed | tf_op | source)
XLA Modules:
  0.0 21.5 jit_solution(2379682911765605653)
XLA Ops:
  0.0 1.4 %first.1 = (f32[2,2,16,16,256]{4,3,2,1,0:T(8,128)S(1)}, bf16[2,16,16,256]{3,2,1,0:T(8,128)(2,1)S(1)}, bf16[2,16,16,256]{3,2,1,0:T(8,128)(2,1)S(1)}, bf16[16,16,2...) custom-call(f32[32,32,256]{2,1,0:T(8,128)} %density.1, ...), custom_call_target="tpu_custom_call" | custom-call | tf_op jit(solution)/shard_map/first/pallas_call | solution.py:367
  1.4 3.0 %collective-permute-start = (bf16[16,16,256]{2,1,0:T(8,128)(2,1)S(1)}, bf16[16,16,256]{2,1,0:T(8,128)(2,1)S(1)}, u32[]{:S(2)}, u32[]{:S(2)}) collective-permute-start(bf16[16,16,256]{2,1,0:T(8,128)(2,1)S(1)} %get-tuple-element.31), channel_id=1, source_target_pairs={{0,1},{2,3},{4,5},{6,7},{8,9},{10,11},{12,13},{14,15},{16,17},{18,... | collective-permute-start | bytes 393224 | tf_op jit(solution)/shard_map/ppermute | solution.py:360
  4.4 1.6 %collective-permute-start.1 = (bf16[2,16,16,256]{3,2,1,0:T(8,128)(2,1)S(1)}, bf16[2,16,16,256]{3,2,1,0:T(8,128)(2,1)S(1)}, u32[]{:S(2)}, u32[]{:S(2)}) collective-permute-start(bf16[2,16,16,256]{3,2,1,0:T(8,128)(2,1)S(1)} %get-tuple-element.39.xs0), channel_id=1, source_target_pairs={{0,2},{1,3},{4,6},{5,7},{8,10},{9,11},{12,14},{13,15},{16,18},{17,... | collective-permute-start | bytes 786440 | tf_op jit(solution)/shard_map/ppermute | solution.py:360
  6.0 0.0 collective-permute-start.2
  6.0 0.5 %collective-permute-start.3 = (bf16[16,16,256]{2,1,0:T(8,128)(2,1)S(1)}, bf16[16,16,256]{2,1,0:T(8,128)(2,1)S(1)}, u32[]{:S(2)}, u32[]{:S(2)}) collective-permute-start(bf16[16,16,256]{2,1,0:T(8,128)(2,1)S(1)} %get-tuple-element.44), channel_id=1, source_target_pairs={{0,1},{2,3},{4,5},{6,7},{8,9},{10,11},{12,13},{14,15},{16,17},{18,... | collective-permute-start | bytes 393224 | tf_op jit(solution)/shard_map/ppermute | solution.py:360
  6.5 1.1 %cells1.1 = (f32[3,2,16,16,256]{4,3,2,1,0:T(8,128)S(1)}, f32[16,128]{1,0:T(8,128)S(1)}) custom-call(f32[2,2,16,16,256]{4,3,2,1,0:T(8,128)S(1)} %get-tuple-element.33.held, f32[8,24,128]{2,1,0:T(8,128)S(1)} %get-tuple-element.34.table, s32[2,2,8,128]{3,2,1,0:T(8,128)S(1)} %get-tuple-element.35.signs), custom_call_target="tpu_custom_call" | custom-call | flops 262144 | bytes 262144 | tf_op jit(solution)/shard_map/cells1/pallas_call | solution.py:391
  7.7 0.6 %matrices.1 = (bf16[256,768]{1,0:T(8,128)(2,1)S(1)}, bf16[256,768]{1,0:T(8,128)(2,1)S(1)}) custom-call(f32[2,33]{1,0:T(2,128)S(1)} %convert_element_type.3.taps), custom_call_target="tpu_custom_call" | custom-call | tf_op jit(solution)/shard_map/matrices/pallas_call | solution.py:382
  8.3 0.0 collective-permute-done.near0
  8.3 3.2 %collective-permute-start.4 = (bf16[16,16,256]{2,1,0:T(8,128)(2,1)S(1)}, bf16[16,16,256]{2,1,0:T(8,128)(2,1)S(1)}, u32[]{:S(2)}, u32[]{:S(2)}) collective-permute-start(bf16[16,16,256]{2,1,0:T(8,128)(2,1)S(1)} %collective-permute-done.near0), channel_id=1, source_target_pairs={{0,2},{1,3},{4,6},{5,7},{8,10},{9,11},{12,14},{13,15},{16,18},{17,... | collective-permute-start | bytes 393224 | tf_op jit(solution)/shard_map/ppermute | solution.py:360
  11.5 0.0 collective-permute-start.5
  11.5 1.1 %cells0.1 = (f32[3,2,16,16,256]{4,3,2,1,0:T(8,128)S(1)}, f32[16,128]{1,0:T(8,128)S(1)}) custom-call(f32[2,2,16,16,256]{4,3,2,1,0:T(8,128)S(1)} %get-tuple-element.33.held, f32[8,24,128]{2,1,0:T(8,128)S(1)} %get-tuple-element.34.table, s32[2,2,8,128]{3,2,1,0:T(8,128)S(1)} %get-tuple-element.35.signs), custom_call_target="tpu_custom_call" | custom-call | flops 26214400000 | bytes 2621440000 | tf_op jit(solution)/shard_map/cells0/pallas_call | solution.py:391
  12.7 0.5 %collective-permute-done.1.halo0 = bf16[2,16,16,256]{3,2,1,0:T(8,128)(2,1)S(1)} collective-permute-done((bf16[2,16,16,256]{3,2,1,0:T(8,128)(2,1)S(1)}, bf16[2,16,16,256]{3,2,1,0:T(8,128)(2,1)S(1)}, u32[]{:S(2)}, u32[]{:S(2)}) %collective-permute-start.1) | collective-permute-done | bytes 262176 | tf_op jit(solution)/shard_map/ppermute | solution.py:360
  13.1 0.0 collective-permute-done.2.halo1
  13.1 1.1 %own.1 = (f32[3,16,128]{2,1,0:T(8,128)S(1)}, f32[1,2,256,256]{3,2,1,0:T(8,128)S(1)}) custom-call(bf16[256,768]{1,0:T(8,128)(2,1)S(1)} %get-tuple-element.37.mx.refs_0_, bf16[256,768]{1,0:T(8,128)(2,1)S(1)} %get-tuple-element.38.my.refs_1_, bf16[2,16,16,256]{3,2,1,0:T(8,128)(2,1)S(1)} %get-tuple-element.39.xs0, ...), custom_call_target="tpu_custom_call" | custom-call | tf_op jit(solution)/shard_map/own/pallas_call | solution.py:415
  14.3 0.0 collective-permute-done.3.near1
  14.3 0.3 %near0.1.refs_2_ = f32[2,256,256]{2,1,0:T(8,128)S(1)} custom-call(bf16[256,768]{1,0:T(8,128)(2,1)S(1)} %get-tuple-element.37.mx.refs_0_, bf16[16,16,256]{2,1,0:T(8,128)(2,1)S(1)} %collective-permute-done.near0, f32[1,2,256,256]{3,2,1,0:T(8,128)S(1)} %get-tuple-element.42.order.refs_3_, bf16[16,16,256]{2,1,0:T(8,128)(2,1)S(1)} %collective-permute-done.3.near1), custom_call_target="tpu_custom_call" | custom-call | tf_op jit(solution)/shard_map/near0/pallas_call | solution.py:423
  14.6 0.4 %collective-permute-done.4.refs_4_ = bf16[16,16,256]{2,1,0:T(8,128)(2,1)S(1)} collective-permute-done((bf16[16,16,256]{2,1,0:T(8,128)(2,1)S(1)}, bf16[16,16,256]{2,1,0:T(8,128)(2,1)S(1)}, u32[]{:S(2)}, u32[]{:S(2)}) %collective-permute-start.4) | collective-permute-done | bytes 131104 | tf_op jit(solution)/shard_map/ppermute | solution.py:360
  15.0 0.0 collective-permute-done.5.refs_5_
  15.0 0.8 %last.1 = (f32[2,4,8,32]{3,2,1,0:T(8,128)S(1)}, f32[2,4,8,32]{3,2,1,0:T(8,128)S(1)}) custom-call(bf16[256,768]{1,0:T(8,128)(2,1)S(1)} %get-tuple-element.37.mx.refs_0_, bf16[256,768]{1,0:T(8,128)(2,1)S(1)} %get-tuple-element.38.my.refs_1_, f32[2,256,256]{2,1,0:T(8,128)S(1)} %near0.1.refs_2_, f32[1,2,256,256]{3,2,1,0:T(8,128)S(1)} %get-tuple-element.42.order.refs_3_, ...), custom_call_target="tpu_custom_call" | custom-call | tf_op jit(solution)/shard_map/last/pallas_call | solution.py:437
  15.8 0.1 collective-permute-start.6
  15.9 1.2 %collective-permute-done.6.theirs = f32[2,4,8,32]{3,2,1,0:T(8,128)S(1)} collective-permute-done((f32[2,4,8,32]{3,2,1,0:T(8,128)S(1)}, f32[2,4,8,32]{3,2,1,0:T(8,128)S(1)}, u32[]{:S(2)}, u32[]{:S(2)}) %collective-permute-start.6) | collective-permute-done | bytes 8224 | tf_op jit(solution)/shard_map/ppermute | solution.py:446
  17.1 1.6 %collective-permute-start.7 = (f32[1,4,8,32]{3,2,1,0:T(8,128)S(1)}, f32[1,4,8,32]{3,2,1,0:T(8,128)S(1)}, u32[]{:S(2)}, u32[]{:S(2)}) collective-permute-start(f32[1,4,8,32]{3,2,1,0:T(8,128)S(1)} %get-tuple-element.52), channel_id=1, source_target_pairs={{0,16},{8,24},{16,0},{24,8},{1,17},{9,25},{17,1},{25,9},{2,18},{10... | collective-permute-start | bytes 12296 | tf_op jit(solution)/shard_map/ppermute | solution.py:446
  18.6 2.2 %collective-permute-done.7.theirs = f32[1,4,8,32]{3,2,1,0:T(8,128)S(1)} collective-permute-done((f32[1,4,8,32]{3,2,1,0:T(8,128)S(1)}, f32[1,4,8,32]{3,2,1,0:T(8,128)S(1)}, u32[]{:S(2)}, u32[]{:S(2)}) %collective-permute-start.7) | collective-permute-done | bytes 4128 | tf_op jit(solution)/shard_map/ppermute | solution.py:446
  20.9 0.6 %merge1.1 = f32[4,1,1,8,32]{4,3,2,1,0:T(8,128)} custom-call(s32[4,8,32]{2,1,0:T(8,128)S(1)} %get-tuple-element.29.order_map, f32[1,4,8,32]{3,2,1,0:T(8,128)S(1)} %get-tuple-element.51.kept, f32[1,4,8,32]{3,2,1,0:T(8,128)S(1)} %collective-permute-done.7.theirs), custom_call_target="tpu_custom_call" | custom-call | tf_op jit(solution)/shard_map/merge1/pallas_call | solution.py:449
  (4 shorter events, 0.0 us)
Async XLA Ops:
  0.0 7.7 %copy-start = (bf16[2,33]{1,0:T(2,128)(2,1)S(1)}, bf16[2,33]{1,0:T(2,128)(2,1)}, u32[]{:S(2)}) copy-start(bf16[2,33]{1,0:T(2,128)(2,1)} %param.9) | copy-start | bytes 400
  1.4 6.9 %collective-permute-start = (bf16[16,16,256]{2,1,0:T(8,128)(2,1)S(1)}, bf16[16,16,256]{2,1,0:T(8,128)(2,1)S(1)}, u32[]{:S(2)}, u32[]{:S(2)}) collective-permute-start(bf16[16,16,256]{2,1,0:T(8,128)(2,1)S(1)} %get-tuple-element.31), channel_id=1, source_target_pairs={{0,1},{2,3},{4,5},{6,7},{8,9},{10,11},{12,13},{14,15},{16,17},{18,... | collective-permute-start | bytes 393224 | tf_op jit(solution)/shard_map/ppermute | solution.py:360
  4.4 8.7 %collective-permute-start.1 = (bf16[2,16,16,256]{3,2,1,0:T(8,128)(2,1)S(1)}, bf16[2,16,16,256]{3,2,1,0:T(8,128)(2,1)S(1)}, u32[]{:S(2)}, u32[]{:S(2)}) collective-permute-start(bf16[2,16,16,256]{3,2,1,0:T(8,128)(2,1)S(1)} %get-tuple-element.39.xs0), channel_id=1, source_target_pairs={{0,2},{1,3},{4,6},{5,7},{8,10},{9,11},{12,14},{13,15},{16,18},{17,... | collective-permute-start | bytes 786440 | tf_op jit(solution)/shard_map/ppermute | solution.py:360
  6.0 7.1 %collective-permute-start.2 = (bf16[2,16,16,256]{3,2,1,0:T(8,128)(2,1)S(1)}, bf16[2,16,16,256]{3,2,1,0:T(8,128)(2,1)S(1)}, u32[]{:S(2)}, u32[]{:S(2)}) collective-permute-start(bf16[2,16,16,256]{3,2,1,0:T(8,128)(2,1)S(1)} %get-tuple-element.40.xs1), channel_id=1, source_target_pairs={{2,4},{3,5},{10,12},{11,13},{18,20},{19,21},{26,28},{27,29},{0,8},... | collective-permute-start | bytes 786440 | tf_op jit(solution)/shard_map/ppermute | solution.py:360
  6.0 8.2 %collective-permute-start.3 = (bf16[16,16,256]{2,1,0:T(8,128)(2,1)S(1)}, bf16[16,16,256]{2,1,0:T(8,128)(2,1)S(1)}, u32[]{:S(2)}, u32[]{:S(2)}) collective-permute-start(bf16[16,16,256]{2,1,0:T(8,128)(2,1)S(1)} %get-tuple-element.44), channel_id=1, source_target_pairs={{0,1},{2,3},{4,5},{6,7},{8,9},{10,11},{12,13},{14,15},{16,17},{18,... | collective-permute-start | bytes 393224 | tf_op jit(solution)/shard_map/ppermute | solution.py:360
  8.3 6.7 %collective-permute-start.4 = (bf16[16,16,256]{2,1,0:T(8,128)(2,1)S(1)}, bf16[16,16,256]{2,1,0:T(8,128)(2,1)S(1)}, u32[]{:S(2)}, u32[]{:S(2)}) collective-permute-start(bf16[16,16,256]{2,1,0:T(8,128)(2,1)S(1)} %collective-permute-done.near0), channel_id=1, source_target_pairs={{0,2},{1,3},{4,6},{5,7},{8,10},{9,11},{12,14},{13,15},{16,18},{17,... | collective-permute-start | bytes 393224 | tf_op jit(solution)/shard_map/ppermute | solution.py:360
  11.5 3.5 %collective-permute-start.5 = (bf16[16,16,256]{2,1,0:T(8,128)(2,1)S(1)}, bf16[16,16,256]{2,1,0:T(8,128)(2,1)S(1)}, u32[]{:S(2)}, u32[]{:S(2)}) collective-permute-start(bf16[16,16,256]{2,1,0:T(8,128)(2,1)S(1)} %get-tuple-element.44), channel_id=1, source_target_pairs={{2,5},{3,4},{10,13},{11,12},{18,21},{19,20},{26,29},{27,28},{0,8},... | collective-permute-start | bytes 393224 | tf_op jit(solution)/shard_map/ppermute | solution.py:360
  15.8 1.3 %collective-permute-start.6 = (f32[2,4,8,32]{3,2,1,0:T(8,128)S(1)}, f32[2,4,8,32]{3,2,1,0:T(8,128)S(1)}, u32[]{:S(2)}, u32[]{:S(2)}) collective-permute-start(f32[2,4,8,32]{3,2,1,0:T(8,128)S(1)} %get-tuple-element.50), channel_id=1, source_target_pairs={{0,8},{8,0},{16,24},{24,16},{1,9},{9,1},{17,25},{25,17},{2,10},{10... | collective-permute-start | bytes 24584 | tf_op jit(solution)/shard_map/ppermute | solution.py:446
  17.1 3.8 %collective-permute-start.7 = (f32[1,4,8,32]{3,2,1,0:T(8,128)S(1)}, f32[1,4,8,32]{3,2,1,0:T(8,128)S(1)}, u32[]{:S(2)}, u32[]{:S(2)}) collective-permute-start(f32[1,4,8,32]{3,2,1,0:T(8,128)S(1)} %get-tuple-element.52), channel_id=1, source_target_pairs={{0,16},{8,24},{16,0},{24,8},{1,17},{9,25},{17,1},{25,9},{2,18},{10... | collective-permute-start | bytes 12296 | tf_op jit(solution)/shard_map/ppermute | solution.py:446

commit v23 on v22

--- a/solution.py
+++ b/solution.py
@@ -82,7 +82,7 @@
             copies.append(pltpu.make_async_copy(rows, held.at[g, h], sems.at[2 * g + h]))
     for i, (src, dst) in enumerate(zip(tables, local_tables)):
         copies.append(pltpu.make_async_copy(src, dst, sems.at[4 + i]))
-    for copy in copies[4:] + copies[:4]:
+    for copy in copies:
         copy.start()
     for copy in copies[4:]:
         copy.wait()

time: 21.9 us -> 22 us (level)
  no operation moved by 1% of the time
where the time goes in v23:
time: 22 us; the launch traced here: 21.6 us
  starting transfers between devices  9.96 us (45%)
  Pallas kernels  7.13 us (32%)
  waiting for transfers between devices  4.37 us (20%)
    ppermute x6, starting transfers between devices, swap(): return lax.ppermute(piece, axes, swaps(counts, x_round, y_round))  8.33 us
    ppermute x2, waiting for transfers between devices, per_device(): lax.ppermute(given, 'depth', [(i, i ^ 1 << level) for i in range(depth_co...  3.44 us
    pallas_call x2, Pallas kernels, per_device(): call(functools.partial(cells_kernel, rim, bumps, g), f'cells{g}', [VMEM]...  2.25 us
    ppermute x2, starting transfers between devices, per_device(): lax.ppermute(given, 'depth', [(i, i ^ 1 << level) for i in range(depth_co...  1.63 us
    pallas_call x1, Pallas kernels, per_device(): call(functools.partial(first_kernel, rim, rounds), 'first', [HBM] * (1 +...  1.47 us
    pallas_call x1, Pallas kernels, per_device(): call(functools.partial(own_kernel, rim, early), 'own', [VMEM] * (7 if ear...  1.1 us
    ppermute x6, waiting for transfers between devices, swap(): return lax.ppermute(piece, axes, swaps(counts, x_round, y_round))  0.93 us
    pallas_call x1, Pallas kernels, per_device(): call(functools.partial(last_kernel, rim, depth_count), 'last', [VMEM] * 1...  0.76 us
  transfers between devices with their start and end apart: 8, of which 4 were waited for; matrix products, arithmetic and copies ran while one was open for 0% of the time, Pallas kernels for 20%

profile of v23, /device:TPU:0, one launch (start us, length us, event | category | flops | bytes accessed | tf_op | source)
XLA Modules:
  0.0 21.6 jit_solution(5133916722923336007)
XLA Ops:
  0.0 1.5 %first.1 = (f32[2,2,16,16,256]{4,3,2,1,0:T(8,128)S(1)}, bf16[2,16,16,256]{3,2,1,0:T(8,128)(2,1)S(1)}, bf16[2,16,16,256]{3,2,1,0:T(8,128)(2,1)S(1)}, bf16[16,16,2...) custom-call(f32[32,32,256]{2,1,0:T(8,128)} %density.1, ...), custom_call_target="tpu_custom_call" | custom-call | tf_op jit(solution)/shard_map/first/pallas_call | solution.py:367
  1.5 3.0 %collective-permute-start = (bf16[16,16,256]{2,1,0:T(8,128)(2,1)S(1)}, bf16[16,16,256]{2,1,0:T(8,128)(2,1)S(1)}, u32[]{:S(2)}, u32[]{:S(2)}) collective-permute-start(bf16[16,16,256]{2,1,0:T(8,128)(2,1)S(1)} %get-tuple-element.31), channel_id=1, source_target_pairs={{0,1},{2,3},{4,5},{6,7},{8,9},{10,11},{12,13},{14,15},{16,17},{18,... | collective-permute-start | bytes 393224 | tf_op jit(solution)/shard_map/ppermute | solution.py:360
  4.5 1.6 %collective-permute-start.1 = (bf16[2,16,16,256]{3,2,1,0:T(8,128)(2,1)S(1)}, bf16[2,16,16,256]{3,2,1,0:T(8,128)(2,1)S(1)}, u32[]{:S(2)}, u32[]{:S(2)}) collective-permute-start(bf16[2,16,16,256]{3,2,1,0:T(8,128)(2,1)S(1)} %get-tuple-element.39.xs0), channel_id=1, source_target_pairs={{0,2},{1,3},{4,6},{5,7},{8,10},{9,11},{12,14},{13,15},{16,18},{17,... | collective-permute-start | bytes 786440 | tf_op jit(solution)/shard_map/ppermute | solution.py:360
  6.1 0.0 collective-permute-start.2
  6.1 0.5 %collective-permute-start.3 = (bf16[16,16,256]{2,1,0:T(8,128)(2,1)S(1)}, bf16[16,16,256]{2,1,0:T(8,128)(2,1)S(1)}, u32[]{:S(2)}, u32[]{:S(2)}) collective-permute-start(bf16[16,16,256]{2,1,0:T(8,128)(2,1)S(1)} %get-tuple-element.44), channel_id=1, source_target_pairs={{0,1},{2,3},{4,5},{6,7},{8,9},{10,11},{12,13},{14,15},{16,17},{18,... | collective-permute-start | bytes 393224 | tf_op jit(solution)/shard_map/ppermute | solution.py:360
  6.6 1.1 %cells1.1 = (f32[3,2,16,16,256]{4,3,2,1,0:T(8,128)S(1)}, f32[16,128]{1,0:T(8,128)S(1)}) custom-call(f32[2,2,16,16,256]{4,3,2,1,0:T(8,128)S(1)} %get-tuple-element.33.held, f32[8,24,128]{2,1,0:T(8,128)S(1)} %get-tuple-element.34.table, s32[2,2,8,128]{3,2,1,0:T(8,128)S(1)} %get-tuple-element.35.signs), custom_call_target="tpu_custom_call" | custom-call | flops 262144 | bytes 262144 | tf_op jit(solution)/shard_map/cells1/pallas_call | solution.py:391
  7.8 0.6 %matrices.1 = (bf16[256,768]{1,0:T(8,128)(2,1)S(1)}, bf16[256,768]{1,0:T(8,128)(2,1)S(1)}) custom-call(f32[2,33]{1,0:T(2,128)S(1)} %convert_element_type.3.taps), custom_call_target="tpu_custom_call" | custom-call | tf_op jit(solution)/shard_map/matrices/pallas_call | solution.py:382
  8.4 0.0 collective-permute-done.near0
  8.4 3.2 %collective-permute-start.4 = (bf16[16,16,256]{2,1,0:T(8,128)(2,1)S(1)}, bf16[16,16,256]{2,1,0:T(8,128)(2,1)S(1)}, u32[]{:S(2)}, u32[]{:S(2)}) collective-permute-start(bf16[16,16,256]{2,1,0:T(8,128)(2,1)S(1)} %collective-permute-done.near0), channel_id=1, source_target_pairs={{0,2},{1,3},{4,6},{5,7},{8,10},{9,11},{12,14},{13,15},{16,18},{17,... | collective-permute-start | bytes 393224 | tf_op jit(solution)/shard_map/ppermute | solution.py:360
  11.6 0.0 collective-permute-start.5
  11.6 1.1 %cells0.1 = (f32[3,2,16,16,256]{4,3,2,1,0:T(8,128)S(1)}, f32[16,128]{1,0:T(8,128)S(1)}) custom-call(f32[2,2,16,16,256]{4,3,2,1,0:T(8,128)S(1)} %get-tuple-element.33.held, f32[8,24,128]{2,1,0:T(8,128)S(1)} %get-tuple-element.34.table, s32[2,2,8,128]{3,2,1,0:T(8,128)S(1)} %get-tuple-element.35.signs), custom_call_target="tpu_custom_call" | custom-call | flops 26214400000 | bytes 2621440000 | tf_op jit(solution)/shard_map/cells0/pallas_call | solution.py:391
  12.7 0.5 %collective-permute-done.1.halo0 = bf16[2,16,16,256]{3,2,1,0:T(8,128)(2,1)S(1)} collective-permute-done((bf16[2,16,16,256]{3,2,1,0:T(8,128)(2,1)S(1)}, bf16[2,16,16,256]{3,2,1,0:T(8,128)(2,1)S(1)}, u32[]{:S(2)}, u32[]{:S(2)}) %collective-permute-start.1) | collective-permute-done | bytes 262176 | tf_op jit(solution)/shard_map/ppermute | solution.py:360
  13.2 0.0 collective-permute-done.2.halo1
  13.2 1.1 %own.1 = (f32[3,16,128]{2,1,0:T(8,128)S(1)}, f32[1,2,256,256]{3,2,1,0:T(8,128)S(1)}) custom-call(bf16[256,768]{1,0:T(8,128)(2,1)S(1)} %get-tuple-element.37.mx.refs_0_, bf16[256,768]{1,0:T(8,128)(2,1)S(1)} %get-tuple-element.38.my.refs_1_, bf16[2,16,16,256]{3,2,1,0:T(8,128)(2,1)S(1)} %get-tuple-element.39.xs0, ...), custom_call_target="tpu_custom_call" | custom-call | tf_op jit(solution)/shard_map/own/pallas_call | solution.py:415
  14.3 0.0 collective-permute-done.3.near1
  14.3 0.3 %near0.1.refs_2_ = f32[2,256,256]{2,1,0:T(8,128)S(1)} custom-call(bf16[256,768]{1,0:T(8,128)(2,1)S(1)} %get-tuple-element.37.mx.refs_0_, bf16[16,16,256]{2,1,0:T(8,128)(2,1)S(1)} %collective-permute-done.near0, f32[1,2,256,256]{3,2,1,0:T(8,128)S(1)} %get-tuple-element.42.order.refs_3_, bf16[16,16,256]{2,1,0:T(8,128)(2,1)S(1)} %collective-permute-done.3.near1), custom_call_target="tpu_custom_call" | custom-call | tf_op jit(solution)/shard_map/near0/pallas_call | solution.py:423
  14.6 0.4 %collective-permute-done.4.refs_4_ = bf16[16,16,256]{2,1,0:T(8,128)(2,1)S(1)} collective-permute-done((bf16[16,16,256]{2,1,0:T(8,128)(2,1)S(1)}, bf16[16,16,256]{2,1,0:T(8,128)(2,1)S(1)}, u32[]{:S(2)}, u32[]{:S(2)}) %collective-permute-start.4) | collective-permute-done | bytes 131104 | tf_op jit(solution)/shard_map/ppermute | solution.py:360
  15.1 0.0 collective-permute-done.5.refs_5_
  15.1 0.8 %last.1 = (f32[2,4,8,32]{3,2,1,0:T(8,128)S(1)}, f32[2,4,8,32]{3,2,1,0:T(8,128)S(1)}) custom-call(bf16[256,768]{1,0:T(8,128)(2,1)S(1)} %get-tuple-element.37.mx.refs_0_, bf16[256,768]{1,0:T(8,128)(2,1)S(1)} %get-tuple-element.38.my.refs_1_, f32[2,256,256]{2,1,0:T(8,128)S(1)} %near0.1.refs_2_, f32[1,2,256,256]{3,2,1,0:T(8,128)S(1)} %get-tuple-element.42.order.refs_3_, ...), custom_call_target="tpu_custom_call" | custom-call | tf_op jit(solution)/shard_map/last/pallas_call | solution.py:437
  15.9 0.1 collective-permute-start.6
  15.9 1.2 %collective-permute-done.6.theirs = f32[2,4,8,32]{3,2,1,0:T(8,128)S(1)} collective-permute-done((f32[2,4,8,32]{3,2,1,0:T(8,128)S(1)}, f32[2,4,8,32]{3,2,1,0:T(8,128)S(1)}, u32[]{:S(2)}, u32[]{:S(2)}) %collective-permute-start.6) | collective-permute-done | bytes 8224 | tf_op jit(solution)/shard_map/ppermute | solution.py:446
  17.1 1.6 %collective-permute-start.7 = (f32[1,4,8,32]{3,2,1,0:T(8,128)S(1)}, f32[1,4,8,32]{3,2,1,0:T(8,128)S(1)}, u32[]{:S(2)}, u32[]{:S(2)}) collective-permute-start(f32[1,4,8,32]{3,2,1,0:T(8,128)S(1)} %get-tuple-element.52), channel_id=1, source_target_pairs={{0,16},{8,24},{16,0},{24,8},{1,17},{9,25},{17,1},{25,9},{2,18},{10... | collective-permute-start | bytes 12296 | tf_op jit(solution)/shard_map/ppermute | solution.py:446
  18.7 2.2 %collective-permute-done.7.theirs = f32[1,4,8,32]{3,2,1,0:T(8,128)S(1)} collective-permute-done((f32[1,4,8,32]{3,2,1,0:T(8,128)S(1)}, f32[1,4,8,32]{3,2,1,0:T(8,128)S(1)}, u32[]{:S(2)}, u32[]{:S(2)}) %collective-permute-start.7) | collective-permute-done | bytes 4128 | tf_op jit(solution)/shard_map/ppermute | solution.py:446
  21.0 0.6 %merge1.1 = f32[4,1,1,8,32]{4,3,2,1,0:T(8,128)} custom-call(s32[4,8,32]{2,1,0:T(8,128)S(1)} %get-tuple-element.29.order_map, f32[1,4,8,32]{3,2,1,0:T(8,128)S(1)} %get-tuple-element.51.kept, f32[1,4,8,32]{3,2,1,0:T(8,128)S(1)} %collective-permute-done.7.theirs), custom_call_target="tpu_custom_call" | custom-call | tf_op jit(solution)/shard_map/merge1/pallas_call | solution.py:449
  (4 shorter events, 0.0 us)
Async XLA Ops:
  0.0 7.7 %copy-start = (bf16[2,33]{1,0:T(2,128)(2,1)S(1)}, bf16[2,33]{1,0:T(2,128)(2,1)}, u32[]{:S(2)}) copy-start(bf16[2,33]{1,0:T(2,128)(2,1)} %param.9) | copy-start | bytes 400
  1.5 6.9 %collective-permute-start = (bf16[16,16,256]{2,1,0:T(8,128)(2,1)S(1)}, bf16[16,16,256]{2,1,0:T(8,128)(2,1)S(1)}, u32[]{:S(2)}, u32[]{:S(2)}) collective-permute-start(bf16[16,16,256]{2,1,0:T(8,128)(2,1)S(1)} %get-tuple-element.31), channel_id=1, source_target_pairs={{0,1},{2,3},{4,5},{6,7},{8,9},{10,11},{12,13},{14,15},{16,17},{18,... | collective-permute-start | bytes 393224 | tf_op jit(solution)/shard_map/ppermute | solution.py:360
  4.5 8.7 %collective-permute-start.1 = (bf16[2,16,16,256]{3,2,1,0:T(8,128)(2,1)S(1)}, bf16[2,16,16,256]{3,2,1,0:T(8,128)(2,1)S(1)}, u32[]{:S(2)}, u32[]{:S(2)}) collective-permute-start(bf16[2,16,16,256]{3,2,1,0:T(8,128)(2,1)S(1)} %get-tuple-element.39.xs0), channel_id=1, source_target_pairs={{0,2},{1,3},{4,6},{5,7},{8,10},{9,11},{12,14},{13,15},{16,18},{17,... | collective-permute-start | bytes 786440 | tf_op jit(solution)/shard_map/ppermute | solution.py:360
  6.1 7.1 %collective-permute-start.2 = (bf16[2,16,16,256]{3,2,1,0:T(8,128)(2,1)S(1)}, bf16[2,16,16,256]{3,2,1,0:T(8,128)(2,1)S(1)}, u32[]{:S(2)}, u32[]{:S(2)}) collective-permute-start(bf16[2,16,16,256]{3,2,1,0:T(8,128)(2,1)S(1)} %get-tuple-element.40.xs1), channel_id=1, source_target_pairs={{2,4},{3,5},{10,12},{11,13},{18,20},{19,21},{26,28},{27,29},{0,8},... | collective-permute-start | bytes 786440 | tf_op jit(solution)/shard_map/ppermute | solution.py:360
  6.1 8.2 %collective-permute-start.3 = (bf16[16,16,256]{2,1,0:T(8,128)(2,1)S(1)}, bf16[16,16,256]{2,1,0:T(8,128)(2,1)S(1)}, u32[]{:S(2)}, u32[]{:S(2)}) collective-permute-start(bf16[16,16,256]{2,1,0:T(8,128)(2,1)S(1)} %get-tuple-element.44), channel_id=1, source_target_pairs={{0,1},{2,3},{4,5},{6,7},{8,9},{10,11},{12,13},{14,15},{16,17},{18,... | collective-permute-start | bytes 393224 | tf_op jit(solution)/shard_map/ppermute | solution.py:360
  8.4 6.7 %collective-permute-start.4 = (bf16[16,16,256]{2,1,0:T(8,128)(2,1)S(1)}, bf16[16,16,256]{2,1,0:T(8,128)(2,1)S(1)}, u32[]{:S(2)}, u32[]{:S(2)}) collective-permute-start(bf16[16,16,256]{2,1,0:T(8,128)(2,1)S(1)} %collective-permute-done.near0), channel_id=1, source_target_pairs={{0,2},{1,3},{4,6},{5,7},{8,10},{9,11},{12,14},{13,15},{16,18},{17,... | collective-permute-start | bytes 393224 | tf_op jit(solution)/shard_map/ppermute | solution.py:360
  11.6 3.5 %collective-permute-start.5 = (bf16[16,16,256]{2,1,0:T(8,128)(2,1)S(1)}, bf16[16,16,256]{2,1,0:T(8,128)(2,1)S(1)}, u32[]{:S(2)}, u32[]{:S(2)}) collective-permute-start(bf16[16,16,256]{2,1,0:T(8,128)(2,1)S(1)} %get-tuple-element.44), channel_id=1, source_target_pairs={{2,5},{3,4},{10,13},{11,12},{18,21},{19,20},{26,29},{27,28},{0,8},... | collective-permute-start | bytes 393224 | tf_op jit(solution)/shard_map/ppermute | solution.py:360
  15.9 1.3 %collective-permute-start.6 = (f32[2,4,8,32]{3,2,1,0:T(8,128)S(1)}, f32[2,4,8,32]{3,2,1,0:T(8,128)S(1)}, u32[]{:S(2)}, u32[]{:S(2)}) collective-permute-start(f32[2,4,8,32]{3,2,1,0:T(8,128)S(1)} %get-tuple-element.50), channel_id=1, source_target_pairs={{0,8},{8,0},{16,24},{24,16},{1,9},{9,1},{17,25},{25,17},{2,10},{10... | collective-permute-start | bytes 24584 | tf_op jit(solution)/shard_map/ppermute | solution.py:446
  17.1 3.8 %collective-permute-start.7 = (f32[1,4,8,32]{3,2,1,0:T(8,128)S(1)}, f32[1,4,8,32]{3,2,1,0:T(8,128)S(1)}, u32[]{:S(2)}, u32[]{:S(2)}) collective-permute-start(f32[1,4,8,32]{3,2,1,0:T(8,128)S(1)} %get-tuple-element.52), channel_id=1, source_target_pairs={{0,16},{8,24},{16,0},{24,8},{1,17},{9,25},{17,1},{25,9},{2,18},{10... | collective-permute-start | bytes 12296 | tf_op jit(solution)/shard_map/ppermute | solution.py:446
